TPU v7x, 32 devices: a whole 2x2x4 slice. The times are simulated.
32 devices in a mesh: row: 4 (over x, core), col: 8 (over z, y).
Axes of the slice: x: 2, y: 2, z: 4, core: 2. Of those that a mesh axis runs over, the one named last changes fastest.
Arguments:
- source: float32 [32768, 256], P(('row', 'col')), may hold values from -6 to 6
- leaf_in: float32 [128, 128, 256], P(('row', 'col')), may hold values from -0.375 to 0.375
- factors: float32 [7, 128, 128, 256], P(None, ('row', 'col')), may hold values from -0.375 to 0.375
- leaf_out: float32 [128, 256, 128], P(('row', 'col')), may hold values from -0.5 to 0.5
- weight_table: float32 [128, 256], P(('row', 'col')), may hold values from 0.25 to 4
- block_index: int32 [128], P(('row', 'col')), may hold values from 0 to 127
Outputs:
- result: float32 [32768, 256], P(('row', 'col'))
All inputs are finite; a program needn't handle non-finite values.
Results may differ from a plain program's by a relative error of at most 0.0001.
Values sent between devices are 32-bit elements; how exact they have to be, the bound alone decides.
No kernel may reach another device: no remote copies, remote signals or barrier semaphores. Data moves between devices by JAX's collectives and lax.ppermute only.
A program may use at most 64 MiB of HBM per device.

v0:
```python
import jax
import jax.numpy as jnp
from jax import lax
from jax.sharding import PartitionSpec as P

HIGH = lax.Precision.HIGHEST


def partner_2(value, axis, bit):
    return lax.ppermute(value, axis, [(i, i ^ 1 << bit) for i in range(lax.axis_size(axis))])


def local_partner(blocks, level_index):
    stride = 1 << level_index
    node_count = blocks.shape[0]
    shaped = blocks.reshape(node_count // (2 * stride), 2, stride, blocks.shape[1], blocks.shape[2])
    return shaped[:, ::-1].reshape(blocks.shape)


def partner(blocks, level_index, local_bits, col_bits):
    if level_index < local_bits:
        return local_partner(blocks, level_index)
    position = level_index - local_bits
    if position < col_bits:
        return partner_2(blocks, "col", position)
    return partner_2(blocks, "row", position - col_bits)


def body(source, leaf_in, factors, leaf_out, weight_table, block_index):
    level_count = factors.shape[0]
    node_count = leaf_in.shape[0]
    rank_size = leaf_in.shape[1]
    leaf_size = leaf_in.shape[2]
    column_count = source.shape[1]
    local_bits = node_count.bit_length() - 1
    col_bits = lax.axis_size("col").bit_length() - 1
    leaves = source.reshape(node_count, leaf_size, column_count)
    coefficients = jnp.einsum("nrk,nks->nrs", leaf_in, leaves, precision=HIGH)
    for level_index in range(level_count):
        received = partner(coefficients, level_index, local_bits, col_bits)
        stacked = jnp.concatenate([coefficients, received], axis=1)
        coefficients = jnp.einsum("nrk,nks->nrs", factors[level_index], stacked, precision=HIGH)
    image = jnp.einsum("nlr,nrs->nls", leaf_out, coefficients, precision=HIGH)
    whole_table = lax.all_gather(weight_table, ("row", "col"), axis=0, tiled=True)
    profiles = whole_table[block_index]
    scaled = profiles[:, :, None] * image
    adjoint = jnp.einsum("nlr,nls->nrs", leaf_out, scaled, precision=HIGH)
    for level_index in reversed(range(level_count)):
        own_part = factors[level_index][:, :, :rank_size]
        cross_part = factors[level_index][:, :, rank_size:]
        own_cross = jnp.einsum("nrk,nrs->nks", cross_part, adjoint, precision=HIGH)
        cross_term = partner(own_cross, level_index, local_bits, col_bits)
        adjoint = jnp.einsum("nrk,nrs->nks", own_part, adjoint, precision=HIGH) + cross_term
    result = jnp.einsum("nrl,nrs->nls", leaf_in, adjoint, precision=HIGH)
    return result.reshape(node_count * leaf_size, column_count)


def solution(mesh):
    placed = (
        P(("row", "col"), None),
        P(("row", "col"), None, None),
        P(None, ("row", "col"), None, None),
        P(("row", "col"), None, None),
        P(("row", "col"), None),
        P(("row", "col")),
    )
    return jax.shard_map(
        body, mesh=mesh, in_specs=placed, out_specs=P(("row", "col"), None), check_vma=False
    )
```

profile of v0, /device:TPU:0, one launch (start us, length us, event | category | flops | bytes accessed | tf_op | source)
XLA Modules:
  0.0 222.5 jit_solution(57989006901257129)
XLA Ops:
  0.0 0.0 copy-start
  0.0 1.2 copy-done
  1.2 1.8 fusion.53
  3.1 1.8 fusion.7
  4.9 1.8 convolution_bitcast_fusion.16
  6.7 3.0 %collective-permute-start = (f32[4,128,256]{2,1,0:T(8,128)S(1)}, f32[4,128,256]{2,1,0:T(8,128)S(1)}, u32[]{:S(2)}, u32[]{:S(2)}) collective-permute-start(f32[4,128,256]{2,1,0:T(8,128)S(1)} %convolution_bitcast_fusion.16), channel_id=1, source_target_pairs={{0,1},{1,0},{2,3},{3,2},{4,5},{5,4},{6,7},{7,6},{8,9},{9,8},{10,11... | collective-permute-start | bytes 1572872 | tf_op jit(solution)/shard_map/ppermute | solution.py:10
  9.8 11.9 %collective-permute-done = f32[4,128,256]{2,1,0:T(8,128)S(1)} collective-permute-done((f32[4,128,256]{2,1,0:T(8,128)S(1)}, f32[4,128,256]{2,1,0:T(8,128)S(1)}, u32[]{:S(2)}, u32[]{:S(2)}) %collective-permute-start) | collective-permute-done | bytes 524320 | tf_op jit(solution)/shard_map/ppermute | solution.py:10
  21.7 1.8 convolution_bitcast_fusion.15
  23.5 0.0 copy-start.3
  23.5 0.0 copy-start.2
  23.5 1.9 collective-permute-start.1
  25.4 11.3 %collective-permute-done.1 = f32[4,128,256]{2,1,0:T(8,128)S(1)} collective-permute-done((f32[4,128,256]{2,1,0:T(8,128)S(1)}, f32[4,128,256]{2,1,0:T(8,128)S(1)}, u32[]{:S(2)}, u32[]{:S(2)}) %collective-permute-start.1) | collective-permute-done | bytes 524320 | tf_op jit(solution)/shard_map/ppermute | solution.py:10
  36.7 1.8 convolution_bitcast_fusion.14
  38.5 2.6 %collective-permute-start.2 = (f32[4,128,256]{2,1,0:T(8,128)S(1)}, f32[4,128,256]{2,1,0:T(8,128)S(1)}, u32[]{:S(2)}, u32[]{:S(2)}) collective-permute-start(f32[4,128,256]{2,1,0:T(8,128)S(1)} %convolution_bitcast_fusion.14), channel_id=1, source_target_pairs={{0,4},{1,5},{2,6},{3,7},{4,0},{5,1},{6,2},{7,3},{8,12},{9,13},{10,... | collective-permute-start | bytes 1572872 | tf_op jit(solution)/shard_map/ppermute | solution.py:10
  41.1 21.8 %collective-permute-done.2 = f32[4,128,256]{2,1,0:T(8,128)S(1)} collective-permute-done((f32[4,128,256]{2,1,0:T(8,128)S(1)}, f32[4,128,256]{2,1,0:T(8,128)S(1)}, u32[]{:S(2)}, u32[]{:S(2)}) %collective-permute-start.2) | collective-permute-done | bytes 524320 | tf_op jit(solution)/shard_map/ppermute | solution.py:10
  62.9 1.8 convolution_bitcast_fusion.13
  64.7 0.1 collective-permute-start.3
  64.8 1.9 collective-permute-done.3
  66.7 1.8 convolution_bitcast_fusion.12
  68.5 1.2 collective-permute-start.4
  69.6 0.0 copy-done.3
  69.7 0.0 copy-done.2
  69.7 68.3 %all-gather = f32[32,4,256]{2,1,0:T(4,128)S(1)} all-gather(f32[1,4,256]{2,1,0:T(4,128)S(1)} %bitcast.120), channel_id=1, replica_groups=mesh['row'=4,'col'=8] {'row','col'}, dimensions={0}, use_global_device_ids=true | all-gather | bytes 135168 | tf_op jit(solution)/shard_map/all_gather | solution.py:44
  138.1 0.6 gather_fusion
  138.6 0.0 copy-start.1
  138.6 2.3 %slice_bitcast_fusion.6 = (f32[4,128,256]{2,1,0:T(8,128)S(1)}, f32[4,128,256]{2,1,0:T(8,128)S(1)}, f32[4,128,256]{2,1,0:T(8,128)S(1)}, f32[4,128,256]{2,1,0:T(8,...) fusion(f32[7,4,128,256]{3,2,1,0:T(8,128)} %param.8), kind=kLoop, calls=%fused_computation.55 | loop fusion | bytes 7340032 | tf_op jit(solution)/shard_map/squeeze | solution.py:49
  140.9 0.0 collective-permute-done.4
  141.0 2.9 %fusion.26 = f32[4,256,128]{2,1,0:T(8,128)S(1)} fusion(f32[4,128,256]{2,1,0:T(8,128)S(1)} %collective-permute-done.4, f32[4,128,256]{2,1,0:T(8,128)S(1)} %convolution_bitcast_fusion.12, f32[7,4,128,256]{3,2,1,0:T(8,128)} %param.8), kind=kOutput, calls=%fused_computation.45 | convolution fusion | flops 402915328 | bytes 2097152 | tf_op jit(solution)/shard_map/nrk,nks->nrs/dot_general | solution.py:42
  143.9 0.0 copy-done.1
  143.9 1.0 convolution_multiply_fusion
  144.9 1.1 fusion.54
  145.9 0.6 convolution_bitcast_fusion.10
  146.6 1.4 collective-permute-start.5
  148.0 7.8 %collective-permute-done.5 = f32[4,128,256]{1,2,0:T(8,128)S(1)} collective-permute-done((f32[4,128,256]{1,2,0:T(8,128)S(1)}, f32[4,128,256]{1,2,0:T(8,128)S(1)}, u32[]{:S(2)}, u32[]{:S(2)}) %collective-permute-start.5) | collective-permute-done | bytes 524320 | tf_op jit(solution)/shard_map/ppermute | solution.py:10
  155.8 0.6 fusion
  156.4 0.6 convolution_bitcast_fusion.8
  157.0 0.1 collective-permute-start.6
  157.1 1.9 collective-permute-done.6
  159.0 0.6 fusion.1
  159.6 0.6 convolution_bitcast_fusion.6
  160.2 0.1 collective-permute-start.7
  160.3 24.3 %collective-permute-done.7 = f32[4,128,256]{1,2,0:T(8,128)S(1)} collective-permute-done((f32[4,128,256]{1,2,0:T(8,128)S(1)}, f32[4,128,256]{1,2,0:T(8,128)S(1)}, u32[]{:S(2)}, u32[]{:S(2)}) %collective-permute-start.7) | collective-permute-done | bytes 524320 | tf_op jit(solution)/shard_map/ppermute | solution.py:10
  184.6 0.6 fusion.2
  185.2 0.6 convolution_bitcast_fusion.4
  185.8 0.1 collective-permute-start.8
  185.9 13.8 %collective-permute-done.8 = f32[4,128,256]{1,2,0:T(8,128)S(1)} collective-permute-done((f32[4,128,256]{1,2,0:T(8,128)S(1)}, f32[4,128,256]{1,2,0:T(8,128)S(1)}, u32[]{:S(2)}, u32[]{:S(2)}) %collective-permute-start.8) | collective-permute-done | bytes 524320 | tf_op jit(solution)/shard_map/ppermute | solution.py:10
  199.7 0.6 fusion.3
  200.3 0.6 convolution_bitcast_fusion.2
  201.0 0.1 collective-permute-start.9
  201.0 13.0 %collective-permute-done.9 = f32[4,128,256]{1,2,0:T(8,128)S(1)} collective-permute-done((f32[4,128,256]{1,2,0:T(8,128)S(1)}, f32[4,128,256]{1,2,0:T(8,128)S(1)}, u32[]{:S(2)}, u32[]{:S(2)}) %collective-permute-start.9) | collective-permute-done | bytes 524320 | tf_op jit(solution)/shard_map/ppermute | solution.py:10
  214.0 0.6 fusion.4
  214.7 0.6 fusion.33
  215.3 0.8 rev.14
  216.1 1.9 fusion.5
  218.0 0.6 fusion.30
  218.6 0.2 copy.9
  218.8 0.6 fusion.6
  219.5 3.0 %fusion.55 = f32[4,256,256]{1,2,0:T(8,128)} fusion(f32[4,128,256]{2,1,0:T(8,128)S(1)} %fusion.6, f32[4,128,256]{2,1,0:T(8,128)} %param.7), kind=kOutput, calls=%fused_computation.83 | convolution fusion | flops 402653184 | bytes 2097152 | tf_op jit(solution)/shard_map/nrl,nrs->nls/dot_general | solution.py:54
  (6 shorter events, 0.2 us)
Async XLA Ops:
  0.0 1.2 copy-start
  6.7 15.0 %collective-permute-start = (f32[4,128,256]{2,1,0:T(8,128)S(1)}, f32[4,128,256]{2,1,0:T(8,128)S(1)}, u32[]{:S(2)}, u32[]{:S(2)}) collective-permute-start(f32[4,128,256]{2,1,0:T(8,128)S(1)} %convolution_bitcast_fusion.16), channel_id=1, source_target_pairs={{0,1},{1,0},{2,3},{3,2},{4,5},{5,4},{6,7},{7,6},{8,9},{9,8},{10,11... | collective-permute-start | bytes 1572872 | tf_op jit(solution)/shard_map/ppermute | solution.py:10
  23.5 46.1 %copy-start.3 = (s32[4]{0:T(128)S(1)}, s32[4]{0:T(128)}, u32[]{:S(2)}) copy-start(s32[4]{0:T(128)} %param.11) | copy-start | bytes 52
  23.5 46.1 %copy-start.2 = (f32[4,256]{1,0:T(4,128)S(1)}, f32[4,256]{1,0:T(4,128)}, u32[]{:S(2)}) copy-start(f32[4,256]{1,0:T(4,128)} %param.10) | copy-start | bytes 12292
  23.5 13.2 %collective-permute-start.1 = (f32[4,128,256]{2,1,0:T(8,128)S(1)}, f32[4,128,256]{2,1,0:T(8,128)S(1)}, u32[]{:S(2)}, u32[]{:S(2)}) collective-permute-start(f32[4,128,256]{2,1,0:T(8,128)S(1)} %convolution_bitcast_fusion.15), channel_id=1, source_target_pairs={{0,2},{1,3},{2,0},{3,1},{4,6},{5,7},{6,4},{7,5},{8,10},{9,11},{10,... | collective-permute-start | bytes 1572872 | tf_op jit(solution)/shard_map/ppermute | solution.py:10
  38.5 24.4 %collective-permute-start.2 = (f32[4,128,256]{2,1,0:T(8,128)S(1)}, f32[4,128,256]{2,1,0:T(8,128)S(1)}, u32[]{:S(2)}, u32[]{:S(2)}) collective-permute-start(f32[4,128,256]{2,1,0:T(8,128)S(1)} %convolution_bitcast_fusion.14), channel_id=1, source_target_pairs={{0,4},{1,5},{2,6},{3,7},{4,0},{5,1},{6,2},{7,3},{8,12},{9,13},{10,... | collective-permute-start | bytes 1572872 | tf_op jit(solution)/shard_map/ppermute | solution.py:10
  64.7 2.0 collective-permute-start.3
  68.5 72.5 %collective-permute-start.4 = (f32[4,128,256]{2,1,0:T(8,128)S(1)}, f32[4,128,256]{2,1,0:T(8,128)S(1)}, u32[]{:S(2)}, u32[]{:S(2)}) collective-permute-start(f32[4,128,256]{2,1,0:T(8,128)S(1)} %convolution_bitcast_fusion.12), channel_id=1, source_target_pairs={{0,16},{8,24},{16,0},{24,8},{1,17},{9,25},{17,1},{25,9},{2,18},{10... | collective-permute-start | bytes 1572872 | tf_op jit(solution)/shard_map/ppermute | solution.py:10
  138.6 5.2 %copy-start.1 = (f32[4,256,128]{2,1,0:T(8,128)S(1)}, f32[4,256,128]{2,1,0:T(8,128)}, u32[]{:S(2)}) copy-start(f32[4,256,128]{2,1,0:T(8,128)} %param.9) | copy-start | bytes 1572868
  146.6 9.2 %collective-permute-start.5 = (f32[4,128,256]{1,2,0:T(8,128)S(1)}, f32[4,128,256]{1,2,0:T(8,128)S(1)}, u32[]{:S(2)}, u32[]{:S(2)}) collective-permute-start(f32[4,128,256]{1,2,0:T(8,128)S(1)} %convolution_bitcast_fusion.10), channel_id=1, source_target_pairs={{0,16},{8,24},{16,0},{24,8},{1,17},{9,25},{17,1},{25,9},{2,18},{10... | collective-permute-start | bytes 1572872 | tf_op jit(solution)/shard_map/ppermute | solution.py:10
  157.0 2.0 collective-permute-start.6
  160.2 24.3 %collective-permute-start.7 = (f32[4,128,256]{1,2,0:T(8,128)S(1)}, f32[4,128,256]{1,2,0:T(8,128)S(1)}, u32[]{:S(2)}, u32[]{:S(2)}) collective-permute-start(f32[4,128,256]{1,2,0:T(8,128)S(1)} %convolution_bitcast_fusion.6), channel_id=1, source_target_pairs={{0,4},{1,5},{2,6},{3,7},{4,0},{5,1},{6,2},{7,3},{8,12},{9,13},{10,... | collective-permute-start | bytes 1572872 | tf_op jit(solution)/shard_map/ppermute | solution.py:10
  185.8 13.9 %collective-permute-start.8 = (f32[4,128,256]{1,2,0:T(8,128)S(1)}, f32[4,128,256]{1,2,0:T(8,128)S(1)}, u32[]{:S(2)}, u32[]{:S(2)}) collective-permute-start(f32[4,128,256]{1,2,0:T(8,128)S(1)} %convolution_bitcast_fusion.4), channel_id=1, source_target_pairs={{0,2},{1,3},{2,0},{3,1},{4,6},{5,7},{6,4},{7,5},{8,10},{9,11},{10,... | collective-permute-start | bytes 1572872 | tf_op jit(solution)/shard_map/ppermute | solution.py:10
  201.0 13.1 %collective-permute-start.9 = (f32[4,128,256]{1,2,0:T(8,128)S(1)}, f32[4,128,256]{1,2,0:T(8,128)S(1)}, u32[]{:S(2)}, u32[]{:S(2)}) collective-permute-start(f32[4,128,256]{1,2,0:T(8,128)S(1)} %convolution_bitcast_fusion.2), channel_id=1, source_target_pairs={{0,1},{1,0},{2,3},{3,2},{4,5},{5,4},{6,7},{7,6},{8,9},{9,8},{10,11... | collective-permute-start | bytes 1572872 | tf_op jit(solution)/shard_map/ppermute | solution.py:10
where the time goes:
time: 223 us
  waiting for transfers between devices  108 us (48%)
  blocking collectives  68.3 us (31%)
  matrix products  30.4 us (14%)
  starting transfers between devices  10.4 us (5%)
  local copies, waits for them, and re-layouts  5.28 us (2%)
    ppermute x10, waiting for transfers between devices, partner_2(): lax.ppermute(value, axis, [(i, i ^ 1 << bit) for i in range(lax.axis_size...  108 us
    all_gather x1, blocking collectives, body(): lax.all_gather(weight_table, ('row', 'col'), axis=0, tiled=True)  68.3 us
    dot_general x7, matrix products, body(): jnp.einsum('nrk,nks->nrs', factors[level_index], stacked, precision=HIGH)  13.7 us
    ppermute x10, starting transfers between devices, partner_2(): lax.ppermute(value, axis, [(i, i ^ 1 << bit) for i in range(lax.axis_size...  10.4 us
    dot_general x7, matrix products, body(): jnp.einsum('nrk,nrs->nks', own_part, adjoint, precision=HIGH) + cross_term  5.54 us
  transfers between devices with their start and end apart: 10, of which 9 were waited for; matrix products, arithmetic and copies ran while one was open for 1% of the time, Pallas kernels for 0%

commit v1 on v0

v1 whole, which is shorter than its diff:
```python
import jax
import jax.numpy as jnp
from jax import lax
from jax.sharding import PartitionSpec as P

HIGH = lax.Precision.HIGHEST


def exchange(value, axis, bit):
    return lax.ppermute(value, axis, [(i, i ^ 1 << bit) for i in range(lax.axis_size(axis))])


def gather_rows(weight_table, block_index, steps):
    table = weight_table
    col_size = lax.axis_size("col")
    own = lax.axis_index("row") * col_size + lax.axis_index("col")
    rows_each = weight_table.shape[0]
    differs = (block_index // rows_each) ^ own
    place = jnp.zeros_like(block_index)
    for count, (axis, bit) in enumerate(steps):
        table = jnp.concatenate([table, exchange(table, axis, bit)], axis=0)
        shift = bit if axis == "col" else bit + col_size.bit_length() - 1
        place = place | (((differs >> shift) & 1) << count)
    return table[place * rows_each + block_index % rows_each]


def body(source, leaf_in, factors, leaf_out, weight_table, block_index):
    level_count = factors.shape[0]
    node_count, rank_size, leaf_size = leaf_in.shape
    column_count = source.shape[1]
    local_bits = node_count.bit_length() - 1
    col_bits = lax.axis_size("col").bit_length() - 1
    row_bits = lax.axis_size("row").bit_length() - 1
    where = {}
    for level_index in range(local_bits, level_count):
        position = level_index - local_bits
        where[level_index] = ("col", position) if position < col_bits else ("row", position - col_bits)
    steps = [("col", b) for b in reversed(range(col_bits))] + [("row", b) for b in reversed(range(row_bits))]
    profiles = gather_rows(weight_table, block_index, steps)

    leaves = source.reshape(node_count, leaf_size, column_count)
    coefficients = [jnp.dot(leaf_in[j], leaves[j], precision=HIGH) for j in range(node_count)]
    for level_index in range(local_bits):
        coefficients = [
            jnp.dot(
                factors[level_index, j],
                jnp.concatenate([coefficients[j], coefficients[j ^ 1 << level_index]], axis=0),
                precision=HIGH,
            )
            for j in range(node_count)
        ]

    def remote_part(j, value):
        for level_index in range(local_bits, level_count):
            received = exchange(value, *where[level_index])
            value = jnp.dot(factors[level_index, j], jnp.concatenate([value, received], axis=0), precision=HIGH)
        image = jnp.dot(leaf_out[j], value, precision=HIGH)
        scaled = profiles[j][:, None] * image
        value = jnp.einsum("lr,ls->rs", leaf_out[j], scaled, precision=HIGH)
        for level_index in reversed(range(local_bits, level_count)):
            both = jnp.einsum("rk,rs->ks", factors[level_index, j], value, precision=HIGH)
            value = both[:rank_size] + exchange(both[rank_size:], *where[level_index])
        return value

    adjoint = [remote_part(j, coefficients[j]) for j in range(node_count)]
    for level_index in reversed(range(local_bits)):
        both = [jnp.einsum("rk,rs->ks", factors[level_index, j], adjoint[j], precision=HIGH) for j in range(node_count)]
        adjoint = [both[j][:rank_size] + both[j ^ 1 << level_index][rank_size:] for j in range(node_count)]
    result = [jnp.einsum("rl,rs->ls", leaf_in[j], adjoint[j], precision=HIGH) for j in range(node_count)]
    return jnp.concatenate(result, axis=0)


def solution(mesh):
    placed = (
        P(("row", "col"), None),
        P(("row", "col"), None, None),
        P(None, ("row", "col"), None, None),
        P(("row", "col"), None, None),
        P(("row", "col"), None),
        P(("row", "col")),
    )
    return jax.shard_map(
        body, mesh=mesh, in_specs=placed, out_specs=P(("row", "col"), None), check_vma=False
    )
```

time: 223 us -> 147 us (0.66)
  blocking collectives: 68.3 us -> 0 us
  waiting for transfers between devices: 108 us -> 41.9 us
  starting transfers between devices: 10.4 us -> 46.5 us
  matrix products: 30.4 us -> 55.4 us
  local copies, waits for them, and re-layouts: 5.28 us -> 0.85 us
    all_gather x1 -> x0, blocking collectives: 68.3 us -> none  [body(): lax.all_gather(weight_table, ('row', 'col'), axis=0, tiled=True)]
    ppermute x10 -> x45, waiting for transfers between devices: 108 us -> 41.9 us  [exchange(): lax.ppermute(value, axis, [(i, i ^ 1 << bit) for i in range(lax.axis_size...]
    ppermute x10 -> x45, starting transfers between devices: 10.4 us -> 46.5 us  [exchange(): lax.ppermute(value, axis, [(i, i ^ 1 << bit) for i in range(lax.axis_size...]
    dot_general x25 -> x72, matrix products: 30.4 us -> 55.4 us  [the longest x20 19 us: remote_part(): jnp.einsum('rk,rs->ks', factors[level_index, j], value, precision=HIGH)]
    squeeze x1 -> x0, local copies, waits for them, and re-layouts: 2.3 us -> none  [body(): own_part = factors[level_index][:, :, :rank_size]]
  transfers between devices with their start and end apart: 10 -> 45, of which waited for: 9 -> 19; matrix products, arithmetic and copies ran while one was open for 1% -> 37% of each run, Pallas kernels for 0% -> 0%
where the time goes in v1:
time: 147 us
  matrix products  55.4 us (38%)
  starting transfers between devices  46.5 us (32%)
  waiting for transfers between devices  41.9 us (29%)
    ppermute x45, starting transfers between devices, exchange(): lax.ppermute(value, axis, [(i, i ^ 1 << bit) for i in range(lax.axis_size...  46.5 us
    ppermute x45, waiting for transfers between devices, exchange(): lax.ppermute(value, axis, [(i, i ^ 1 << bit) for i in range(lax.axis_size...  41.9 us
    dot_general x20, matrix products, remote_part(): jnp.einsum('rk,rs->ks', factors[level_index, j], value, precision=HIGH)  19 us
    dot_general x20, matrix products, remote_part(): jnp.dot(factors[level_index, j], jnp.concatenate([value, received], axis=...  13.9 us
    dot_general x8, matrix products, body(): jnp.dot(factors[level_index, j], jnp.concatenate([coefficients[j], coeffi...  9.65 us
    dot_general x4, matrix products, body(): jnp.dot(leaf_in[j], leaves[j], precision=HIGH)  5.21 us
    dot_general x8, matrix products, body(): jnp.einsum('rk,rs->ks', factors[level_index, j], adjoint[j], precision=HIGH)  3.1 us
  transfers between devices with their start and end apart: 45, of which 19 were waited for; matrix products, arithmetic and copies ran while one was open for 37% of the time, Pallas kernels for 0%

profile of v1, /device:TPU:0, one launch (start us, length us, event | category | flops | bytes accessed | tf_op | source)
XLA Modules:
  0.0 146.7 jit_solution(3273431162248275809)
XLA Ops:
  0.0 4.0 %collective-permute-start = (f32[4,256]{1,0:T(4,128)}, f32[4,256]{1,0:T(4,128)S(1)}, u32[]{:S(2)}, u32[]{:S(2)}) collective-permute-start(f32[4,256]{1,0:T(4,128)} %param.10), channel_id=1, source_target_pairs={{0,4},{1,5},{2,6},{3,7},{4,0},{5,1},{6,2},{7,3},{8,12},{9,13},{10,... | collective-permute-start | bytes 12296 | tf_op jit(solution)/shard_map/ppermute | solution.py:10
  4.0 1.3 fusion.100
  5.3 1.3 fusion.102
  6.7 1.3 fusion.96
  8.0 1.3 fusion.98
  9.3 1.2 convolution_bitcast_fusion.43
  10.5 1.2 convolution_bitcast_fusion.42
  11.7 1.2 convolution_bitcast_fusion.41
  12.9 1.6 %collective-permute-start.25 = (f32[128,256]{1,0:T(8,128)S(1)}, f32[128,256]{1,0:T(8,128)S(1)}, u32[]{:S(2)}, u32[]{:S(2)}) collective-permute-start(f32[128,256]{1,0:T(8,128)S(1)} %convolution_bitcast_fusion.41), channel_id=1, source_target_pairs={{0,1},{1,0},{2,3},{3,2},{4,5},{5,4},{6,7},{7,6},{8,9},{9,8},{10,11... | collective-permute-start | bytes 393224 | tf_op jit(solution)/shard_map/ppermute | solution.py:10
  14.5 1.2 convolution_bitcast_fusion.36
  16.3 1.2 convolution_bitcast_fusion.55
  17.5 1.2 convolution_bitcast_fusion.54
  18.8 1.6 %collective-permute-start.1 = (f32[8,256]{1,0:T(8,128)S(1)}, f32[8,256]{1,0:T(8,128)S(1)}, u32[]{:S(2)}, u32[]{:S(2)}) collective-permute-start(f32[8,256]{1,0:T(8,128)S(1)} %pad_maximum_fusion.3), channel_id=1, source_target_pairs={{0,2},{1,3},{2,0},{3,1},{4,6},{5,7},{6,4},{7,5},{8,10},{9,11},{10,... | collective-permute-start | bytes 24584 | tf_op jit(solution)/shard_map/ppermute | solution.py:10
  20.4 1.2 convolution_bitcast_fusion.53
  21.6 1.6 %collective-permute-start.5 = (f32[128,256]{1,0:T(8,128)S(1)}, f32[128,256]{1,0:T(8,128)S(1)}, u32[]{:S(2)}, u32[]{:S(2)}) collective-permute-start(f32[128,256]{1,0:T(8,128)S(1)} %convolution_bitcast_fusion.53), channel_id=1, source_target_pairs={{0,1},{1,0},{2,3},{3,2},{4,5},{5,4},{6,7},{7,6},{8,9},{9,8},{10,11... | collective-permute-start | bytes 393224 | tf_op jit(solution)/shard_map/ppermute | solution.py:10
  24.1 1.2 convolution_bitcast_fusion.48
  25.3 1.3 collective-permute-start.15
  26.6 1.3 collective-permute-done.2
  27.9 1.5 %collective-permute-start.3 = (f32[32,256]{1,0:T(8,128)S(1)}, f32[32,256]{1,0:T(8,128)S(1)}, u32[]{:S(2)}, u32[]{:S(2)}) collective-permute-start(f32[32,256]{1,0:T(8,128)S(1)} %pad_maximum_fusion.1), channel_id=1, source_target_pairs={{0,16},{8,24},{16,0},{24,8},{1,17},{9,25},{17,1},{25,9},{2,18},{10... | collective-permute-start | bytes 98312 | tf_op jit(solution)/shard_map/ppermute | solution.py:10
  29.5 2.4 %collective-permute-done.3 = f32[32,256]{1,0:T(8,128)S(1)} collective-permute-done((f32[32,256]{1,0:T(8,128)S(1)}, f32[32,256]{1,0:T(8,128)S(1)}, u32[]{:S(2)}, u32[]{:S(2)}) %collective-permute-start.3) | collective-permute-done | bytes 32800 | tf_op jit(solution)/shard_map/ppermute | solution.py:10
  32.0 1.2 collective-permute-done.4
  33.9 1.4 convolution_bitcast_fusion.40
  35.4 1.2 convolution_bitcast_fusion.35
  36.6 2.0 %collective-permute-start.36 = (f32[128,256]{1,0:T(8,128)S(1)}, f32[128,256]{1,0:T(8,128)S(1)}, u32[]{:S(2)}, u32[]{:S(2)}) collective-permute-start(f32[128,256]{1,0:T(8,128)S(1)} %convolution_bitcast_fusion.35), channel_id=1, source_target_pairs={{0,2},{1,3},{2,0},{3,1},{4,6},{5,7},{6,4},{7,5},{8,10},{9,11},{10,... | collective-permute-start | bytes 393224 | tf_op jit(solution)/shard_map/ppermute | solution.py:10
  38.6 1.2 convolution_bitcast_fusion.52
  40.0 1.2 convolution_bitcast_fusion.47
  41.2 2.0 %collective-permute-start.16 = (f32[128,256]{1,0:T(8,128)S(1)}, f32[128,256]{1,0:T(8,128)S(1)}, u32[]{:S(2)}, u32[]{:S(2)}) collective-permute-start(f32[128,256]{1,0:T(8,128)S(1)} %convolution_bitcast_fusion.47), channel_id=1, source_target_pairs={{0,2},{1,3},{2,0},{3,1},{4,6},{5,7},{6,4},{7,5},{8,10},{9,11},{10,... | collective-permute-start | bytes 393224 | tf_op jit(solution)/shard_map/ppermute | solution.py:10
  43.2 1.2 convolution_bitcast_fusion.39
  44.8 1.2 convolution_bitcast_fusion.34
  46.0 2.7 %collective-permute-start.37 = (f32[128,256]{1,0:T(8,128)S(1)}, f32[128,256]{1,0:T(8,128)S(1)}, u32[]{:S(2)}, u32[]{:S(2)}) collective-permute-start(f32[128,256]{1,0:T(8,128)S(1)} %convolution_bitcast_fusion.34), channel_id=1, source_target_pairs={{0,4},{1,5},{2,6},{3,7},{4,0},{5,1},{6,2},{7,3},{8,12},{9,13},{10,... | collective-permute-start | bytes 393224 | tf_op jit(solution)/shard_map/ppermute | solution.py:10
  48.7 1.2 convolution_bitcast_fusion.51
  51.7 1.6 %collective-permute-start.17 = (f32[128,256]{1,0:T(8,128)S(1)}, f32[128,256]{1,0:T(8,128)S(1)}, u32[]{:S(2)}, u32[]{:S(2)}) collective-permute-start(f32[128,256]{1,0:T(8,128)S(1)} %convolution_bitcast_fusion.46), channel_id=1, source_target_pairs={{0,4},{1,5},{2,6},{3,7},{4,0},{5,1},{6,2},{7,3},{8,12},{9,13},{10,... | collective-permute-start | bytes 393224 | tf_op jit(solution)/shard_map/ppermute | solution.py:10
  53.3 9.4 %collective-permute-done.27 = f32[128,256]{1,0:T(8,128)S(1)} collective-permute-done((f32[128,256]{1,0:T(8,128)S(1)}, f32[128,256]{1,0:T(8,128)S(1)}, u32[]{:S(2)}, u32[]{:S(2)}) %collective-permute-start.27) | collective-permute-done | bytes 131104 | tf_op jit(solution)/shard_map/ppermute | solution.py:10
  63.1 2.4 %collective-permute-done.37 = f32[128,256]{1,0:T(8,128)S(1)} collective-permute-done((f32[128,256]{1,0:T(8,128)S(1)}, f32[128,256]{1,0:T(8,128)S(1)}, u32[]{:S(2)}, u32[]{:S(2)}) %collective-permute-start.37) | collective-permute-done | bytes 131104 | tf_op jit(solution)/shard_map/ppermute | solution.py:10
  65.9 2.2 %collective-permute-done.7 = f32[128,256]{1,0:T(8,128)S(1)} collective-permute-done((f32[128,256]{1,0:T(8,128)S(1)}, f32[128,256]{1,0:T(8,128)S(1)}, u32[]{:S(2)}, u32[]{:S(2)}) %collective-permute-start.7) | collective-permute-done | bytes 131104 | tf_op jit(solution)/shard_map/ppermute | solution.py:10
  70.2 1.5 %collective-permute-start.29 = (f32[128,256]{1,0:T(8,128)S(1)}, f32[128,256]{1,0:T(8,128)S(1)}, u32[]{:S(2)}, u32[]{:S(2)}) collective-permute-start(f32[128,256]{1,0:T(8,128)S(1)} %convolution_bitcast_fusion.37), channel_id=1, source_target_pairs={{0,16},{8,24},{16,0},{24,8},{1,17},{9,25},{17,1},{25,9},{2,18},{10... | collective-permute-start | bytes 393224 | tf_op jit(solution)/shard_map/ppermute | solution.py:10
  73.0 1.5 %collective-permute-start.9 = (f32[128,256]{1,0:T(8,128)S(1)}, f32[128,256]{1,0:T(8,128)S(1)}, u32[]{:S(2)}, u32[]{:S(2)}) collective-permute-start(f32[128,256]{1,0:T(8,128)S(1)} %convolution_bitcast_fusion.49), channel_id=1, source_target_pairs={{0,16},{8,24},{16,0},{24,8},{1,17},{9,25},{17,1},{25,9},{2,18},{10... | collective-permute-start | bytes 393224 | tf_op jit(solution)/shard_map/ppermute | solution.py:10
  78.4 1.5 %collective-permute-start.30 = (f32[128,256]{0,1:T(8,128)S(1)}, f32[128,256]{0,1:T(8,128)S(1)}, u32[]{:S(2)}, u32[]{:S(2)}) collective-permute-start(f32[128,256]{0,1:T(8,128)S(1)} %slice.469), channel_id=1, source_target_pairs={{0,16},{8,24},{16,0},{24,8},{1,17},{9,25},{17,1},{25,9},{2,18},{10... | collective-permute-start | bytes 393224 | tf_op jit(solution)/shard_map/ppermute | solution.py:10
  84.6 1.1 collective-permute-start.10
  89.0 1.6 %collective-permute-done.40 = f32[128,256]{0,1:T(8,128)S(1)} collective-permute-done((f32[128,256]{0,1:T(8,128)S(1)}, f32[128,256]{0,1:T(8,128)S(1)}, u32[]{:S(2)}, u32[]{:S(2)}) %collective-permute-start.40) | collective-permute-done | bytes 131104 | tf_op jit(solution)/shard_map/ppermute | solution.py:10
  91.1 2.3 %collective-permute-done.10 = f32[128,256]{0,1:T(8,128)S(1)} collective-permute-done((f32[128,256]{0,1:T(8,128)S(1)}, f32[128,256]{0,1:T(8,128)S(1)}, u32[]{:S(2)}, u32[]{:S(2)}) %collective-permute-start.10) | collective-permute-done | bytes 131104 | tf_op jit(solution)/shard_map/ppermute | solution.py:10
  93.9 1.9 %collective-permute-done.20 = f32[128,256]{0,1:T(8,128)S(1)} collective-permute-done((f32[128,256]{0,1:T(8,128)S(1)}, f32[128,256]{0,1:T(8,128)S(1)}, u32[]{:S(2)}, u32[]{:S(2)}) %collective-permute-start.20) | collective-permute-done | bytes 131104 | tf_op jit(solution)/shard_map/ppermute | solution.py:10
  95.9 1.3 convolution_bitcast_fusion.24
  97.2 1.3 convolution_bitcast_fusion.16
  98.6 1.3 convolution_bitcast_fusion.10
  99.9 3.0 %collective-permute-start.42 = (f32[128,256]{0,1:T(8,128)S(1)}, f32[128,256]{0,1:T(8,128)S(1)}, u32[]{:S(2)}, u32[]{:S(2)}) collective-permute-start(f32[128,256]{0,1:T(8,128)S(1)} %slice.485), channel_id=1, source_target_pairs={{0,4},{1,5},{2,6},{3,7},{4,0},{5,1},{6,2},{7,3},{8,12},{9,13},{10,... | collective-permute-start | bytes 393224 | tf_op jit(solution)/shard_map/ppermute | solution.py:10
  102.9 1.3 convolution_bitcast_fusion.29
  104.3 1.3 convolution_bitcast_fusion.23
  105.6 3.0 %collective-permute-start.22 = (f32[128,256]{0,1:T(8,128)S(1)}, f32[128,256]{0,1:T(8,128)S(1)}, u32[]{:S(2)}, u32[]{:S(2)}) collective-permute-start(f32[128,256]{0,1:T(8,128)S(1)} %slice.460), channel_id=1, source_target_pairs={{0,4},{1,5},{2,6},{3,7},{4,0},{5,1},{6,2},{7,3},{8,12},{9,13},{10,... | collective-permute-start | bytes 393224 | tf_op jit(solution)/shard_map/ppermute | solution.py:10
  108.5 6.2 %collective-permute-done.32 = f32[128,256]{0,1:T(8,128)S(1)} collective-permute-done((f32[128,256]{0,1:T(8,128)S(1)}, f32[128,256]{0,1:T(8,128)S(1)}, u32[]{:S(2)}, u32[]{:S(2)}) %collective-permute-start.32) | collective-permute-done | bytes 131104 | tf_op jit(solution)/shard_map/ppermute | solution.py:10
  114.7 1.3 convolution_bitcast_fusion.15
  116.2 1.3 collective-permute-done.42
  117.5 1.3 convolution_bitcast_fusion.9
  120.4 1.3 convolution_bitcast_fusion.28
  123.2 1.3 convolution_bitcast_fusion.22
  126.0 1.3 convolution_bitcast_fusion.14
  127.3 1.6 %collective-permute-start.34 = (f32[128,256]{0,1:T(8,128)S(1)}, f32[128,256]{0,1:T(8,128)S(1)}, u32[]{:S(2)}, u32[]{:S(2)}) collective-permute-start(f32[128,256]{0,1:T(8,128)S(1)} %slice.477), channel_id=1, source_target_pairs={{0,1},{1,0},{2,3},{3,2},{4,5},{5,4},{6,7},{7,6},{8,9},{9,8},{10,11... | collective-permute-start | bytes 393224 | tf_op jit(solution)/shard_map/ppermute | solution.py:10
  128.9 1.3 convolution_bitcast_fusion.8
  130.2 1.5 %collective-permute-start.44 = (f32[128,256]{0,1:T(8,128)S(1)}, f32[128,256]{0,1:T(8,128)S(1)}, u32[]{:S(2)}, u32[]{:S(2)}) collective-permute-start(f32[128,256]{0,1:T(8,128)S(1)} %slice.489), channel_id=1, source_target_pairs={{0,1},{1,0},{2,3},{3,2},{4,5},{5,4},{6,7},{7,6},{8,9},{9,8},{10,11... | collective-permute-start | bytes 393224 | tf_op jit(solution)/shard_map/ppermute | solution.py:10
  131.7 1.3 convolution_bitcast_fusion.27
  133.0 1.5 %collective-permute-start.14 = (f32[128,256]{0,1:T(8,128)S(1)}, f32[128,256]{0,1:T(8,128)S(1)}, u32[]{:S(2)}, u32[]{:S(2)}) collective-permute-start(f32[128,256]{0,1:T(8,128)S(1)} %slice.452), channel_id=1, source_target_pairs={{0,1},{1,0},{2,3},{3,2},{4,5},{5,4},{6,7},{7,6},{8,9},{9,8},{10,11... | collective-permute-start | bytes 393224 | tf_op jit(solution)/shard_map/ppermute | solution.py:10
  134.5 1.3 convolution_bitcast_fusion.21
  135.8 1.4 collective-permute-start.24
  138.7 2.4 %collective-permute-done.24 = f32[128,256]{0,1:T(8,128)S(1)} collective-permute-done((f32[128,256]{0,1:T(8,128)S(1)}, f32[128,256]{0,1:T(8,128)S(1)}, u32[]{:S(2)}, u32[]{:S(2)}) %collective-permute-start.24) | collective-permute-done | bytes 131104 | tf_op jit(solution)/shard_map/ppermute | solution.py:10
  (138 shorter events, 33.4 us)
Async XLA Ops:
  0.0 18.7 %copy-start.3 = (f32[4,256]{1,0:T(4,128)S(1)}, f32[4,256]{1,0:T(4,128)}, u32[]{:S(2)}) copy-start(f32[4,256]{1,0:T(4,128)} %param.10) | copy-start | bytes 12292
  0.0 29.5 %copy-start.4 = (s32[4]{0:T(128)S(1)}, s32[4]{0:T(128)}, u32[]{:S(2)}) copy-start(s32[4]{0:T(128)} %param.11) | copy-start | bytes 52
  0.0 18.7 %collective-permute-start = (f32[4,256]{1,0:T(4,128)}, f32[4,256]{1,0:T(4,128)S(1)}, u32[]{:S(2)}, u32[]{:S(2)}) collective-permute-start(f32[4,256]{1,0:T(4,128)} %param.10), channel_id=1, source_target_pairs={{0,4},{1,5},{2,6},{3,7},{4,0},{5,1},{6,2},{7,3},{8,12},{9,13},{10,... | collective-permute-start | bytes 12296 | tf_op jit(solution)/shard_map/ppermute | solution.py:10
  12.9 20.9 %collective-permute-start.25 = (f32[128,256]{1,0:T(8,128)S(1)}, f32[128,256]{1,0:T(8,128)S(1)}, u32[]{:S(2)}, u32[]{:S(2)}) collective-permute-start(f32[128,256]{1,0:T(8,128)S(1)} %convolution_bitcast_fusion.41), channel_id=1, source_target_pairs={{0,1},{1,0},{2,3},{3,2},{4,5},{5,4},{6,7},{7,6},{8,9},{9,8},{10,11... | collective-permute-start | bytes 393224 | tf_op jit(solution)/shard_map/ppermute | solution.py:10
  15.7 19.7 %collective-permute-start.35 = (f32[128,256]{1,0:T(8,128)S(1)}, f32[128,256]{1,0:T(8,128)S(1)}, u32[]{:S(2)}, u32[]{:S(2)}) collective-permute-start(f32[128,256]{1,0:T(8,128)S(1)} %convolution_bitcast_fusion.36), channel_id=1, source_target_pairs={{0,1},{1,0},{2,3},{3,2},{4,5},{5,4},{6,7},{7,6},{8,9},{9,8},{10,11... | collective-permute-start | bytes 393224 | tf_op jit(solution)/shard_map/ppermute | solution.py:10
  18.8 4.4 %collective-permute-start.1 = (f32[8,256]{1,0:T(8,128)S(1)}, f32[8,256]{1,0:T(8,128)S(1)}, u32[]{:S(2)}, u32[]{:S(2)}) collective-permute-start(f32[8,256]{1,0:T(8,128)S(1)} %pad_maximum_fusion.3), channel_id=1, source_target_pairs={{0,2},{1,3},{2,0},{3,1},{4,6},{5,7},{6,4},{7,5},{8,10},{9,11},{10,... | collective-permute-start | bytes 24584 | tf_op jit(solution)/shard_map/ppermute | solution.py:10
  21.6 17.0 %collective-permute-start.5 = (f32[128,256]{1,0:T(8,128)S(1)}, f32[128,256]{1,0:T(8,128)S(1)}, u32[]{:S(2)}, u32[]{:S(2)}) collective-permute-start(f32[128,256]{1,0:T(8,128)S(1)} %convolution_bitcast_fusion.53), channel_id=1, source_target_pairs={{0,1},{1,0},{2,3},{3,2},{4,5},{5,4},{6,7},{7,6},{8,9},{9,8},{10,11... | collective-permute-start | bytes 393224 | tf_op jit(solution)/shard_map/ppermute | solution.py:10
  23.2 4.7 %collective-permute-start.2 = (f32[16,256]{1,0:T(8,128)S(1)}, f32[16,256]{1,0:T(8,128)S(1)}, u32[]{:S(2)}, u32[]{:S(2)}) collective-permute-start(f32[16,256]{1,0:T(8,128)S(1)} %pad_maximum_fusion.2), channel_id=1, source_target_pairs={{0,1},{1,0},{2,3},{3,2},{4,5},{5,4},{6,7},{7,6},{8,9},{9,8},{10,11... | collective-permute-start | bytes 49160 | tf_op jit(solution)/shard_map/ppermute | solution.py:10
  25.3 14.7 %collective-permute-start.15 = (f32[128,256]{1,0:T(8,128)S(1)}, f32[128,256]{1,0:T(8,128)S(1)}, u32[]{:S(2)}, u32[]{:S(2)}) collective-permute-start(f32[128,256]{1,0:T(8,128)S(1)} %convolution_bitcast_fusion.48), channel_id=1, source_target_pairs={{0,1},{1,0},{2,3},{3,2},{4,5},{5,4},{6,7},{7,6},{8,9},{9,8},{10,11... | collective-permute-start | bytes 393224 | tf_op jit(solution)/shard_map/ppermute | solution.py:10
  27.9 4.0 %collective-permute-start.3 = (f32[32,256]{1,0:T(8,128)S(1)}, f32[32,256]{1,0:T(8,128)S(1)}, u32[]{:S(2)}, u32[]{:S(2)}) collective-permute-start(f32[32,256]{1,0:T(8,128)S(1)} %pad_maximum_fusion.1), channel_id=1, source_target_pairs={{0,16},{8,24},{16,0},{24,8},{1,17},{9,25},{17,1},{25,9},{2,18},{10... | collective-permute-start | bytes 98312 | tf_op jit(solution)/shard_map/ppermute | solution.py:10
  31.9 1.3 collective-permute-start.4
  33.8 17.5 %copy-start = (f32[7,4,128,256]{3,2,1,0:T(8,128)S(1)}, f32[7,4,128,256]{3,2,1,0:T(8,128)}, u32[]{:S(2)}) copy-start(f32[7,4,128,256]{3,2,1,0:T(8,128)} %param.8) | copy-start | bytes 11010052
  35.2 8.0 %collective-permute-start.26 = (f32[128,256]{1,0:T(8,128)S(1)}, f32[128,256]{1,0:T(8,128)S(1)}, u32[]{:S(2)}, u32[]{:S(2)}) collective-permute-start(f32[128,256]{1,0:T(8,128)S(1)} %convolution_bitcast_fusion.40), channel_id=1, source_target_pairs={{0,2},{1,3},{2,0},{3,1},{4,6},{5,7},{6,4},{7,5},{8,10},{9,11},{10,... | collective-permute-start | bytes 393224 | tf_op jit(solution)/shard_map/ppermute | solution.py:10
  36.6 8.2 %collective-permute-start.36 = (f32[128,256]{1,0:T(8,128)S(1)}, f32[128,256]{1,0:T(8,128)S(1)}, u32[]{:S(2)}, u32[]{:S(2)}) collective-permute-start(f32[128,256]{1,0:T(8,128)S(1)} %convolution_bitcast_fusion.35), channel_id=1, source_target_pairs={{0,2},{1,3},{2,0},{3,1},{4,6},{5,7},{6,4},{7,5},{8,10},{9,11},{10,... | collective-permute-start | bytes 393224 | tf_op jit(solution)/shard_map/ppermute | solution.py:10
  39.8 37.4 %copy-start.2 = (f32[4,256,128]{2,1,0:T(8,128)S(1)}, f32[4,256,128]{2,1,0:T(8,128)}, u32[]{:S(2)}) copy-start(f32[4,256,128]{2,1,0:T(8,128)} %param.9) | copy-start | bytes 1572868
  39.8 8.9 %collective-permute-start.6 = (f32[128,256]{1,0:T(8,128)S(1)}, f32[128,256]{1,0:T(8,128)S(1)}, u32[]{:S(2)}, u32[]{:S(2)}) collective-permute-start(f32[128,256]{1,0:T(8,128)S(1)} %convolution_bitcast_fusion.52), channel_id=1, source_target_pairs={{0,2},{1,3},{2,0},{3,1},{4,6},{5,7},{6,4},{7,5},{8,10},{9,11},{10,... | collective-permute-start | bytes 393224 | tf_op jit(solution)/shard_map/ppermute | solution.py:10
  41.2 10.1 %collective-permute-start.16 = (f32[128,256]{1,0:T(8,128)S(1)}, f32[128,256]{1,0:T(8,128)S(1)}, u32[]{:S(2)}, u32[]{:S(2)}) collective-permute-start(f32[128,256]{1,0:T(8,128)S(1)} %convolution_bitcast_fusion.47), channel_id=1, source_target_pairs={{0,2},{1,3},{2,0},{3,1},{4,6},{5,7},{6,4},{7,5},{8,10},{9,11},{10,... | collective-permute-start | bytes 393224 | tf_op jit(solution)/shard_map/ppermute | solution.py:10
  44.4 18.3 %collective-permute-start.27 = (f32[128,256]{1,0:T(8,128)S(1)}, f32[128,256]{1,0:T(8,128)S(1)}, u32[]{:S(2)}, u32[]{:S(2)}) collective-permute-start(f32[128,256]{1,0:T(8,128)S(1)} %convolution_bitcast_fusion.39), channel_id=1, source_target_pairs={{0,4},{1,5},{2,6},{3,7},{4,0},{5,1},{6,2},{7,3},{8,12},{9,13},{10,... | collective-permute-start | bytes 393224 | tf_op jit(solution)/shard_map/ppermute | solution.py:10
  46.0 19.5 %collective-permute-start.37 = (f32[128,256]{1,0:T(8,128)S(1)}, f32[128,256]{1,0:T(8,128)S(1)}, u32[]{:S(2)}, u32[]{:S(2)}) collective-permute-start(f32[128,256]{1,0:T(8,128)S(1)} %convolution_bitcast_fusion.34), channel_id=1, source_target_pairs={{0,4},{1,5},{2,6},{3,7},{4,0},{5,1},{6,2},{7,3},{8,12},{9,13},{10,... | collective-permute-start | bytes 393224 | tf_op jit(solution)/shard_map/ppermute | solution.py:10
  49.9 18.2 %collective-permute-start.7 = (f32[128,256]{1,0:T(8,128)S(1)}, f32[128,256]{1,0:T(8,128)S(1)}, u32[]{:S(2)}, u32[]{:S(2)}) collective-permute-start(f32[128,256]{1,0:T(8,128)S(1)} %convolution_bitcast_fusion.51), channel_id=1, source_target_pairs={{0,4},{1,5},{2,6},{3,7},{4,0},{5,1},{6,2},{7,3},{8,12},{9,13},{10,... | collective-permute-start | bytes 393224 | tf_op jit(solution)/shard_map/ppermute | solution.py:10
  51.7 17.9 %collective-permute-start.17 = (f32[128,256]{1,0:T(8,128)S(1)}, f32[128,256]{1,0:T(8,128)S(1)}, u32[]{:S(2)}, u32[]{:S(2)}) collective-permute-start(f32[128,256]{1,0:T(8,128)S(1)} %convolution_bitcast_fusion.46), channel_id=1, source_target_pairs={{0,4},{1,5},{2,6},{3,7},{4,0},{5,1},{6,2},{7,3},{8,12},{9,13},{10,... | collective-permute-start | bytes 393224 | tf_op jit(solution)/shard_map/ppermute | solution.py:10
  63.0 6.9 %collective-permute-start.28 = (f32[128,256]{1,0:T(8,128)S(1)}, f32[128,256]{1,0:T(8,128)S(1)}, u32[]{:S(2)}, u32[]{:S(2)}) collective-permute-start(f32[128,256]{1,0:T(8,128)S(1)} %convolution_bitcast_fusion.38), channel_id=1, source_target_pairs={{0,8},{8,0},{16,24},{24,16},{1,9},{9,1},{17,25},{25,17},{2,10},{10... | collective-permute-start | bytes 393224 | tf_op jit(solution)/shard_map/ppermute | solution.py:10
  65.8 6.0 %collective-permute-start.38 = (f32[128,256]{1,0:T(8,128)S(1)}, f32[128,256]{1,0:T(8,128)S(1)}, u32[]{:S(2)}, u32[]{:S(2)}) collective-permute-start(f32[128,256]{1,0:T(8,128)S(1)} %convolution_bitcast_fusion.33), channel_id=1, source_target_pairs={{0,8},{8,0},{16,24},{24,16},{1,9},{9,1},{17,25},{25,17},{2,10},{10... | collective-permute-start | bytes 393224 | tf_op jit(solution)/shard_map/ppermute | solution.py:10
  68.4 4.3 %collective-permute-start.8 = (f32[128,256]{1,0:T(8,128)S(1)}, f32[128,256]{1,0:T(8,128)S(1)}, u32[]{:S(2)}, u32[]{:S(2)}) collective-permute-start(f32[128,256]{1,0:T(8,128)S(1)} %convolution_bitcast_fusion.50), channel_id=1, source_target_pairs={{0,8},{8,0},{16,24},{24,16},{1,9},{9,1},{17,25},{25,17},{2,10},{10... | collective-permute-start | bytes 393224 | tf_op jit(solution)/shard_map/ppermute | solution.py:10
  69.8 4.7 %collective-permute-start.18 = (f32[128,256]{1,0:T(8,128)S(1)}, f32[128,256]{1,0:T(8,128)S(1)}, u32[]{:S(2)}, u32[]{:S(2)}) collective-permute-start(f32[128,256]{1,0:T(8,128)S(1)} %convolution_bitcast_fusion.45), channel_id=1, source_target_pairs={{0,8},{8,0},{16,24},{24,16},{1,9},{9,1},{17,25},{25,17},{2,10},{10... | collective-permute-start | bytes 393224 | tf_op jit(solution)/shard_map/ppermute | solution.py:10
  70.2 6.4 %collective-permute-start.29 = (f32[128,256]{1,0:T(8,128)S(1)}, f32[128,256]{1,0:T(8,128)S(1)}, u32[]{:S(2)}, u32[]{:S(2)}) collective-permute-start(f32[128,256]{1,0:T(8,128)S(1)} %convolution_bitcast_fusion.37), channel_id=1, source_target_pairs={{0,16},{8,24},{16,0},{24,8},{1,17},{9,25},{17,1},{25,9},{2,18},{10... | collective-permute-start | bytes 393224 | tf_op jit(solution)/shard_map/ppermute | solution.py:10
  72.1 7.8 %collective-permute-start.39 = (f32[128,256]{1,0:T(8,128)S(1)}, f32[128,256]{1,0:T(8,128)S(1)}, u32[]{:S(2)}, u32[]{:S(2)}) collective-permute-start(f32[128,256]{1,0:T(8,128)S(1)} %convolution_bitcast_fusion.32), channel_id=1, source_target_pairs={{0,16},{8,24},{16,0},{24,8},{1,17},{9,25},{17,1},{25,9},{2,18},{10... | collective-permute-start | bytes 393224 | tf_op jit(solution)/shard_map/ppermute | solution.py:10
  73.0 9.7 %collective-permute-start.9 = (f32[128,256]{1,0:T(8,128)S(1)}, f32[128,256]{1,0:T(8,128)S(1)}, u32[]{:S(2)}, u32[]{:S(2)}) collective-permute-start(f32[128,256]{1,0:T(8,128)S(1)} %convolution_bitcast_fusion.49), channel_id=1, source_target_pairs={{0,16},{8,24},{16,0},{24,8},{1,17},{9,25},{17,1},{25,9},{2,18},{10... | collective-permute-start | bytes 393224 | tf_op jit(solution)/shard_map/ppermute | solution.py:10
  74.9 10.9 %collective-permute-start.19 = (f32[128,256]{1,0:T(8,128)S(1)}, f32[128,256]{1,0:T(8,128)S(1)}, u32[]{:S(2)}, u32[]{:S(2)}) collective-permute-start(f32[128,256]{1,0:T(8,128)S(1)} %convolution_bitcast_fusion.44), channel_id=1, source_target_pairs={{0,16},{8,24},{16,0},{24,8},{1,17},{9,25},{17,1},{25,9},{2,18},{10... | collective-permute-start | bytes 393224 | tf_op jit(solution)/shard_map/ppermute | solution.py:10
  78.4 10.2 %collective-permute-start.30 = (f32[128,256]{0,1:T(8,128)S(1)}, f32[128,256]{0,1:T(8,128)S(1)}, u32[]{:S(2)}, u32[]{:S(2)}) collective-permute-start(f32[128,256]{0,1:T(8,128)S(1)} %slice.469), channel_id=1, source_target_pairs={{0,16},{8,24},{16,0},{24,8},{1,17},{9,25},{17,1},{25,9},{2,18},{10... | collective-permute-start | bytes 393224 | tf_op jit(solution)/shard_map/ppermute | solution.py:10
  81.7 9.0 %collective-permute-start.40 = (f32[128,256]{0,1:T(8,128)S(1)}, f32[128,256]{0,1:T(8,128)S(1)}, u32[]{:S(2)}, u32[]{:S(2)}) collective-permute-start(f32[128,256]{0,1:T(8,128)S(1)} %slice.481), channel_id=1, source_target_pairs={{0,16},{8,24},{16,0},{24,8},{1,17},{9,25},{17,1},{25,9},{2,18},{10... | collective-permute-start | bytes 393224 | tf_op jit(solution)/shard_map/ppermute | solution.py:10
  84.6 8.8 %collective-permute-start.10 = (f32[128,256]{0,1:T(8,128)S(1)}, f32[128,256]{0,1:T(8,128)S(1)}, u32[]{:S(2)}, u32[]{:S(2)}) collective-permute-start(f32[128,256]{0,1:T(8,128)S(1)} %slice.444), channel_id=1, source_target_pairs={{0,16},{8,24},{16,0},{24,8},{1,17},{9,25},{17,1},{25,9},{2,18},{10... | collective-permute-start | bytes 393224 | tf_op jit(solution)/shard_map/ppermute | solution.py:10
  87.5 8.4 %collective-permute-start.20 = (f32[128,256]{0,1:T(8,128)S(1)}, f32[128,256]{0,1:T(8,128)S(1)}, u32[]{:S(2)}, u32[]{:S(2)}) collective-permute-start(f32[128,256]{0,1:T(8,128)S(1)} %slice.456), channel_id=1, source_target_pairs={{0,16},{8,24},{16,0},{24,8},{1,17},{9,25},{17,1},{25,9},{2,18},{10... | collective-permute-start | bytes 393224 | tf_op jit(solution)/shard_map/ppermute | solution.py:10
  88.9 8.3 %collective-permute-start.31 = (f32[128,256]{0,1:T(8,128)S(1)}, f32[128,256]{0,1:T(8,128)S(1)}, u32[]{:S(2)}, u32[]{:S(2)}) collective-permute-start(f32[128,256]{0,1:T(8,128)S(1)} %slice.471), channel_id=1, source_target_pairs={{0,8},{8,0},{16,24},{24,16},{1,9},{9,1},{17,25},{25,17},{2,10},{10... | collective-permute-start | bytes 393224 | tf_op jit(solution)/shard_map/ppermute | solution.py:10
  91.0 7.6 %collective-permute-start.41 = (f32[128,256]{0,1:T(8,128)S(1)}, f32[128,256]{0,1:T(8,128)S(1)}, u32[]{:S(2)}, u32[]{:S(2)}) collective-permute-start(f32[128,256]{0,1:T(8,128)S(1)} %slice.483), channel_id=1, source_target_pairs={{0,8},{8,0},{16,24},{24,16},{1,9},{9,1},{17,25},{25,17},{2,10},{10... | collective-permute-start | bytes 393224 | tf_op jit(solution)/shard_map/ppermute | solution.py:10
  93.8 9.1 %collective-permute-start.11 = (f32[128,256]{0,1:T(8,128)S(1)}, f32[128,256]{0,1:T(8,128)S(1)}, u32[]{:S(2)}, u32[]{:S(2)}) collective-permute-start(f32[128,256]{0,1:T(8,128)S(1)} %slice.446), channel_id=1, source_target_pairs={{0,8},{8,0},{16,24},{24,16},{1,9},{9,1},{17,25},{25,17},{2,10},{10... | collective-permute-start | bytes 393224 | tf_op jit(solution)/shard_map/ppermute | solution.py:10
  97.2 7.1 %collective-permute-start.21 = (f32[128,256]{0,1:T(8,128)S(1)}, f32[128,256]{0,1:T(8,128)S(1)}, u32[]{:S(2)}, u32[]{:S(2)}) collective-permute-start(f32[128,256]{0,1:T(8,128)S(1)} %slice.458), channel_id=1, source_target_pairs={{0,8},{8,0},{16,24},{24,16},{1,9},{9,1},{17,25},{25,17},{2,10},{10... | collective-permute-start | bytes 393224 | tf_op jit(solution)/shard_map/ppermute | solution.py:10
  98.5 16.1 %collective-permute-start.32 = (f32[128,256]{0,1:T(8,128)S(1)}, f32[128,256]{0,1:T(8,128)S(1)}, u32[]{:S(2)}, u32[]{:S(2)}) collective-permute-start(f32[128,256]{0,1:T(8,128)S(1)} %slice.473), channel_id=1, source_target_pairs={{0,4},{1,5},{2,6},{3,7},{4,0},{5,1},{6,2},{7,3},{8,12},{9,13},{10,... | collective-permute-start | bytes 393224 | tf_op jit(solution)/shard_map/ppermute | solution.py:10
  99.9 17.6 %collective-permute-start.42 = (f32[128,256]{0,1:T(8,128)S(1)}, f32[128,256]{0,1:T(8,128)S(1)}, u32[]{:S(2)}, u32[]{:S(2)}) collective-permute-start(f32[128,256]{0,1:T(8,128)S(1)} %slice.485), channel_id=1, source_target_pairs={{0,4},{1,5},{2,6},{3,7},{4,0},{5,1},{6,2},{7,3},{8,12},{9,13},{10,... | collective-permute-start | bytes 393224 | tf_op jit(solution)/shard_map/ppermute | solution.py:10
  104.2 16.2 %collective-permute-start.12 = (f32[128,256]{0,1:T(8,128)S(1)}, f32[128,256]{0,1:T(8,128)S(1)}, u32[]{:S(2)}, u32[]{:S(2)}) collective-permute-start(f32[128,256]{0,1:T(8,128)S(1)} %slice.448), channel_id=1, source_target_pairs={{0,4},{1,5},{2,6},{3,7},{4,0},{5,1},{6,2},{7,3},{8,12},{9,13},{10,... | collective-permute-start | bytes 393224 | tf_op jit(solution)/shard_map/ppermute | solution.py:10
  105.6 17.6 %collective-permute-start.22 = (f32[128,256]{0,1:T(8,128)S(1)}, f32[128,256]{0,1:T(8,128)S(1)}, u32[]{:S(2)}, u32[]{:S(2)}) collective-permute-start(f32[128,256]{0,1:T(8,128)S(1)} %slice.460), channel_id=1, source_target_pairs={{0,4},{1,5},{2,6},{3,7},{4,0},{5,1},{6,2},{7,3},{8,12},{9,13},{10,... | collective-permute-start | bytes 393224 | tf_op jit(solution)/shard_map/ppermute | solution.py:10
  116.0 10.0 %collective-permute-start.33 = (f32[128,256]{0,1:T(8,128)S(1)}, f32[128,256]{0,1:T(8,128)S(1)}, u32[]{:S(2)}, u32[]{:S(2)}) collective-permute-start(f32[128,256]{0,1:T(8,128)S(1)} %slice.475), channel_id=1, source_target_pairs={{0,2},{1,3},{2,0},{3,1},{4,6},{5,7},{6,4},{7,5},{8,10},{9,11},{10,... | collective-permute-start | bytes 393224 | tf_op jit(solution)/shard_map/ppermute | solution.py:10
  118.8 10.1 %collective-permute-start.43 = (f32[128,256]{0,1:T(8,128)S(1)}, f32[128,256]{0,1:T(8,128)S(1)}, u32[]{:S(2)}, u32[]{:S(2)}) collective-permute-start(f32[128,256]{0,1:T(8,128)S(1)} %slice.487), channel_id=1, source_target_pairs={{0,2},{1,3},{2,0},{3,1},{4,6},{5,7},{6,4},{7,5},{8,10},{9,11},{10,... | collective-permute-start | bytes 393224 | tf_op jit(solution)/shard_map/ppermute | solution.py:10
  121.7 10.0 %collective-permute-start.13 = (f32[128,256]{0,1:T(8,128)S(1)}, f32[128,256]{0,1:T(8,128)S(1)}, u32[]{:S(2)}, u32[]{:S(2)}) collective-permute-start(f32[128,256]{0,1:T(8,128)S(1)} %slice.450), channel_id=1, source_target_pairs={{0,2},{1,3},{2,0},{3,1},{4,6},{5,7},{6,4},{7,5},{8,10},{9,11},{10,... | collective-permute-start | bytes 393224 | tf_op jit(solution)/shard_map/ppermute | solution.py:10
  124.5 10.0 %collective-permute-start.23 = (f32[128,256]{0,1:T(8,128)S(1)}, f32[128,256]{0,1:T(8,128)S(1)}, u32[]{:S(2)}, u32[]{:S(2)}) collective-permute-start(f32[128,256]{0,1:T(8,128)S(1)} %slice.462), channel_id=1, source_target_pairs={{0,2},{1,3},{2,0},{3,1},{4,6},{5,7},{6,4},{7,5},{8,10},{9,11},{10,... | collective-permute-start | bytes 393224 | tf_op jit(solution)/shard_map/ppermute | solution.py:10
  127.3 15.0 %collective-permute-start.34 = (f32[128,256]{0,1:T(8,128)S(1)}, f32[128,256]{0,1:T(8,128)S(1)}, u32[]{:S(2)}, u32[]{:S(2)}) collective-permute-start(f32[128,256]{0,1:T(8,128)S(1)} %slice.477), channel_id=1, source_target_pairs={{0,1},{1,0},{2,3},{3,2},{4,5},{5,4},{6,7},{7,6},{8,9},{9,8},{10,11... | collective-permute-start | bytes 393224 | tf_op jit(solution)/shard_map/ppermute | solution.py:10
  130.1 13.8 %copy-start.1 = (f32[4,128,256]{2,1,0:T(8,128)S(1)}, f32[4,128,256]{2,1,0:T(8,128)}, u32[]{:S(2)}) copy-start(f32[4,128,256]{2,1,0:T(8,128)} %param.7) | copy-start | bytes 1572868
  130.2 12.6 %collective-permute-start.44 = (f32[128,256]{0,1:T(8,128)S(1)}, f32[128,256]{0,1:T(8,128)S(1)}, u32[]{:S(2)}, u32[]{:S(2)}) collective-permute-start(f32[128,256]{0,1:T(8,128)S(1)} %slice.489), channel_id=1, source_target_pairs={{0,1},{1,0},{2,3},{3,2},{4,5},{5,4},{6,7},{7,6},{8,9},{9,8},{10,11... | collective-permute-start | bytes 393224 | tf_op jit(solution)/shard_map/ppermute | solution.py:10
  133.0 5.3 %collective-permute-start.14 = (f32[128,256]{0,1:T(8,128)S(1)}, f32[128,256]{0,1:T(8,128)S(1)}, u32[]{:S(2)}, u32[]{:S(2)}) collective-permute-start(f32[128,256]{0,1:T(8,128)S(1)} %slice.452), channel_id=1, source_target_pairs={{0,1},{1,0},{2,3},{3,2},{4,5},{5,4},{6,7},{7,6},{8,9},{9,8},{10,11... | collective-permute-start | bytes 393224 | tf_op jit(solution)/shard_map/ppermute | solution.py:10
  135.8 5.3 %collective-permute-start.24 = (f32[128,256]{0,1:T(8,128)S(1)}, f32[128,256]{0,1:T(8,128)S(1)}, u32[]{:S(2)}, u32[]{:S(2)}) collective-permute-start(f32[128,256]{0,1:T(8,128)S(1)} %slice.464), channel_id=1, source_target_pairs={{0,1},{1,0},{2,3},{3,2},{4,5},{5,4},{6,7},{7,6},{8,9},{9,8},{10,11... | collective-permute-start | bytes 393224 | tf_op jit(solution)/shard_map/ppermute | solution.py:10

commit v2 on v0

v2 whole, which is shorter than its diff:
```python
import functools

import jax
import jax.numpy as jnp
from jax import lax
from jax.experimental import pallas as pl
from jax.experimental.pallas import tpu as pltpu
from jax.sharding import PartitionSpec as P

CHUNKS = 2
MIB = 1 << 20
VMEM = pl.BlockSpec(memory_space=pltpu.VMEM)
SMEM = pl.BlockSpec(memory_space=pltpu.SMEM)
HBM = pl.BlockSpec(memory_space=pltpu.HBM)


def exchange(value, axis, bit):
    return lax.ppermute(value, axis, [(i, i ^ 1 << bit) for i in range(lax.axis_size(axis))])


def split(value):
    high = value.astype(jnp.bfloat16)
    return high, (value - high.astype(jnp.float32)).astype(jnp.bfloat16)


def product(a, b):
    one = functools.partial(jnp.dot, preferred_element_type=jnp.float32)
    return one(a[0], b[1]) + one(a[1], b[0]) + one(a[0], b[0])


def turned(value):
    return split(value.T)


def call(kernel, outs, specs, out_specs, flops, traffic, scratch=(), limit=8 * MIB):
    return pl.pallas_call(
        kernel,
        out_shape=outs,
        in_specs=specs,
        out_specs=out_specs,
        scratch_shapes=scratch,
        cost_estimate=pl.CostEstimate(flops=flops, bytes_accessed=traffic, transcendentals=0),
        compiler_params=pltpu.CompilerParams(vmem_limit_bytes=limit),
    )


def start_kernel(nodes, rank, leaf, local_bits, chunks, source, leaf_in, factors, table, *rest):
    outs, (x, a, f, sems) = rest[:chunks], rest[chunks:]
    levels = [pltpu.make_async_copy(factors.at[l], f.at[l], sems.at[2 * nodes + l]) for l in range(local_bits)]
    xs = [pltpu.make_async_copy(source.at[pl.ds(j * leaf, leaf)], x.at[j], sems.at[j]) for j in range(nodes)]
    ins = [pltpu.make_async_copy(leaf_in.at[j], a.at[j], sems.at[nodes + j]) for j in range(nodes)]
    for j in range(nodes):
        ins[j].start()
        xs[j].start()
    for copy in levels:
        copy.start()
    values = []
    for j in range(nodes):
        ins[j].wait()
        xs[j].wait()
        values.append(product(split(a[j]), split(x[j])))
    for l in range(local_bits):
        levels[l].wait()
        halves = [split(v) for v in values]
        values = []
        for j in range(nodes):
            mine, other = halves[j], halves[j ^ 1 << l]
            both = tuple(jnp.concatenate([m, o], axis=0) for m, o in zip(mine, other))
            values.append(product(split(f[l, j]), both))
    per = nodes // chunks
    for j in range(nodes):
        outs[j // per][pl.ds((j % per) * rank, rank), :] = values[j]
    extra = table.shape[0]
    outs[0][pl.ds(per * rank, extra), :] = table[...]


def forward_kernel(first, per, rank, level, own, got, factors, out):
    for i in range(per):
        rows = pl.ds(i * rank, rank)
        both = split(jnp.concatenate([own[rows, :], got[rows, :]], axis=0))
        out[rows, :] = product(split(factors[level, first + i]), both)
    extra = own.shape[0] - per * rank
    if extra:
        tail = pl.ds(per * rank, extra)
        out[tail, :] = own[tail, :]
        out[pl.ds(per * rank + extra, extra), :] = got[tail, :]


def middle_kernel(first, per, rank, level, index, own, got, tab_own, tab_got, factors, leaf_out, keep, send):
    half = tab_own.shape[0] - per * rank
    for i in range(per):
        rows = pl.ds(i * rank, rank)
        f = factors[level, first + i]
        value = product(split(f), split(jnp.concatenate([own[rows, :], got[rows, :]], axis=0)))
        l = leaf_out[first + i]
        image = product(split(l), split(value))
        at = index[first + i]
        near = per * rank + jnp.where(at < half, at, at - half)
        weights = jnp.where(at < half, tab_own[pl.ds(near, 1), :], tab_got[pl.ds(near, 1), :])
        value = product(split(l.T * weights), split(image))
        both = product(turned(f), split(value))
        keep[rows, :] = both[:rank]
        send[rows, :] = both[rank:]


def backward_kernel(first, per, rank, level, own, got, factors, keep, send):
    for i in range(per):
        rows = pl.ds(i * rank, rank)
        both = product(turned(factors[level, first + i]), split(own[rows, :] + got[rows, :]))
        keep[rows, :] = both[:rank]
        send[rows, :] = both[rank:]


def end_kernel(nodes, rank, leaf, local_bits, chunks, leaf_in, factors, *rest):
    pairs, out, (y, sems) = rest[: 2 * chunks], rest[2 * chunks], rest[2 * chunks + 1 :]
    per = nodes // chunks
    values = []
    for j in range(nodes):
        rows = pl.ds((j % per) * rank, rank)
        values.append(pairs[2 * (j // per)][rows, :] + pairs[2 * (j // per) + 1][rows, :])
    for l in reversed(range(local_bits)):
        both = [product(turned(factors[l, j]), split(values[j])) for j in range(nodes)]
        values = [both[j][:rank] + both[j ^ 1 << l][rank:] for j in range(nodes)]
    copies = []
    for j in range(nodes):
        y[j] = product(turned(leaf_in[j]), split(values[j]))
        copies.append(pltpu.make_async_copy(y.at[j], out.at[pl.ds(j * leaf, leaf)], sems.at[j]))
        copies[-1].start()
    for copy in copies:
        copy.wait()


def body(source, leaf_in, factors, leaf_out, weight_table, block_index):
    level_count = factors.shape[0]
    nodes, rank, leaf = leaf_in.shape
    width = source.shape[1]
    f32 = jnp.float32
    local_bits = nodes.bit_length() - 1
    col_size = lax.axis_size("col")
    col_bits = col_size.bit_length() - 1
    where = {}
    for level in range(local_bits, level_count):
        position = level - local_bits
        where[level] = ("col", position) if position < col_bits else ("row", position - col_bits)
    chunks, per = CHUNKS, nodes // CHUNKS
    table_rows = weight_table.shape[0]
    flat = per * rank

    own = lax.axis_index("row") * col_size + lax.axis_index("col")
    place = ((block_index // table_rows) ^ own) * table_rows + block_index % table_rows

    def shape(rows):
        return jax.ShapeDtypeStruct((rows, width), f32)

    unit = 2 * per * rank * 2 * rank * width
    size = 4 * (flat * width * 3 + per * rank * 2 * rank)
    values = list(
        call(
            functools.partial(start_kernel, nodes, rank, leaf, local_bits, chunks),
            [shape(flat + (table_rows if c == 0 else 0)) for c in range(chunks)],
            [HBM, HBM, HBM, VMEM],
            [VMEM] * chunks,
            3 * chunks * unit,
            3 * chunks * size,
            [
                pltpu.VMEM((nodes, leaf, width), f32),
                pltpu.VMEM((nodes, rank, leaf), f32),
                pltpu.VMEM((local_bits, nodes, rank, 2 * rank), f32),
                pltpu.SemaphoreType.DMA((2 * nodes + local_bits,)),
            ],
        )(source, leaf_in, factors, weight_table)
    )
    for level in range(local_bits, level_count - 1):
        got = [exchange(v, *where[level]) for v in values]
        values = [
            call(
                functools.partial(forward_kernel, c * per, per, rank, level),
                shape(2 * values[c].shape[0] - flat),
                [VMEM] * 3,
                VMEM,
                unit,
                size,
            )(values[c], got[c], factors)
            for c in range(chunks)
        ]
    level = level_count - 1
    got = [exchange(v, *where[level]) for v in values]
    pairs = [
        call(
            functools.partial(middle_kernel, c * per, per, rank, level),
            [shape(flat)] * 2,
            [SMEM] + [VMEM] * 6,
            [VMEM] * 2,
            4 * unit,
            2 * size,
        )(place, values[c], got[c], values[0], got[0], factors, leaf_out)
        for c in range(chunks)
    ]
    for level in reversed(range(local_bits, level_count)):
        pairs = [(keep, exchange(send, *where[level])) for keep, send in pairs]
        if level > local_bits:
            pairs = [
                call(
                    functools.partial(backward_kernel, c * per, per, rank, level - 1),
                    [shape(flat)] * 2,
                    [VMEM] * 3,
                    [VMEM] * 2,
                    unit,
                    size,
                )(*pairs[c], factors)
                for c in range(chunks)
            ]
    return call(
        functools.partial(end_kernel, nodes, rank, leaf, local_bits, chunks),
        shape(nodes * leaf),
        [VMEM] * (2 + 2 * chunks),
        HBM,
        3 * chunks * unit,
        3 * chunks * size,
        [pltpu.VMEM((nodes, leaf, width), f32), pltpu.SemaphoreType.DMA((nodes,))],
    )(leaf_in, factors, *[v for pair in pairs for v in pair])


def solution(mesh):
    placed = (
        P(("row", "col"), None),
        P(("row", "col"), None, None),
        P(None, ("row", "col"), None, None),
        P(("row", "col"), None, None),
        P(("row", "col"), None),
        P(("row", "col")),
    )
    return jax.shard_map(
        body, mesh=mesh, in_specs=placed, out_specs=P(("row", "col"), None), check_vma=False
    )
```

time: 223 us -> 135 us (0.61)
  blocking collectives: 68.3 us -> 0 us
  matrix products: 30.4 us -> 0 us
  waiting for transfers between devices: 108 us -> 91.2 us
  Pallas kernels: 0 us -> 15.4 us
  starting transfers between devices: 10.4 us -> 21.2 us
    all_gather x1 -> x0, blocking collectives: 68.3 us -> none  [body(): lax.all_gather(weight_table, ('row', 'col'), axis=0, tiled=True)]
    dot_general x25 -> x0, matrix products: 30.4 us -> none  [the longest x7 13.7 us: body(): jnp.einsum('nrk,nks->nrs', factors[level_index], stacked, precision=HIGH)]
    ppermute x10 -> x20, waiting for transfers between devices: 108 us -> 91.2 us  [exchange(): lax.ppermute(value, axis, [(i, i ^ 1 << bit) for i in range(lax.axis_size...]
    pallas_call x0 -> x20, Pallas kernels: none -> 15.4 us  [the longest x2 4.44 us: body(): call(functools.partial(middle_kernel, c * per, per, rank, level), [shape(...]
    ppermute x10 -> x20, starting transfers between devices: 10.4 us -> 21.2 us  [exchange(): lax.ppermute(value, axis, [(i, i ^ 1 << bit) for i in range(lax.axis_size...]
    unnamed x9 -> x20, local copies, waits for them, and re-layouts: 1.29 us -> 7.05 us
    squeeze x1 -> x0, local copies, waits for them, and re-layouts: 2.3 us -> none  [body(): own_part = factors[level_index][:, :, :rank_size]]
  transfers between devices with their start and end apart: 10 -> 20, of which waited for: 9 -> 16; matrix products, arithmetic and copies ran while one was open for 1% -> 0% of each run, Pallas kernels for 0% -> 6%
where the time goes in v2:
time: 135 us
  waiting for transfers between devices  91.2 us (68%)
  starting transfers between devices  21.2 us (16%)
  Pallas kernels  15.4 us (11%)
  local copies, waits for them, and re-layouts  7.05 us (5%)
    ppermute x20, waiting for transfers between devices, exchange(): lax.ppermute(value, axis, [(i, i ^ 1 << bit) for i in range(lax.axis_size...  91.2 us
    ppermute x20, starting transfers between devices, exchange(): lax.ppermute(value, axis, [(i, i ^ 1 << bit) for i in range(lax.axis_size...  21.2 us
    unnamed x20, local copies, waits for them, and re-layouts  7.05 us
    pallas_call x2, Pallas kernels, body(): call(functools.partial(middle_kernel, c * per, per, rank, level), [shape(...  4.44 us
    pallas_call x8, Pallas kernels, body(): call(functools.partial(backward_kernel, c * per, per, rank, level - 1), [...  3.3 us
    pallas_call x1, Pallas kernels, body(): call(functools.partial(start_kernel, nodes, rank, leaf, local_bits, chunk...  2.71 us
  transfers between devices with their start and end apart: 20, of which 16 were waited for; matrix products, arithmetic and copies ran while one was open for 0% of the time, Pallas kernels for 6%

profile of v2, /device:TPU:0, one launch (start us, length us, event | category | flops | bytes accessed | tf_op | source)
XLA Modules:
  0.0 135.1 jit_solution(15516776498000494354)
XLA Ops:
  0.0 2.0 %copy-done = f32[7,4,128,256]{3,2,1,0:T(8,128)S(1)} copy-done((f32[7,4,128,256]{3,2,1,0:T(8,128)S(1)}, f32[7,4,128,256]{3,2,1,0:T(8,128)}, u32[]{:S(2)}) %copy-start) | copy-done | bytes 3670040
  2.0 1.0 copy-done.4
  3.1 1.2 copy-done.7
  4.3 0.7 copy-done.8
  5.0 2.7 %shard_map.64 = (f32[260,256]{1,0:T(8,128)S(1)}, f32[256,256]{1,0:T(8,128)S(1)}) custom-call(f32[1024,256]{1,0:T(8,128)S(1)} %copy-done.7, f32[4,128,256]{2,1,0:T(8,128)S(1)} %copy-done.4, f32[7,4,128,256]{3,2,1,0:T(8,128)S(1)} %copy-done, f32[4,256]{1,0:T(4,128)S(1)} %copy-done.8), custom_call_target="tpu_custom_call" | custom-call | flops 201326592 | bytes 6291456 | tf_op jit(solution)/shard_map/pallas_call | solution.py:158
  7.7 3.0 %collective-permute-start = (f32[260,256]{1,0:T(8,128)S(1)}, f32[260,256]{1,0:T(8,128)S(1)}, u32[]{:S(2)}, u32[]{:S(2)}) collective-permute-start(f32[260,256]{1,0:T(8,128)S(1)} %get-tuple-element.27.own), channel_id=1, source_target_pairs={{0,1},{1,0},{2,3},{3,2},{4,5},{5,4},{6,7},{7,6},{8,9},{9,8},{10,11... | collective-permute-start | bytes 798728 | tf_op jit(solution)/shard_map/ppermute | solution.py:18
  10.7 0.1 collective-permute-start.10
  10.8 7.2 %collective-permute-done.got = f32[260,256]{1,0:T(8,128)S(1)} collective-permute-done((f32[260,256]{1,0:T(8,128)S(1)}, f32[260,256]{1,0:T(8,128)S(1)}, u32[]{:S(2)}, u32[]{:S(2)}) %collective-permute-start) | collective-permute-done | bytes 266272 | tf_op jit(solution)/shard_map/ppermute | solution.py:18
  18.1 0.3 shard_map.65.own
  18.4 2.2 %collective-permute-start.1 = (f32[264,256]{1,0:T(8,128)S(1)}, f32[264,256]{1,0:T(8,128)S(1)}, u32[]{:S(2)}, u32[]{:S(2)}) collective-permute-start(f32[264,256]{1,0:T(8,128)S(1)} %shard_map.65.own), channel_id=1, source_target_pairs={{0,2},{1,3},{2,0},{3,1},{4,6},{5,7},{6,4},{7,5},{8,10},{9,11},{10,... | collective-permute-start | bytes 811016 | tf_op jit(solution)/shard_map/ppermute | solution.py:18
  20.6 2.3 %collective-permute-done.10.got = f32[256,256]{1,0:T(8,128)S(1)} collective-permute-done((f32[256,256]{1,0:T(8,128)S(1)}, f32[256,256]{1,0:T(8,128)S(1)}, u32[]{:S(2)}, u32[]{:S(2)}) %collective-permute-start.10) | collective-permute-done | bytes 262176 | tf_op jit(solution)/shard_map/ppermute | solution.py:18
  22.9 0.3 shard_map.74.own
  23.2 1.8 %collective-permute-start.11 = (f32[256,256]{1,0:T(8,128)S(1)}, f32[256,256]{1,0:T(8,128)S(1)}, u32[]{:S(2)}, u32[]{:S(2)}) collective-permute-start(f32[256,256]{1,0:T(8,128)S(1)} %shard_map.74.own), channel_id=1, source_target_pairs={{0,2},{1,3},{2,0},{3,1},{4,6},{5,7},{6,4},{7,5},{8,10},{9,11},{10,... | collective-permute-start | bytes 786440 | tf_op jit(solution)/shard_map/ppermute | solution.py:18
  25.0 0.4 collective-permute-done.1.got
  25.4 0.3 shard_map.66.own
  25.7 3.1 %collective-permute-start.2 = (f32[272,256]{1,0:T(8,128)S(1)}, f32[272,256]{1,0:T(8,128)S(1)}, u32[]{:S(2)}, u32[]{:S(2)}) collective-permute-start(f32[272,256]{1,0:T(8,128)S(1)} %shard_map.66.own), channel_id=1, source_target_pairs={{0,4},{1,5},{2,6},{3,7},{4,0},{5,1},{6,2},{7,3},{8,12},{9,13},{10,... | collective-permute-start | bytes 835592 | tf_op jit(solution)/shard_map/ppermute | solution.py:18
  28.8 7.7 %collective-permute-done.11.got = f32[256,256]{1,0:T(8,128)S(1)} collective-permute-done((f32[256,256]{1,0:T(8,128)S(1)}, f32[256,256]{1,0:T(8,128)S(1)}, u32[]{:S(2)}, u32[]{:S(2)}) %collective-permute-start.11) | collective-permute-done | bytes 262176 | tf_op jit(solution)/shard_map/ppermute | solution.py:18
  36.5 0.3 shard_map.75.own
  36.8 0.3 collective-permute-start.12
  37.1 8.4 %collective-permute-done.2.got = f32[272,256]{1,0:T(8,128)S(1)} collective-permute-done((f32[272,256]{1,0:T(8,128)S(1)}, f32[272,256]{1,0:T(8,128)S(1)}, u32[]{:S(2)}, u32[]{:S(2)}) %collective-permute-start.2) | collective-permute-done | bytes 278560 | tf_op jit(solution)/shard_map/ppermute | solution.py:18
  45.5 0.3 shard_map.67.own
  45.8 0.1 collective-permute-start.3
  45.8 4.9 %collective-permute-done.12.got = f32[256,256]{1,0:T(8,128)S(1)} collective-permute-done((f32[256,256]{1,0:T(8,128)S(1)}, f32[256,256]{1,0:T(8,128)S(1)}, u32[]{:S(2)}, u32[]{:S(2)}) %collective-permute-start.12) | collective-permute-done | bytes 262176 | tf_op jit(solution)/shard_map/ppermute | solution.py:18
  50.8 0.3 shard_map.76.own
  51.1 0.0 copy-start.9
  51.1 0.0 copy-start.6
  51.1 0.1 collective-permute-start.13
  51.2 0.0 collective-permute-done.3.got
  51.2 0.3 shard_map.68.own.tab_own
  51.5 1.6 %collective-permute-start.4 = (f32[320,256]{1,0:T(8,128)S(1)}, f32[320,256]{1,0:T(8,128)S(1)}, u32[]{:S(2)}, u32[]{:S(2)}) collective-permute-start(f32[320,256]{1,0:T(8,128)S(1)} %shard_map.68.own.tab_own), channel_id=1, source_target_pairs={{0,16},{8,24},{16,0},{24,8},{1,17},{9,25},{17,1},{25,9},{2,18},{10... | collective-permute-start | bytes 983048 | tf_op jit(solution)/shard_map/ppermute | solution.py:18
  53.1 0.3 shard_map.77.own
  53.4 1.2 collective-permute-start.14
  54.6 12.7 %collective-permute-done.14.got = f32[256,256]{1,0:T(8,128)S(1)} collective-permute-done((f32[256,256]{1,0:T(8,128)S(1)}, f32[256,256]{1,0:T(8,128)S(1)}, u32[]{:S(2)}, u32[]{:S(2)}) %collective-permute-start.14) | collective-permute-done | bytes 262176 | tf_op jit(solution)/shard_map/ppermute | solution.py:18
  67.3 2.0 %copy-done.2 = f32[7,4,128,256]{3,2,1,0:T(8,128)S(1)} copy-done((f32[7,4,128,256]{3,2,1,0:T(8,128)S(1)}, f32[7,4,128,256]{3,2,1,0:T(8,128)}, u32[]{:S(2)}) %copy-start.2) | copy-done | bytes 3670040
  69.3 2.2 %shard_map.78 = (f32[256,256]{1,0:T(8,128)S(1)}, f32[256,256]{1,0:T(8,128)S(1)}) custom-call(s32[4]{0:T(128)S(1)} %fusion.index, f32[256,256]{1,0:T(8,128)S(1)} %shard_map.77.own, f32[256,256]{1,0:T(8,128)S(1)} %collective-permute-done.14.got, f32[320,256]{1,0:T(8,128)S(1)} %shard_map.68.own.tab_own, f32[320,256]{1,0:T(8,128)S(1)} %collective-permute-done.4.got.tab_got, ...), custom_call_target="tpu_custom_call" | custom-call | flops 134217728 | bytes 2097152 | tf_op jit(solution)/shard_map/pallas_call | solution.py:189
  71.6 1.6 %collective-permute-start.15 = (f32[256,256]{1,0:T(8,128)S(1)}, f32[256,256]{1,0:T(8,128)S(1)}, u32[]{:S(2)}, u32[]{:S(2)}) collective-permute-start(f32[256,256]{1,0:T(8,128)S(1)} %get-tuple-element.40), channel_id=1, source_target_pairs={{0,16},{8,24},{16,0},{24,8},{1,17},{9,25},{17,1},{25,9},{2,18},{10... | collective-permute-start | bytes 786440 | tf_op jit(solution)/shard_map/ppermute | solution.py:18
  73.2 2.2 %shard_map.69 = (f32[256,256]{1,0:T(8,128)S(1)}, f32[256,256]{1,0:T(8,128)S(1)}) custom-call(s32[4]{0:T(128)S(1)} %fusion.index, f32[320,256]{1,0:T(8,128)S(1)} %shard_map.68.own.tab_own, f32[320,256]{1,0:T(8,128)S(1)} %collective-permute-done.4.got.tab_got, f32[320,256]{1,0:T(8,128)S(1)} %shard_map.68.own.tab_own, ...), custom_call_target="tpu_custom_call" | custom-call | flops 134217728 | bytes 2097152 | tf_op jit(solution)/shard_map/pallas_call | solution.py:189
  75.4 0.6 collective-permute-start.5
  75.9 4.9 %collective-permute-done.15.got = f32[256,256]{1,0:T(8,128)S(1)} collective-permute-done((f32[256,256]{1,0:T(8,128)S(1)}, f32[256,256]{1,0:T(8,128)S(1)}, u32[]{:S(2)}, u32[]{:S(2)}) %collective-permute-start.15) | collective-permute-done | bytes 262176 | tf_op jit(solution)/shard_map/ppermute | solution.py:18
  80.8 0.4 shard_map.79
  81.3 0.1 collective-permute-start.16
  81.4 3.8 %collective-permute-done.5.got = f32[256,256]{1,0:T(8,128)S(1)} collective-permute-done((f32[256,256]{1,0:T(8,128)S(1)}, f32[256,256]{1,0:T(8,128)S(1)}, u32[]{:S(2)}, u32[]{:S(2)}) %collective-permute-start.5) | collective-permute-done | bytes 262176 | tf_op jit(solution)/shard_map/ppermute | solution.py:18
  85.2 0.4 shard_map.70
  85.6 0.1 collective-permute-start.6
  85.7 0.4 shard_map.80
  86.1 0.1 collective-permute-start.17
  86.2 1.0 collective-permute-done.6.got
  87.2 0.4 shard_map.71
  87.6 2.0 %collective-permute-start.7 = (f32[256,256]{1,0:T(8,128)S(1)}, f32[256,256]{1,0:T(8,128)S(1)}, u32[]{:S(2)}, u32[]{:S(2)}) collective-permute-start(f32[256,256]{1,0:T(8,128)S(1)} %get-tuple-element.33), channel_id=1, source_target_pairs={{0,4},{1,5},{2,6},{3,7},{4,0},{5,1},{6,2},{7,3},{8,12},{9,13},{10,... | collective-permute-start | bytes 786440 | tf_op jit(solution)/shard_map/ppermute | solution.py:18
  89.6 17.8 %collective-permute-done.17.got = f32[256,256]{1,0:T(8,128)S(1)} collective-permute-done((f32[256,256]{1,0:T(8,128)S(1)}, f32[256,256]{1,0:T(8,128)S(1)}, u32[]{:S(2)}, u32[]{:S(2)}) %collective-permute-start.17) | collective-permute-done | bytes 262176 | tf_op jit(solution)/shard_map/ppermute | solution.py:18
  107.4 0.4 shard_map.81
  107.8 0.1 collective-permute-start.18
  107.9 4.9 %collective-permute-done.7.got = f32[256,256]{1,0:T(8,128)S(1)} collective-permute-done((f32[256,256]{1,0:T(8,128)S(1)}, f32[256,256]{1,0:T(8,128)S(1)}, u32[]{:S(2)}, u32[]{:S(2)}) %collective-permute-start.7) | collective-permute-done | bytes 262176 | tf_op jit(solution)/shard_map/ppermute | solution.py:18
  112.7 0.4 shard_map.72
  113.1 0.1 collective-permute-start.8
  113.2 5.1 %collective-permute-done.18.got = f32[256,256]{1,0:T(8,128)S(1)} collective-permute-done((f32[256,256]{1,0:T(8,128)S(1)}, f32[256,256]{1,0:T(8,128)S(1)}, u32[]{:S(2)}, u32[]{:S(2)}) %collective-permute-start.18) | collective-permute-done | bytes 262176 | tf_op jit(solution)/shard_map/ppermute | solution.py:18
  118.3 0.4 shard_map.82
  118.7 1.6 %collective-permute-start.19 = (f32[256,256]{1,0:T(8,128)S(1)}, f32[256,256]{1,0:T(8,128)S(1)}, u32[]{:S(2)}, u32[]{:S(2)}) collective-permute-start(f32[256,256]{1,0:T(8,128)S(1)} %get-tuple-element.48), channel_id=1, source_target_pairs={{0,1},{1,0},{2,3},{3,2},{4,5},{5,4},{6,7},{7,6},{8,9},{9,8},{10,11... | collective-permute-start | bytes 786440 | tf_op jit(solution)/shard_map/ppermute | solution.py:18
  120.4 3.5 %collective-permute-done.8.got = f32[256,256]{1,0:T(8,128)S(1)} collective-permute-done((f32[256,256]{1,0:T(8,128)S(1)}, f32[256,256]{1,0:T(8,128)S(1)}, u32[]{:S(2)}, u32[]{:S(2)}) %collective-permute-start.8) | collective-permute-done | bytes 262176 | tf_op jit(solution)/shard_map/ppermute | solution.py:18
  123.8 0.4 shard_map.73
  124.3 1.6 %collective-permute-start.9 = (f32[256,256]{1,0:T(8,128)S(1)}, f32[256,256]{1,0:T(8,128)S(1)}, u32[]{:S(2)}, u32[]{:S(2)}) collective-permute-start(f32[256,256]{1,0:T(8,128)S(1)} %get-tuple-element.37), channel_id=1, source_target_pairs={{0,1},{1,0},{2,3},{3,2},{4,5},{5,4},{6,7},{7,6},{8,9},{9,8},{10,11... | collective-permute-start | bytes 786440 | tf_op jit(solution)/shard_map/ppermute | solution.py:18
  125.9 1.0 collective-permute-done.19.rest_3_
  126.9 5.6 %collective-permute-done.9.rest_1_ = f32[256,256]{1,0:T(8,128)S(1)} collective-permute-done((f32[256,256]{1,0:T(8,128)S(1)}, f32[256,256]{1,0:T(8,128)S(1)}, u32[]{:S(2)}, u32[]{:S(2)}) %collective-permute-start.9) | collective-permute-done | bytes 262176 | tf_op jit(solution)/shard_map/ppermute | solution.py:18
  132.6 2.5 %shard_map.83 = f32[1024,256]{1,0:T(8,128)} custom-call(f32[4,128,256]{2,1,0:T(8,128)S(1)} %copy-done.5, f32[7,4,128,256]{3,2,1,0:T(8,128)S(1)} %copy-done.3, f32[256,256]{1,0:T(8,128)S(1)} %get-tuple-element.36.rest_0_, f32[256,256]{1,0:T(8,128)S(1)} %collective-permute-done.9.rest_1_, f32[256,256]{1,0:T(8,128)S(1)} %get-tuple-element.47.rest_2_, ...), custom_call_target="tpu_custom_call" | custom-call | flops 201326592 | bytes 6291456 | tf_op jit(solution)/shard_map/pallas_call | solution.py:213
  (17 shorter events, 0.0 us)
Async XLA Ops:
  0.0 2.0 %copy-start = (f32[7,4,128,256]{3,2,1,0:T(8,128)S(1)}, f32[7,4,128,256]{3,2,1,0:T(8,128)}, u32[]{:S(2)}) copy-start(f32[7,4,128,256]{3,2,1,0:T(8,128)} %factors.39) | copy-start | bytes 11010052
  2.0 1.0 copy-start.4
  3.1 1.2 copy-start.7
  4.3 0.7 copy-start.8
  5.0 13.1 %copy-start.1 = (f32[7,4,128,256]{3,2,1,0:T(8,128)S(1)}, f32[7,4,128,256]{3,2,1,0:T(8,128)}, u32[]{:S(2)}) copy-start(f32[7,4,128,256]{3,2,1,0:T(8,128)} %factors.39) | copy-start | bytes 11010052
  7.7 10.3 %collective-permute-start = (f32[260,256]{1,0:T(8,128)S(1)}, f32[260,256]{1,0:T(8,128)S(1)}, u32[]{:S(2)}, u32[]{:S(2)}) collective-permute-start(f32[260,256]{1,0:T(8,128)S(1)} %get-tuple-element.27.own), channel_id=1, source_target_pairs={{0,1},{1,0},{2,3},{3,2},{4,5},{5,4},{6,7},{7,6},{8,9},{9,8},{10,11... | collective-permute-start | bytes 798728 | tf_op jit(solution)/shard_map/ppermute | solution.py:18
  10.7 12.1 %collective-permute-start.10 = (f32[256,256]{1,0:T(8,128)S(1)}, f32[256,256]{1,0:T(8,128)S(1)}, u32[]{:S(2)}, u32[]{:S(2)}) collective-permute-start(f32[256,256]{1,0:T(8,128)S(1)} %get-tuple-element.38.own), channel_id=1, source_target_pairs={{0,1},{1,0},{2,3},{3,2},{4,5},{5,4},{6,7},{7,6},{8,9},{9,8},{10,11... | collective-permute-start | bytes 786440 | tf_op jit(solution)/shard_map/ppermute | solution.py:18
  18.4 7.0 %collective-permute-start.1 = (f32[264,256]{1,0:T(8,128)S(1)}, f32[264,256]{1,0:T(8,128)S(1)}, u32[]{:S(2)}, u32[]{:S(2)}) collective-permute-start(f32[264,256]{1,0:T(8,128)S(1)} %shard_map.65.own), channel_id=1, source_target_pairs={{0,2},{1,3},{2,0},{3,1},{4,6},{5,7},{6,4},{7,5},{8,10},{9,11},{10,... | collective-permute-start | bytes 811016 | tf_op jit(solution)/shard_map/ppermute | solution.py:18
  23.2 13.3 %collective-permute-start.11 = (f32[256,256]{1,0:T(8,128)S(1)}, f32[256,256]{1,0:T(8,128)S(1)}, u32[]{:S(2)}, u32[]{:S(2)}) collective-permute-start(f32[256,256]{1,0:T(8,128)S(1)} %shard_map.74.own), channel_id=1, source_target_pairs={{0,2},{1,3},{2,0},{3,1},{4,6},{5,7},{6,4},{7,5},{8,10},{9,11},{10,... | collective-permute-start | bytes 786440 | tf_op jit(solution)/shard_map/ppermute | solution.py:18
  25.7 19.8 %collective-permute-start.2 = (f32[272,256]{1,0:T(8,128)S(1)}, f32[272,256]{1,0:T(8,128)S(1)}, u32[]{:S(2)}, u32[]{:S(2)}) collective-permute-start(f32[272,256]{1,0:T(8,128)S(1)} %shard_map.66.own), channel_id=1, source_target_pairs={{0,4},{1,5},{2,6},{3,7},{4,0},{5,1},{6,2},{7,3},{8,12},{9,13},{10,... | collective-permute-start | bytes 835592 | tf_op jit(solution)/shard_map/ppermute | solution.py:18
  36.8 14.0 %collective-permute-start.12 = (f32[256,256]{1,0:T(8,128)S(1)}, f32[256,256]{1,0:T(8,128)S(1)}, u32[]{:S(2)}, u32[]{:S(2)}) collective-permute-start(f32[256,256]{1,0:T(8,128)S(1)} %shard_map.75.own), channel_id=1, source_target_pairs={{0,4},{1,5},{2,6},{3,7},{4,0},{5,1},{6,2},{7,3},{8,12},{9,13},{10,... | collective-permute-start | bytes 786440 | tf_op jit(solution)/shard_map/ppermute | solution.py:18
  45.8 5.4 %collective-permute-start.3 = (f32[288,256]{1,0:T(8,128)S(1)}, f32[288,256]{1,0:T(8,128)S(1)}, u32[]{:S(2)}, u32[]{:S(2)}) collective-permute-start(f32[288,256]{1,0:T(8,128)S(1)} %shard_map.67.own), channel_id=1, source_target_pairs={{0,8},{8,0},{16,24},{24,16},{1,9},{9,1},{17,25},{25,17},{2,10},{10... | collective-permute-start | bytes 884744 | tf_op jit(solution)/shard_map/ppermute | solution.py:18
  51.1 3.5 %copy-start.9 = (s32[4]{0:T(128)S(1)}, s32[4]{0:T(128)}, u32[]{:S(2)}) copy-start(s32[4]{0:T(128)} %param.11) | copy-start | bytes 52
  51.1 16.2 %copy-start.6 = (f32[4,256,128]{2,1,0:T(8,128)S(1)}, f32[4,256,128]{2,1,0:T(8,128)}, u32[]{:S(2)}) copy-start(f32[4,256,128]{2,1,0:T(8,128)} %leaf_out.3) | copy-start | bytes 1572868
  51.1 2.0 %collective-permute-start.13 = (f32[256,256]{1,0:T(8,128)S(1)}, f32[256,256]{1,0:T(8,128)S(1)}, u32[]{:S(2)}, u32[]{:S(2)}) collective-permute-start(f32[256,256]{1,0:T(8,128)S(1)} %shard_map.76.own), channel_id=1, source_target_pairs={{0,8},{8,0},{16,24},{24,16},{1,9},{9,1},{17,25},{25,17},{2,10},{10... | collective-permute-start | bytes 786440 | tf_op jit(solution)/shard_map/ppermute | solution.py:18
  51.5 15.8 %collective-permute-start.4 = (f32[320,256]{1,0:T(8,128)S(1)}, f32[320,256]{1,0:T(8,128)S(1)}, u32[]{:S(2)}, u32[]{:S(2)}) collective-permute-start(f32[320,256]{1,0:T(8,128)S(1)} %shard_map.68.own.tab_own), channel_id=1, source_target_pairs={{0,16},{8,24},{16,0},{24,8},{1,17},{9,25},{17,1},{25,9},{2,18},{10... | collective-permute-start | bytes 983048 | tf_op jit(solution)/shard_map/ppermute | solution.py:18
  53.4 13.9 %collective-permute-start.14 = (f32[256,256]{1,0:T(8,128)S(1)}, f32[256,256]{1,0:T(8,128)S(1)}, u32[]{:S(2)}, u32[]{:S(2)}) collective-permute-start(f32[256,256]{1,0:T(8,128)S(1)} %shard_map.77.own), channel_id=1, source_target_pairs={{0,16},{8,24},{16,0},{24,8},{1,17},{9,25},{17,1},{25,9},{2,18},{10... | collective-permute-start | bytes 786440 | tf_op jit(solution)/shard_map/ppermute | solution.py:18
  67.3 2.0 %copy-start.2 = (f32[7,4,128,256]{3,2,1,0:T(8,128)S(1)}, f32[7,4,128,256]{3,2,1,0:T(8,128)}, u32[]{:S(2)}) copy-start(f32[7,4,128,256]{3,2,1,0:T(8,128)} %factors.39) | copy-start | bytes 11010052
  71.6 9.3 %collective-permute-start.15 = (f32[256,256]{1,0:T(8,128)S(1)}, f32[256,256]{1,0:T(8,128)S(1)}, u32[]{:S(2)}, u32[]{:S(2)}) collective-permute-start(f32[256,256]{1,0:T(8,128)S(1)} %get-tuple-element.40), channel_id=1, source_target_pairs={{0,16},{8,24},{16,0},{24,8},{1,17},{9,25},{17,1},{25,9},{2,18},{10... | collective-permute-start | bytes 786440 | tf_op jit(solution)/shard_map/ppermute | solution.py:18
  75.4 9.8 %collective-permute-start.5 = (f32[256,256]{1,0:T(8,128)S(1)}, f32[256,256]{1,0:T(8,128)S(1)}, u32[]{:S(2)}, u32[]{:S(2)}) collective-permute-start(f32[256,256]{1,0:T(8,128)S(1)} %get-tuple-element.29), channel_id=1, source_target_pairs={{0,16},{8,24},{16,0},{24,8},{1,17},{9,25},{17,1},{25,9},{2,18},{10... | collective-permute-start | bytes 786440 | tf_op jit(solution)/shard_map/ppermute | solution.py:18
  81.3 4.4 %collective-permute-start.16 = (f32[256,256]{1,0:T(8,128)S(1)}, f32[256,256]{1,0:T(8,128)S(1)}, u32[]{:S(2)}, u32[]{:S(2)}) collective-permute-start(f32[256,256]{1,0:T(8,128)S(1)} %get-tuple-element.42), channel_id=1, source_target_pairs={{0,8},{8,0},{16,24},{24,16},{1,9},{9,1},{17,25},{25,17},{2,10},{10... | collective-permute-start | bytes 786440 | tf_op jit(solution)/shard_map/ppermute | solution.py:18
  85.6 1.6 %collective-permute-start.6 = (f32[256,256]{1,0:T(8,128)S(1)}, f32[256,256]{1,0:T(8,128)S(1)}, u32[]{:S(2)}, u32[]{:S(2)}) collective-permute-start(f32[256,256]{1,0:T(8,128)S(1)} %get-tuple-element.31), channel_id=1, source_target_pairs={{0,8},{8,0},{16,24},{24,16},{1,9},{9,1},{17,25},{25,17},{2,10},{10... | collective-permute-start | bytes 786440 | tf_op jit(solution)/shard_map/ppermute | solution.py:18
  86.1 21.3 %collective-permute-start.17 = (f32[256,256]{1,0:T(8,128)S(1)}, f32[256,256]{1,0:T(8,128)S(1)}, u32[]{:S(2)}, u32[]{:S(2)}) collective-permute-start(f32[256,256]{1,0:T(8,128)S(1)} %get-tuple-element.44), channel_id=1, source_target_pairs={{0,4},{1,5},{2,6},{3,7},{4,0},{5,1},{6,2},{7,3},{8,12},{9,13},{10,... | collective-permute-start | bytes 786440 | tf_op jit(solution)/shard_map/ppermute | solution.py:18
  87.6 25.1 %collective-permute-start.7 = (f32[256,256]{1,0:T(8,128)S(1)}, f32[256,256]{1,0:T(8,128)S(1)}, u32[]{:S(2)}, u32[]{:S(2)}) collective-permute-start(f32[256,256]{1,0:T(8,128)S(1)} %get-tuple-element.33), channel_id=1, source_target_pairs={{0,4},{1,5},{2,6},{3,7},{4,0},{5,1},{6,2},{7,3},{8,12},{9,13},{10,... | collective-permute-start | bytes 786440 | tf_op jit(solution)/shard_map/ppermute | solution.py:18
  107.8 10.5 %collective-permute-start.18 = (f32[256,256]{1,0:T(8,128)S(1)}, f32[256,256]{1,0:T(8,128)S(1)}, u32[]{:S(2)}, u32[]{:S(2)}) collective-permute-start(f32[256,256]{1,0:T(8,128)S(1)} %get-tuple-element.46), channel_id=1, source_target_pairs={{0,2},{1,3},{2,0},{3,1},{4,6},{5,7},{6,4},{7,5},{8,10},{9,11},{10,... | collective-permute-start | bytes 786440 | tf_op jit(solution)/shard_map/ppermute | solution.py:18
  113.1 10.7 %collective-permute-start.8 = (f32[256,256]{1,0:T(8,128)S(1)}, f32[256,256]{1,0:T(8,128)S(1)}, u32[]{:S(2)}, u32[]{:S(2)}) collective-permute-start(f32[256,256]{1,0:T(8,128)S(1)} %get-tuple-element.35), channel_id=1, source_target_pairs={{0,2},{1,3},{2,0},{3,1},{4,6},{5,7},{6,4},{7,5},{8,10},{9,11},{10,... | collective-permute-start | bytes 786440 | tf_op jit(solution)/shard_map/ppermute | solution.py:18
  118.3 14.2 %copy-start.3 = (f32[7,4,128,256]{3,2,1,0:T(8,128)S(1)}, f32[7,4,128,256]{3,2,1,0:T(8,128)}, u32[]{:S(2)}) copy-start(f32[7,4,128,256]{3,2,1,0:T(8,128)} %factors.39) | copy-start | bytes 11010052
  118.3 14.2 %copy-start.5 = (f32[4,128,256]{2,1,0:T(8,128)S(1)}, f32[4,128,256]{2,1,0:T(8,128)}, u32[]{:S(2)}) copy-start(f32[4,128,256]{2,1,0:T(8,128)} %leaf_in.3) | copy-start | bytes 1572868
  118.7 8.2 %collective-permute-start.19 = (f32[256,256]{1,0:T(8,128)S(1)}, f32[256,256]{1,0:T(8,128)S(1)}, u32[]{:S(2)}, u32[]{:S(2)}) collective-permute-start(f32[256,256]{1,0:T(8,128)S(1)} %get-tuple-element.48), channel_id=1, source_target_pairs={{0,1},{1,0},{2,3},{3,2},{4,5},{5,4},{6,7},{7,6},{8,9},{9,8},{10,11... | collective-permute-start | bytes 786440 | tf_op jit(solution)/shard_map/ppermute | solution.py:18
  124.3 8.3 %collective-permute-start.9 = (f32[256,256]{1,0:T(8,128)S(1)}, f32[256,256]{1,0:T(8,128)S(1)}, u32[]{:S(2)}, u32[]{:S(2)}) collective-permute-start(f32[256,256]{1,0:T(8,128)S(1)} %get-tuple-element.37), channel_id=1, source_target_pairs={{0,1},{1,0},{2,3},{3,2},{4,5},{5,4},{6,7},{7,6},{8,9},{9,8},{10,11... | collective-permute-start | bytes 786440 | tf_op jit(solution)/shard_map/ppermute | solution.py:18

commit v3 on v2

v3 whole, which is shorter than its diff:
```python
import functools

import jax
import jax.numpy as jnp
from jax import lax
from jax.experimental import pallas as pl
from jax.experimental.pallas import tpu as pltpu
from jax.sharding import PartitionSpec as P

MIB = 1 << 20
OFFSET = 1.5
TURN = 1.0
VMEM = pl.BlockSpec(memory_space=pltpu.VMEM)
SMEM = pl.BlockSpec(memory_space=pltpu.SMEM)
HBM = pl.BlockSpec(memory_space=pltpu.HBM)


def exchange(value, axis, bit):
    return lax.ppermute(value, axis, [(i, i ^ 1 << bit) for i in range(lax.axis_size(axis))])


def split(value):
    high = value.astype(jnp.bfloat16)
    return high, (value - high.astype(jnp.float32)).astype(jnp.bfloat16)


def product(a, b):
    one = functools.partial(jnp.dot, preferred_element_type=jnp.float32)
    return one(a[0], b[1]) + one(a[1], b[0]) + one(a[0], b[0])


def turned(value):
    return split(value.T)


def call(kernel, outs, specs, out_specs, flops, traffic, scratch=(), limit=8 * MIB):
    return pl.pallas_call(
        kernel,
        out_shape=outs,
        in_specs=specs,
        out_specs=out_specs,
        scratch_shapes=scratch,
        cost_estimate=pl.CostEstimate(flops=flops, bytes_accessed=traffic, transcendentals=0),
        compiler_params=pltpu.CompilerParams(vmem_limit_bytes=limit),
    )


def lead_kernel(table, out):
    out[...] = table[...]


def start_kernel(nodes, rank, leaf, local_bits, source, leaf_in, factors, table, *rest):
    outs, (x, a, f, sems) = rest[: nodes + 1], rest[nodes + 1 :]
    levels = [pltpu.make_async_copy(factors.at[l], f.at[l], sems.at[2 * nodes + l]) for l in range(local_bits)]
    xs = [pltpu.make_async_copy(source.at[pl.ds(j * leaf, leaf)], x.at[j], sems.at[j]) for j in range(nodes)]
    ins = [pltpu.make_async_copy(leaf_in.at[j], a.at[j], sems.at[nodes + j]) for j in range(nodes)]
    for j in range(nodes):
        ins[j].start()
        xs[j].start()
    for copy in levels:
        copy.start()
    values = []
    for j in range(nodes):
        ins[j].wait()
        xs[j].wait()
        values.append(product(split(a[j]), split(x[j])))
    for l in range(local_bits - 1):
        levels[l].wait()
        halves = [split(v) for v in values]
        values = []
        for j in range(nodes):
            mine, other = halves[j], halves[j ^ 1 << l]
            both = tuple(jnp.concatenate([m, o], axis=0) for m, o in zip(mine, other))
            values.append(product(split(f[l, j]), both))
    levels[-1].wait()
    both = split(jnp.concatenate([values[0], values[nodes // 2]], axis=0))
    outs[0][pl.ds(0, rank), :] = product(split(f[local_bits - 1, 0]), both)
    outs[0][pl.ds(rank, table.shape[0]), :] = table[...]
    for j in range(1, nodes):
        outs[j][...] = values[j]
    outs[nodes][0] = values[0]


def forward_kernel(node, rank, level, own, got, factors, token, out):
    both = split(jnp.concatenate([own[pl.ds(0, rank), :], got[pl.ds(0, rank), :]], axis=0))
    out[pl.ds(0, rank), :] = product(split(factors[level, node]), both)
    extra = out.shape[0] - rank
    if extra:
        half = extra // 2
        out[pl.ds(rank, half), :] = own[pl.ds(rank, half), :]
        out[pl.ds(rank + half, half), :] = got[pl.ds(rank, half), :]


def middle_kernel(node, rank, level, index, own, got, tab_own, tab_got, factors, leaf_out, token, keep, send):
    half = tab_own.shape[0] - rank
    f = factors[level, node]
    both = split(jnp.concatenate([own[pl.ds(0, rank), :], got[pl.ds(0, rank), :]], axis=0))
    value = product(split(f), both)
    l = leaf_out[node]
    image = product(split(l), split(value))
    at = index[node]
    near = rank + jnp.where(at < half, at, at - half)
    weights = jnp.where(at < half, tab_own[pl.ds(near, 1), :], tab_got[pl.ds(near, 1), :])
    value = product(split(l.T * weights), split(image))
    both = product(turned(f), split(value))
    keep[...] = both[:rank]
    send[...] = both[rank:]


def backward_kernel(node, rank, level, own, got, factors, token, keep, send):
    both = product(turned(factors[level, node]), split(own[...] + got[...]))
    keep[...] = both[:rank]
    send[...] = both[rank:]


def end_kernel(nodes, rank, leaf, local_bits, leaf_in, factors, *rest):
    pairs, out, (y, sems) = rest[: 2 * nodes], rest[2 * nodes], rest[2 * nodes + 1 :]
    values = [pairs[2 * j][...] + pairs[2 * j + 1][...] for j in range(nodes)]
    for l in reversed(range(local_bits)):
        both = [product(turned(factors[l, j]), split(values[j])) for j in range(nodes)]
        values = [both[j][:rank] + both[j ^ 1 << l][rank:] for j in range(nodes)]
    copies = []
    for j in range(nodes):
        y[j] = product(turned(leaf_in[j]), split(values[j]))
        copies.append(pltpu.make_async_copy(y.at[j], out.at[pl.ds(j * leaf, leaf)], sems.at[j]))
        copies[-1].start()
    for copy in copies:
        copy.wait()


def task_order(chunks, remote, col_levels):
    times = [2.5 if k == col_levels - 1 else 2.0 if k < col_levels else 0.5 if k == col_levels else 1.5 for k in range(remote)]
    times = times + times[::-1]
    starts = [sum(times[:s]) + (TURN if s >= remote else 0.0) for s in range(2 * remote)]
    tasks = [(c, s) for c in range(chunks) for s in range(2 * remote)]
    return sorted(tasks, key=lambda t: (starts[t[1]] + OFFSET * t[0], -t[1]))


def body(source, leaf_in, factors, leaf_out, weight_table, block_index):
    level_count = factors.shape[0]
    nodes, rank, leaf = leaf_in.shape
    width = source.shape[1]
    f32 = jnp.float32
    local_bits = nodes.bit_length() - 1
    col_size = lax.axis_size("col")
    col_bits = col_size.bit_length() - 1
    remote = level_count - local_bits
    where = {}
    for level in range(local_bits, level_count):
        position = level - local_bits
        where[level] = ("col", position) if position < col_bits else ("row", position - col_bits)
    table_rows = weight_table.shape[0]

    me = lax.axis_index("row") * col_size + lax.axis_index("col")
    place = ((block_index // table_rows) ^ me) * table_rows + block_index % table_rows

    def shape(rows):
        return jax.ShapeDtypeStruct((rows, width), f32)

    unit, size = 1, 1
    rows = call(lead_kernel, shape(table_rows), [VMEM], VMEM, 1 << 33, 1)(weight_table)
    values = list(
        call(
            functools.partial(start_kernel, nodes, rank, leaf, local_bits),
            [shape(rank + (table_rows if c == 0 else 0)) for c in range(nodes)] + [jax.ShapeDtypeStruct((1, rank, width), f32)],
            [HBM, HBM, HBM, VMEM],
            [VMEM] * (nodes + 1),
            2 * nodes * unit,
            2 * nodes * size,
            [
                pltpu.VMEM((nodes, leaf, width), f32),
                pltpu.VMEM((nodes, rank, leaf), f32),
                pltpu.VMEM((local_bits, nodes, rank, 2 * rank), f32),
                pltpu.SemaphoreType.DMA((2 * nodes + local_bits,)),
            ],
        )(source, leaf_in, factors, rows)
    )
    first = values.pop()[0]
    before = [first] + values[1:]
    token = values[0]
    pairs = [None] * nodes
    for c, s in task_order(nodes, remote, col_bits):
        if s == 0:
            level = local_bits
            if c:
                other = c ^ nodes // 2
                values[c] = call(
                    functools.partial(forward_kernel, c, rank, local_bits - 1),
                    shape(rank), [VMEM] * 4, VMEM, unit, size,
                )(before[c], before[other], factors, token)
                token = values[c]
            pairs[c] = (values[c], exchange(values[c], *where[level]))
        elif s < remote:
            level = local_bits + s
            own, got = pairs[c]
            token = call(
                functools.partial(forward_kernel, c, rank, level - 1),
                shape(2 * own.shape[0] - rank), [VMEM] * 4, VMEM, unit, size,
            )(own, got, factors, token)
            pairs[c] = (token, exchange(token, *where[level]))
            if c == 0:
                table = pairs[0]
        else:
            level = level_count - 1 - (s - remote)
            if s == remote:
                keep, send = call(
                    functools.partial(middle_kernel, c, rank, level),
                    [shape(rank)] * 2, [SMEM] + [VMEM] * 7, [VMEM] * 2, 4 * unit, 2 * size,
                )(place, *pairs[c], *table, factors, leaf_out, token)
            else:
                keep, send = call(
                    functools.partial(backward_kernel, c, rank, level),
                    [shape(rank)] * 2, [VMEM] * 4, [VMEM] * 2, unit, size,
                )(*pairs[c], factors, token)
            token = keep
            pairs[c] = (keep, exchange(send, *where[level]))
    return call(
        functools.partial(end_kernel, nodes, rank, leaf, local_bits),
        shape(nodes * leaf),
        [VMEM] * (2 + 2 * nodes),
        HBM,
        3 * nodes * unit,
        3 * nodes * size,
        [pltpu.VMEM((nodes, leaf, width), f32), pltpu.SemaphoreType.DMA((nodes,))],
    )(leaf_in, factors, *[v for pair in pairs for v in pair])


def solution(mesh):
    placed = (
        P(("row", "col"), None),
        P(("row", "col"), None, None),
        P(None, ("row", "col"), None, None),
        P(("row", "col"), None, None),
        P(("row", "col"), None),
        P(("row", "col")),
    )
    return jax.shard_map(
        body, mesh=mesh, in_specs=placed, out_specs=P(("row", "col"), None), check_vma=False
    )
```

time: 135 us -> 118 us (0.87)
  waiting for transfers between devices: 91.2 us -> 57.3 us
  starting transfers between devices: 21.2 us -> 35.3 us
  Pallas kernels: 15.4 us -> 20.6 us
  local copies, waits for them, and re-layouts: 7.05 us -> 4.55 us
    ppermute x20 -> x40, waiting for transfers between devices: 91.2 us -> 57.3 us  [exchange(): lax.ppermute(value, axis, [(i, i ^ 1 << bit) for i in range(lax.axis_size...]
    ppermute x20 -> x40, starting transfers between devices: 21.2 us -> 35.3 us  [exchange(): lax.ppermute(value, axis, [(i, i ^ 1 << bit) for i in range(lax.axis_size...]
    pallas_call x20 -> x42, Pallas kernels: 15.4 us -> 20.6 us  [the longest x4 6.33 us: body(): call(functools.partial(middle_kernel, c, rank, level), [shape(rank)] * 2,...]
    unnamed x20 -> x16, local copies, waits for them, and re-layouts: 7.05 us -> 4.55 us
  transfers between devices with their start and end apart: 20 -> 40, of which waited for: 16 -> 23; matrix products, arithmetic and copies ran while one was open for 0% -> 0% of each run, Pallas kernels for 6% -> 12%
where the time goes in v3:
time: 118 us
  waiting for transfers between devices  57.3 us (49%)
  starting transfers between devices  35.3 us (30%)
  Pallas kernels  20.6 us (17%)
  local copies, waits for them, and re-layouts  4.55 us (4%)
    ppermute x40, waiting for transfers between devices, exchange(): lax.ppermute(value, axis, [(i, i ^ 1 << bit) for i in range(lax.axis_size...  57.3 us
    ppermute x40, starting transfers between devices, exchange(): lax.ppermute(value, axis, [(i, i ^ 1 << bit) for i in range(lax.axis_size...  35.3 us
    pallas_call x4, Pallas kernels, body(): call(functools.partial(middle_kernel, c, rank, level), [shape(rank)] * 2,...  6.33 us
    pallas_call x16, Pallas kernels, body(): call(functools.partial(backward_kernel, c, rank, level), [shape(rank)] *...  5.03 us
    unnamed x16, local copies, waits for them, and re-layouts  4.55 us
    pallas_call x16, Pallas kernels, body(): call(functools.partial(forward_kernel, c, rank, level - 1), shape(2 * own...  3.49 us
    pallas_call x1, Pallas kernels, body(): call(functools.partial(end_kernel, nodes, rank, leaf, local_bits), shape(...  2.53 us
    pallas_call x1, Pallas kernels, body(): call(functools.partial(start_kernel, nodes, rank, leaf, local_bits), [sha...  2.53 us
  transfers between devices with their start and end apart: 40, of which 23 were waited for; matrix products, arithmetic and copies ran while one was open for 0% of the time, Pallas kernels for 12%

profile of v3, /device:TPU:0, one launch (start us, length us, event | category | flops | bytes accessed | tf_op | source)
XLA Modules:
  0.0 118.2 jit_solution(8853922578632832468)
XLA Ops:
  0.0 0.8 copy-done.6
  0.8 1.2 %copy-done = f32[7,4,128,256]{3,2,1,0:T(8,128)S(1)} copy-done((f32[7,4,128,256]{3,2,1,0:T(8,128)S(1)}, f32[7,4,128,256]{3,2,1,0:T(8,128)}, u32[]{:S(2)}) %copy-start) | copy-done | bytes 3670040
  2.2 0.3 copy-done.5
  2.5 2.5 %shard_map.65 = (f32[132,256]{1,0:T(8,128)S(1)}, f32[128,256]{1,0:T(8,128)S(1)}, f32[128,256]{1,0:T(8,128)S(1)}, f32[128,256]{1,0:T(8,128)S(1)}, f32[1,128,256]{2,1,0:T(8,128)S(1)}) custom-call(f32[1024,256]{1,0:T(8,128)S(1)} %copy-done.5, f32[4,128,256]{2,1,0:T(8,128)S(1)} %copy-done.4, f32[7,4,128,256]{3,2,1,0:T(8,128)S(1)} %copy-done, ...), custom_call_target="tpu_custom_call" | custom-call | flops 8 | bytes 8 | tf_op jit(solution)/shard_map/pallas_call | solution.py:163
  5.0 3.0 %collective-permute-start = (f32[132,256]{1,0:T(8,128)S(1)}, f32[132,256]{1,0:T(8,128)S(1)}, u32[]{:S(2)}, u32[]{:S(2)}) collective-permute-start(f32[132,256]{1,0:T(8,128)S(1)} %get-tuple-element.50.token.own), channel_id=1, source_target_pairs={{0,1},{1,0},{2,3},{3,2},{4,5},{5,4},{6,7},{7,6},{8,9},{9,8},{10,11... | collective-permute-start | bytes 405512 | tf_op jit(solution)/shard_map/ppermute | solution.py:19
  8.3 3.4 %collective-permute-done.got = f32[132,256]{1,0:T(8,128)S(1)} collective-permute-done((f32[132,256]{1,0:T(8,128)S(1)}, f32[132,256]{1,0:T(8,128)S(1)}, u32[]{:S(2)}, u32[]{:S(2)}) %collective-permute-start) | collective-permute-done | bytes 135200 | tf_op jit(solution)/shard_map/ppermute | solution.py:19
  12.0 1.9 %collective-permute-start.1 = (f32[136,256]{1,0:T(8,128)S(1)}, f32[136,256]{1,0:T(8,128)S(1)}, u32[]{:S(2)}, u32[]{:S(2)}) collective-permute-start(f32[136,256]{1,0:T(8,128)S(1)} %shard_map.67.token.own), channel_id=1, source_target_pairs={{0,2},{1,3},{2,0},{3,1},{4,6},{5,7},{6,4},{7,5},{8,10},{9,11},{10,... | collective-permute-start | bytes 417800 | tf_op jit(solution)/shard_map/ppermute | solution.py:19
  13.8 1.5 %collective-permute-start.2 = (f32[128,256]{1,0:T(8,128)S(1)}, f32[128,256]{1,0:T(8,128)S(1)}, u32[]{:S(2)}, u32[]{:S(2)}) collective-permute-start(f32[128,256]{1,0:T(8,128)S(1)} %shard_map.66.token.own), channel_id=1, source_target_pairs={{0,1},{1,0},{2,3},{3,2},{4,5},{5,4},{6,7},{7,6},{8,9},{9,8},{10,11... | collective-permute-start | bytes 393224 | tf_op jit(solution)/shard_map/ppermute | solution.py:19
  15.6 3.2 %collective-permute-done.2.got = f32[128,256]{1,0:T(8,128)S(1)} collective-permute-done((f32[128,256]{1,0:T(8,128)S(1)}, f32[128,256]{1,0:T(8,128)S(1)}, u32[]{:S(2)}, u32[]{:S(2)}) %collective-permute-start.2) | collective-permute-done | bytes 131104 | tf_op jit(solution)/shard_map/ppermute | solution.py:19
  19.3 2.7 %collective-permute-start.3 = (f32[144,256]{1,0:T(8,128)S(1)}, f32[144,256]{1,0:T(8,128)S(1)}, u32[]{:S(2)}, u32[]{:S(2)}) collective-permute-start(f32[144,256]{1,0:T(8,128)S(1)} %shard_map.70.token.own), channel_id=1, source_target_pairs={{0,4},{1,5},{2,6},{3,7},{4,0},{5,1},{6,2},{7,3},{8,12},{9,13},{10,... | collective-permute-start | bytes 442376 | tf_op jit(solution)/shard_map/ppermute | solution.py:19
  21.9 1.5 %collective-permute-start.5 = (f32[128,256]{1,0:T(8,128)S(1)}, f32[128,256]{1,0:T(8,128)S(1)}, u32[]{:S(2)}, u32[]{:S(2)}) collective-permute-start(f32[128,256]{1,0:T(8,128)S(1)} %shard_map.68.token.own), channel_id=1, source_target_pairs={{0,1},{1,0},{2,3},{3,2},{4,5},{5,4},{6,7},{7,6},{8,9},{9,8},{10,11... | collective-permute-start | bytes 393224 | tf_op jit(solution)/shard_map/ppermute | solution.py:19
  23.4 0.5 collective-permute-start.4
  24.1 2.8 %collective-permute-done.5.got = f32[128,256]{1,0:T(8,128)S(1)} collective-permute-done((f32[128,256]{1,0:T(8,128)S(1)}, f32[128,256]{1,0:T(8,128)S(1)}, u32[]{:S(2)}, u32[]{:S(2)}) %collective-permute-start.5) | collective-permute-done | bytes 131104 | tf_op jit(solution)/shard_map/ppermute | solution.py:19
  27.1 1.3 %collective-permute-done.4.got = f32[128,256]{1,0:T(8,128)S(1)} collective-permute-done((f32[128,256]{1,0:T(8,128)S(1)}, f32[128,256]{1,0:T(8,128)S(1)}, u32[]{:S(2)}, u32[]{:S(2)}) %collective-permute-start.4) | collective-permute-done | bytes 131104 | tf_op jit(solution)/shard_map/ppermute | solution.py:19
  28.9 1.4 %collective-permute-start.7 = (f32[128,256]{1,0:T(8,128)S(1)}, f32[128,256]{1,0:T(8,128)S(1)}, u32[]{:S(2)}, u32[]{:S(2)}) collective-permute-start(f32[128,256]{1,0:T(8,128)S(1)} %shard_map.71.token.own), channel_id=1, source_target_pairs={{0,1},{1,0},{2,3},{3,2},{4,5},{5,4},{6,7},{7,6},{8,9},{9,8},{10,11... | collective-permute-start | bytes 393224 | tf_op jit(solution)/shard_map/ppermute | solution.py:19
  30.6 1.2 %collective-permute-start.10 = (f32[128,256]{1,0:T(8,128)S(1)}, f32[128,256]{1,0:T(8,128)S(1)}, u32[]{:S(2)}, u32[]{:S(2)}) collective-permute-start(f32[128,256]{1,0:T(8,128)S(1)} %shard_map.73.token.own), channel_id=1, source_target_pairs={{0,4},{1,5},{2,6},{3,7},{4,0},{5,1},{6,2},{7,3},{8,12},{9,13},{10,... | collective-permute-start | bytes 393224 | tf_op jit(solution)/shard_map/ppermute | solution.py:19
  31.9 3.0 %collective-permute-done.7.got = f32[128,256]{1,0:T(8,128)S(1)} collective-permute-done((f32[128,256]{1,0:T(8,128)S(1)}, f32[128,256]{1,0:T(8,128)S(1)}, u32[]{:S(2)}, u32[]{:S(2)}) %collective-permute-start.7) | collective-permute-done | bytes 131104 | tf_op jit(solution)/shard_map/ppermute | solution.py:19
  34.9 2.0 %copy-done.1 = f32[7,4,128,256]{3,2,1,0:T(8,128)S(1)} copy-done((f32[7,4,128,256]{3,2,1,0:T(8,128)S(1)}, f32[7,4,128,256]{3,2,1,0:T(8,128)}, u32[]{:S(2)}) %copy-start.1) | copy-done | bytes 3670040
  37.1 0.5 collective-permute-start.9
  37.9 1.6 %collective-permute-start.8 = (f32[192,256]{1,0:T(8,128)S(1)}, f32[192,256]{1,0:T(8,128)S(1)}, u32[]{:S(2)}, u32[]{:S(2)}) collective-permute-start(f32[192,256]{1,0:T(8,128)S(1)} %shard_map.76.token.own.tab_own), channel_id=1, source_target_pairs={{0,16},{8,24},{16,0},{24,8},{1,17},{9,25},{17,1},{25,9},{2,18},{10... | collective-permute-start | bytes 589832 | tf_op jit(solution)/shard_map/ppermute | solution.py:19
  39.7 1.0 collective-permute-start.14
  41.0 1.3 %collective-permute-done.12.got = f32[128,256]{1,0:T(8,128)S(1)} collective-permute-done((f32[128,256]{1,0:T(8,128)S(1)}, f32[128,256]{1,0:T(8,128)S(1)}, u32[]{:S(2)}, u32[]{:S(2)}) %collective-permute-start.12) | collective-permute-done | bytes 131104 | tf_op jit(solution)/shard_map/ppermute | solution.py:19
  42.5 1.1 collective-permute-done.9.got
  43.8 0.3 collective-permute-done.8.got.tab_got
  44.2 1.6 %shard_map.81 = (f32[128,256]{1,0:T(8,128)S(1)}, f32[128,256]{1,0:T(8,128)S(1)}) custom-call(s32[4]{0:T(128)S(1)} %fusion.index, f32[192,256]{1,0:T(8,128)S(1)} %shard_map.76.token.own.tab_own, f32[192,256]{1,0:T(8,128)S(1)} %collective-permute-done.8.got.tab_got, f32[192,256]{1,0:T(8,128)S(1)} %shard_map.76.token.own.tab_own, ...), custom_call_target="tpu_custom_call" | custom-call | flops 4 | bytes 2 | tf_op jit(solution)/shard_map/pallas_call | solution.py:206
  45.7 2.3 %collective-permute-done.14.got = f32[128,256]{1,0:T(8,128)S(1)} collective-permute-done((f32[128,256]{1,0:T(8,128)S(1)}, f32[128,256]{1,0:T(8,128)S(1)}, u32[]{:S(2)}, u32[]{:S(2)}) %collective-permute-start.14) | collective-permute-done | bytes 131104 | tf_op jit(solution)/shard_map/ppermute | solution.py:19
  48.3 0.6 collective-permute-start.13
  48.9 1.5 %collective-permute-start.18 = (f32[128,256]{1,0:T(8,128)S(1)}, f32[128,256]{1,0:T(8,128)S(1)}, u32[]{:S(2)}, u32[]{:S(2)}) collective-permute-start(f32[128,256]{1,0:T(8,128)S(1)} %shard_map.79.token.own), channel_id=1, source_target_pairs={{0,16},{8,24},{16,0},{24,8},{1,17},{9,25},{17,1},{25,9},{2,18},{10... | collective-permute-start | bytes 393224 | tf_op jit(solution)/shard_map/ppermute | solution.py:19
  50.6 4.0 %collective-permute-done.13.got = f32[128,256]{1,0:T(8,128)S(1)} collective-permute-done((f32[128,256]{1,0:T(8,128)S(1)}, f32[128,256]{1,0:T(8,128)S(1)}, u32[]{:S(2)}, u32[]{:S(2)}) %collective-permute-start.13) | collective-permute-done | bytes 131104 | tf_op jit(solution)/shard_map/ppermute | solution.py:19
  55.1 2.0 %collective-permute-done.18.got = f32[128,256]{1,0:T(8,128)S(1)} collective-permute-done((f32[128,256]{1,0:T(8,128)S(1)}, f32[128,256]{1,0:T(8,128)S(1)}, u32[]{:S(2)}, u32[]{:S(2)}) %collective-permute-start.18) | collective-permute-done | bytes 131104 | tf_op jit(solution)/shard_map/ppermute | solution.py:19
  57.0 1.6 %shard_map.85 = (f32[128,256]{1,0:T(8,128)S(1)}, f32[128,256]{1,0:T(8,128)S(1)}) custom-call(s32[4]{0:T(128)S(1)} %fusion.index, f32[128,256]{1,0:T(8,128)S(1)} %shard_map.79.token.own, f32[128,256]{1,0:T(8,128)S(1)} %collective-permute-done.18.got, f32[192,256]{1,0:T(8,128)S(1)} %shard_map.76.token.own.tab_own, ...), custom_call_target="tpu_custom_call" | custom-call | flops 4 | bytes 2 | tf_op jit(solution)/shard_map/pallas_call | solution.py:206
  58.9 1.1 collective-permute-start.20
  60.0 1.0 collective-permute-start.23
  61.0 0.3 shard_map.87
  61.6 3.7 %collective-permute-done.20.got = f32[128,256]{1,0:T(8,128)S(1)} collective-permute-done((f32[128,256]{1,0:T(8,128)S(1)}, f32[128,256]{1,0:T(8,128)S(1)}, u32[]{:S(2)}, u32[]{:S(2)}) %collective-permute-start.20) | collective-permute-done | bytes 131104 | tf_op jit(solution)/shard_map/ppermute | solution.py:19
  65.8 1.9 %collective-permute-done.23.got = f32[128,256]{1,0:T(8,128)S(1)} collective-permute-done((f32[128,256]{1,0:T(8,128)S(1)}, f32[128,256]{1,0:T(8,128)S(1)}, u32[]{:S(2)}, u32[]{:S(2)}) %collective-permute-start.23) | collective-permute-done | bytes 131104 | tf_op jit(solution)/shard_map/ppermute | solution.py:19
  67.7 1.6 %shard_map.90 = (f32[128,256]{1,0:T(8,128)S(1)}, f32[128,256]{1,0:T(8,128)S(1)}) custom-call(s32[4]{0:T(128)S(1)} %fusion.index, f32[128,256]{1,0:T(8,128)S(1)} %shard_map.83.token.own, f32[128,256]{1,0:T(8,128)S(1)} %collective-permute-done.23.got, f32[192,256]{1,0:T(8,128)S(1)} %shard_map.76.token.own.tab_own, ...), custom_call_target="tpu_custom_call" | custom-call | flops 4 | bytes 2 | tf_op jit(solution)/shard_map/pallas_call | solution.py:206
  69.3 1.1 collective-permute-start.26
  70.4 1.0 collective-permute-start.25
  71.3 0.3 shard_map.91
  71.7 3.0 %collective-permute-done.19.got = f32[128,256]{1,0:T(8,128)S(1)} collective-permute-done((f32[128,256]{1,0:T(8,128)S(1)}, f32[128,256]{1,0:T(8,128)S(1)}, u32[]{:S(2)}, u32[]{:S(2)}) %collective-permute-start.19) | collective-permute-done | bytes 131104 | tf_op jit(solution)/shard_map/ppermute | solution.py:19
  74.9 0.8 collective-permute-done.26.got
  76.1 1.0 collective-permute-start.28
  77.2 1.6 %shard_map.94 = (f32[128,256]{1,0:T(8,128)S(1)}, f32[128,256]{1,0:T(8,128)S(1)}) custom-call(s32[4]{0:T(128)S(1)} %fusion.index, f32[128,256]{1,0:T(8,128)S(1)} %shard_map.88.token.own, f32[128,256]{1,0:T(8,128)S(1)} %collective-permute-done.25.got, f32[192,256]{1,0:T(8,128)S(1)} %shard_map.76.token.own.tab_own, ...), custom_call_target="tpu_custom_call" | custom-call | flops 4 | bytes 2 | tf_op jit(solution)/shard_map/pallas_call | solution.py:206
  78.8 1.1 collective-permute-start.27
  79.9 1.0 collective-permute-start.24
  81.2 4.7 %collective-permute-done.28.got = f32[128,256]{1,0:T(8,128)S(1)} collective-permute-done((f32[128,256]{1,0:T(8,128)S(1)}, f32[128,256]{1,0:T(8,128)S(1)}, u32[]{:S(2)}, u32[]{:S(2)}) %collective-permute-start.28) | collective-permute-done | bytes 131104 | tf_op jit(solution)/shard_map/ppermute | solution.py:19
  86.2 0.3 shard_map.97
  86.7 2.4 %collective-permute-start.32 = (f32[128,256]{1,0:T(8,128)S(1)}, f32[128,256]{1,0:T(8,128)S(1)}, u32[]{:S(2)}, u32[]{:S(2)}) collective-permute-start(f32[128,256]{1,0:T(8,128)S(1)} %get-tuple-element.81), channel_id=1, source_target_pairs={{0,4},{1,5},{2,6},{3,7},{4,0},{5,1},{6,2},{7,3},{8,12},{9,13},{10,... | collective-permute-start | bytes 393224 | tf_op jit(solution)/shard_map/ppermute | solution.py:19
  89.4 0.3 shard_map.99
  89.7 0.6 collective-permute-start.36
  90.4 9.2 %collective-permute-done.32.got = f32[128,256]{1,0:T(8,128)S(1)} collective-permute-done((f32[128,256]{1,0:T(8,128)S(1)}, f32[128,256]{1,0:T(8,128)S(1)}, u32[]{:S(2)}, u32[]{:S(2)}) %collective-permute-start.32) | collective-permute-done | bytes 131104 | tf_op jit(solution)/shard_map/ppermute | solution.py:19
  100.3 1.5 %collective-permute-done.36.got = f32[128,256]{1,0:T(8,128)S(1)} collective-permute-done((f32[128,256]{1,0:T(8,128)S(1)}, f32[128,256]{1,0:T(8,128)S(1)}, u32[]{:S(2)}, u32[]{:S(2)}) %collective-permute-start.36) | collective-permute-done | bytes 131104 | tf_op jit(solution)/shard_map/ppermute | solution.py:19
  102.2 0.5 collective-permute-start.38
  102.7 1.2 collective-permute-start.30
  103.9 0.9 collective-permute-start.34
  104.8 0.8 collective-permute-done.35.got
  105.9 1.2 %collective-permute-start.37 = (f32[128,256]{1,0:T(8,128)S(1)}, f32[128,256]{1,0:T(8,128)S(1)}, u32[]{:S(2)}, u32[]{:S(2)}) collective-permute-start(f32[128,256]{1,0:T(8,128)S(1)} %get-tuple-element.91), channel_id=1, source_target_pairs={{0,1},{1,0},{2,3},{3,2},{4,5},{5,4},{6,7},{7,6},{8,9},{9,8},{10,11... | collective-permute-start | bytes 393224 | tf_op jit(solution)/shard_map/ppermute | solution.py:19
  107.1 0.7 collective-permute-done.38.got
  108.1 1.2 %collective-permute-start.39 = (f32[128,256]{1,0:T(8,128)S(1)}, f32[128,256]{1,0:T(8,128)S(1)}, u32[]{:S(2)}, u32[]{:S(2)}) collective-permute-start(f32[128,256]{1,0:T(8,128)S(1)} %get-tuple-element.94), channel_id=1, source_target_pairs={{0,1},{1,0},{2,3},{3,2},{4,5},{5,4},{6,7},{7,6},{8,9},{9,8},{10,11... | collective-permute-start | bytes 393224 | tf_op jit(solution)/shard_map/ppermute | solution.py:19
  109.3 2.7 %collective-permute-done.34.rest_3_ = f32[128,256]{1,0:T(8,128)S(1)} collective-permute-done((f32[128,256]{1,0:T(8,128)S(1)}, f32[128,256]{1,0:T(8,128)S(1)}, u32[]{:S(2)}, u32[]{:S(2)}) %collective-permute-start.34) | collective-permute-done | bytes 131104 | tf_op jit(solution)/shard_map/ppermute | solution.py:19
  112.0 2.3 %collective-permute-done.37.rest_5_ = f32[128,256]{1,0:T(8,128)S(1)} collective-permute-done((f32[128,256]{1,0:T(8,128)S(1)}, f32[128,256]{1,0:T(8,128)S(1)}, u32[]{:S(2)}, u32[]{:S(2)}) %collective-permute-start.37) | collective-permute-done | bytes 131104 | tf_op jit(solution)/shard_map/ppermute | solution.py:19
  114.3 1.4 %collective-permute-done.39.rest_7_ = f32[128,256]{1,0:T(8,128)S(1)} collective-permute-done((f32[128,256]{1,0:T(8,128)S(1)}, f32[128,256]{1,0:T(8,128)S(1)}, u32[]{:S(2)}, u32[]{:S(2)}) %collective-permute-start.39) | collective-permute-done | bytes 131104 | tf_op jit(solution)/shard_map/ppermute | solution.py:19
  115.7 2.5 %shard_map.105 = f32[1024,256]{1,0:T(8,128)} custom-call(f32[4,128,256]{2,1,0:T(8,128)S(1)} %copy-done.4, f32[7,4,128,256]{3,2,1,0:T(8,128)S(1)} %copy-done.2, f32[128,256]{1,0:T(8,128)S(1)} %get-tuple-element.78.token.rest_0_, f32[128,256]{1,0:T(8,128)S(1)} %collective-permute-done.30.rest_1_, f32[128,256]{1,0:T(8,128)S(1)} %get-tuple-element.85.token.rest_2_, ...), custom_call_target="tpu_custom_call" | custom-call | flops 12 | bytes 12 | tf_op jit(solution)/shard_map/pallas_call | solution.py:217
  (75 shorter events, 9.2 us)
Async XLA Ops:
  0.0 2.1 %copy-start = (f32[7,4,128,256]{3,2,1,0:T(8,128)S(1)}, f32[7,4,128,256]{3,2,1,0:T(8,128)}, u32[]{:S(2)}) copy-start(f32[7,4,128,256]{3,2,1,0:T(8,128)} %factors.81) | copy-start | bytes 11010052
  0.0 2.2 %copy-start.4 = (f32[4,128,256]{2,1,0:T(8,128)S(1)}, f32[4,128,256]{2,1,0:T(8,128)}, u32[]{:S(2)}) copy-start(f32[4,128,256]{2,1,0:T(8,128)} %leaf_in.3) | copy-start | bytes 1572868
  0.0 2.5 %copy-start.5 = (f32[1024,256]{1,0:T(8,128)S(1)}, f32[1024,256]{1,0:T(8,128)}, u32[]{:S(2)}) copy-start(f32[1024,256]{1,0:T(8,128)} %source.1) | copy-start | bytes 3145732
  0.0 0.8 copy-start.6
  5.0 6.7 %collective-permute-start = (f32[132,256]{1,0:T(8,128)S(1)}, f32[132,256]{1,0:T(8,128)S(1)}, u32[]{:S(2)}, u32[]{:S(2)}) collective-permute-start(f32[132,256]{1,0:T(8,128)S(1)} %get-tuple-element.50.token.own), channel_id=1, source_target_pairs={{0,1},{1,0},{2,3},{3,2},{4,5},{5,4},{6,7},{7,6},{8,9},{9,8},{10,11... | collective-permute-start | bytes 405512 | tf_op jit(solution)/shard_map/ppermute | solution.py:19
  12.0 7.0 %collective-permute-start.1 = (f32[136,256]{1,0:T(8,128)S(1)}, f32[136,256]{1,0:T(8,128)S(1)}, u32[]{:S(2)}, u32[]{:S(2)}) collective-permute-start(f32[136,256]{1,0:T(8,128)S(1)} %shard_map.67.token.own), channel_id=1, source_target_pairs={{0,2},{1,3},{2,0},{3,1},{4,6},{5,7},{6,4},{7,5},{8,10},{9,11},{10,... | collective-permute-start | bytes 417800 | tf_op jit(solution)/shard_map/ppermute | solution.py:19
  13.8 5.0 %collective-permute-start.2 = (f32[128,256]{1,0:T(8,128)S(1)}, f32[128,256]{1,0:T(8,128)S(1)}, u32[]{:S(2)}, u32[]{:S(2)}) collective-permute-start(f32[128,256]{1,0:T(8,128)S(1)} %shard_map.66.token.own), channel_id=1, source_target_pairs={{0,1},{1,0},{2,3},{3,2},{4,5},{5,4},{6,7},{7,6},{8,9},{9,8},{10,11... | collective-permute-start | bytes 393224 | tf_op jit(solution)/shard_map/ppermute | solution.py:19
  19.3 9.4 %collective-permute-start.3 = (f32[144,256]{1,0:T(8,128)S(1)}, f32[144,256]{1,0:T(8,128)S(1)}, u32[]{:S(2)}, u32[]{:S(2)}) collective-permute-start(f32[144,256]{1,0:T(8,128)S(1)} %shard_map.70.token.own), channel_id=1, source_target_pairs={{0,4},{1,5},{2,6},{3,7},{4,0},{5,1},{6,2},{7,3},{8,12},{9,13},{10,... | collective-permute-start | bytes 442376 | tf_op jit(solution)/shard_map/ppermute | solution.py:19
  21.9 5.0 %collective-permute-start.5 = (f32[128,256]{1,0:T(8,128)S(1)}, f32[128,256]{1,0:T(8,128)S(1)}, u32[]{:S(2)}, u32[]{:S(2)}) collective-permute-start(f32[128,256]{1,0:T(8,128)S(1)} %shard_map.68.token.own), channel_id=1, source_target_pairs={{0,1},{1,0},{2,3},{3,2},{4,5},{5,4},{6,7},{7,6},{8,9},{9,8},{10,11... | collective-permute-start | bytes 393224 | tf_op jit(solution)/shard_map/ppermute | solution.py:19
  23.4 5.0 %collective-permute-start.4 = (f32[128,256]{1,0:T(8,128)S(1)}, f32[128,256]{1,0:T(8,128)S(1)}, u32[]{:S(2)}, u32[]{:S(2)}) collective-permute-start(f32[128,256]{1,0:T(8,128)S(1)} %shard_map.69.token.own), channel_id=1, source_target_pairs={{0,2},{1,3},{2,0},{3,1},{4,6},{5,7},{6,4},{7,5},{8,10},{9,11},{10,... | collective-permute-start | bytes 393224 | tf_op jit(solution)/shard_map/ppermute | solution.py:19
  28.9 8.8 %collective-permute-start.6 = (f32[160,256]{1,0:T(8,128)S(1)}, f32[160,256]{1,0:T(8,128)S(1)}, u32[]{:S(2)}, u32[]{:S(2)}) collective-permute-start(f32[160,256]{1,0:T(8,128)S(1)} %shard_map.74.token.own), channel_id=1, source_target_pairs={{0,8},{8,0},{16,24},{24,16},{1,9},{9,1},{17,25},{25,17},{2,10},{10... | collective-permute-start | bytes 491528 | tf_op jit(solution)/shard_map/ppermute | solution.py:19
  28.9 5.9 %collective-permute-start.7 = (f32[128,256]{1,0:T(8,128)S(1)}, f32[128,256]{1,0:T(8,128)S(1)}, u32[]{:S(2)}, u32[]{:S(2)}) collective-permute-start(f32[128,256]{1,0:T(8,128)S(1)} %shard_map.71.token.own), channel_id=1, source_target_pairs={{0,1},{1,0},{2,3},{3,2},{4,5},{5,4},{6,7},{7,6},{8,9},{9,8},{10,11... | collective-permute-start | bytes 393224 | tf_op jit(solution)/shard_map/ppermute | solution.py:19
  30.4 9.1 %collective-permute-start.11 = (f32[128,256]{1,0:T(8,128)S(1)}, f32[128,256]{1,0:T(8,128)S(1)}, u32[]{:S(2)}, u32[]{:S(2)}) collective-permute-start(f32[128,256]{1,0:T(8,128)S(1)} %shard_map.72.token.own), channel_id=1, source_target_pairs={{0,2},{1,3},{2,0},{3,1},{4,6},{5,7},{6,4},{7,5},{8,10},{9,11},{10,... | collective-permute-start | bytes 393224 | tf_op jit(solution)/shard_map/ppermute | solution.py:19
  30.6 10.0 %collective-permute-start.10 = (f32[128,256]{1,0:T(8,128)S(1)}, f32[128,256]{1,0:T(8,128)S(1)}, u32[]{:S(2)}, u32[]{:S(2)}) collective-permute-start(f32[128,256]{1,0:T(8,128)S(1)} %shard_map.73.token.own), channel_id=1, source_target_pairs={{0,4},{1,5},{2,6},{3,7},{4,0},{5,1},{6,2},{7,3},{8,12},{9,13},{10,... | collective-permute-start | bytes 393224 | tf_op jit(solution)/shard_map/ppermute | solution.py:19
  34.9 2.0 %copy-start.1 = (f32[7,4,128,256]{3,2,1,0:T(8,128)S(1)}, f32[7,4,128,256]{3,2,1,0:T(8,128)}, u32[]{:S(2)}) copy-start(f32[7,4,128,256]{3,2,1,0:T(8,128)} %factors.81) | copy-start | bytes 11010052
  37.1 6.5 %collective-permute-start.9 = (f32[128,256]{1,0:T(8,128)S(1)}, f32[128,256]{1,0:T(8,128)S(1)}, u32[]{:S(2)}, u32[]{:S(2)}) collective-permute-start(f32[128,256]{1,0:T(8,128)S(1)} %shard_map.75.token.own), channel_id=1, source_target_pairs={{0,2},{1,3},{2,0},{3,1},{4,6},{5,7},{6,4},{7,5},{8,10},{9,11},{10,... | collective-permute-start | bytes 393224 | tf_op jit(solution)/shard_map/ppermute | solution.py:19
  37.9 3.1 %copy-start.7 = (s32[4]{0:T(128)S(1)}, s32[4]{0:T(128)}, u32[]{:S(2)}) copy-start(s32[4]{0:T(128)} %param.11) | copy-start | bytes 52
  37.9 4.4 %copy-start.2 = (f32[7,4,128,256]{3,2,1,0:T(8,128)S(1)}, f32[7,4,128,256]{3,2,1,0:T(8,128)}, u32[]{:S(2)}) copy-start(f32[7,4,128,256]{3,2,1,0:T(8,128)} %factors.81) | copy-start | bytes 11010052
  37.9 6.3 %collective-permute-start.8 = (f32[192,256]{1,0:T(8,128)S(1)}, f32[192,256]{1,0:T(8,128)S(1)}, u32[]{:S(2)}, u32[]{:S(2)}) collective-permute-start(f32[192,256]{1,0:T(8,128)S(1)} %shard_map.76.token.own.tab_own), channel_id=1, source_target_pairs={{0,16},{8,24},{16,0},{24,8},{1,17},{9,25},{17,1},{25,9},{2,18},{10... | collective-permute-start | bytes 589832 | tf_op jit(solution)/shard_map/ppermute | solution.py:19
  39.7 8.3 %collective-permute-start.14 = (f32[128,256]{1,0:T(8,128)S(1)}, f32[128,256]{1,0:T(8,128)S(1)}, u32[]{:S(2)}, u32[]{:S(2)}) collective-permute-start(f32[128,256]{1,0:T(8,128)S(1)} %shard_map.77.token.own), channel_id=1, source_target_pairs={{0,4},{1,5},{2,6},{3,7},{4,0},{5,1},{6,2},{7,3},{8,12},{9,13},{10,... | collective-permute-start | bytes 393224 | tf_op jit(solution)/shard_map/ppermute | solution.py:19
  40.9 1.4 %collective-permute-start.12 = (f32[128,256]{1,0:T(8,128)S(1)}, f32[128,256]{1,0:T(8,128)S(1)}, u32[]{:S(2)}, u32[]{:S(2)}) collective-permute-start(f32[128,256]{1,0:T(8,128)S(1)} %shard_map.78.own.token), channel_id=1, source_target_pairs={{0,8},{8,0},{16,24},{24,16},{1,9},{9,1},{17,25},{25,17},{2,10},{10... | collective-permute-start | bytes 393224 | tf_op jit(solution)/shard_map/ppermute | solution.py:19
  41.0 3.2 %copy-start.3 = (f32[4,256,128]{2,1,0:T(8,128)S(1)}, f32[4,256,128]{2,1,0:T(8,128)}, u32[]{:S(2)}) copy-start(f32[4,256,128]{2,1,0:T(8,128)} %leaf_out.7) | copy-start | bytes 1572868
  48.2 2.2 %collective-permute-start.15 = (f32[128,256]{1,0:T(8,128)S(1)}, f32[128,256]{1,0:T(8,128)S(1)}, u32[]{:S(2)}, u32[]{:S(2)}) collective-permute-start(f32[128,256]{1,0:T(8,128)S(1)} %shard_map.82.own.token), channel_id=1, source_target_pairs={{0,8},{8,0},{16,24},{24,16},{1,9},{9,1},{17,25},{25,17},{2,10},{10... | collective-permute-start | bytes 393224 | tf_op jit(solution)/shard_map/ppermute | solution.py:19
  48.3 6.4 %collective-permute-start.13 = (f32[128,256]{1,0:T(8,128)S(1)}, f32[128,256]{1,0:T(8,128)S(1)}, u32[]{:S(2)}, u32[]{:S(2)}) collective-permute-start(f32[128,256]{1,0:T(8,128)S(1)} %get-tuple-element.56), channel_id=1, source_target_pairs={{0,16},{8,24},{16,0},{24,8},{1,17},{9,25},{17,1},{25,9},{2,18},{10... | collective-permute-start | bytes 393224 | tf_op jit(solution)/shard_map/ppermute | solution.py:19
  48.9 8.1 %collective-permute-start.18 = (f32[128,256]{1,0:T(8,128)S(1)}, f32[128,256]{1,0:T(8,128)S(1)}, u32[]{:S(2)}, u32[]{:S(2)}) collective-permute-start(f32[128,256]{1,0:T(8,128)S(1)} %shard_map.79.token.own), channel_id=1, source_target_pairs={{0,16},{8,24},{16,0},{24,8},{1,17},{9,25},{17,1},{25,9},{2,18},{10... | collective-permute-start | bytes 393224 | tf_op jit(solution)/shard_map/ppermute | solution.py:19
  50.4 8.2 %collective-permute-start.17 = (f32[128,256]{1,0:T(8,128)S(1)}, f32[128,256]{1,0:T(8,128)S(1)}, u32[]{:S(2)}, u32[]{:S(2)}) collective-permute-start(f32[128,256]{1,0:T(8,128)S(1)} %shard_map.80.token.own), channel_id=1, source_target_pairs={{0,4},{1,5},{2,6},{3,7},{4,0},{5,1},{6,2},{7,3},{8,12},{9,13},{10,... | collective-permute-start | bytes 393224 | tf_op jit(solution)/shard_map/ppermute | solution.py:19
  55.0 6.0 %collective-permute-start.16 = (f32[128,256]{1,0:T(8,128)S(1)}, f32[128,256]{1,0:T(8,128)S(1)}, u32[]{:S(2)}, u32[]{:S(2)}) collective-permute-start(f32[128,256]{1,0:T(8,128)S(1)} %get-tuple-element.58), channel_id=1, source_target_pairs={{0,8},{8,0},{16,24},{24,16},{1,9},{9,1},{17,25},{25,17},{2,10},{10... | collective-permute-start | bytes 393224 | tf_op jit(solution)/shard_map/ppermute | solution.py:19
  58.9 2.5 %collective-permute-start.21 = (f32[128,256]{1,0:T(8,128)S(1)}, f32[128,256]{1,0:T(8,128)S(1)}, u32[]{:S(2)}, u32[]{:S(2)}) collective-permute-start(f32[128,256]{1,0:T(8,128)S(1)} %shard_map.86.token.own), channel_id=1, source_target_pairs={{0,8},{8,0},{16,24},{24,16},{1,9},{9,1},{17,25},{25,17},{2,10},{10... | collective-permute-start | bytes 393224 | tf_op jit(solution)/shard_map/ppermute | solution.py:19
  58.9 6.4 %collective-permute-start.20 = (f32[128,256]{1,0:T(8,128)S(1)}, f32[128,256]{1,0:T(8,128)S(1)}, u32[]{:S(2)}, u32[]{:S(2)}) collective-permute-start(f32[128,256]{1,0:T(8,128)S(1)} %get-tuple-element.62), channel_id=1, source_target_pairs={{0,16},{8,24},{16,0},{24,8},{1,17},{9,25},{17,1},{25,9},{2,18},{10... | collective-permute-start | bytes 393224 | tf_op jit(solution)/shard_map/ppermute | solution.py:19
  60.0 7.6 %collective-permute-start.23 = (f32[128,256]{1,0:T(8,128)S(1)}, f32[128,256]{1,0:T(8,128)S(1)}, u32[]{:S(2)}, u32[]{:S(2)}) collective-permute-start(f32[128,256]{1,0:T(8,128)S(1)} %shard_map.83.token.own), channel_id=1, source_target_pairs={{0,16},{8,24},{16,0},{24,8},{1,17},{9,25},{17,1},{25,9},{2,18},{10... | collective-permute-start | bytes 393224 | tf_op jit(solution)/shard_map/ppermute | solution.py:19
  65.6 5.7 %collective-permute-start.22 = (f32[128,256]{1,0:T(8,128)S(1)}, f32[128,256]{1,0:T(8,128)S(1)}, u32[]{:S(2)}, u32[]{:S(2)}) collective-permute-start(f32[128,256]{1,0:T(8,128)S(1)} %get-tuple-element.64), channel_id=1, source_target_pairs={{0,8},{8,0},{16,24},{24,16},{1,9},{9,1},{17,25},{25,17},{2,10},{10... | collective-permute-start | bytes 393224 | tf_op jit(solution)/shard_map/ppermute | solution.py:19
  65.7 8.9 %collective-permute-start.19 = (f32[128,256]{1,0:T(8,128)S(1)}, f32[128,256]{1,0:T(8,128)S(1)}, u32[]{:S(2)}, u32[]{:S(2)}) collective-permute-start(f32[128,256]{1,0:T(8,128)S(1)} %get-tuple-element.61), channel_id=1, source_target_pairs={{0,4},{1,5},{2,6},{3,7},{4,0},{5,1},{6,2},{7,3},{8,12},{9,13},{10,... | collective-permute-start | bytes 393224 | tf_op jit(solution)/shard_map/ppermute | solution.py:19
  69.3 6.5 %collective-permute-start.26 = (f32[128,256]{1,0:T(8,128)S(1)}, f32[128,256]{1,0:T(8,128)S(1)}, u32[]{:S(2)}, u32[]{:S(2)}) collective-permute-start(f32[128,256]{1,0:T(8,128)S(1)} %get-tuple-element.69), channel_id=1, source_target_pairs={{0,16},{8,24},{16,0},{24,8},{1,17},{9,25},{17,1},{25,9},{2,18},{10... | collective-permute-start | bytes 393224 | tf_op jit(solution)/shard_map/ppermute | solution.py:19
  70.4 6.8 %collective-permute-start.25 = (f32[128,256]{1,0:T(8,128)S(1)}, f32[128,256]{1,0:T(8,128)S(1)}, u32[]{:S(2)}, u32[]{:S(2)}) collective-permute-start(f32[128,256]{1,0:T(8,128)S(1)} %shard_map.88.token.own), channel_id=1, source_target_pairs={{0,16},{8,24},{16,0},{24,8},{1,17},{9,25},{17,1},{25,9},{2,18},{10... | collective-permute-start | bytes 393224 | tf_op jit(solution)/shard_map/ppermute | solution.py:19
  76.0 4.8 %collective-permute-start.29 = (f32[128,256]{1,0:T(8,128)S(1)}, f32[128,256]{1,0:T(8,128)S(1)}, u32[]{:S(2)}, u32[]{:S(2)}) collective-permute-start(f32[128,256]{1,0:T(8,128)S(1)} %get-tuple-element.74), channel_id=1, source_target_pairs={{0,8},{8,0},{16,24},{24,16},{1,9},{9,1},{17,25},{25,17},{2,10},{10... | collective-permute-start | bytes 393224 | tf_op jit(solution)/shard_map/ppermute | solution.py:19
  76.1 9.7 %collective-permute-start.28 = (f32[128,256]{1,0:T(8,128)S(1)}, f32[128,256]{1,0:T(8,128)S(1)}, u32[]{:S(2)}, u32[]{:S(2)}) collective-permute-start(f32[128,256]{1,0:T(8,128)S(1)} %get-tuple-element.73), channel_id=1, source_target_pairs={{0,4},{1,5},{2,6},{3,7},{4,0},{5,1},{6,2},{7,3},{8,12},{9,13},{10,... | collective-permute-start | bytes 393224 | tf_op jit(solution)/shard_map/ppermute | solution.py:19
  78.8 7.4 %collective-permute-start.27 = (f32[128,256]{1,0:T(8,128)S(1)}, f32[128,256]{1,0:T(8,128)S(1)}, u32[]{:S(2)}, u32[]{:S(2)}) collective-permute-start(f32[128,256]{1,0:T(8,128)S(1)} %get-tuple-element.72), channel_id=1, source_target_pairs={{0,16},{8,24},{16,0},{24,8},{1,17},{9,25},{17,1},{25,9},{2,18},{10... | collective-permute-start | bytes 393224 | tf_op jit(solution)/shard_map/ppermute | solution.py:19
  79.9 9.2 %collective-permute-start.24 = (f32[128,256]{1,0:T(8,128)S(1)}, f32[128,256]{1,0:T(8,128)S(1)}, u32[]{:S(2)}, u32[]{:S(2)}) collective-permute-start(f32[128,256]{1,0:T(8,128)S(1)} %get-tuple-element.68), channel_id=1, source_target_pairs={{0,2},{1,3},{2,0},{3,1},{4,6},{5,7},{6,4},{7,5},{8,10},{9,11},{10,... | collective-permute-start | bytes 393224 | tf_op jit(solution)/shard_map/ppermute | solution.py:19
  86.5 2.9 %collective-permute-start.33 = (f32[128,256]{1,0:T(8,128)S(1)}, f32[128,256]{1,0:T(8,128)S(1)}, u32[]{:S(2)}, u32[]{:S(2)}) collective-permute-start(f32[128,256]{1,0:T(8,128)S(1)} %get-tuple-element.82), channel_id=1, source_target_pairs={{0,8},{8,0},{16,24},{24,16},{1,9},{9,1},{17,25},{25,17},{2,10},{10... | collective-permute-start | bytes 393224 | tf_op jit(solution)/shard_map/ppermute | solution.py:19
  86.6 13.4 %collective-permute-start.31 = (f32[128,256]{1,0:T(8,128)S(1)}, f32[128,256]{1,0:T(8,128)S(1)}, u32[]{:S(2)}, u32[]{:S(2)}) collective-permute-start(f32[128,256]{1,0:T(8,128)S(1)} %get-tuple-element.80), channel_id=1, source_target_pairs={{0,2},{1,3},{2,0},{3,1},{4,6},{5,7},{6,4},{7,5},{8,10},{9,11},{10,... | collective-permute-start | bytes 393224 | tf_op jit(solution)/shard_map/ppermute | solution.py:19
  86.7 12.9 %collective-permute-start.32 = (f32[128,256]{1,0:T(8,128)S(1)}, f32[128,256]{1,0:T(8,128)S(1)}, u32[]{:S(2)}, u32[]{:S(2)}) collective-permute-start(f32[128,256]{1,0:T(8,128)S(1)} %get-tuple-element.81), channel_id=1, source_target_pairs={{0,4},{1,5},{2,6},{3,7},{4,0},{5,1},{6,2},{7,3},{8,12},{9,13},{10,... | collective-permute-start | bytes 393224 | tf_op jit(solution)/shard_map/ppermute | solution.py:19
  89.7 12.1 %collective-permute-start.36 = (f32[128,256]{1,0:T(8,128)S(1)}, f32[128,256]{1,0:T(8,128)S(1)}, u32[]{:S(2)}, u32[]{:S(2)}) collective-permute-start(f32[128,256]{1,0:T(8,128)S(1)} %get-tuple-element.88), channel_id=1, source_target_pairs={{0,4},{1,5},{2,6},{3,7},{4,0},{5,1},{6,2},{7,3},{8,12},{9,13},{10,... | collective-permute-start | bytes 393224 | tf_op jit(solution)/shard_map/ppermute | solution.py:19
  99.9 5.6 %collective-permute-start.35 = (f32[128,256]{1,0:T(8,128)S(1)}, f32[128,256]{1,0:T(8,128)S(1)}, u32[]{:S(2)}, u32[]{:S(2)}) collective-permute-start(f32[128,256]{1,0:T(8,128)S(1)} %get-tuple-element.87), channel_id=1, source_target_pairs={{0,2},{1,3},{2,0},{3,1},{4,6},{5,7},{6,4},{7,5},{8,10},{9,11},{10,... | collective-permute-start | bytes 393224 | tf_op jit(solution)/shard_map/ppermute | solution.py:19
  102.2 5.6 %collective-permute-start.38 = (f32[128,256]{1,0:T(8,128)S(1)}, f32[128,256]{1,0:T(8,128)S(1)}, u32[]{:S(2)}, u32[]{:S(2)}) collective-permute-start(f32[128,256]{1,0:T(8,128)S(1)} %get-tuple-element.92), channel_id=1, source_target_pairs={{0,2},{1,3},{2,0},{3,1},{4,6},{5,7},{6,4},{7,5},{8,10},{9,11},{10,... | collective-permute-start | bytes 393224 | tf_op jit(solution)/shard_map/ppermute | solution.py:19
  102.7 6.6 %collective-permute-start.30 = (f32[128,256]{1,0:T(8,128)S(1)}, f32[128,256]{1,0:T(8,128)S(1)}, u32[]{:S(2)}, u32[]{:S(2)}) collective-permute-start(f32[128,256]{1,0:T(8,128)S(1)} %get-tuple-element.79), channel_id=1, source_target_pairs={{0,1},{1,0},{2,3},{3,2},{4,5},{5,4},{6,7},{7,6},{8,9},{9,8},{10,11... | collective-permute-start | bytes 393224 | tf_op jit(solution)/shard_map/ppermute | solution.py:19
  103.9 8.1 %collective-permute-start.34 = (f32[128,256]{1,0:T(8,128)S(1)}, f32[128,256]{1,0:T(8,128)S(1)}, u32[]{:S(2)}, u32[]{:S(2)}) collective-permute-start(f32[128,256]{1,0:T(8,128)S(1)} %get-tuple-element.86), channel_id=1, source_target_pairs={{0,1},{1,0},{2,3},{3,2},{4,5},{5,4},{6,7},{7,6},{8,9},{9,8},{10,11... | collective-permute-start | bytes 393224 | tf_op jit(solution)/shard_map/ppermute | solution.py:19
  105.9 8.4 %collective-permute-start.37 = (f32[128,256]{1,0:T(8,128)S(1)}, f32[128,256]{1,0:T(8,128)S(1)}, u32[]{:S(2)}, u32[]{:S(2)}) collective-permute-start(f32[128,256]{1,0:T(8,128)S(1)} %get-tuple-element.91), channel_id=1, source_target_pairs={{0,1},{1,0},{2,3},{3,2},{4,5},{5,4},{6,7},{7,6},{8,9},{9,8},{10,11... | collective-permute-start | bytes 393224 | tf_op jit(solution)/shard_map/ppermute | solution.py:19
  108.1 7.6 %collective-permute-start.39 = (f32[128,256]{1,0:T(8,128)S(1)}, f32[128,256]{1,0:T(8,128)S(1)}, u32[]{:S(2)}, u32[]{:S(2)}) collective-permute-start(f32[128,256]{1,0:T(8,128)S(1)} %get-tuple-element.94), channel_id=1, source_target_pairs={{0,1},{1,0},{2,3},{3,2},{4,5},{5,4},{6,7},{7,6},{8,9},{9,8},{10,11... | collective-permute-start | bytes 393224 | tf_op jit(solution)/shard_map/ppermute | solution.py:19

commit v4 on v3

--- a/solution.py
+++ b/solution.py
@@ -8,8 +8,7 @@
 from jax.sharding import PartitionSpec as P
 
 MIB = 1 << 20
-OFFSET = 1.5
-TURN = 1.0
+UNIT = 1 << 26
 VMEM = pl.BlockSpec(memory_space=pltpu.VMEM)
 SMEM = pl.BlockSpec(memory_space=pltpu.SMEM)
 HBM = pl.BlockSpec(memory_space=pltpu.HBM)
@@ -45,11 +44,11 @@
     )
 
 
-def lead_kernel(table, out):
-    out[...] = table[...]
-
-
-def start_kernel(nodes, rank, leaf, local_bits, source, leaf_in, factors, table, *rest):
+def lead_kernel(out):
+    out[...] = jnp.zeros_like(out)
+
+
+def start_kernel(nodes, rank, leaf, local_bits, source, leaf_in, factors, table, lead, *rest):
     outs, (x, a, f, sems) = rest[: nodes + 1], rest[nodes + 1 :]
     levels = [pltpu.make_async_copy(factors.at[l], f.at[l], sems.at[2 * nodes + l]) for l in range(local_bits)]
     xs = [pltpu.make_async_copy(source.at[pl.ds(j * leaf, leaf)], x.at[j], sems.at[j]) for j in range(nodes)]
@@ -115,8 +114,8 @@
 
 def end_kernel(nodes, rank, leaf, local_bits, leaf_in, factors, *rest):
     pairs, out, (y, sems) = rest[: 2 * nodes], rest[2 * nodes], rest[2 * nodes + 1 :]
-    values = [pairs[2 * j][...] + pairs[2 * j + 1][...] for j in range(nodes)]
-    for l in reversed(range(local_bits)):
+    values = [pairs[2 * j][...] + pairs[2 * (j ^ nodes // 2) + 1][...] for j in range(nodes)]
+    for l in reversed(range(local_bits - 1)):
         both = [product(turned(factors[l, j]), split(values[j])) for j in range(nodes)]
         values = [both[j][:rank] + both[j ^ 1 << l][rank:] for j in range(nodes)]
     copies = []
@@ -128,12 +127,19 @@
         copy.wait()
 
 
-def task_order(chunks, remote, col_levels):
-    times = [2.5 if k == col_levels - 1 else 2.0 if k < col_levels else 0.5 if k == col_levels else 1.5 for k in range(remote)]
-    times = times + times[::-1]
-    starts = [sum(times[:s]) + (TURN if s >= remote else 0.0) for s in range(2 * remote)]
-    tasks = [(c, s) for c in range(chunks) for s in range(2 * remote)]
-    return sorted(tasks, key=lambda t: (starts[t[1]] + OFFSET * t[0], -t[1]))
+def task_order(chunks, stages):
+    order, queue, waits, entered = [], [], 0, 0
+    while len(order) < chunks * stages:
+        while entered < chunks and entered <= waits:
+            order.append((entered, 0))
+            queue.append((entered, 0))
+            entered += 1
+        c, s = queue.pop(0)
+        waits += 1
+        if s + 1 < stages:
+            order.append((c, s + 1))
+            queue.append((c, s + 1))
+    return order
 
 
 def body(source, leaf_in, factors, leaf_out, weight_table, block_index):
@@ -157,13 +163,13 @@
     def shape(rows):
         return jax.ShapeDtypeStruct((rows, width), f32)
 
-    unit, size = 1, 1
-    rows = call(lead_kernel, shape(table_rows), [VMEM], VMEM, 1 << 33, 1)(weight_table)
+    unit, size = UNIT, 1
+    lead = call(lead_kernel, shape(8), [], VMEM, 1 << 33, 1)()
     values = list(
         call(
             functools.partial(start_kernel, nodes, rank, leaf, local_bits),
             [shape(rank + (table_rows if c == 0 else 0)) for c in range(nodes)] + [jax.ShapeDtypeStruct((1, rank, width), f32)],
-            [HBM, HBM, HBM, VMEM],
+            [HBM, HBM, HBM, VMEM, VMEM],
             [VMEM] * (nodes + 1),
             2 * nodes * unit,
             2 * nodes * size,
@@ -173,13 +179,13 @@
                 pltpu.VMEM((local_bits, nodes, rank, 2 * rank), f32),
                 pltpu.SemaphoreType.DMA((2 * nodes + local_bits,)),
             ],
-        )(source, leaf_in, factors, rows)
+        )(source, leaf_in, factors, weight_table, lead)
     )
     first = values.pop()[0]
     before = [first] + values[1:]
     token = values[0]
     pairs = [None] * nodes
-    for c, s in task_order(nodes, remote, col_bits):
+    for c, s in task_order(nodes, 2 * remote + 1):
         if s == 0:
             level = local_bits
             if c:
@@ -213,7 +219,7 @@
                     [shape(rank)] * 2, [VMEM] * 4, [VMEM] * 2, unit, size,
                 )(*pairs[c], factors, token)
             token = keep
-            pairs[c] = (keep, exchange(send, *where[level]))
+            pairs[c] = (keep, exchange(send, *where[level]) if level in where else send)
     return call(
         functools.partial(end_kernel, nodes, rank, leaf, local_bits),
         shape(nodes * leaf),

time: 118 us -> 105 us (0.89)
  waiting for transfers between devices: 57.3 us -> 36.1 us
  starting transfers between devices: 35.3 us -> 42.7 us
    ppermute x40, waiting for transfers between devices: 57.3 us -> 36.1 us  [exchange(): lax.ppermute(value, axis, [(i, i ^ 1 << bit) for i in range(lax.axis_size...]
    ppermute x40, starting transfers between devices: 35.3 us -> 42.7 us  [exchange(): lax.ppermute(value, axis, [(i, i ^ 1 << bit) for i in range(lax.axis_size...]
    pallas_call x16 -> x20, Pallas kernels: 5.03 us -> 6.31 us  [body(): call(functools.partial(backward_kernel, c, rank, level), [shape(rank)] *...]
  transfers between devices with their start and end apart: 40 -> 40, of which waited for: 23 -> 20; matrix products, arithmetic and copies ran while one was open for 0% -> 0% of each run, Pallas kernels for 12% -> 15%
where the time goes in v4:
time: 105 us
  starting transfers between devices  42.7 us (41%)
  waiting for transfers between devices  36.1 us (34%)
  Pallas kernels  21.3 us (20%)
  local copies, waits for them, and re-layouts  4.55 us (4%)
    ppermute x40, starting transfers between devices, exchange(): lax.ppermute(value, axis, [(i, i ^ 1 << bit) for i in range(lax.axis_size...  42.7 us
    ppermute x40, waiting for transfers between devices, exchange(): lax.ppermute(value, axis, [(i, i ^ 1 << bit) for i in range(lax.axis_size...  36.1 us
    pallas_call x4, Pallas kernels, body(): call(functools.partial(middle_kernel, c, rank, level), [shape(rank)] * 2,...  6.34 us
    pallas_call x20, Pallas kernels, body(): call(functools.partial(backward_kernel, c, rank, level), [shape(rank)] *...  6.31 us
    unnamed x16, local copies, waits for them, and re-layouts  4.55 us
    pallas_call x16, Pallas kernels, body(): call(functools.partial(forward_kernel, c, rank, level - 1), shape(2 * own...  3.49 us
    pallas_call x1, Pallas kernels, body(): call(functools.partial(start_kernel, nodes, rank, leaf, local_bits), [sha...  2.53 us
  transfers between devices with their start and end apart: 40, of which 20 were waited for; matrix products, arithmetic and copies ran while one was open for 0% of the time, Pallas kernels for 15%

profile of v4, /device:TPU:0, one launch (start us, length us, event | category | flops | bytes accessed | tf_op | source)
XLA Modules:
  0.0 105.3 jit_solution(5162988288224739389)
XLA Ops:
  0.0 2.0 %copy-done = f32[7,4,128,256]{3,2,1,0:T(8,128)S(1)} copy-done((f32[7,4,128,256]{3,2,1,0:T(8,128)S(1)}, f32[7,4,128,256]{3,2,1,0:T(8,128)}, u32[]{:S(2)}) %copy-start) | copy-done | bytes 3670040
  2.1 0.4 copy-done.5
  2.5 2.5 %shard_map.65 = (f32[132,256]{1,0:T(8,128)S(1)}, f32[128,256]{1,0:T(8,128)S(1)}, f32[128,256]{1,0:T(8,128)S(1)}, f32[128,256]{1,0:T(8,128)S(1)}, f32[1,128,256]{2,1,0:T(8,128)S(1)}) custom-call(f32[1024,256]{1,0:T(8,128)S(1)} %copy-done.5, f32[4,128,256]{2,1,0:T(8,128)S(1)} %copy-done.4, f32[7,4,128,256]{3,2,1,0:T(8,128)S(1)} %copy-done, ...), custom_call_target="tpu_custom_call" | custom-call | flops 536870912 | bytes 8 | tf_op jit(solution)/shard_map/pallas_call | solution.py:169
  5.0 3.0 %collective-permute-start = (f32[132,256]{1,0:T(8,128)S(1)}, f32[132,256]{1,0:T(8,128)S(1)}, u32[]{:S(2)}, u32[]{:S(2)}) collective-permute-start(f32[132,256]{1,0:T(8,128)S(1)} %get-tuple-element.58.own.token), channel_id=1, source_target_pairs={{0,1},{1,0},{2,3},{3,2},{4,5},{5,4},{6,7},{7,6},{8,9},{9,8},{10,11... | collective-permute-start | bytes 405512 | tf_op jit(solution)/shard_map/ppermute | solution.py:18
  8.1 3.7 %collective-permute-done.got = f32[132,256]{1,0:T(8,128)S(1)} collective-permute-done((f32[132,256]{1,0:T(8,128)S(1)}, f32[132,256]{1,0:T(8,128)S(1)}, u32[]{:S(2)}, u32[]{:S(2)}) %collective-permute-start) | collective-permute-done | bytes 135200 | tf_op jit(solution)/shard_map/ppermute | solution.py:18
  12.0 1.9 %collective-permute-start.1 = (f32[136,256]{1,0:T(8,128)S(1)}, f32[136,256]{1,0:T(8,128)S(1)}, u32[]{:S(2)}, u32[]{:S(2)}) collective-permute-start(f32[136,256]{1,0:T(8,128)S(1)} %shard_map.66.token.own), channel_id=1, source_target_pairs={{0,2},{1,3},{2,0},{3,1},{4,6},{5,7},{6,4},{7,5},{8,10},{9,11},{10,... | collective-permute-start | bytes 417800 | tf_op jit(solution)/shard_map/ppermute | solution.py:18
  14.1 1.6 %collective-permute-start.3 = (f32[128,256]{1,0:T(8,128)S(1)}, f32[128,256]{1,0:T(8,128)S(1)}, u32[]{:S(2)}, u32[]{:S(2)}) collective-permute-start(f32[128,256]{1,0:T(8,128)S(1)} %shard_map.67.token.own), channel_id=1, source_target_pairs={{0,1},{1,0},{2,3},{3,2},{4,5},{5,4},{6,7},{7,6},{8,9},{9,8},{10,11... | collective-permute-start | bytes 393224 | tf_op jit(solution)/shard_map/ppermute | solution.py:18
  15.7 1.4 %collective-permute-done.1.got = f32[136,256]{1,0:T(8,128)S(1)} collective-permute-done((f32[136,256]{1,0:T(8,128)S(1)}, f32[136,256]{1,0:T(8,128)S(1)}, u32[]{:S(2)}, u32[]{:S(2)}) %collective-permute-start.1) | collective-permute-done | bytes 139296 | tf_op jit(solution)/shard_map/ppermute | solution.py:18
  17.3 2.9 %collective-permute-start.2 = (f32[144,256]{1,0:T(8,128)S(1)}, f32[144,256]{1,0:T(8,128)S(1)}, u32[]{:S(2)}, u32[]{:S(2)}) collective-permute-start(f32[144,256]{1,0:T(8,128)S(1)} %shard_map.68.token.own), channel_id=1, source_target_pairs={{0,4},{1,5},{2,6},{3,7},{4,0},{5,1},{6,2},{7,3},{8,12},{9,13},{10,... | collective-permute-start | bytes 442376 | tf_op jit(solution)/shard_map/ppermute | solution.py:18
  20.4 1.6 %collective-permute-start.7 = (f32[128,256]{1,0:T(8,128)S(1)}, f32[128,256]{1,0:T(8,128)S(1)}, u32[]{:S(2)}, u32[]{:S(2)}) collective-permute-start(f32[128,256]{1,0:T(8,128)S(1)} %shard_map.69.token.own), channel_id=1, source_target_pairs={{0,1},{1,0},{2,3},{3,2},{4,5},{5,4},{6,7},{7,6},{8,9},{9,8},{10,11... | collective-permute-start | bytes 393224 | tf_op jit(solution)/shard_map/ppermute | solution.py:18
  22.2 1.6 %collective-permute-start.6 = (f32[128,256]{1,0:T(8,128)S(1)}, f32[128,256]{1,0:T(8,128)S(1)}, u32[]{:S(2)}, u32[]{:S(2)}) collective-permute-start(f32[128,256]{1,0:T(8,128)S(1)} %shard_map.70.token.own), channel_id=1, source_target_pairs={{0,2},{1,3},{2,0},{3,1},{4,6},{5,7},{6,4},{7,5},{8,10},{9,11},{10,... | collective-permute-start | bytes 393224 | tf_op jit(solution)/shard_map/ppermute | solution.py:18
  24.1 0.6 collective-permute-start.5
  24.7 0.7 collective-permute-done.2.got
  25.6 0.9 collective-permute-done.7.got
  26.7 0.6 collective-permute-start.11
  27.5 2.7 %collective-permute-start.10 = (f32[128,256]{1,0:T(8,128)S(1)}, f32[128,256]{1,0:T(8,128)S(1)}, u32[]{:S(2)}, u32[]{:S(2)}) collective-permute-start(f32[128,256]{1,0:T(8,128)S(1)} %shard_map.74.token.own), channel_id=1, source_target_pairs={{0,4},{1,5},{2,6},{3,7},{4,0},{5,1},{6,2},{7,3},{8,12},{9,13},{10,... | collective-permute-start | bytes 393224 | tf_op jit(solution)/shard_map/ppermute | solution.py:18
  30.5 0.4 collective-permute-start.9
  30.9 2.0 %copy-done.1 = f32[7,4,128,256]{3,2,1,0:T(8,128)S(1)} copy-done((f32[7,4,128,256]{3,2,1,0:T(8,128)S(1)}, f32[7,4,128,256]{3,2,1,0:T(8,128)}, u32[]{:S(2)}) %copy-start.1) | copy-done | bytes 3670040
  33.2 1.6 %collective-permute-start.8 = (f32[192,256]{1,0:T(8,128)S(1)}, f32[192,256]{1,0:T(8,128)S(1)}, u32[]{:S(2)}, u32[]{:S(2)}) collective-permute-start(f32[192,256]{1,0:T(8,128)S(1)} %shard_map.76.token.own.tab_own), channel_id=1, source_target_pairs={{0,16},{8,24},{16,0},{24,8},{1,17},{9,25},{17,1},{25,9},{2,18},{10... | collective-permute-start | bytes 589832 | tf_op jit(solution)/shard_map/ppermute | solution.py:18
  35.0 1.5 %collective-permute-start.15 = (f32[128,256]{1,0:T(8,128)S(1)}, f32[128,256]{1,0:T(8,128)S(1)}, u32[]{:S(2)}, u32[]{:S(2)}) collective-permute-start(f32[128,256]{1,0:T(8,128)S(1)} %shard_map.77.token.own), channel_id=1, source_target_pairs={{0,4},{1,5},{2,6},{3,7},{4,0},{5,1},{6,2},{7,3},{8,12},{9,13},{10,... | collective-permute-start | bytes 393224 | tf_op jit(solution)/shard_map/ppermute | solution.py:18
  36.5 0.5 collective-permute-done.10.got
  37.7 2.6 %collective-permute-start.13 = (f32[128,256]{1,0:T(8,128)S(1)}, f32[128,256]{1,0:T(8,128)S(1)}, u32[]{:S(2)}, u32[]{:S(2)}) collective-permute-start(f32[128,256]{1,0:T(8,128)S(1)} %shard_map.79.token.own), channel_id=1, source_target_pairs={{0,4},{1,5},{2,6},{3,7},{4,0},{5,1},{6,2},{7,3},{8,12},{9,13},{10,... | collective-permute-start | bytes 393224 | tf_op jit(solution)/shard_map/ppermute | solution.py:18
  40.4 1.6 %shard_map.80 = (f32[128,256]{1,0:T(8,128)S(1)}, f32[128,256]{1,0:T(8,128)S(1)}) custom-call(s32[4]{0:T(128)S(1)} %fusion.index, f32[192,256]{1,0:T(8,128)S(1)} %shard_map.76.token.own.tab_own, f32[192,256]{1,0:T(8,128)S(1)} %collective-permute-done.8.got.tab_got, f32[192,256]{1,0:T(8,128)S(1)} %shard_map.76.token.own.tab_own, ...), custom_call_target="tpu_custom_call" | custom-call | flops 268435456 | bytes 2 | tf_op jit(solution)/shard_map/pallas_call | solution.py:212
  41.9 1.8 %collective-permute-start.12 = (f32[128,256]{1,0:T(8,128)S(1)}, f32[128,256]{1,0:T(8,128)S(1)}, u32[]{:S(2)}, u32[]{:S(2)}) collective-permute-start(f32[128,256]{1,0:T(8,128)S(1)} %get-tuple-element.64), channel_id=1, source_target_pairs={{0,16},{8,24},{16,0},{24,8},{1,17},{9,25},{17,1},{25,9},{2,18},{10... | collective-permute-start | bytes 393224 | tf_op jit(solution)/shard_map/ppermute | solution.py:18
  43.8 4.0 %collective-permute-done.15.got = f32[128,256]{1,0:T(8,128)S(1)} collective-permute-done((f32[128,256]{1,0:T(8,128)S(1)}, f32[128,256]{1,0:T(8,128)S(1)}, u32[]{:S(2)}, u32[]{:S(2)}) %collective-permute-start.15) | collective-permute-done | bytes 131104 | tf_op jit(solution)/shard_map/ppermute | solution.py:18
  48.3 0.9 collective-permute-start.18
  49.7 0.3 shard_map.84
  50.0 0.4 collective-permute-start.16
  50.6 1.3 %collective-permute-start.23 = (f32[128,256]{1,0:T(8,128)S(1)}, f32[128,256]{1,0:T(8,128)S(1)}, u32[]{:S(2)}, u32[]{:S(2)}) collective-permute-start(f32[128,256]{1,0:T(8,128)S(1)} %shard_map.85.token.own), channel_id=1, source_target_pairs={{0,16},{8,24},{16,0},{24,8},{1,17},{9,25},{17,1},{25,9},{2,18},{10... | collective-permute-start | bytes 393224 | tf_op jit(solution)/shard_map/ppermute | solution.py:18
  51.9 2.7 %collective-permute-done.18.got = f32[128,256]{1,0:T(8,128)S(1)} collective-permute-done((f32[128,256]{1,0:T(8,128)S(1)}, f32[128,256]{1,0:T(8,128)S(1)}, u32[]{:S(2)}, u32[]{:S(2)}) %collective-permute-start.18) | collective-permute-done | bytes 131104 | tf_op jit(solution)/shard_map/ppermute | solution.py:18
  54.7 1.6 %shard_map.86 = (f32[128,256]{1,0:T(8,128)S(1)}, f32[128,256]{1,0:T(8,128)S(1)}) custom-call(s32[4]{0:T(128)S(1)} %fusion.index, f32[128,256]{1,0:T(8,128)S(1)} %shard_map.82.token.own, f32[128,256]{1,0:T(8,128)S(1)} %collective-permute-done.18.got, f32[192,256]{1,0:T(8,128)S(1)} %shard_map.76.token.own.tab_own, ...), custom_call_target="tpu_custom_call" | custom-call | flops 268435456 | bytes 2 | tf_op jit(solution)/shard_map/pallas_call | solution.py:212
  56.2 0.8 collective-permute-start.22
  57.2 1.4 %collective-permute-start.21 = (f32[128,256]{1,0:T(8,128)S(1)}, f32[128,256]{1,0:T(8,128)S(1)}, u32[]{:S(2)}, u32[]{:S(2)}) collective-permute-start(f32[128,256]{1,0:T(8,128)S(1)} %shard_map.87.token.own), channel_id=1, source_target_pairs={{0,16},{8,24},{16,0},{24,8},{1,17},{9,25},{17,1},{25,9},{2,18},{10... | collective-permute-start | bytes 393224 | tf_op jit(solution)/shard_map/ppermute | solution.py:18
  59.0 1.6 %shard_map.89 = (f32[128,256]{1,0:T(8,128)S(1)}, f32[128,256]{1,0:T(8,128)S(1)}) custom-call(s32[4]{0:T(128)S(1)} %fusion.index, f32[128,256]{1,0:T(8,128)S(1)} %shard_map.85.token.own, f32[128,256]{1,0:T(8,128)S(1)} %collective-permute-done.23.got, f32[192,256]{1,0:T(8,128)S(1)} %shard_map.76.token.own.tab_own, ...), custom_call_target="tpu_custom_call" | custom-call | flops 268435456 | bytes 2 | tf_op jit(solution)/shard_map/pallas_call | solution.py:212
  60.6 1.8 %collective-permute-done.22.got = f32[128,256]{1,0:T(8,128)S(1)} collective-permute-done((f32[128,256]{1,0:T(8,128)S(1)}, f32[128,256]{1,0:T(8,128)S(1)}, u32[]{:S(2)}, u32[]{:S(2)}) %collective-permute-start.22) | collective-permute-done | bytes 131104 | tf_op jit(solution)/shard_map/ppermute | solution.py:18
  62.8 0.9 collective-permute-start.27
  63.8 1.6 %shard_map.91 = (f32[128,256]{1,0:T(8,128)S(1)}, f32[128,256]{1,0:T(8,128)S(1)}) custom-call(s32[4]{0:T(128)S(1)} %fusion.index, f32[128,256]{1,0:T(8,128)S(1)} %shard_map.87.token.own, f32[128,256]{1,0:T(8,128)S(1)} %collective-permute-done.21.got, f32[192,256]{1,0:T(8,128)S(1)} %shard_map.76.token.own.tab_own, ...), custom_call_target="tpu_custom_call" | custom-call | flops 268435456 | bytes 2 | tf_op jit(solution)/shard_map/pallas_call | solution.py:212
  65.4 1.2 %collective-permute-start.25 = (f32[128,256]{1,0:T(8,128)S(1)}, f32[128,256]{1,0:T(8,128)S(1)}, u32[]{:S(2)}, u32[]{:S(2)}) collective-permute-start(f32[128,256]{1,0:T(8,128)S(1)} %get-tuple-element.76), channel_id=1, source_target_pairs={{0,16},{8,24},{16,0},{24,8},{1,17},{9,25},{17,1},{25,9},{2,18},{10... | collective-permute-start | bytes 393224 | tf_op jit(solution)/shard_map/ppermute | solution.py:18
  67.0 2.2 %collective-permute-done.27.got = f32[128,256]{1,0:T(8,128)S(1)} collective-permute-done((f32[128,256]{1,0:T(8,128)S(1)}, f32[128,256]{1,0:T(8,128)S(1)}, u32[]{:S(2)}, u32[]{:S(2)}) %collective-permute-start.27) | collective-permute-done | bytes 131104 | tf_op jit(solution)/shard_map/ppermute | solution.py:18
  69.2 0.3 shard_map.93
  69.6 0.3 shard_map.94
  69.9 1.2 %collective-permute-start.30 = (f32[128,256]{1,0:T(8,128)S(1)}, f32[128,256]{1,0:T(8,128)S(1)}, u32[]{:S(2)}, u32[]{:S(2)}) collective-permute-start(f32[128,256]{1,0:T(8,128)S(1)} %get-tuple-element.85), channel_id=1, source_target_pairs={{0,4},{1,5},{2,6},{3,7},{4,0},{5,1},{6,2},{7,3},{8,12},{9,13},{10,... | collective-permute-start | bytes 393224 | tf_op jit(solution)/shard_map/ppermute | solution.py:18
  71.1 0.4 collective-permute-done.25.got
  71.5 0.3 shard_map.95
  72.3 0.3 shard_map.96
  72.6 1.5 %collective-permute-start.28 = (f32[128,256]{1,0:T(8,128)S(1)}, f32[128,256]{1,0:T(8,128)S(1)}, u32[]{:S(2)}, u32[]{:S(2)}) collective-permute-start(f32[128,256]{1,0:T(8,128)S(1)} %get-tuple-element.83), channel_id=1, source_target_pairs={{0,1},{1,0},{2,3},{3,2},{4,5},{5,4},{6,7},{7,6},{8,9},{9,8},{10,11... | collective-permute-start | bytes 393224 | tf_op jit(solution)/shard_map/ppermute | solution.py:18
  74.1 0.3 shard_map.97
  74.4 1.2 %collective-permute-start.33 = (f32[128,256]{1,0:T(8,128)S(1)}, f32[128,256]{1,0:T(8,128)S(1)}, u32[]{:S(2)}, u32[]{:S(2)}) collective-permute-start(f32[128,256]{1,0:T(8,128)S(1)} %get-tuple-element.93), channel_id=1, source_target_pairs={{0,4},{1,5},{2,6},{3,7},{4,0},{5,1},{6,2},{7,3},{8,12},{9,13},{10,... | collective-permute-start | bytes 393224 | tf_op jit(solution)/shard_map/ppermute | solution.py:18
  75.7 6.0 %collective-permute-done.30.got = f32[128,256]{1,0:T(8,128)S(1)} collective-permute-done((f32[128,256]{1,0:T(8,128)S(1)}, f32[128,256]{1,0:T(8,128)S(1)}, u32[]{:S(2)}, u32[]{:S(2)}) %collective-permute-start.30) | collective-permute-done | bytes 131104 | tf_op jit(solution)/shard_map/ppermute | solution.py:18
  82.1 0.3 shard_map.99
  82.4 2.5 %collective-permute-start.36 = (f32[128,256]{1,0:T(8,128)S(1)}, f32[128,256]{1,0:T(8,128)S(1)}, u32[]{:S(2)}, u32[]{:S(2)}) collective-permute-start(f32[128,256]{1,0:T(8,128)S(1)} %get-tuple-element.98), channel_id=1, source_target_pairs={{0,4},{1,5},{2,6},{3,7},{4,0},{5,1},{6,2},{7,3},{8,12},{9,13},{10,... | collective-permute-start | bytes 393224 | tf_op jit(solution)/shard_map/ppermute | solution.py:18
  85.2 0.3 shard_map.101
  85.7 4.7 %collective-permute-done.32.got = f32[128,256]{1,0:T(8,128)S(1)} collective-permute-done((f32[128,256]{1,0:T(8,128)S(1)}, f32[128,256]{1,0:T(8,128)S(1)}, u32[]{:S(2)}, u32[]{:S(2)}) %collective-permute-start.32) | collective-permute-done | bytes 131104 | tf_op jit(solution)/shard_map/ppermute | solution.py:18
  90.4 0.3 shard_map.102
  90.7 1.5 %collective-permute-start.34 = (f32[128,256]{1,0:T(8,128)S(1)}, f32[128,256]{1,0:T(8,128)S(1)}, u32[]{:S(2)}, u32[]{:S(2)}) collective-permute-start(f32[128,256]{1,0:T(8,128)S(1)} %get-tuple-element.96), channel_id=1, source_target_pairs={{0,1},{1,0},{2,3},{3,2},{4,5},{5,4},{6,7},{7,6},{8,9},{9,8},{10,11... | collective-permute-start | bytes 393224 | tf_op jit(solution)/shard_map/ppermute | solution.py:18
  92.6 0.5 collective-permute-done.35.got
  93.4 1.5 %collective-permute-start.37 = (f32[128,256]{1,0:T(8,128)S(1)}, f32[128,256]{1,0:T(8,128)S(1)}, u32[]{:S(2)}, u32[]{:S(2)}) collective-permute-start(f32[128,256]{1,0:T(8,128)S(1)} %get-tuple-element.103), channel_id=1, source_target_pairs={{0,1},{1,0},{2,3},{3,2},{4,5},{5,4},{6,7},{7,6},{8,9},{9,8},{10,11... | collective-permute-start | bytes 393224 | tf_op jit(solution)/shard_map/ppermute | solution.py:18
  95.0 1.2 %collective-permute-done.34.got = f32[128,256]{1,0:T(8,128)S(1)} collective-permute-done((f32[128,256]{1,0:T(8,128)S(1)}, f32[128,256]{1,0:T(8,128)S(1)}, u32[]{:S(2)}, u32[]{:S(2)}) %collective-permute-start.34) | collective-permute-done | bytes 131104 | tf_op jit(solution)/shard_map/ppermute | solution.py:18
  96.5 1.1 %collective-permute-done.38.got = f32[128,256]{1,0:T(8,128)S(1)} collective-permute-done((f32[128,256]{1,0:T(8,128)S(1)}, f32[128,256]{1,0:T(8,128)S(1)}, u32[]{:S(2)}, u32[]{:S(2)}) %collective-permute-start.38) | collective-permute-done | bytes 131104 | tf_op jit(solution)/shard_map/ppermute | solution.py:18
  97.9 1.1 %collective-permute-start.39 = (f32[128,256]{1,0:T(8,128)S(1)}, f32[128,256]{1,0:T(8,128)S(1)}, u32[]{:S(2)}, u32[]{:S(2)}) collective-permute-start(f32[128,256]{1,0:T(8,128)S(1)} %get-tuple-element.108), channel_id=1, source_target_pairs={{0,1},{1,0},{2,3},{3,2},{4,5},{5,4},{6,7},{7,6},{8,9},{9,8},{10,11... | collective-permute-start | bytes 393224 | tf_op jit(solution)/shard_map/ppermute | solution.py:18
  99.2 0.3 shard_map.107
  99.6 3.4 %collective-permute-done.39.got = f32[128,256]{1,0:T(8,128)S(1)} collective-permute-done((f32[128,256]{1,0:T(8,128)S(1)}, f32[128,256]{1,0:T(8,128)S(1)}, u32[]{:S(2)}, u32[]{:S(2)}) %collective-permute-start.39) | collective-permute-done | bytes 131104 | tf_op jit(solution)/shard_map/ppermute | solution.py:18
  102.9 0.3 shard_map.108
  103.3 2.0 %shard_map.109 = f32[1024,256]{1,0:T(8,128)} custom-call(f32[4,128,256]{2,1,0:T(8,128)S(1)} %copy-done.4, f32[7,4,128,256]{3,2,1,0:T(8,128)S(1)} %copy-done.2, f32[128,256]{1,0:T(8,128)S(1)} %get-tuple-element.90.token.rest_0_, f32[128,256]{1,0:T(8,128)S(1)} %get-tuple-element.91.rest_1_, f32[128,256]{1,0:T(8,128)S(1)} %get-tuple-element.101.token.rest_2_, ...), custom_call_target="tpu_custom_call" | custom-call | flops 805306368 | bytes 12 | tf_op jit(solution)/shard_map/pallas_call | solution.py:223
  (79 shorter events, 9.0 us)
Async XLA Ops:
  0.0 2.0 %copy-start = (f32[7,4,128,256]{3,2,1,0:T(8,128)S(1)}, f32[7,4,128,256]{3,2,1,0:T(8,128)}, u32[]{:S(2)}) copy-start(f32[7,4,128,256]{3,2,1,0:T(8,128)} %factors.89) | copy-start | bytes 11010052
  0.0 2.1 %copy-start.4 = (f32[4,128,256]{2,1,0:T(8,128)S(1)}, f32[4,128,256]{2,1,0:T(8,128)}, u32[]{:S(2)}) copy-start(f32[4,128,256]{2,1,0:T(8,128)} %leaf_in.3) | copy-start | bytes 1572868
  0.0 2.1 %copy-start.6 = (f32[4,256]{1,0:T(4,128)S(1)}, f32[4,256]{1,0:T(4,128)}, u32[]{:S(2)}) copy-start(f32[4,256]{1,0:T(4,128)} %table.1) | copy-start | bytes 12292
  0.0 2.5 %copy-start.5 = (f32[1024,256]{1,0:T(8,128)S(1)}, f32[1024,256]{1,0:T(8,128)}, u32[]{:S(2)}) copy-start(f32[1024,256]{1,0:T(8,128)} %source.1) | copy-start | bytes 3145732
  5.0 6.7 %collective-permute-start = (f32[132,256]{1,0:T(8,128)S(1)}, f32[132,256]{1,0:T(8,128)S(1)}, u32[]{:S(2)}, u32[]{:S(2)}) collective-permute-start(f32[132,256]{1,0:T(8,128)S(1)} %get-tuple-element.58.own.token), channel_id=1, source_target_pairs={{0,1},{1,0},{2,3},{3,2},{4,5},{5,4},{6,7},{7,6},{8,9},{9,8},{10,11... | collective-permute-start | bytes 405512 | tf_op jit(solution)/shard_map/ppermute | solution.py:18
  12.0 5.1 %collective-permute-start.1 = (f32[136,256]{1,0:T(8,128)S(1)}, f32[136,256]{1,0:T(8,128)S(1)}, u32[]{:S(2)}, u32[]{:S(2)}) collective-permute-start(f32[136,256]{1,0:T(8,128)S(1)} %shard_map.66.token.own), channel_id=1, source_target_pairs={{0,2},{1,3},{2,0},{3,1},{4,6},{5,7},{6,4},{7,5},{8,10},{9,11},{10,... | collective-permute-start | bytes 417800 | tf_op jit(solution)/shard_map/ppermute | solution.py:18
  14.1 7.9 %collective-permute-start.3 = (f32[128,256]{1,0:T(8,128)S(1)}, f32[128,256]{1,0:T(8,128)S(1)}, u32[]{:S(2)}, u32[]{:S(2)}) collective-permute-start(f32[128,256]{1,0:T(8,128)S(1)} %shard_map.67.token.own), channel_id=1, source_target_pairs={{0,1},{1,0},{2,3},{3,2},{4,5},{5,4},{6,7},{7,6},{8,9},{9,8},{10,11... | collective-permute-start | bytes 393224 | tf_op jit(solution)/shard_map/ppermute | solution.py:18
  17.3 8.0 %collective-permute-start.2 = (f32[144,256]{1,0:T(8,128)S(1)}, f32[144,256]{1,0:T(8,128)S(1)}, u32[]{:S(2)}, u32[]{:S(2)}) collective-permute-start(f32[144,256]{1,0:T(8,128)S(1)} %shard_map.68.token.own), channel_id=1, source_target_pairs={{0,4},{1,5},{2,6},{3,7},{4,0},{5,1},{6,2},{7,3},{8,12},{9,13},{10,... | collective-permute-start | bytes 442376 | tf_op jit(solution)/shard_map/ppermute | solution.py:18
  20.4 6.1 %collective-permute-start.7 = (f32[128,256]{1,0:T(8,128)S(1)}, f32[128,256]{1,0:T(8,128)S(1)}, u32[]{:S(2)}, u32[]{:S(2)}) collective-permute-start(f32[128,256]{1,0:T(8,128)S(1)} %shard_map.69.token.own), channel_id=1, source_target_pairs={{0,1},{1,0},{2,3},{3,2},{4,5},{5,4},{6,7},{7,6},{8,9},{9,8},{10,11... | collective-permute-start | bytes 393224 | tf_op jit(solution)/shard_map/ppermute | solution.py:18
  22.2 5.1 %collective-permute-start.6 = (f32[128,256]{1,0:T(8,128)S(1)}, f32[128,256]{1,0:T(8,128)S(1)}, u32[]{:S(2)}, u32[]{:S(2)}) collective-permute-start(f32[128,256]{1,0:T(8,128)S(1)} %shard_map.70.token.own), channel_id=1, source_target_pairs={{0,2},{1,3},{2,0},{3,1},{4,6},{5,7},{6,4},{7,5},{8,10},{9,11},{10,... | collective-permute-start | bytes 393224 | tf_op jit(solution)/shard_map/ppermute | solution.py:18
  24.1 6.2 %collective-permute-start.5 = (f32[128,256]{1,0:T(8,128)S(1)}, f32[128,256]{1,0:T(8,128)S(1)}, u32[]{:S(2)}, u32[]{:S(2)}) collective-permute-start(f32[128,256]{1,0:T(8,128)S(1)} %shard_map.71.token.own), channel_id=1, source_target_pairs={{0,1},{1,0},{2,3},{3,2},{4,5},{5,4},{6,7},{7,6},{8,9},{9,8},{10,11... | collective-permute-start | bytes 393224 | tf_op jit(solution)/shard_map/ppermute | solution.py:18
  25.6 5.3 %collective-permute-start.4 = (f32[160,256]{1,0:T(8,128)S(1)}, f32[160,256]{1,0:T(8,128)S(1)}, u32[]{:S(2)}, u32[]{:S(2)}) collective-permute-start(f32[160,256]{1,0:T(8,128)S(1)} %shard_map.72.token.own), channel_id=1, source_target_pairs={{0,8},{8,0},{16,24},{24,16},{1,9},{9,1},{17,25},{25,17},{2,10},{10... | collective-permute-start | bytes 491528 | tf_op jit(solution)/shard_map/ppermute | solution.py:18
  26.7 8.0 %collective-permute-start.11 = (f32[128,256]{1,0:T(8,128)S(1)}, f32[128,256]{1,0:T(8,128)S(1)}, u32[]{:S(2)}, u32[]{:S(2)}) collective-permute-start(f32[128,256]{1,0:T(8,128)S(1)} %shard_map.73.token.own), channel_id=1, source_target_pairs={{0,2},{1,3},{2,0},{3,1},{4,6},{5,7},{6,4},{7,5},{8,10},{9,11},{10,... | collective-permute-start | bytes 393224 | tf_op jit(solution)/shard_map/ppermute | solution.py:18
  27.5 9.5 %collective-permute-start.10 = (f32[128,256]{1,0:T(8,128)S(1)}, f32[128,256]{1,0:T(8,128)S(1)}, u32[]{:S(2)}, u32[]{:S(2)}) collective-permute-start(f32[128,256]{1,0:T(8,128)S(1)} %shard_map.74.token.own), channel_id=1, source_target_pairs={{0,4},{1,5},{2,6},{3,7},{4,0},{5,1},{6,2},{7,3},{8,12},{9,13},{10,... | collective-permute-start | bytes 393224 | tf_op jit(solution)/shard_map/ppermute | solution.py:18
  30.5 7.0 %collective-permute-start.9 = (f32[128,256]{1,0:T(8,128)S(1)}, f32[128,256]{1,0:T(8,128)S(1)}, u32[]{:S(2)}, u32[]{:S(2)}) collective-permute-start(f32[128,256]{1,0:T(8,128)S(1)} %shard_map.75.token.own), channel_id=1, source_target_pairs={{0,2},{1,3},{2,0},{3,1},{4,6},{5,7},{6,4},{7,5},{8,10},{9,11},{10,... | collective-permute-start | bytes 393224 | tf_op jit(solution)/shard_map/ppermute | solution.py:18
  30.9 2.0 %copy-start.1 = (f32[7,4,128,256]{3,2,1,0:T(8,128)S(1)}, f32[7,4,128,256]{3,2,1,0:T(8,128)}, u32[]{:S(2)}) copy-start(f32[7,4,128,256]{3,2,1,0:T(8,128)} %factors.89) | copy-start | bytes 11010052
  33.2 7.2 %collective-permute-start.8 = (f32[192,256]{1,0:T(8,128)S(1)}, f32[192,256]{1,0:T(8,128)S(1)}, u32[]{:S(2)}, u32[]{:S(2)}) collective-permute-start(f32[192,256]{1,0:T(8,128)S(1)} %shard_map.76.token.own.tab_own), channel_id=1, source_target_pairs={{0,16},{8,24},{16,0},{24,8},{1,17},{9,25},{17,1},{25,9},{2,18},{10... | collective-permute-start | bytes 589832 | tf_op jit(solution)/shard_map/ppermute | solution.py:18
  35.0 5.3 %copy-start.7 = (s32[4]{0:T(128)S(1)}, s32[4]{0:T(128)}, u32[]{:S(2)}) copy-start(s32[4]{0:T(128)} %param.11) | copy-start | bytes 52
  35.0 5.3 %copy-start.2 = (f32[7,4,128,256]{3,2,1,0:T(8,128)S(1)}, f32[7,4,128,256]{3,2,1,0:T(8,128)}, u32[]{:S(2)}) copy-start(f32[7,4,128,256]{3,2,1,0:T(8,128)} %factors.89) | copy-start | bytes 11010052
  35.0 5.3 %copy-start.3 = (f32[4,256,128]{2,1,0:T(8,128)S(1)}, f32[4,256,128]{2,1,0:T(8,128)}, u32[]{:S(2)}) copy-start(f32[4,256,128]{2,1,0:T(8,128)} %leaf_out.7) | copy-start | bytes 1572868
  35.0 12.7 %collective-permute-start.15 = (f32[128,256]{1,0:T(8,128)S(1)}, f32[128,256]{1,0:T(8,128)S(1)}, u32[]{:S(2)}, u32[]{:S(2)}) collective-permute-start(f32[128,256]{1,0:T(8,128)S(1)} %shard_map.77.token.own), channel_id=1, source_target_pairs={{0,4},{1,5},{2,6},{3,7},{4,0},{5,1},{6,2},{7,3},{8,12},{9,13},{10,... | collective-permute-start | bytes 393224 | tf_op jit(solution)/shard_map/ppermute | solution.py:18
  37.3 10.8 %collective-permute-start.14 = (f32[128,256]{1,0:T(8,128)S(1)}, f32[128,256]{1,0:T(8,128)S(1)}, u32[]{:S(2)}, u32[]{:S(2)}) collective-permute-start(f32[128,256]{1,0:T(8,128)S(1)} %shard_map.78.token.own), channel_id=1, source_target_pairs={{0,8},{8,0},{16,24},{24,16},{1,9},{9,1},{17,25},{25,17},{2,10},{10... | collective-permute-start | bytes 393224 | tf_op jit(solution)/shard_map/ppermute | solution.py:18
  37.7 11.5 %collective-permute-start.13 = (f32[128,256]{1,0:T(8,128)S(1)}, f32[128,256]{1,0:T(8,128)S(1)}, u32[]{:S(2)}, u32[]{:S(2)}) collective-permute-start(f32[128,256]{1,0:T(8,128)S(1)} %shard_map.79.token.own), channel_id=1, source_target_pairs={{0,4},{1,5},{2,6},{3,7},{4,0},{5,1},{6,2},{7,3},{8,12},{9,13},{10,... | collective-permute-start | bytes 393224 | tf_op jit(solution)/shard_map/ppermute | solution.py:18
  41.9 7.7 %collective-permute-start.12 = (f32[128,256]{1,0:T(8,128)S(1)}, f32[128,256]{1,0:T(8,128)S(1)}, u32[]{:S(2)}, u32[]{:S(2)}) collective-permute-start(f32[128,256]{1,0:T(8,128)S(1)} %get-tuple-element.64), channel_id=1, source_target_pairs={{0,16},{8,24},{16,0},{24,8},{1,17},{9,25},{17,1},{25,9},{2,18},{10... | collective-permute-start | bytes 393224 | tf_op jit(solution)/shard_map/ppermute | solution.py:18
  48.0 2.4 %collective-permute-start.19 = (f32[128,256]{1,0:T(8,128)S(1)}, f32[128,256]{1,0:T(8,128)S(1)}, u32[]{:S(2)}, u32[]{:S(2)}) collective-permute-start(f32[128,256]{1,0:T(8,128)S(1)} %shard_map.81.token.own), channel_id=1, source_target_pairs={{0,8},{8,0},{16,24},{24,16},{1,9},{9,1},{17,25},{25,17},{2,10},{10... | collective-permute-start | bytes 393224 | tf_op jit(solution)/shard_map/ppermute | solution.py:18
  48.3 6.4 %collective-permute-start.18 = (f32[128,256]{1,0:T(8,128)S(1)}, f32[128,256]{1,0:T(8,128)S(1)}, u32[]{:S(2)}, u32[]{:S(2)}) collective-permute-start(f32[128,256]{1,0:T(8,128)S(1)} %shard_map.82.token.own), channel_id=1, source_target_pairs={{0,16},{8,24},{16,0},{24,8},{1,17},{9,25},{17,1},{25,9},{2,18},{10... | collective-permute-start | bytes 393224 | tf_op jit(solution)/shard_map/ppermute | solution.py:18
  49.4 7.6 %collective-permute-start.17 = (f32[128,256]{1,0:T(8,128)S(1)}, f32[128,256]{1,0:T(8,128)S(1)}, u32[]{:S(2)}, u32[]{:S(2)}) collective-permute-start(f32[128,256]{1,0:T(8,128)S(1)} %shard_map.83.token.own), channel_id=1, source_target_pairs={{0,8},{8,0},{16,24},{24,16},{1,9},{9,1},{17,25},{25,17},{2,10},{10... | collective-permute-start | bytes 393224 | tf_op jit(solution)/shard_map/ppermute | solution.py:18
  50.0 8.6 %collective-permute-start.16 = (f32[128,256]{1,0:T(8,128)S(1)}, f32[128,256]{1,0:T(8,128)S(1)}, u32[]{:S(2)}, u32[]{:S(2)}) collective-permute-start(f32[128,256]{1,0:T(8,128)S(1)} %get-tuple-element.66), channel_id=1, source_target_pairs={{0,8},{8,0},{16,24},{24,16},{1,9},{9,1},{17,25},{25,17},{2,10},{10... | collective-permute-start | bytes 393224 | tf_op jit(solution)/shard_map/ppermute | solution.py:18
  50.6 8.4 %collective-permute-start.23 = (f32[128,256]{1,0:T(8,128)S(1)}, f32[128,256]{1,0:T(8,128)S(1)}, u32[]{:S(2)}, u32[]{:S(2)}) collective-permute-start(f32[128,256]{1,0:T(8,128)S(1)} %shard_map.85.token.own), channel_id=1, source_target_pairs={{0,16},{8,24},{16,0},{24,8},{1,17},{9,25},{17,1},{25,9},{2,18},{10... | collective-permute-start | bytes 393224 | tf_op jit(solution)/shard_map/ppermute | solution.py:18
  56.2 6.2 %collective-permute-start.22 = (f32[128,256]{1,0:T(8,128)S(1)}, f32[128,256]{1,0:T(8,128)S(1)}, u32[]{:S(2)}, u32[]{:S(2)}) collective-permute-start(f32[128,256]{1,0:T(8,128)S(1)} %get-tuple-element.70), channel_id=1, source_target_pairs={{0,16},{8,24},{16,0},{24,8},{1,17},{9,25},{17,1},{25,9},{2,18},{10... | collective-permute-start | bytes 393224 | tf_op jit(solution)/shard_map/ppermute | solution.py:18
  57.2 6.6 %collective-permute-start.21 = (f32[128,256]{1,0:T(8,128)S(1)}, f32[128,256]{1,0:T(8,128)S(1)}, u32[]{:S(2)}, u32[]{:S(2)}) collective-permute-start(f32[128,256]{1,0:T(8,128)S(1)} %shard_map.87.token.own), channel_id=1, source_target_pairs={{0,16},{8,24},{16,0},{24,8},{1,17},{9,25},{17,1},{25,9},{2,18},{10... | collective-permute-start | bytes 393224 | tf_op jit(solution)/shard_map/ppermute | solution.py:18
  59.0 7.6 %collective-permute-start.20 = (f32[128,256]{1,0:T(8,128)S(1)}, f32[128,256]{1,0:T(8,128)S(1)}, u32[]{:S(2)}, u32[]{:S(2)}) collective-permute-start(f32[128,256]{1,0:T(8,128)S(1)} %get-tuple-element.69), channel_id=1, source_target_pairs={{0,4},{1,5},{2,6},{3,7},{4,0},{5,1},{6,2},{7,3},{8,12},{9,13},{10,... | collective-permute-start | bytes 393224 | tf_op jit(solution)/shard_map/ppermute | solution.py:18
  62.7 6.8 %collective-permute-start.26 = (f32[128,256]{1,0:T(8,128)S(1)}, f32[128,256]{1,0:T(8,128)S(1)}, u32[]{:S(2)}, u32[]{:S(2)}) collective-permute-start(f32[128,256]{1,0:T(8,128)S(1)} %get-tuple-element.77), channel_id=1, source_target_pairs={{0,8},{8,0},{16,24},{24,16},{1,9},{9,1},{17,25},{25,17},{2,10},{10... | collective-permute-start | bytes 393224 | tf_op jit(solution)/shard_map/ppermute | solution.py:18
  62.8 6.4 %collective-permute-start.27 = (f32[128,256]{1,0:T(8,128)S(1)}, f32[128,256]{1,0:T(8,128)S(1)}, u32[]{:S(2)}, u32[]{:S(2)}) collective-permute-start(f32[128,256]{1,0:T(8,128)S(1)} %get-tuple-element.78), channel_id=1, source_target_pairs={{0,16},{8,24},{16,0},{24,8},{1,17},{9,25},{17,1},{25,9},{2,18},{10... | collective-permute-start | bytes 393224 | tf_op jit(solution)/shard_map/ppermute | solution.py:18
  65.4 6.1 %collective-permute-start.25 = (f32[128,256]{1,0:T(8,128)S(1)}, f32[128,256]{1,0:T(8,128)S(1)}, u32[]{:S(2)}, u32[]{:S(2)}) collective-permute-start(f32[128,256]{1,0:T(8,128)S(1)} %get-tuple-element.76), channel_id=1, source_target_pairs={{0,16},{8,24},{16,0},{24,8},{1,17},{9,25},{17,1},{25,9},{2,18},{10... | collective-permute-start | bytes 393224 | tf_op jit(solution)/shard_map/ppermute | solution.py:18
  66.9 5.4 %collective-permute-start.24 = (f32[128,256]{1,0:T(8,128)S(1)}, f32[128,256]{1,0:T(8,128)S(1)}, u32[]{:S(2)}, u32[]{:S(2)}) collective-permute-start(f32[128,256]{1,0:T(8,128)S(1)} %get-tuple-element.75), channel_id=1, source_target_pairs={{0,2},{1,3},{2,0},{3,1},{4,6},{5,7},{6,4},{7,5},{8,10},{9,11},{10,... | collective-permute-start | bytes 393224 | tf_op jit(solution)/shard_map/ppermute | solution.py:18
  69.5 4.6 %collective-permute-start.31 = (f32[128,256]{1,0:T(8,128)S(1)}, f32[128,256]{1,0:T(8,128)S(1)}, u32[]{:S(2)}, u32[]{:S(2)}) collective-permute-start(f32[128,256]{1,0:T(8,128)S(1)} %get-tuple-element.86), channel_id=1, source_target_pairs={{0,8},{8,0},{16,24},{24,16},{1,9},{9,1},{17,25},{25,17},{2,10},{10... | collective-permute-start | bytes 393224 | tf_op jit(solution)/shard_map/ppermute | solution.py:18
  69.9 11.8 %collective-permute-start.30 = (f32[128,256]{1,0:T(8,128)S(1)}, f32[128,256]{1,0:T(8,128)S(1)}, u32[]{:S(2)}, u32[]{:S(2)}) collective-permute-start(f32[128,256]{1,0:T(8,128)S(1)} %get-tuple-element.85), channel_id=1, source_target_pairs={{0,4},{1,5},{2,6},{3,7},{4,0},{5,1},{6,2},{7,3},{8,12},{9,13},{10,... | collective-permute-start | bytes 393224 | tf_op jit(solution)/shard_map/ppermute | solution.py:18
  71.9 10.2 %collective-permute-start.29 = (f32[128,256]{1,0:T(8,128)S(1)}, f32[128,256]{1,0:T(8,128)S(1)}, u32[]{:S(2)}, u32[]{:S(2)}) collective-permute-start(f32[128,256]{1,0:T(8,128)S(1)} %get-tuple-element.84), channel_id=1, source_target_pairs={{0,8},{8,0},{16,24},{24,16},{1,9},{9,1},{17,25},{25,17},{2,10},{10... | collective-permute-start | bytes 393224 | tf_op jit(solution)/shard_map/ppermute | solution.py:18
  72.6 12.3 %collective-permute-start.28 = (f32[128,256]{1,0:T(8,128)S(1)}, f32[128,256]{1,0:T(8,128)S(1)}, u32[]{:S(2)}, u32[]{:S(2)}) collective-permute-start(f32[128,256]{1,0:T(8,128)S(1)} %get-tuple-element.83), channel_id=1, source_target_pairs={{0,1},{1,0},{2,3},{3,2},{4,5},{5,4},{6,7},{7,6},{8,9},{9,8},{10,11... | collective-permute-start | bytes 393224 | tf_op jit(solution)/shard_map/ppermute | solution.py:18
  74.4 10.8 %collective-permute-start.33 = (f32[128,256]{1,0:T(8,128)S(1)}, f32[128,256]{1,0:T(8,128)S(1)}, u32[]{:S(2)}, u32[]{:S(2)}) collective-permute-start(f32[128,256]{1,0:T(8,128)S(1)} %get-tuple-element.93), channel_id=1, source_target_pairs={{0,4},{1,5},{2,6},{3,7},{4,0},{5,1},{6,2},{7,3},{8,12},{9,13},{10,... | collective-permute-start | bytes 393224 | tf_op jit(solution)/shard_map/ppermute | solution.py:18
  82.0 8.4 %collective-permute-start.32 = (f32[128,256]{1,0:T(8,128)S(1)}, f32[128,256]{1,0:T(8,128)S(1)}, u32[]{:S(2)}, u32[]{:S(2)}) collective-permute-start(f32[128,256]{1,0:T(8,128)S(1)} %get-tuple-element.92), channel_id=1, source_target_pairs={{0,2},{1,3},{2,0},{3,1},{4,6},{5,7},{6,4},{7,5},{8,10},{9,11},{10,... | collective-permute-start | bytes 393224 | tf_op jit(solution)/shard_map/ppermute | solution.py:18
  82.4 9.8 %collective-permute-start.36 = (f32[128,256]{1,0:T(8,128)S(1)}, f32[128,256]{1,0:T(8,128)S(1)}, u32[]{:S(2)}, u32[]{:S(2)}) collective-permute-start(f32[128,256]{1,0:T(8,128)S(1)} %get-tuple-element.98), channel_id=1, source_target_pairs={{0,4},{1,5},{2,6},{3,7},{4,0},{5,1},{6,2},{7,3},{8,12},{9,13},{10,... | collective-permute-start | bytes 393224 | tf_op jit(solution)/shard_map/ppermute | solution.py:18
  85.6 7.5 %collective-permute-start.35 = (f32[128,256]{1,0:T(8,128)S(1)}, f32[128,256]{1,0:T(8,128)S(1)}, u32[]{:S(2)}, u32[]{:S(2)}) collective-permute-start(f32[128,256]{1,0:T(8,128)S(1)} %get-tuple-element.97), channel_id=1, source_target_pairs={{0,2},{1,3},{2,0},{3,1},{4,6},{5,7},{6,4},{7,5},{8,10},{9,11},{10,... | collective-permute-start | bytes 393224 | tf_op jit(solution)/shard_map/ppermute | solution.py:18
  90.7 5.5 %collective-permute-start.34 = (f32[128,256]{1,0:T(8,128)S(1)}, f32[128,256]{1,0:T(8,128)S(1)}, u32[]{:S(2)}, u32[]{:S(2)}) collective-permute-start(f32[128,256]{1,0:T(8,128)S(1)} %get-tuple-element.96), channel_id=1, source_target_pairs={{0,1},{1,0},{2,3},{3,2},{4,5},{5,4},{6,7},{7,6},{8,9},{9,8},{10,11... | collective-permute-start | bytes 393224 | tf_op jit(solution)/shard_map/ppermute | solution.py:18
  92.5 5.0 %collective-permute-start.38 = (f32[128,256]{1,0:T(8,128)S(1)}, f32[128,256]{1,0:T(8,128)S(1)}, u32[]{:S(2)}, u32[]{:S(2)}) collective-permute-start(f32[128,256]{1,0:T(8,128)S(1)} %get-tuple-element.104), channel_id=1, source_target_pairs={{0,2},{1,3},{2,0},{3,1},{4,6},{5,7},{6,4},{7,5},{8,10},{9,11},{10,... | collective-permute-start | bytes 393224 | tf_op jit(solution)/shard_map/ppermute | solution.py:18
  93.4 5.8 %collective-permute-start.37 = (f32[128,256]{1,0:T(8,128)S(1)}, f32[128,256]{1,0:T(8,128)S(1)}, u32[]{:S(2)}, u32[]{:S(2)}) collective-permute-start(f32[128,256]{1,0:T(8,128)S(1)} %get-tuple-element.103), channel_id=1, source_target_pairs={{0,1},{1,0},{2,3},{3,2},{4,5},{5,4},{6,7},{7,6},{8,9},{9,8},{10,11... | collective-permute-start | bytes 393224 | tf_op jit(solution)/shard_map/ppermute | solution.py:18
  97.9 5.0 %collective-permute-start.39 = (f32[128,256]{1,0:T(8,128)S(1)}, f32[128,256]{1,0:T(8,128)S(1)}, u32[]{:S(2)}, u32[]{:S(2)}) collective-permute-start(f32[128,256]{1,0:T(8,128)S(1)} %get-tuple-element.108), channel_id=1, source_target_pairs={{0,1},{1,0},{2,3},{3,2},{4,5},{5,4},{6,7},{7,6},{8,9},{9,8},{10,11... | collective-permute-start | bytes 393224 | tf_op jit(solution)/shard_map/ppermute | solution.py:18

commit v5 on v4

--- a/solution.py
+++ b/solution.py
@@ -130,7 +130,7 @@
 def task_order(chunks, stages):
     order, queue, waits, entered = [], [], 0, 0
     while len(order) < chunks * stages:
-        while entered < chunks and entered <= waits:
+        while entered < chunks and entered * (entered + 1) // 4 <= waits:
             order.append((entered, 0))
             queue.append((entered, 0))
             entered += 1

time: 105 us -> 101 us (0.962)
  waiting for transfers between devices: 36.1 us -> 29 us
  starting transfers between devices: 42.7 us -> 45.4 us
    ppermute x40, waiting for transfers between devices: 36.1 us -> 29 us  [exchange(): lax.ppermute(value, axis, [(i, i ^ 1 << bit) for i in range(lax.axis_size...]
    ppermute x40, starting transfers between devices: 42.7 us -> 45.4 us  [exchange(): lax.ppermute(value, axis, [(i, i ^ 1 << bit) for i in range(lax.axis_size...]
  transfers between devices with their start and end apart: 40 -> 40, of which waited for: 20 -> 20; matrix products, arithmetic and copies ran while one was open for 0% -> 0% of each run, Pallas kernels for 15% -> 16%
where the time goes in v5:
time: 101 us
  starting transfers between devices  45.4 us (45%)
  waiting for transfers between devices  29 us (29%)
  Pallas kernels  21.3 us (21%)
  local copies, waits for them, and re-layouts  4.55 us (5%)
    ppermute x40, starting transfers between devices, exchange(): lax.ppermute(value, axis, [(i, i ^ 1 << bit) for i in range(lax.axis_size...  45.4 us
    ppermute x40, waiting for transfers between devices, exchange(): lax.ppermute(value, axis, [(i, i ^ 1 << bit) for i in range(lax.axis_size...  29 us
    pallas_call x4, Pallas kernels, body(): call(functools.partial(middle_kernel, c, rank, level), [shape(rank)] * 2,...  6.34 us
    pallas_call x20, Pallas kernels, body(): call(functools.partial(backward_kernel, c, rank, level), [shape(rank)] *...  6.3 us
    unnamed x16, local copies, waits for them, and re-layouts  4.55 us
    pallas_call x16, Pallas kernels, body(): call(functools.partial(forward_kernel, c, rank, level - 1), shape(2 * own...  3.49 us
    pallas_call x1, Pallas kernels, body(): call(functools.partial(start_kernel, nodes, rank, leaf, local_bits), [sha...  2.53 us
  transfers between devices with their start and end apart: 40, of which 20 were waited for; matrix products, arithmetic and copies ran while one was open for 0% of the time, Pallas kernels for 16%

profile of v5, /device:TPU:0, one launch (start us, length us, event | category | flops | bytes accessed | tf_op | source)
XLA Modules:
  0.0 100.8 jit_solution(5634222412251641042)
XLA Ops:
  0.0 2.0 %copy-done = f32[7,4,128,256]{3,2,1,0:T(8,128)S(1)} copy-done((f32[7,4,128,256]{3,2,1,0:T(8,128)S(1)}, f32[7,4,128,256]{3,2,1,0:T(8,128)}, u32[]{:S(2)}) %copy-start) | copy-done | bytes 3670040
  2.1 0.4 copy-done.5
  2.5 2.5 %shard_map.65 = (f32[132,256]{1,0:T(8,128)S(1)}, f32[128,256]{1,0:T(8,128)S(1)}, f32[128,256]{1,0:T(8,128)S(1)}, f32[128,256]{1,0:T(8,128)S(1)}, f32[1,128,256]{2,1,0:T(8,128)S(1)}) custom-call(f32[1024,256]{1,0:T(8,128)S(1)} %copy-done.5, f32[4,128,256]{2,1,0:T(8,128)S(1)} %copy-done.4, f32[7,4,128,256]{3,2,1,0:T(8,128)S(1)} %copy-done, ...), custom_call_target="tpu_custom_call" | custom-call | flops 536870912 | bytes 8 | tf_op jit(solution)/shard_map/pallas_call | solution.py:169
  5.0 3.0 %collective-permute-start = (f32[132,256]{1,0:T(8,128)S(1)}, f32[132,256]{1,0:T(8,128)S(1)}, u32[]{:S(2)}, u32[]{:S(2)}) collective-permute-start(f32[132,256]{1,0:T(8,128)S(1)} %get-tuple-element.58.token.own), channel_id=1, source_target_pairs={{0,1},{1,0},{2,3},{3,2},{4,5},{5,4},{6,7},{7,6},{8,9},{9,8},{10,11... | collective-permute-start | bytes 405512 | tf_op jit(solution)/shard_map/ppermute | solution.py:18
  8.4 4.2 %collective-permute-done.got = f32[132,256]{1,0:T(8,128)S(1)} collective-permute-done((f32[132,256]{1,0:T(8,128)S(1)}, f32[132,256]{1,0:T(8,128)S(1)}, u32[]{:S(2)}, u32[]{:S(2)}) %collective-permute-start) | collective-permute-done | bytes 135200 | tf_op jit(solution)/shard_map/ppermute | solution.py:18
  12.8 2.2 %collective-permute-start.1 = (f32[136,256]{1,0:T(8,128)S(1)}, f32[136,256]{1,0:T(8,128)S(1)}, u32[]{:S(2)}, u32[]{:S(2)}) collective-permute-start(f32[136,256]{1,0:T(8,128)S(1)} %shard_map.67.token.own), channel_id=1, source_target_pairs={{0,2},{1,3},{2,0},{3,1},{4,6},{5,7},{6,4},{7,5},{8,10},{9,11},{10,... | collective-permute-start | bytes 417800 | tf_op jit(solution)/shard_map/ppermute | solution.py:18
  15.2 1.6 %collective-permute-start.5 = (f32[128,256]{1,0:T(8,128)S(1)}, f32[128,256]{1,0:T(8,128)S(1)}, u32[]{:S(2)}, u32[]{:S(2)}) collective-permute-start(f32[128,256]{1,0:T(8,128)S(1)} %shard_map.68.token.own), channel_id=1, source_target_pairs={{0,1},{1,0},{2,3},{3,2},{4,5},{5,4},{6,7},{7,6},{8,9},{9,8},{10,11... | collective-permute-start | bytes 393224 | tf_op jit(solution)/shard_map/ppermute | solution.py:18
  17.0 0.5 collective-permute-start.4
  17.5 1.7 %collective-permute-done.1.got = f32[136,256]{1,0:T(8,128)S(1)} collective-permute-done((f32[136,256]{1,0:T(8,128)S(1)}, f32[136,256]{1,0:T(8,128)S(1)}, u32[]{:S(2)}, u32[]{:S(2)}) %collective-permute-start.1) | collective-permute-done | bytes 139296 | tf_op jit(solution)/shard_map/ppermute | solution.py:18
  19.4 3.4 %collective-permute-start.3 = (f32[144,256]{1,0:T(8,128)S(1)}, f32[144,256]{1,0:T(8,128)S(1)}, u32[]{:S(2)}, u32[]{:S(2)}) collective-permute-start(f32[144,256]{1,0:T(8,128)S(1)} %shard_map.70.token.own), channel_id=1, source_target_pairs={{0,4},{1,5},{2,6},{3,7},{4,0},{5,1},{6,2},{7,3},{8,12},{9,13},{10,... | collective-permute-start | bytes 442376 | tf_op jit(solution)/shard_map/ppermute | solution.py:18
  23.1 1.5 %collective-permute-start.9 = (f32[128,256]{1,0:T(8,128)S(1)}, f32[128,256]{1,0:T(8,128)S(1)}, u32[]{:S(2)}, u32[]{:S(2)}) collective-permute-start(f32[128,256]{1,0:T(8,128)S(1)} %shard_map.71.token.own), channel_id=1, source_target_pairs={{0,1},{1,0},{2,3},{3,2},{4,5},{5,4},{6,7},{7,6},{8,9},{9,8},{10,11... | collective-permute-start | bytes 393224 | tf_op jit(solution)/shard_map/ppermute | solution.py:18
  24.8 2.4 %collective-permute-start.8 = (f32[128,256]{1,0:T(8,128)S(1)}, f32[128,256]{1,0:T(8,128)S(1)}, u32[]{:S(2)}, u32[]{:S(2)}) collective-permute-start(f32[128,256]{1,0:T(8,128)S(1)} %shard_map.72.token.own), channel_id=1, source_target_pairs={{0,2},{1,3},{2,0},{3,1},{4,6},{5,7},{6,4},{7,5},{8,10},{9,11},{10,... | collective-permute-start | bytes 393224 | tf_op jit(solution)/shard_map/ppermute | solution.py:18
  27.5 2.5 %collective-permute-done.3.got = f32[144,256]{1,0:T(8,128)S(1)} collective-permute-done((f32[144,256]{1,0:T(8,128)S(1)}, f32[144,256]{1,0:T(8,128)S(1)}, u32[]{:S(2)}, u32[]{:S(2)}) %collective-permute-start.3) | collective-permute-done | bytes 147488 | tf_op jit(solution)/shard_map/ppermute | solution.py:18
  30.6 0.6 collective-permute-done.8.got
  31.4 2.7 %collective-permute-start.12 = (f32[128,256]{1,0:T(8,128)S(1)}, f32[128,256]{1,0:T(8,128)S(1)}, u32[]{:S(2)}, u32[]{:S(2)}) collective-permute-start(f32[128,256]{1,0:T(8,128)S(1)} %shard_map.76.token.own), channel_id=1, source_target_pairs={{0,4},{1,5},{2,6},{3,7},{4,0},{5,1},{6,2},{7,3},{8,12},{9,13},{10,... | collective-permute-start | bytes 393224 | tf_op jit(solution)/shard_map/ppermute | solution.py:18
  34.6 2.0 %copy-done.1 = f32[7,4,128,256]{3,2,1,0:T(8,128)S(1)} copy-done((f32[7,4,128,256]{3,2,1,0:T(8,128)S(1)}, f32[7,4,128,256]{3,2,1,0:T(8,128)}, u32[]{:S(2)}) %copy-start.1) | copy-done | bytes 3670040
  36.9 1.7 %collective-permute-start.10 = (f32[192,256]{1,0:T(8,128)S(1)}, f32[192,256]{1,0:T(8,128)S(1)}, u32[]{:S(2)}, u32[]{:S(2)}) collective-permute-start(f32[192,256]{1,0:T(8,128)S(1)} %shard_map.78.token.own.tab_own), channel_id=1, source_target_pairs={{0,16},{8,24},{16,0},{24,8},{1,17},{9,25},{17,1},{25,9},{2,18},{10... | collective-permute-start | bytes 589832 | tf_op jit(solution)/shard_map/ppermute | solution.py:18
  38.5 0.8 collective-permute-done.13.got
  39.8 1.0 %collective-permute-done.12.got = f32[128,256]{1,0:T(8,128)S(1)} collective-permute-done((f32[128,256]{1,0:T(8,128)S(1)}, f32[128,256]{1,0:T(8,128)S(1)}, u32[]{:S(2)}, u32[]{:S(2)}) %collective-permute-start.12) | collective-permute-done | bytes 131104 | tf_op jit(solution)/shard_map/ppermute | solution.py:18
  41.4 2.6 %collective-permute-start.15 = (f32[128,256]{1,0:T(8,128)S(1)}, f32[128,256]{1,0:T(8,128)S(1)}, u32[]{:S(2)}, u32[]{:S(2)}) collective-permute-start(f32[128,256]{1,0:T(8,128)S(1)} %shard_map.81.token.own), channel_id=1, source_target_pairs={{0,16},{8,24},{16,0},{24,8},{1,17},{9,25},{17,1},{25,9},{2,18},{10... | collective-permute-start | bytes 393224 | tf_op jit(solution)/shard_map/ppermute | solution.py:18
  44.2 1.6 %shard_map.82 = (f32[128,256]{1,0:T(8,128)S(1)}, f32[128,256]{1,0:T(8,128)S(1)}) custom-call(s32[4]{0:T(128)S(1)} %fusion.index, f32[192,256]{1,0:T(8,128)S(1)} %shard_map.78.token.own.tab_own, f32[192,256]{1,0:T(8,128)S(1)} %collective-permute-done.10.got.tab_got, f32[192,256]{1,0:T(8,128)S(1)} %shard_map.78.token.own.tab_own, ...), custom_call_target="tpu_custom_call" | custom-call | flops 268435456 | bytes 2 | tf_op jit(solution)/shard_map/pallas_call | solution.py:212
  45.8 1.7 %collective-permute-start.14 = (f32[128,256]{1,0:T(8,128)S(1)}, f32[128,256]{1,0:T(8,128)S(1)}, u32[]{:S(2)}, u32[]{:S(2)}) collective-permute-start(f32[128,256]{1,0:T(8,128)S(1)} %get-tuple-element.64), channel_id=1, source_target_pairs={{0,16},{8,24},{16,0},{24,8},{1,17},{9,25},{17,1},{25,9},{2,18},{10... | collective-permute-start | bytes 393224 | tf_op jit(solution)/shard_map/ppermute | solution.py:18
  47.5 1.3 %collective-permute-done.17.got = f32[128,256]{1,0:T(8,128)S(1)} collective-permute-done((f32[128,256]{1,0:T(8,128)S(1)}, f32[128,256]{1,0:T(8,128)S(1)}, u32[]{:S(2)}, u32[]{:S(2)}) %collective-permute-start.17) | collective-permute-done | bytes 131104 | tf_op jit(solution)/shard_map/ppermute | solution.py:18
  49.4 1.1 %collective-permute-start.20 = (f32[128,256]{1,0:T(8,128)S(1)}, f32[128,256]{1,0:T(8,128)S(1)}, u32[]{:S(2)}, u32[]{:S(2)}) collective-permute-start(f32[128,256]{1,0:T(8,128)S(1)} %shard_map.84.token.own), channel_id=1, source_target_pairs={{0,16},{8,24},{16,0},{24,8},{1,17},{9,25},{17,1},{25,9},{2,18},{10... | collective-permute-start | bytes 393224 | tf_op jit(solution)/shard_map/ppermute | solution.py:18
  50.4 1.6 %shard_map.85 = (f32[128,256]{1,0:T(8,128)S(1)}, f32[128,256]{1,0:T(8,128)S(1)}) custom-call(s32[4]{0:T(128)S(1)} %fusion.index, f32[128,256]{1,0:T(8,128)S(1)} %shard_map.81.token.own, f32[128,256]{1,0:T(8,128)S(1)} %collective-permute-done.15.got, f32[192,256]{1,0:T(8,128)S(1)} %shard_map.78.token.own.tab_own, ...), custom_call_target="tpu_custom_call" | custom-call | flops 268435456 | bytes 2 | tf_op jit(solution)/shard_map/pallas_call | solution.py:212
  52.0 1.1 %collective-permute-start.19 = (f32[128,256]{1,0:T(8,128)S(1)}, f32[128,256]{1,0:T(8,128)S(1)}, u32[]{:S(2)}, u32[]{:S(2)}) collective-permute-start(f32[128,256]{1,0:T(8,128)S(1)} %get-tuple-element.68), channel_id=1, source_target_pairs={{0,16},{8,24},{16,0},{24,8},{1,17},{9,25},{17,1},{25,9},{2,18},{10... | collective-permute-start | bytes 393224 | tf_op jit(solution)/shard_map/ppermute | solution.py:18
  53.7 1.1 %collective-permute-start.25 = (f32[128,256]{1,0:T(8,128)S(1)}, f32[128,256]{1,0:T(8,128)S(1)}, u32[]{:S(2)}, u32[]{:S(2)}) collective-permute-start(f32[128,256]{1,0:T(8,128)S(1)} %shard_map.87.token.own), channel_id=1, source_target_pairs={{0,16},{8,24},{16,0},{24,8},{1,17},{9,25},{17,1},{25,9},{2,18},{10... | collective-permute-start | bytes 393224 | tf_op jit(solution)/shard_map/ppermute | solution.py:18
  54.8 0.9 collective-permute-done.20.got
  55.7 1.6 %shard_map.88 = (f32[128,256]{1,0:T(8,128)S(1)}, f32[128,256]{1,0:T(8,128)S(1)}) custom-call(s32[4]{0:T(128)S(1)} %fusion.index, f32[128,256]{1,0:T(8,128)S(1)} %shard_map.84.token.own, f32[128,256]{1,0:T(8,128)S(1)} %collective-permute-done.20.got, f32[192,256]{1,0:T(8,128)S(1)} %shard_map.78.token.own.tab_own, ...), custom_call_target="tpu_custom_call" | custom-call | flops 268435456 | bytes 2 | tf_op jit(solution)/shard_map/pallas_call | solution.py:212
  57.3 1.2 %collective-permute-done.19.got = f32[128,256]{1,0:T(8,128)S(1)} collective-permute-done((f32[128,256]{1,0:T(8,128)S(1)}, f32[128,256]{1,0:T(8,128)S(1)}, u32[]{:S(2)}, u32[]{:S(2)}) %collective-permute-start.19) | collective-permute-done | bytes 131104 | tf_op jit(solution)/shard_map/ppermute | solution.py:18
  58.5 0.3 shard_map.89
  58.9 1.0 collective-permute-start.24
  59.9 0.3 shard_map.90
  60.5 0.4 collective-permute-done.25.got
  60.9 1.6 %shard_map.91 = (f32[128,256]{1,0:T(8,128)S(1)}, f32[128,256]{1,0:T(8,128)S(1)}) custom-call(s32[4]{0:T(128)S(1)} %fusion.index, f32[128,256]{1,0:T(8,128)S(1)} %shard_map.87.token.own, f32[128,256]{1,0:T(8,128)S(1)} %collective-permute-done.25.got, f32[192,256]{1,0:T(8,128)S(1)} %shard_map.78.token.own.tab_own, ...), custom_call_target="tpu_custom_call" | custom-call | flops 268435456 | bytes 2 | tf_op jit(solution)/shard_map/pallas_call | solution.py:212
  62.5 1.1 %collective-permute-start.29 = (f32[128,256]{1,0:T(8,128)S(1)}, f32[128,256]{1,0:T(8,128)S(1)}, u32[]{:S(2)}, u32[]{:S(2)}) collective-permute-start(f32[128,256]{1,0:T(8,128)S(1)} %get-tuple-element.82), channel_id=1, source_target_pairs={{0,16},{8,24},{16,0},{24,8},{1,17},{9,25},{17,1},{25,9},{2,18},{10... | collective-permute-start | bytes 393224 | tf_op jit(solution)/shard_map/ppermute | solution.py:18
  63.6 1.3 %collective-permute-done.24.got = f32[128,256]{1,0:T(8,128)S(1)} collective-permute-done((f32[128,256]{1,0:T(8,128)S(1)}, f32[128,256]{1,0:T(8,128)S(1)}, u32[]{:S(2)}, u32[]{:S(2)}) %collective-permute-start.24) | collective-permute-done | bytes 131104 | tf_op jit(solution)/shard_map/ppermute | solution.py:18
  65.3 0.3 shard_map.93
  65.6 1.2 %collective-permute-start.27 = (f32[128,256]{1,0:T(8,128)S(1)}, f32[128,256]{1,0:T(8,128)S(1)}, u32[]{:S(2)}, u32[]{:S(2)}) collective-permute-start(f32[128,256]{1,0:T(8,128)S(1)} %get-tuple-element.80), channel_id=1, source_target_pairs={{0,4},{1,5},{2,6},{3,7},{4,0},{5,1},{6,2},{7,3},{8,12},{9,13},{10,... | collective-permute-start | bytes 393224 | tf_op jit(solution)/shard_map/ppermute | solution.py:18
  66.8 2.8 %collective-permute-done.22.got = f32[128,256]{1,0:T(8,128)S(1)} collective-permute-done((f32[128,256]{1,0:T(8,128)S(1)}, f32[128,256]{1,0:T(8,128)S(1)}, u32[]{:S(2)}, u32[]{:S(2)}) %collective-permute-start.22) | collective-permute-done | bytes 131104 | tf_op jit(solution)/shard_map/ppermute | solution.py:18
  69.6 0.3 shard_map.94
  69.9 0.8 collective-permute-start.26
  70.7 0.3 shard_map.95
  71.1 0.3 shard_map.96
  71.5 1.3 %collective-permute-start.32 = (f32[128,256]{1,0:T(8,128)S(1)}, f32[128,256]{1,0:T(8,128)S(1)}, u32[]{:S(2)}, u32[]{:S(2)}) collective-permute-start(f32[128,256]{1,0:T(8,128)S(1)} %get-tuple-element.89), channel_id=1, source_target_pairs={{0,4},{1,5},{2,6},{3,7},{4,0},{5,1},{6,2},{7,3},{8,12},{9,13},{10,... | collective-permute-start | bytes 393224 | tf_op jit(solution)/shard_map/ppermute | solution.py:18
  72.8 2.5 %collective-permute-done.27.got = f32[128,256]{1,0:T(8,128)S(1)} collective-permute-done((f32[128,256]{1,0:T(8,128)S(1)}, f32[128,256]{1,0:T(8,128)S(1)}, u32[]{:S(2)}, u32[]{:S(2)}) %collective-permute-start.27) | collective-permute-done | bytes 131104 | tf_op jit(solution)/shard_map/ppermute | solution.py:18
  75.6 0.6 collective-permute-start.31
  76.2 0.3 shard_map.98
  76.5 1.8 %collective-permute-start.30 = (f32[128,256]{1,0:T(8,128)S(1)}, f32[128,256]{1,0:T(8,128)S(1)}, u32[]{:S(2)}, u32[]{:S(2)}) collective-permute-start(f32[128,256]{1,0:T(8,128)S(1)} %get-tuple-element.87), channel_id=1, source_target_pairs={{0,1},{1,0},{2,3},{3,2},{4,5},{5,4},{6,7},{7,6},{8,9},{9,8},{10,11... | collective-permute-start | bytes 393224 | tf_op jit(solution)/shard_map/ppermute | solution.py:18
  78.6 3.2 %collective-permute-start.36 = (f32[128,256]{1,0:T(8,128)S(1)}, f32[128,256]{1,0:T(8,128)S(1)}, u32[]{:S(2)}, u32[]{:S(2)}) collective-permute-start(f32[128,256]{1,0:T(8,128)S(1)} %get-tuple-element.98), channel_id=1, source_target_pairs={{0,4},{1,5},{2,6},{3,7},{4,0},{5,1},{6,2},{7,3},{8,12},{9,13},{10,... | collective-permute-start | bytes 393224 | tf_op jit(solution)/shard_map/ppermute | solution.py:18
  81.8 0.3 shard_map.100
  82.2 0.3 shard_map.101
  82.5 1.4 %collective-permute-start.34 = (f32[128,256]{1,0:T(8,128)S(1)}, f32[128,256]{1,0:T(8,128)S(1)}, u32[]{:S(2)}, u32[]{:S(2)}) collective-permute-start(f32[128,256]{1,0:T(8,128)S(1)} %get-tuple-element.96), channel_id=1, source_target_pairs={{0,1},{1,0},{2,3},{3,2},{4,5},{5,4},{6,7},{7,6},{8,9},{9,8},{10,11... | collective-permute-start | bytes 393224 | tf_op jit(solution)/shard_map/ppermute | solution.py:18
  83.9 1.5 %collective-permute-start.35 = (f32[128,256]{1,0:T(8,128)S(1)}, f32[128,256]{1,0:T(8,128)S(1)}, u32[]{:S(2)}, u32[]{:S(2)}) collective-permute-start(f32[128,256]{1,0:T(8,128)S(1)} %get-tuple-element.97), channel_id=1, source_target_pairs={{0,2},{1,3},{2,0},{3,1},{4,6},{5,7},{6,4},{7,5},{8,10},{9,11},{10,... | collective-permute-start | bytes 393224 | tf_op jit(solution)/shard_map/ppermute | solution.py:18
  85.7 2.0 %collective-permute-done.36.got = f32[128,256]{1,0:T(8,128)S(1)} collective-permute-done((f32[128,256]{1,0:T(8,128)S(1)}, f32[128,256]{1,0:T(8,128)S(1)}, u32[]{:S(2)}, u32[]{:S(2)}) %collective-permute-start.36) | collective-permute-done | bytes 131104 | tf_op jit(solution)/shard_map/ppermute | solution.py:18
  88.1 0.8 collective-permute-start.38
  89.1 0.3 shard_map.104
  89.5 2.0 %collective-permute-start.37 = (f32[128,256]{1,0:T(8,128)S(1)}, f32[128,256]{1,0:T(8,128)S(1)}, u32[]{:S(2)}, u32[]{:S(2)}) collective-permute-start(f32[128,256]{1,0:T(8,128)S(1)} %get-tuple-element.103), channel_id=1, source_target_pairs={{0,1},{1,0},{2,3},{3,2},{4,5},{5,4},{6,7},{7,6},{8,9},{9,8},{10,11... | collective-permute-start | bytes 393224 | tf_op jit(solution)/shard_map/ppermute | solution.py:18
  91.8 1.3 %collective-permute-done.38.got = f32[128,256]{1,0:T(8,128)S(1)} collective-permute-done((f32[128,256]{1,0:T(8,128)S(1)}, f32[128,256]{1,0:T(8,128)S(1)}, u32[]{:S(2)}, u32[]{:S(2)}) %collective-permute-start.38) | collective-permute-done | bytes 131104 | tf_op jit(solution)/shard_map/ppermute | solution.py:18
  93.4 0.9 collective-permute-start.39
  94.3 1.0 collective-permute-done.37.got
  95.6 2.9 %collective-permute-done.39.got = f32[128,256]{1,0:T(8,128)S(1)} collective-permute-done((f32[128,256]{1,0:T(8,128)S(1)}, f32[128,256]{1,0:T(8,128)S(1)}, u32[]{:S(2)}, u32[]{:S(2)}) %collective-permute-start.39) | collective-permute-done | bytes 131104 | tf_op jit(solution)/shard_map/ppermute | solution.py:18
  98.5 0.3 shard_map.108
  98.8 2.0 %shard_map.109 = f32[1024,256]{1,0:T(8,128)} custom-call(f32[4,128,256]{2,1,0:T(8,128)S(1)} %copy-done.4, f32[7,4,128,256]{3,2,1,0:T(8,128)S(1)} %copy-done.2, f32[128,256]{1,0:T(8,128)S(1)} %get-tuple-element.94.token.rest_0_, f32[128,256]{1,0:T(8,128)S(1)} %get-tuple-element.95.rest_1_, f32[128,256]{1,0:T(8,128)S(1)} %get-tuple-element.101.token.rest_2_, ...), custom_call_target="tpu_custom_call" | custom-call | flops 805306368 | bytes 12 | tf_op jit(solution)/shard_map/pallas_call | solution.py:223
  (79 shorter events, 9.1 us)
Async XLA Ops:
  0.0 2.0 %copy-start = (f32[7,4,128,256]{3,2,1,0:T(8,128)S(1)}, f32[7,4,128,256]{3,2,1,0:T(8,128)}, u32[]{:S(2)}) copy-start(f32[7,4,128,256]{3,2,1,0:T(8,128)} %factors.89) | copy-start | bytes 11010052
  0.0 2.1 %copy-start.4 = (f32[4,128,256]{2,1,0:T(8,128)S(1)}, f32[4,128,256]{2,1,0:T(8,128)}, u32[]{:S(2)}) copy-start(f32[4,128,256]{2,1,0:T(8,128)} %leaf_in.3) | copy-start | bytes 1572868
  0.0 2.1 %copy-start.6 = (f32[4,256]{1,0:T(4,128)S(1)}, f32[4,256]{1,0:T(4,128)}, u32[]{:S(2)}) copy-start(f32[4,256]{1,0:T(4,128)} %table.1) | copy-start | bytes 12292
  0.0 2.5 %copy-start.5 = (f32[1024,256]{1,0:T(8,128)S(1)}, f32[1024,256]{1,0:T(8,128)}, u32[]{:S(2)}) copy-start(f32[1024,256]{1,0:T(8,128)} %source.1) | copy-start | bytes 3145732
  5.0 7.5 %collective-permute-start = (f32[132,256]{1,0:T(8,128)S(1)}, f32[132,256]{1,0:T(8,128)S(1)}, u32[]{:S(2)}, u32[]{:S(2)}) collective-permute-start(f32[132,256]{1,0:T(8,128)S(1)} %get-tuple-element.58.token.own), channel_id=1, source_target_pairs={{0,1},{1,0},{2,3},{3,2},{4,5},{5,4},{6,7},{7,6},{8,9},{9,8},{10,11... | collective-permute-start | bytes 405512 | tf_op jit(solution)/shard_map/ppermute | solution.py:18
  8.3 8.5 %collective-permute-start.2 = (f32[128,256]{1,0:T(8,128)S(1)}, f32[128,256]{1,0:T(8,128)S(1)}, u32[]{:S(2)}, u32[]{:S(2)}) collective-permute-start(f32[128,256]{1,0:T(8,128)S(1)} %shard_map.66.token.own), channel_id=1, source_target_pairs={{0,1},{1,0},{2,3},{3,2},{4,5},{5,4},{6,7},{7,6},{8,9},{9,8},{10,11... | collective-permute-start | bytes 393224 | tf_op jit(solution)/shard_map/ppermute | solution.py:18
  12.8 6.4 %collective-permute-start.1 = (f32[136,256]{1,0:T(8,128)S(1)}, f32[136,256]{1,0:T(8,128)S(1)}, u32[]{:S(2)}, u32[]{:S(2)}) collective-permute-start(f32[136,256]{1,0:T(8,128)S(1)} %shard_map.67.token.own), channel_id=1, source_target_pairs={{0,2},{1,3},{2,0},{3,1},{4,6},{5,7},{6,4},{7,5},{8,10},{9,11},{10,... | collective-permute-start | bytes 417800 | tf_op jit(solution)/shard_map/ppermute | solution.py:18
  15.2 9.3 %collective-permute-start.5 = (f32[128,256]{1,0:T(8,128)S(1)}, f32[128,256]{1,0:T(8,128)S(1)}, u32[]{:S(2)}, u32[]{:S(2)}) collective-permute-start(f32[128,256]{1,0:T(8,128)S(1)} %shard_map.68.token.own), channel_id=1, source_target_pairs={{0,1},{1,0},{2,3},{3,2},{4,5},{5,4},{6,7},{7,6},{8,9},{9,8},{10,11... | collective-permute-start | bytes 393224 | tf_op jit(solution)/shard_map/ppermute | solution.py:18
  17.0 10.2 %collective-permute-start.4 = (f32[128,256]{1,0:T(8,128)S(1)}, f32[128,256]{1,0:T(8,128)S(1)}, u32[]{:S(2)}, u32[]{:S(2)}) collective-permute-start(f32[128,256]{1,0:T(8,128)S(1)} %shard_map.69.token.own), channel_id=1, source_target_pairs={{0,2},{1,3},{2,0},{3,1},{4,6},{5,7},{6,4},{7,5},{8,10},{9,11},{10,... | collective-permute-start | bytes 393224 | tf_op jit(solution)/shard_map/ppermute | solution.py:18
  19.4 10.6 %collective-permute-start.3 = (f32[144,256]{1,0:T(8,128)S(1)}, f32[144,256]{1,0:T(8,128)S(1)}, u32[]{:S(2)}, u32[]{:S(2)}) collective-permute-start(f32[144,256]{1,0:T(8,128)S(1)} %shard_map.70.token.own), channel_id=1, source_target_pairs={{0,4},{1,5},{2,6},{3,7},{4,0},{5,1},{6,2},{7,3},{8,12},{9,13},{10,... | collective-permute-start | bytes 442376 | tf_op jit(solution)/shard_map/ppermute | solution.py:18
  23.1 7.2 %collective-permute-start.9 = (f32[128,256]{1,0:T(8,128)S(1)}, f32[128,256]{1,0:T(8,128)S(1)}, u32[]{:S(2)}, u32[]{:S(2)}) collective-permute-start(f32[128,256]{1,0:T(8,128)S(1)} %shard_map.71.token.own), channel_id=1, source_target_pairs={{0,1},{1,0},{2,3},{3,2},{4,5},{5,4},{6,7},{7,6},{8,9},{9,8},{10,11... | collective-permute-start | bytes 393224 | tf_op jit(solution)/shard_map/ppermute | solution.py:18
  24.8 6.4 %collective-permute-start.8 = (f32[128,256]{1,0:T(8,128)S(1)}, f32[128,256]{1,0:T(8,128)S(1)}, u32[]{:S(2)}, u32[]{:S(2)}) collective-permute-start(f32[128,256]{1,0:T(8,128)S(1)} %shard_map.72.token.own), channel_id=1, source_target_pairs={{0,2},{1,3},{2,0},{3,1},{4,6},{5,7},{6,4},{7,5},{8,10},{9,11},{10,... | collective-permute-start | bytes 393224 | tf_op jit(solution)/shard_map/ppermute | solution.py:18
  27.4 6.8 %collective-permute-start.7 = (f32[128,256]{1,0:T(8,128)S(1)}, f32[128,256]{1,0:T(8,128)S(1)}, u32[]{:S(2)}, u32[]{:S(2)}) collective-permute-start(f32[128,256]{1,0:T(8,128)S(1)} %shard_map.73.token.own), channel_id=1, source_target_pairs={{0,4},{1,5},{2,6},{3,7},{4,0},{5,1},{6,2},{7,3},{8,12},{9,13},{10,... | collective-permute-start | bytes 393224 | tf_op jit(solution)/shard_map/ppermute | solution.py:18
  30.2 4.4 %collective-permute-start.6 = (f32[160,256]{1,0:T(8,128)S(1)}, f32[160,256]{1,0:T(8,128)S(1)}, u32[]{:S(2)}, u32[]{:S(2)}) collective-permute-start(f32[160,256]{1,0:T(8,128)S(1)} %shard_map.74.token.own), channel_id=1, source_target_pairs={{0,8},{8,0},{16,24},{24,16},{1,9},{9,1},{17,25},{25,17},{2,10},{10... | collective-permute-start | bytes 491528 | tf_op jit(solution)/shard_map/ppermute | solution.py:18
  30.5 8.8 %collective-permute-start.13 = (f32[128,256]{1,0:T(8,128)S(1)}, f32[128,256]{1,0:T(8,128)S(1)}, u32[]{:S(2)}, u32[]{:S(2)}) collective-permute-start(f32[128,256]{1,0:T(8,128)S(1)} %shard_map.75.token.own), channel_id=1, source_target_pairs={{0,2},{1,3},{2,0},{3,1},{4,6},{5,7},{6,4},{7,5},{8,10},{9,11},{10,... | collective-permute-start | bytes 393224 | tf_op jit(solution)/shard_map/ppermute | solution.py:18
  31.4 9.4 %collective-permute-start.12 = (f32[128,256]{1,0:T(8,128)S(1)}, f32[128,256]{1,0:T(8,128)S(1)}, u32[]{:S(2)}, u32[]{:S(2)}) collective-permute-start(f32[128,256]{1,0:T(8,128)S(1)} %shard_map.76.token.own), channel_id=1, source_target_pairs={{0,4},{1,5},{2,6},{3,7},{4,0},{5,1},{6,2},{7,3},{8,12},{9,13},{10,... | collective-permute-start | bytes 393224 | tf_op jit(solution)/shard_map/ppermute | solution.py:18
  34.5 6.7 %collective-permute-start.11 = (f32[128,256]{1,0:T(8,128)S(1)}, f32[128,256]{1,0:T(8,128)S(1)}, u32[]{:S(2)}, u32[]{:S(2)}) collective-permute-start(f32[128,256]{1,0:T(8,128)S(1)} %shard_map.77.token.own), channel_id=1, source_target_pairs={{0,8},{8,0},{16,24},{24,16},{1,9},{9,1},{17,25},{25,17},{2,10},{10... | collective-permute-start | bytes 393224 | tf_op jit(solution)/shard_map/ppermute | solution.py:18
  34.6 2.0 %copy-start.1 = (f32[7,4,128,256]{3,2,1,0:T(8,128)S(1)}, f32[7,4,128,256]{3,2,1,0:T(8,128)}, u32[]{:S(2)}) copy-start(f32[7,4,128,256]{3,2,1,0:T(8,128)} %factors.89) | copy-start | bytes 11010052
  36.9 7.4 %collective-permute-start.10 = (f32[192,256]{1,0:T(8,128)S(1)}, f32[192,256]{1,0:T(8,128)S(1)}, u32[]{:S(2)}, u32[]{:S(2)}) collective-permute-start(f32[192,256]{1,0:T(8,128)S(1)} %shard_map.78.token.own.tab_own), channel_id=1, source_target_pairs={{0,16},{8,24},{16,0},{24,8},{1,17},{9,25},{17,1},{25,9},{2,18},{10... | collective-permute-start | bytes 589832 | tf_op jit(solution)/shard_map/ppermute | solution.py:18
  39.5 4.4 %copy-start.7 = (s32[4]{0:T(128)S(1)}, s32[4]{0:T(128)}, u32[]{:S(2)}) copy-start(s32[4]{0:T(128)} %param.11) | copy-start | bytes 52
  39.5 4.7 %copy-start.2 = (f32[7,4,128,256]{3,2,1,0:T(8,128)S(1)}, f32[7,4,128,256]{3,2,1,0:T(8,128)}, u32[]{:S(2)}) copy-start(f32[7,4,128,256]{3,2,1,0:T(8,128)} %factors.89) | copy-start | bytes 11010052
  39.6 4.7 %copy-start.3 = (f32[4,256,128]{2,1,0:T(8,128)S(1)}, f32[4,256,128]{2,1,0:T(8,128)}, u32[]{:S(2)}) copy-start(f32[4,256,128]{2,1,0:T(8,128)} %leaf_out.7) | copy-start | bytes 1572868
  39.6 9.2 %collective-permute-start.17 = (f32[128,256]{1,0:T(8,128)S(1)}, f32[128,256]{1,0:T(8,128)S(1)}, u32[]{:S(2)}, u32[]{:S(2)}) collective-permute-start(f32[128,256]{1,0:T(8,128)S(1)} %shard_map.79.token.own), channel_id=1, source_target_pairs={{0,4},{1,5},{2,6},{3,7},{4,0},{5,1},{6,2},{7,3},{8,12},{9,13},{10,... | collective-permute-start | bytes 393224 | tf_op jit(solution)/shard_map/ppermute | solution.py:18
  41.1 8.1 %collective-permute-start.16 = (f32[128,256]{1,0:T(8,128)S(1)}, f32[128,256]{1,0:T(8,128)S(1)}, u32[]{:S(2)}, u32[]{:S(2)}) collective-permute-start(f32[128,256]{1,0:T(8,128)S(1)} %shard_map.80.token.own), channel_id=1, source_target_pairs={{0,8},{8,0},{16,24},{24,16},{1,9},{9,1},{17,25},{25,17},{2,10},{10... | collective-permute-start | bytes 393224 | tf_op jit(solution)/shard_map/ppermute | solution.py:18
  41.4 9.0 %collective-permute-start.15 = (f32[128,256]{1,0:T(8,128)S(1)}, f32[128,256]{1,0:T(8,128)S(1)}, u32[]{:S(2)}, u32[]{:S(2)}) collective-permute-start(f32[128,256]{1,0:T(8,128)S(1)} %shard_map.81.token.own), channel_id=1, source_target_pairs={{0,16},{8,24},{16,0},{24,8},{1,17},{9,25},{17,1},{25,9},{2,18},{10... | collective-permute-start | bytes 393224 | tf_op jit(solution)/shard_map/ppermute | solution.py:18
  45.8 7.3 %collective-permute-start.14 = (f32[128,256]{1,0:T(8,128)S(1)}, f32[128,256]{1,0:T(8,128)S(1)}, u32[]{:S(2)}, u32[]{:S(2)}) collective-permute-start(f32[128,256]{1,0:T(8,128)S(1)} %get-tuple-element.64), channel_id=1, source_target_pairs={{0,16},{8,24},{16,0},{24,8},{1,17},{9,25},{17,1},{25,9},{2,18},{10... | collective-permute-start | bytes 393224 | tf_op jit(solution)/shard_map/ppermute | solution.py:18
  49.0 4.5 %collective-permute-start.21 = (f32[128,256]{1,0:T(8,128)S(1)}, f32[128,256]{1,0:T(8,128)S(1)}, u32[]{:S(2)}, u32[]{:S(2)}) collective-permute-start(f32[128,256]{1,0:T(8,128)S(1)} %shard_map.83.token.own), channel_id=1, source_target_pairs={{0,8},{8,0},{16,24},{24,16},{1,9},{9,1},{17,25},{25,17},{2,10},{10... | collective-permute-start | bytes 393224 | tf_op jit(solution)/shard_map/ppermute | solution.py:18
  49.4 6.4 %collective-permute-start.20 = (f32[128,256]{1,0:T(8,128)S(1)}, f32[128,256]{1,0:T(8,128)S(1)}, u32[]{:S(2)}, u32[]{:S(2)}) collective-permute-start(f32[128,256]{1,0:T(8,128)S(1)} %shard_map.84.token.own), channel_id=1, source_target_pairs={{0,16},{8,24},{16,0},{24,8},{1,17},{9,25},{17,1},{25,9},{2,18},{10... | collective-permute-start | bytes 393224 | tf_op jit(solution)/shard_map/ppermute | solution.py:18
  52.0 6.5 %collective-permute-start.19 = (f32[128,256]{1,0:T(8,128)S(1)}, f32[128,256]{1,0:T(8,128)S(1)}, u32[]{:S(2)}, u32[]{:S(2)}) collective-permute-start(f32[128,256]{1,0:T(8,128)S(1)} %get-tuple-element.68), channel_id=1, source_target_pairs={{0,16},{8,24},{16,0},{24,8},{1,17},{9,25},{17,1},{25,9},{2,18},{10... | collective-permute-start | bytes 393224 | tf_op jit(solution)/shard_map/ppermute | solution.py:18
  53.4 6.5 %collective-permute-start.18 = (f32[128,256]{1,0:T(8,128)S(1)}, f32[128,256]{1,0:T(8,128)S(1)}, u32[]{:S(2)}, u32[]{:S(2)}) collective-permute-start(f32[128,256]{1,0:T(8,128)S(1)} %get-tuple-element.67), channel_id=1, source_target_pairs={{0,8},{8,0},{16,24},{24,16},{1,9},{9,1},{17,25},{25,17},{2,10},{10... | collective-permute-start | bytes 393224 | tf_op jit(solution)/shard_map/ppermute | solution.py:18
  53.7 7.2 %collective-permute-start.25 = (f32[128,256]{1,0:T(8,128)S(1)}, f32[128,256]{1,0:T(8,128)S(1)}, u32[]{:S(2)}, u32[]{:S(2)}) collective-permute-start(f32[128,256]{1,0:T(8,128)S(1)} %shard_map.87.token.own), channel_id=1, source_target_pairs={{0,16},{8,24},{16,0},{24,8},{1,17},{9,25},{17,1},{25,9},{2,18},{10... | collective-permute-start | bytes 393224 | tf_op jit(solution)/shard_map/ppermute | solution.py:18
  58.8 6.4 %collective-permute-start.23 = (f32[128,256]{1,0:T(8,128)S(1)}, f32[128,256]{1,0:T(8,128)S(1)}, u32[]{:S(2)}, u32[]{:S(2)}) collective-permute-start(f32[128,256]{1,0:T(8,128)S(1)} %get-tuple-element.73), channel_id=1, source_target_pairs={{0,8},{8,0},{16,24},{24,16},{1,9},{9,1},{17,25},{25,17},{2,10},{10... | collective-permute-start | bytes 393224 | tf_op jit(solution)/shard_map/ppermute | solution.py:18
  58.9 5.9 %collective-permute-start.24 = (f32[128,256]{1,0:T(8,128)S(1)}, f32[128,256]{1,0:T(8,128)S(1)}, u32[]{:S(2)}, u32[]{:S(2)}) collective-permute-start(f32[128,256]{1,0:T(8,128)S(1)} %get-tuple-element.74), channel_id=1, source_target_pairs={{0,16},{8,24},{16,0},{24,8},{1,17},{9,25},{17,1},{25,9},{2,18},{10... | collective-permute-start | bytes 393224 | tf_op jit(solution)/shard_map/ppermute | solution.py:18
  60.2 9.3 %collective-permute-start.22 = (f32[128,256]{1,0:T(8,128)S(1)}, f32[128,256]{1,0:T(8,128)S(1)}, u32[]{:S(2)}, u32[]{:S(2)}) collective-permute-start(f32[128,256]{1,0:T(8,128)S(1)} %get-tuple-element.72), channel_id=1, source_target_pairs={{0,4},{1,5},{2,6},{3,7},{4,0},{5,1},{6,2},{7,3},{8,12},{9,13},{10,... | collective-permute-start | bytes 393224 | tf_op jit(solution)/shard_map/ppermute | solution.py:18
  62.5 8.2 %collective-permute-start.29 = (f32[128,256]{1,0:T(8,128)S(1)}, f32[128,256]{1,0:T(8,128)S(1)}, u32[]{:S(2)}, u32[]{:S(2)}) collective-permute-start(f32[128,256]{1,0:T(8,128)S(1)} %get-tuple-element.82), channel_id=1, source_target_pairs={{0,16},{8,24},{16,0},{24,8},{1,17},{9,25},{17,1},{25,9},{2,18},{10... | collective-permute-start | bytes 393224 | tf_op jit(solution)/shard_map/ppermute | solution.py:18
  65.2 6.0 %collective-permute-start.28 = (f32[128,256]{1,0:T(8,128)S(1)}, f32[128,256]{1,0:T(8,128)S(1)}, u32[]{:S(2)}, u32[]{:S(2)}) collective-permute-start(f32[128,256]{1,0:T(8,128)S(1)} %get-tuple-element.81), channel_id=1, source_target_pairs={{0,8},{8,0},{16,24},{24,16},{1,9},{9,1},{17,25},{25,17},{2,10},{10... | collective-permute-start | bytes 393224 | tf_op jit(solution)/shard_map/ppermute | solution.py:18
  65.6 9.7 %collective-permute-start.27 = (f32[128,256]{1,0:T(8,128)S(1)}, f32[128,256]{1,0:T(8,128)S(1)}, u32[]{:S(2)}, u32[]{:S(2)}) collective-permute-start(f32[128,256]{1,0:T(8,128)S(1)} %get-tuple-element.80), channel_id=1, source_target_pairs={{0,4},{1,5},{2,6},{3,7},{4,0},{5,1},{6,2},{7,3},{8,12},{9,13},{10,... | collective-permute-start | bytes 393224 | tf_op jit(solution)/shard_map/ppermute | solution.py:18
  69.9 6.3 %collective-permute-start.26 = (f32[128,256]{1,0:T(8,128)S(1)}, f32[128,256]{1,0:T(8,128)S(1)}, u32[]{:S(2)}, u32[]{:S(2)}) collective-permute-start(f32[128,256]{1,0:T(8,128)S(1)} %get-tuple-element.79), channel_id=1, source_target_pairs={{0,2},{1,3},{2,0},{3,1},{4,6},{5,7},{6,4},{7,5},{8,10},{9,11},{10,... | collective-permute-start | bytes 393224 | tf_op jit(solution)/shard_map/ppermute | solution.py:18
  71.0 7.2 %collective-permute-start.33 = (f32[128,256]{1,0:T(8,128)S(1)}, f32[128,256]{1,0:T(8,128)S(1)}, u32[]{:S(2)}, u32[]{:S(2)}) collective-permute-start(f32[128,256]{1,0:T(8,128)S(1)} %get-tuple-element.90), channel_id=1, source_target_pairs={{0,8},{8,0},{16,24},{24,16},{1,9},{9,1},{17,25},{25,17},{2,10},{10... | collective-permute-start | bytes 393224 | tf_op jit(solution)/shard_map/ppermute | solution.py:18
  71.5 10.4 %collective-permute-start.32 = (f32[128,256]{1,0:T(8,128)S(1)}, f32[128,256]{1,0:T(8,128)S(1)}, u32[]{:S(2)}, u32[]{:S(2)}) collective-permute-start(f32[128,256]{1,0:T(8,128)S(1)} %get-tuple-element.89), channel_id=1, source_target_pairs={{0,4},{1,5},{2,6},{3,7},{4,0},{5,1},{6,2},{7,3},{8,12},{9,13},{10,... | collective-permute-start | bytes 393224 | tf_op jit(solution)/shard_map/ppermute | solution.py:18
  75.6 6.6 %collective-permute-start.31 = (f32[128,256]{1,0:T(8,128)S(1)}, f32[128,256]{1,0:T(8,128)S(1)}, u32[]{:S(2)}, u32[]{:S(2)}) collective-permute-start(f32[128,256]{1,0:T(8,128)S(1)} %get-tuple-element.88), channel_id=1, source_target_pairs={{0,2},{1,3},{2,0},{3,1},{4,6},{5,7},{6,4},{7,5},{8,10},{9,11},{10,... | collective-permute-start | bytes 393224 | tf_op jit(solution)/shard_map/ppermute | solution.py:18
  76.5 8.9 %collective-permute-start.30 = (f32[128,256]{1,0:T(8,128)S(1)}, f32[128,256]{1,0:T(8,128)S(1)}, u32[]{:S(2)}, u32[]{:S(2)}) collective-permute-start(f32[128,256]{1,0:T(8,128)S(1)} %get-tuple-element.87), channel_id=1, source_target_pairs={{0,1},{1,0},{2,3},{3,2},{4,5},{5,4},{6,7},{7,6},{8,9},{9,8},{10,11... | collective-permute-start | bytes 393224 | tf_op jit(solution)/shard_map/ppermute | solution.py:18
  78.6 9.2 %collective-permute-start.36 = (f32[128,256]{1,0:T(8,128)S(1)}, f32[128,256]{1,0:T(8,128)S(1)}, u32[]{:S(2)}, u32[]{:S(2)}) collective-permute-start(f32[128,256]{1,0:T(8,128)S(1)} %get-tuple-element.98), channel_id=1, source_target_pairs={{0,4},{1,5},{2,6},{3,7},{4,0},{5,1},{6,2},{7,3},{8,12},{9,13},{10,... | collective-permute-start | bytes 393224 | tf_op jit(solution)/shard_map/ppermute | solution.py:18
  82.5 9.0 %collective-permute-start.34 = (f32[128,256]{1,0:T(8,128)S(1)}, f32[128,256]{1,0:T(8,128)S(1)}, u32[]{:S(2)}, u32[]{:S(2)}) collective-permute-start(f32[128,256]{1,0:T(8,128)S(1)} %get-tuple-element.96), channel_id=1, source_target_pairs={{0,1},{1,0},{2,3},{3,2},{4,5},{5,4},{6,7},{7,6},{8,9},{9,8},{10,11... | collective-permute-start | bytes 393224 | tf_op jit(solution)/shard_map/ppermute | solution.py:18
  83.9 5.3 %collective-permute-start.35 = (f32[128,256]{1,0:T(8,128)S(1)}, f32[128,256]{1,0:T(8,128)S(1)}, u32[]{:S(2)}, u32[]{:S(2)}) collective-permute-start(f32[128,256]{1,0:T(8,128)S(1)} %get-tuple-element.97), channel_id=1, source_target_pairs={{0,2},{1,3},{2,0},{3,1},{4,6},{5,7},{6,4},{7,5},{8,10},{9,11},{10,... | collective-permute-start | bytes 393224 | tf_op jit(solution)/shard_map/ppermute | solution.py:18
  88.1 5.0 %collective-permute-start.38 = (f32[128,256]{1,0:T(8,128)S(1)}, f32[128,256]{1,0:T(8,128)S(1)}, u32[]{:S(2)}, u32[]{:S(2)}) collective-permute-start(f32[128,256]{1,0:T(8,128)S(1)} %get-tuple-element.104), channel_id=1, source_target_pairs={{0,2},{1,3},{2,0},{3,1},{4,6},{5,7},{6,4},{7,5},{8,10},{9,11},{10,... | collective-permute-start | bytes 393224 | tf_op jit(solution)/shard_map/ppermute | solution.py:18
  89.5 5.8 %collective-permute-start.37 = (f32[128,256]{1,0:T(8,128)S(1)}, f32[128,256]{1,0:T(8,128)S(1)}, u32[]{:S(2)}, u32[]{:S(2)}) collective-permute-start(f32[128,256]{1,0:T(8,128)S(1)} %get-tuple-element.103), channel_id=1, source_target_pairs={{0,1},{1,0},{2,3},{3,2},{4,5},{5,4},{6,7},{7,6},{8,9},{9,8},{10,11... | collective-permute-start | bytes 393224 | tf_op jit(solution)/shard_map/ppermute | solution.py:18
  93.4 5.0 %collective-permute-start.39 = (f32[128,256]{1,0:T(8,128)S(1)}, f32[128,256]{1,0:T(8,128)S(1)}, u32[]{:S(2)}, u32[]{:S(2)}) collective-permute-start(f32[128,256]{1,0:T(8,128)S(1)} %get-tuple-element.108), channel_id=1, source_target_pairs={{0,1},{1,0},{2,3},{3,2},{4,5},{5,4},{6,7},{7,6},{8,9},{9,8},{10,11... | collective-permute-start | bytes 393224 | tf_op jit(solution)/shard_map/ppermute | solution.py:18

commit v6 on v5

v6 whole, which is shorter than its diff:
```python
import functools

import jax
import jax.numpy as jnp
from jax import lax
from jax.experimental import pallas as pl
from jax.experimental.pallas import tpu as pltpu
from jax.sharding import PartitionSpec as P

MIB = 1 << 20
UNIT = 1 << 26
GAIN = 1 << 25
VMEM = pl.BlockSpec(memory_space=pltpu.VMEM)
SMEM = pl.BlockSpec(memory_space=pltpu.SMEM)
HBM = pl.BlockSpec(memory_space=pltpu.HBM)


def exchange(value, axis, bit):
    return lax.ppermute(value, axis, [(i, i ^ 1 << bit) for i in range(lax.axis_size(axis))])


def split(value):
    high = value.astype(jnp.bfloat16)
    return high, (value - high.astype(jnp.float32)).astype(jnp.bfloat16)


def product(a, b):
    one = functools.partial(jnp.dot, preferred_element_type=jnp.float32)
    return one(a[0], b[1]) + one(a[1], b[0]) + one(a[0], b[0])


def product_turned(a, b):
    one = functools.partial(
        lax.dot_general, dimension_numbers=(((0,), (0,)), ((), ())), preferred_element_type=jnp.float32
    )
    return one(a[0], b[1]) + one(a[1], b[0]) + one(a[0], b[0])


def picked(hot, table):
    total, rest = 0.0, table
    for _ in range(3):
        part = rest.astype(jnp.bfloat16)
        rest = rest - part.astype(jnp.float32)
        total = total + jnp.dot(hot.astype(jnp.bfloat16), part, preferred_element_type=jnp.float32)
    return total


def call(kernel, outs, specs, out_specs, flops, traffic, scratch=(), limit=8 * MIB):
    return pl.pallas_call(
        kernel,
        out_shape=outs,
        in_specs=specs,
        out_specs=out_specs,
        scratch_shapes=scratch,
        cost_estimate=pl.CostEstimate(flops=flops, bytes_accessed=traffic, transcendentals=0),
        compiler_params=pltpu.CompilerParams(vmem_limit_bytes=limit),
    )


def lead_kernel(out):
    out[...] = jnp.zeros_like(out)


def halves(mine, value):
    width = value.shape[1] // 2
    left, right = value[:, :width], value[:, width:]
    return jnp.where(mine, left, right), jnp.where(mine, right, left)


def leading():
    return lax.rem(lax.axis_index("row"), 2) == 0


def stacked(a, b):
    return split(jnp.concatenate([a, b], axis=0))


def start_kernel(nodes, rank, leaf, local_bits, source, leaf_in, factors, table, lead, mid, keep, send, x, a, f, sems):
    levels = [pltpu.make_async_copy(factors.at[l], f.at[l], sems.at[2 * nodes + l]) for l in range(local_bits)]
    xs = [pltpu.make_async_copy(source.at[pl.ds(j * leaf, leaf)], x.at[j], sems.at[j]) for j in range(nodes)]
    ins = [pltpu.make_async_copy(leaf_in.at[j], a.at[j], sems.at[nodes + j]) for j in range(nodes)]
    for j in range(nodes):
        ins[j].start()
        xs[j].start()
    for copy in levels:
        copy.start()
    values = []
    for j in range(nodes):
        ins[j].wait()
        xs[j].wait()
        values.append(product(split(a[j]), split(x[j])))
    for l in range(local_bits - 1):
        levels[l].wait()
        parts = [split(v) for v in values]
        values = []
        for j in range(nodes):
            mine, other = parts[j], parts[j ^ 1 << l]
            both = tuple(jnp.concatenate([m, o], axis=0) for m, o in zip(mine, other))
            values.append(product(split(f[l, j]), both))
    for j in range(nodes):
        mid[j] = values[j]
    levels[-1].wait()
    mine = leading()
    for j in range(nodes // 2):
        value = product(split(f[local_bits - 1, j]), stacked(values[j], values[j ^ nodes // 2]))
        rows = pl.ds(j * rank, rank)
        keep[rows, :], send[rows, :] = halves(mine, value)
    rows, half = table.shape[0], keep.shape[1]
    for k in range(table.shape[1] // half):
        tail = pl.ds(nodes // 2 * rank + k * rows, rows)
        keep[tail, :] = table[:, k * half : (k + 1) * half]
        send[tail, :] = table[:, k * half : (k + 1) * half]


def second_kernel(nodes, rank, level, mid, factors, token, keep, send):
    mine = leading()
    for j in range(nodes // 2):
        node = nodes // 2 + j
        value = product(split(factors[level, node]), stacked(mid[node], mid[j]))
        rows = pl.ds(j * rank, rank)
        keep[rows, :], send[rows, :] = halves(mine, value)


def index_kernel(rows_each, ways, col_size, bits, index, other_index, token, hot):
    me = lax.axis_index("row") * col_size + lax.axis_index("col")
    lane = lax.broadcasted_iota(jnp.int32, (1, hot.shape[1]), 1)
    nodes = index.shape[0]
    for j in range(2 * nodes):
        at = index[j] if j < nodes else other_index[j - nodes]
        differs = lax.div(at, rows_each) ^ me
        place = jnp.int32(0)
        for count, bit in enumerate(bits):
            place = place | (((differs >> bit) & 1) << count)
        place = place * (rows_each * ways) + lax.rem(at, rows_each)
        for k in range(ways):
            hot[pl.ds(k * 2 * nodes + j, 1), :] = (lane == place + k * rows_each).astype(jnp.float32)


def enter_kernel(at, rank, extra, from_row, keep, got, token, out):
    out[pl.ds(0, rank), :] = keep[pl.ds(at * rank, rank), :]
    out[pl.ds(rank, rank), :] = got[pl.ds(at * rank, rank), :]
    if extra:
        out[pl.ds(2 * rank, extra), :] = keep[pl.ds(from_row, extra), :]
        out[pl.ds(2 * rank + extra, extra), :] = got[pl.ds(from_row, extra), :]


def forward_kernel(node, rank, level, core, own, got, factors, others, token, out):
    top, low = pl.ds(0, rank), pl.ds(rank, rank)
    first = product(split(factors[level, node]), stacked(own[top, :], got[top, :]))
    second = product(split(others[level, node]), stacked(own[low, :], got[low, :]))
    if core:
        first, second = (
            product(split(factors[level + 1, node]), stacked(first, second)),
            product(split(others[level + 1, node]), stacked(second, first)),
        )
    out[top, :] = first
    out[low, :] = second
    extra = own.shape[0] - 2 * rank
    if extra:
        out[pl.ds(2 * rank, extra), :] = own[pl.ds(2 * rank, extra), :]
        out[pl.ds(2 * rank + extra, extra), :] = got[pl.ds(2 * rank, extra), :]


def middle_kernel(node, nodes, rank, level, hot, own, got, tab_own, tab_got, factors, others, leaf_out, other_out, token, keep, send):
    extra = tab_own.shape[0] - 2 * rank
    tail = pl.ds(2 * rank, extra)
    table = jnp.concatenate([tab_own[tail, :], tab_got[tail, :]], axis=0)
    rows = picked(hot[...], table)
    for k, (fs, ls) in enumerate(((factors, leaf_out), (others, other_out))):
        here = pl.ds(k * rank, rank)
        f, l = split(fs[level, node]), ls[node]
        value = product(f, stacked(own[here, :], got[here, :]))
        at = k * nodes + node
        weights = jnp.concatenate([rows[at : at + 1], rows[2 * nodes + at : 2 * nodes + at + 1]], axis=1)
        value = product(split(product(split(l.T * weights), split(l))), split(value))
        both = product_turned(f, split(value))
        keep[here, :] = both[:rank]
        send[here, :] = both[rank:]


def backward_kernel(node, rank, level, core, own, got, factors, others, token, keep, send):
    top, low = pl.ds(0, rank), pl.ds(rank, rank)
    first, second = own[top, :] + got[top, :], own[low, :] + got[low, :]
    if core:
        one = product_turned(split(factors[level + 1, node]), split(first))
        two = product_turned(split(others[level + 1, node]), split(second))
        first, second = one[:rank] + two[rank:], two[:rank] + one[rank:]
    one = product_turned(split(factors[level, node]), split(first))
    two = product_turned(split(others[level, node]), split(second))
    keep[top, :], send[top, :] = one[:rank], one[rank:]
    keep[low, :], send[low, :] = two[:rank], two[rank:]


def leave_kernel(rank, own, got, token, keep, send):
    keep[...] = own[pl.ds(0, rank), :] + got[pl.ds(0, rank), :]
    send[...] = own[pl.ds(rank, rank), :] + got[pl.ds(rank, rank), :]


def home_kernel(node, rank, level, own, got, factors, token, keep, send):
    mine = leading()
    a, b = own[...], got[...]
    value = jnp.concatenate([jnp.where(mine, a, b), jnp.where(mine, b, a)], axis=1)
    both = product_turned(split(factors[level, node]), split(value))
    keep[...] = both[:rank]
    send[...] = both[rank:]


def end_kernel(nodes, rank, leaf, local_bits, leaf_in, factors, *rest):
    pairs, out, (y, sems) = rest[: 2 * nodes], rest[2 * nodes], rest[2 * nodes + 1 :]
    values = [pairs[2 * j][...] + pairs[2 * (j ^ nodes // 2) + 1][...] for j in range(nodes)]
    for l in reversed(range(local_bits - 1)):
        both = [product_turned(split(factors[l, j]), split(values[j])) for j in range(nodes)]
        values = [both[j][:rank] + both[j ^ 1 << l][rank:] for j in range(nodes)]
    copies = []
    for j in range(nodes):
        y[j] = product_turned(split(leaf_in[j]), split(values[j]))
        copies.append(pltpu.make_async_copy(y.at[j], out.at[pl.ds(j * leaf, leaf)], sems.at[j]))
        copies[-1].start()
    for copy in copies:
        copy.wait()


def task_order(chunks, stages):
    order, queue, waits, entered = [], [], 0, 0
    while len(order) < chunks * stages:
        while entered < chunks and entered * (entered + 1) // 4 <= waits:
            order.append((entered, 0))
            queue.append((entered, 0))
            entered += 1
        c, s = queue.pop(0)
        waits += 1
        if s + 1 < stages:
            order.append((c, s + 1))
            queue.append((c, s + 1))
    return order


def body(source, leaf_in, factors, leaf_out, weight_table, block_index):
    level_count = factors.shape[0]
    nodes, rank, leaf = leaf_in.shape
    width = source.shape[1]
    f32 = jnp.float32
    local_bits = nodes.bit_length() - 1
    col_size = lax.axis_size("col")
    col_bits = col_size.bit_length() - 1
    core_level = local_bits + col_bits
    chain = [level for level in range(local_bits, level_count) if level != core_level]
    steps = len(chain)
    half = width // 2
    ways = leaf // half
    table_rows = weight_table.shape[0] * ways

    def along(level, value):
        position = level - local_bits
        return exchange(value, "col", position) if position < col_bits else exchange(value, "row", position - col_bits)

    others, other_out, other_index = (along(core_level, v) for v in (factors, leaf_out, block_index))

    def shape(rows, columns=half):
        return jax.ShapeDtypeStruct((rows, columns), f32)

    unit, size = UNIT, 1
    lead = call(lead_kernel, shape(8), [], VMEM, 1 << 33, 1)()
    entry = nodes // 2 * rank
    mid, keep_a, send_a = call(
        functools.partial(start_kernel, nodes, rank, leaf, local_bits),
        [jax.ShapeDtypeStruct((nodes, rank, width), f32)] + [shape(entry + table_rows)] * 2,
        [HBM, HBM, HBM, VMEM, VMEM],
        [VMEM] * 3,
        2 * nodes * unit,
        2 * nodes * size,
        [
            pltpu.VMEM((nodes, leaf, width), f32),
            pltpu.VMEM((nodes, rank, leaf), f32),
            pltpu.VMEM((local_bits, nodes, rank, 2 * rank), f32),
            pltpu.SemaphoreType.DMA((2 * nodes + local_bits,)),
        ],
    )(source, leaf_in, factors, weight_table, lead)
    got_a = along(core_level, send_a)
    keep_b, send_b = call(
        functools.partial(second_kernel, nodes, rank, local_bits - 1),
        [shape(entry)] * 2, [VMEM] * 3, [VMEM] * 2, unit, size,
    )(mid, factors, keep_a)
    got_b = along(core_level, send_b)
    hot = call(
        functools.partial(index_kernel, weight_table.shape[0], ways, col_size, [k - local_bits for k in [core_level] + chain]),
        shape(2 * nodes * ways, table_rows << (steps + 1)), [SMEM, SMEM, VMEM], VMEM, unit, size,
    )(block_index, other_index, keep_b)
    token = hot
    pairs = [None] * nodes
    order = task_order(nodes, 2 * steps + 2)
    for (c, s), after in zip(order, order[1:] + [(1, 0)]):
        unit = UNIT + (GAIN * max(pairs[0][0].shape[0] - 2 * rank, 0) // 2 if after[0] == 0 and after[1] > 0 else 0)
        level = chain[s] if s < steps else chain[2 * steps - 1 - s] if s < 2 * steps else None
        if s == 0:
            extra = table_rows if c == 0 else 0
            keep, got = (keep_a, got_a) if c < nodes // 2 else (keep_b, got_b)
            token = call(
                functools.partial(enter_kernel, c % (nodes // 2), rank, extra, entry),
                shape(2 * rank + 2 * extra), [VMEM] * 3, VMEM, unit, size,
            )(keep, got, token)
            pairs[c] = (token, along(level, token))
        elif s < steps:
            own, got = pairs[c]
            token = call(
                functools.partial(forward_kernel, c, rank, chain[s - 1], chain[s - 1] + 1 == core_level),
                shape(2 * own.shape[0] - 2 * rank), [VMEM] * 5, VMEM, unit, size,
            )(own, got, factors, others, token)
            pairs[c] = (token, along(level, token))
            if c == 0:
                gathered = pairs[0]
        elif s == 2 * steps + 1:
            token, send = call(
                functools.partial(home_kernel, c, rank, local_bits - 1),
                [shape(rank, width)] * 2, [VMEM] * 4, [VMEM] * 2, unit, size,
            )(*pairs[c], factors, token)
            pairs[c] = (token, send)
        else:
            if s == steps:
                token, send = call(
                    functools.partial(middle_kernel, c, nodes, rank, level),
                    [shape(2 * rank)] * 2, [VMEM] * 10, [VMEM] * 2, unit, size,
                )(hot, *pairs[c], *gathered, factors, others, leaf_out, other_out, token)
            elif s < 2 * steps:
                token, send = call(
                    functools.partial(backward_kernel, c, rank, level, level + 1 == core_level),
                    [shape(2 * rank)] * 2, [VMEM] * 5, [VMEM] * 2, unit, size,
                )(*pairs[c], factors, others, token)
            else:
                level = core_level
                token, send = call(
                    functools.partial(leave_kernel, rank), [shape(rank)] * 2, [VMEM] * 3, [VMEM] * 2, unit, size
                )(*pairs[c], token)
            pairs[c] = (token, along(level, send))
    return call(
        functools.partial(end_kernel, nodes, rank, leaf, local_bits),
        shape(nodes * leaf, width),
        [VMEM] * (2 + 2 * nodes),
        HBM,
        3 * nodes * unit,
        3 * nodes * size,
        [pltpu.VMEM((nodes, leaf, width), f32), pltpu.SemaphoreType.DMA((nodes,))],
    )(leaf_in, factors, *[v for pair in pairs for v in pair])


def solution(mesh):
    placed = (
        P(("row", "col"), None),
        P(("row", "col"), None, None),
        P(None, ("row", "col"), None, None),
        P(("row", "col"), None, None),
        P(("row", "col"), None),
        P(("row", "col")),
    )
    return jax.shard_map(
        body, mesh=mesh, in_specs=placed, out_specs=P(("row", "col"), None), check_vma=False
    )
```

time: 101 us -> 95.7 us (0.948)
  starting transfers between devices: 45.4 us -> 39.6 us
  waiting for transfers between devices: 29 us -> 32.7 us
  local copies, waits for them, and re-layouts: 4.55 us -> 1.98 us
    ppermute x40 -> x41, starting transfers between devices: 45.4 us -> 39.6 us  [exchange(): lax.ppermute(value, axis, [(i, i ^ 1 << bit) for i in range(lax.axis_size...]
    ppermute x40 -> x41, waiting for transfers between devices: 29 us -> 32.7 us  [exchange(): lax.ppermute(value, axis, [(i, i ^ 1 << bit) for i in range(lax.axis_size...]
    unnamed x16 -> x12, local copies, waits for them, and re-layouts: 4.55 us -> 1.98 us
    pallas_call x44 -> x43, Pallas kernels: 19.3 us -> 18.8 us  [the longest x12 5.29 us: body(): call(functools.partial(backward_kernel, c, rank, level, level + 1 == core...]
  transfers between devices with their start and end apart: 40 -> 41, of which waited for: 20 -> 16; matrix products, arithmetic and copies ran while one was open for 0% -> 0% of each run, Pallas kernels for 16% -> 19%
where the time goes in v6:
time: 95.7 us; the launch traced here: 95.6 us
  starting transfers between devices  39.6 us (41%)
  waiting for transfers between devices  32.7 us (34%)
  Pallas kernels  20.8 us (22%)
  local copies, waits for them, and re-layouts  1.98 us (2%)
    ppermute x41, starting transfers between devices, exchange(): lax.ppermute(value, axis, [(i, i ^ 1 << bit) for i in range(lax.axis_size...  39.6 us
    ppermute x41, waiting for transfers between devices, exchange(): lax.ppermute(value, axis, [(i, i ^ 1 << bit) for i in range(lax.axis_size...  32.7 us
    pallas_call x12, Pallas kernels, body(): call(functools.partial(backward_kernel, c, rank, level, level + 1 == core...  5.29 us
    pallas_call x4, Pallas kernels, body(): call(functools.partial(middle_kernel, c, nodes, rank, level), [shape(2 *...  4.68 us
    pallas_call x12, Pallas kernels, body(): call(functools.partial(forward_kernel, c, rank, chain[s - 1], chain[s - 1...  4.07 us
    pallas_call x1, Pallas kernels, body(): call(functools.partial(start_kernel, nodes, rank, leaf, local_bits), [jax...  2.59 us
    unnamed x12, local copies, waits for them, and re-layouts  1.98 us
    pallas_call x1, Pallas kernels, body(): call(functools.partial(end_kernel, nodes, rank, leaf, local_bits), shape(...  1.96 us
  transfers between devices with their start and end apart: 41, of which 16 were waited for; matrix products, arithmetic and copies ran while one was open for 0% of the time, Pallas kernels for 19%

profile of v6, /device:TPU:0, one launch (start us, length us, event | category | flops | bytes accessed | tf_op | source)
XLA Modules:
  0.0 95.6 jit_solution(13137033329147586132)
XLA Ops:
  0.0 0.5 collective-permute-start.3
  0.5 1.5 %copy-done = f32[7,4,128,256]{3,2,1,0:T(8,128)S(1)} copy-done((f32[7,4,128,256]{3,2,1,0:T(8,128)S(1)}, f32[7,4,128,256]{3,2,1,0:T(8,128)}, u32[]{:S(2)}) %copy-start) | copy-done | bytes 3670040
  2.1 0.4 copy-done.3
  2.5 2.6 %shard_map.65 = (f32[4,128,256]{2,1,0:T(8,128)S(1)}, f32[264,128]{1,0:T(8,128)S(1)}, f32[264,128]{1,0:T(8,128)S(1)}) custom-call(f32[1024,256]{1,0:T(8,128)S(1)} %copy-done.3, f32[4,128,256]{2,1,0:T(8,128)S(1)} %copy-done.2, f32[7,4,128,256]{3,2,1,0:T(8,128)S(1)} %copy-done, f32[4,256]{1,0:T(4,128)S(1)} %copy-done.4, f32[8,128]{1,0:T(8,128)S(1)} %shard_map.64.lead), custom_call_target="tpu_custom_call" | custom-call | flops 536870912 | bytes 8 | tf_op jit(solution)/shard_map/pallas_call | solution.py:265
  5.1 0.5 collective-permute-start.1
  5.7 0.3 shard_map.66
  6.0 0.5 collective-permute-start.6
  6.8 0.6 shard_map.67.token.hot
  7.4 3.0 %collective-permute-start.2 = (f32[272,128]{1,0:T(8,128)S(1)}, f32[272,128]{1,0:T(8,128)S(1)}, u32[]{:S(2)}, u32[]{:S(2)}) collective-permute-start(f32[272,128]{1,0:T(8,128)S(1)} %shard_map.68.token.own), channel_id=1, source_target_pairs={{0,1},{1,0},{2,3},{3,2},{4,5},{5,4},{6,7},{7,6},{8,9},{9,8},{10,11... | collective-permute-start | bytes 417800 | tf_op jit(solution)/shard_map/ppermute | solution.py:19
  10.5 4.4 %collective-permute-done.2.got = f32[272,128]{1,0:T(8,128)S(1)} collective-permute-done((f32[272,128]{1,0:T(8,128)S(1)}, f32[272,128]{1,0:T(8,128)S(1)}, u32[]{:S(2)}, u32[]{:S(2)}) %collective-permute-start.2) | collective-permute-done | bytes 139296 | tf_op jit(solution)/shard_map/ppermute | solution.py:19
  15.1 2.2 %collective-permute-start.4 = (f32[288,128]{1,0:T(8,128)S(1)}, f32[288,128]{1,0:T(8,128)S(1)}, u32[]{:S(2)}, u32[]{:S(2)}) collective-permute-start(f32[288,128]{1,0:T(8,128)S(1)} %shard_map.70.token.own), channel_id=1, source_target_pairs={{0,2},{1,3},{2,0},{3,1},{4,6},{5,7},{6,4},{7,5},{8,10},{9,11},{10,... | collective-permute-start | bytes 442376 | tf_op jit(solution)/shard_map/ppermute | solution.py:19
  17.3 1.6 %collective-permute-start.9 = (f32[256,128]{1,0:T(8,128)S(1)}, f32[256,128]{1,0:T(8,128)S(1)}, u32[]{:S(2)}, u32[]{:S(2)}) collective-permute-start(f32[256,128]{1,0:T(8,128)S(1)} %shard_map.71.token.own), channel_id=1, source_target_pairs={{0,1},{1,0},{2,3},{3,2},{4,5},{5,4},{6,7},{7,6},{8,9},{9,8},{10,11... | collective-permute-start | bytes 393224 | tf_op jit(solution)/shard_map/ppermute | solution.py:19
  19.2 0.5 collective-permute-start.8
  19.7 1.5 %collective-permute-done.4.got = f32[288,128]{1,0:T(8,128)S(1)} collective-permute-done((f32[288,128]{1,0:T(8,128)S(1)}, f32[288,128]{1,0:T(8,128)S(1)}, u32[]{:S(2)}, u32[]{:S(2)}) %collective-permute-start.4) | collective-permute-done | bytes 147488 | tf_op jit(solution)/shard_map/ppermute | solution.py:19
  21.5 3.5 %collective-permute-start.7 = (f32[320,128]{1,0:T(8,128)S(1)}, f32[320,128]{1,0:T(8,128)S(1)}, u32[]{:S(2)}, u32[]{:S(2)}) collective-permute-start(f32[320,128]{1,0:T(8,128)S(1)} %shard_map.73.token.own), channel_id=1, source_target_pairs={{0,4},{1,5},{2,6},{3,7},{4,0},{5,1},{6,2},{7,3},{8,12},{9,13},{10,... | collective-permute-start | bytes 491528 | tf_op jit(solution)/shard_map/ppermute | solution.py:19
  24.9 1.7 %collective-permute-start.14 = (f32[256,128]{1,0:T(8,128)S(1)}, f32[256,128]{1,0:T(8,128)S(1)}, u32[]{:S(2)}, u32[]{:S(2)}) collective-permute-start(f32[256,128]{1,0:T(8,128)S(1)} %shard_map.74.token.own), channel_id=1, source_target_pairs={{0,1},{1,0},{2,3},{3,2},{4,5},{5,4},{6,7},{7,6},{8,9},{9,8},{10,11... | collective-permute-start | bytes 393224 | tf_op jit(solution)/shard_map/ppermute | solution.py:19
  26.9 1.6 %collective-permute-start.13 = (f32[256,128]{1,0:T(8,128)S(1)}, f32[256,128]{1,0:T(8,128)S(1)}, u32[]{:S(2)}, u32[]{:S(2)}) collective-permute-start(f32[256,128]{1,0:T(8,128)S(1)} %shard_map.75.token.own), channel_id=1, source_target_pairs={{0,2},{1,3},{2,0},{3,1},{4,6},{5,7},{6,4},{7,5},{8,10},{9,11},{10,... | collective-permute-start | bytes 393224 | tf_op jit(solution)/shard_map/ppermute | solution.py:19
  28.8 0.4 collective-permute-start.12
  29.2 4.1 %collective-permute-done.7.got = f32[320,128]{1,0:T(8,128)S(1)} collective-permute-done((f32[320,128]{1,0:T(8,128)S(1)}, f32[320,128]{1,0:T(8,128)S(1)}, u32[]{:S(2)}, u32[]{:S(2)}) %collective-permute-start.7) | collective-permute-done | bytes 163872 | tf_op jit(solution)/shard_map/ppermute | solution.py:19
  33.3 0.5 shard_map.77.token.own.tab_own
  33.8 1.9 %collective-permute-start.10 = (f32[384,128]{1,0:T(8,128)S(1)}, f32[384,128]{1,0:T(8,128)S(1)}, u32[]{:S(2)}, u32[]{:S(2)}) collective-permute-start(f32[384,128]{1,0:T(8,128)S(1)} %shard_map.77.token.own.tab_own), channel_id=1, source_target_pairs={{0,16},{8,24},{16,0},{24,8},{1,17},{9,25},{17,1},{25,9},{2,18},{10... | collective-permute-start | bytes 589832 | tf_op jit(solution)/shard_map/ppermute | solution.py:19
  36.0 2.1 %collective-permute-start.18 = (f32[256,128]{1,0:T(8,128)S(1)}, f32[256,128]{1,0:T(8,128)S(1)}, u32[]{:S(2)}, u32[]{:S(2)}) collective-permute-start(f32[256,128]{1,0:T(8,128)S(1)} %shard_map.78.token.own), channel_id=1, source_target_pairs={{0,2},{1,3},{2,0},{3,1},{4,6},{5,7},{6,4},{7,5},{8,10},{9,11},{10,... | collective-permute-start | bytes 393224 | tf_op jit(solution)/shard_map/ppermute | solution.py:19
  38.4 3.4 %collective-permute-start.17 = (f32[256,128]{1,0:T(8,128)S(1)}, f32[256,128]{1,0:T(8,128)S(1)}, u32[]{:S(2)}, u32[]{:S(2)}) collective-permute-start(f32[256,128]{1,0:T(8,128)S(1)} %shard_map.79.token.own), channel_id=1, source_target_pairs={{0,4},{1,5},{2,6},{3,7},{4,0},{5,1},{6,2},{7,3},{8,12},{9,13},{10,... | collective-permute-start | bytes 393224 | tf_op jit(solution)/shard_map/ppermute | solution.py:19
  41.8 0.5 shard_map.80.token.own
  42.3 0.6 collective-permute-start.16
  42.9 1.2 %shard_map.81 = (f32[256,128]{1,0:T(8,128)S(1)}, f32[256,128]{1,0:T(8,128)S(1)}) custom-call(f32[16,256]{1,0:T(8,128)S(1)} %shard_map.67.token.hot, f32[384,128]{1,0:T(8,128)S(1)} %shard_map.77.token.own.tab_own, f32[384,128]{1,0:T(8,128)S(1)} %collective-permute-done.10.got.tab_got, f32[384,128]{1,0:T(8,128)S(1)} %shard_map.77.token.own.tab_own, ...), custom_call_target="tpu_custom_call" | custom-call | flops 67108864 | bytes 1 | tf_op jit(solution)/shard_map/pallas_call | solution.py:320
  44.1 1.6 %collective-permute-start.15 = (f32[256,128]{1,0:T(8,128)S(1)}, f32[256,128]{1,0:T(8,128)S(1)}, u32[]{:S(2)}, u32[]{:S(2)}) collective-permute-start(f32[256,128]{1,0:T(8,128)S(1)} %get-tuple-element.64), channel_id=1, source_target_pairs={{0,16},{8,24},{16,0},{24,8},{1,17},{9,25},{17,1},{25,9},{2,18},{10... | collective-permute-start | bytes 393224 | tf_op jit(solution)/shard_map/ppermute | solution.py:19
  46.0 2.4 %collective-permute-done.17.got = f32[256,128]{1,0:T(8,128)S(1)} collective-permute-done((f32[256,128]{1,0:T(8,128)S(1)}, f32[256,128]{1,0:T(8,128)S(1)}, u32[]{:S(2)}, u32[]{:S(2)}) %collective-permute-start.17) | collective-permute-done | bytes 131104 | tf_op jit(solution)/shard_map/ppermute | solution.py:19
  48.4 0.5 shard_map.83.token.own
  48.9 0.6 collective-permute-start.21
  49.5 1.2 %shard_map.84 = (f32[256,128]{1,0:T(8,128)S(1)}, f32[256,128]{1,0:T(8,128)S(1)}) custom-call(f32[16,256]{1,0:T(8,128)S(1)} %shard_map.67.token.hot, f32[256,128]{1,0:T(8,128)S(1)} %shard_map.80.token.own, f32[256,128]{1,0:T(8,128)S(1)} %collective-permute-done.16.got, f32[384,128]{1,0:T(8,128)S(1)} %shard_map.77.token.own.tab_own, ...), custom_call_target="tpu_custom_call" | custom-call | flops 67108864 | bytes 1 | tf_op jit(solution)/shard_map/pallas_call | solution.py:320
  50.7 1.6 %collective-permute-start.20 = (f32[256,128]{1,0:T(8,128)S(1)}, f32[256,128]{1,0:T(8,128)S(1)}, u32[]{:S(2)}, u32[]{:S(2)}) collective-permute-start(f32[256,128]{1,0:T(8,128)S(1)} %get-tuple-element.68), channel_id=1, source_target_pairs={{0,16},{8,24},{16,0},{24,8},{1,17},{9,25},{17,1},{25,9},{2,18},{10... | collective-permute-start | bytes 393224 | tf_op jit(solution)/shard_map/ppermute | solution.py:19
  52.2 0.7 shard_map.85
  52.9 0.6 collective-permute-start.19
  53.5 1.1 %collective-permute-done.22.got = f32[256,128]{1,0:T(8,128)S(1)} collective-permute-done((f32[256,128]{1,0:T(8,128)S(1)}, f32[256,128]{1,0:T(8,128)S(1)}, u32[]{:S(2)}, u32[]{:S(2)}) %collective-permute-start.22) | collective-permute-done | bytes 131104 | tf_op jit(solution)/shard_map/ppermute | solution.py:19
  54.7 0.5 shard_map.86.token.own
  55.2 0.8 collective-permute-start.26
  56.0 1.2 %shard_map.87 = (f32[256,128]{1,0:T(8,128)S(1)}, f32[256,128]{1,0:T(8,128)S(1)}) custom-call(f32[16,256]{1,0:T(8,128)S(1)} %shard_map.67.token.hot, f32[256,128]{1,0:T(8,128)S(1)} %shard_map.83.token.own, f32[256,128]{1,0:T(8,128)S(1)} %collective-permute-done.21.got, f32[384,128]{1,0:T(8,128)S(1)} %shard_map.77.token.own.tab_own, ...), custom_call_target="tpu_custom_call" | custom-call | flops 67108864 | bytes 1 | tf_op jit(solution)/shard_map/pallas_call | solution.py:320
  57.1 1.4 %collective-permute-start.25 = (f32[256,128]{1,0:T(8,128)S(1)}, f32[256,128]{1,0:T(8,128)S(1)}, u32[]{:S(2)}, u32[]{:S(2)}) collective-permute-start(f32[256,128]{1,0:T(8,128)S(1)} %get-tuple-element.74), channel_id=1, source_target_pairs={{0,16},{8,24},{16,0},{24,8},{1,17},{9,25},{17,1},{25,9},{2,18},{10... | collective-permute-start | bytes 393224 | tf_op jit(solution)/shard_map/ppermute | solution.py:19
  58.5 0.7 shard_map.88
  59.2 1.3 %collective-permute-start.24 = (f32[256,128]{1,0:T(8,128)S(1)}, f32[256,128]{1,0:T(8,128)S(1)}, u32[]{:S(2)}, u32[]{:S(2)}) collective-permute-start(f32[256,128]{1,0:T(8,128)S(1)} %get-tuple-element.73), channel_id=1, source_target_pairs={{0,4},{1,5},{2,6},{3,7},{4,0},{5,1},{6,2},{7,3},{8,12},{9,13},{10,... | collective-permute-start | bytes 393224 | tf_op jit(solution)/shard_map/ppermute | solution.py:19
  60.5 2.9 %collective-permute-done.19.got = f32[256,128]{1,0:T(8,128)S(1)} collective-permute-done((f32[256,128]{1,0:T(8,128)S(1)}, f32[256,128]{1,0:T(8,128)S(1)}, u32[]{:S(2)}, u32[]{:S(2)}) %collective-permute-start.19) | collective-permute-done | bytes 131104 | tf_op jit(solution)/shard_map/ppermute | solution.py:19
  63.8 1.2 %shard_map.90 = (f32[256,128]{1,0:T(8,128)S(1)}, f32[256,128]{1,0:T(8,128)S(1)}) custom-call(f32[16,256]{1,0:T(8,128)S(1)} %shard_map.67.token.hot, f32[256,128]{1,0:T(8,128)S(1)} %shard_map.86.token.own, f32[256,128]{1,0:T(8,128)S(1)} %collective-permute-done.26.got, f32[384,128]{1,0:T(8,128)S(1)} %shard_map.77.token.own.tab_own, ...), custom_call_target="tpu_custom_call" | custom-call | flops 67108864 | bytes 1 | tf_op jit(solution)/shard_map/pallas_call | solution.py:320
  65.0 0.7 shard_map.91
  65.7 1.0 %collective-permute-start.29 = (f32[256,128]{1,0:T(8,128)S(1)}, f32[256,128]{1,0:T(8,128)S(1)}, u32[]{:S(2)}, u32[]{:S(2)}) collective-permute-start(f32[256,128]{1,0:T(8,128)S(1)} %get-tuple-element.81), channel_id=1, source_target_pairs={{0,4},{1,5},{2,6},{3,7},{4,0},{5,1},{6,2},{7,3},{8,12},{9,13},{10,... | collective-permute-start | bytes 393224 | tf_op jit(solution)/shard_map/ppermute | solution.py:19
  66.7 0.9 collective-permute-done.24.got
  67.9 0.5 collective-permute-start.28
  68.4 4.3 %collective-permute-done.23.got = f32[256,128]{1,0:T(8,128)S(1)} collective-permute-done((f32[256,128]{1,0:T(8,128)S(1)}, f32[256,128]{1,0:T(8,128)S(1)}, u32[]{:S(2)}, u32[]{:S(2)}) %collective-permute-start.23) | collective-permute-done | bytes 131104 | tf_op jit(solution)/shard_map/ppermute | solution.py:19
  73.0 0.7 shard_map.94
  73.7 0.8 collective-permute-start.34
  74.6 0.5 shard_map.95
  75.0 3.3 %collective-permute-start.33 = (f32[256,128]{1,0:T(8,128)S(1)}, f32[256,128]{1,0:T(8,128)S(1)}, u32[]{:S(2)}, u32[]{:S(2)}) collective-permute-start(f32[256,128]{1,0:T(8,128)S(1)} %get-tuple-element.89), channel_id=1, source_target_pairs={{0,2},{1,3},{2,0},{3,1},{4,6},{5,7},{6,4},{7,5},{8,10},{9,11},{10,... | collective-permute-start | bytes 393224 | tf_op jit(solution)/shard_map/ppermute | solution.py:19
  78.3 0.3 shard_map.96
  78.7 2.4 %collective-permute-done.34.got = f32[256,128]{1,0:T(8,128)S(1)} collective-permute-done((f32[256,128]{1,0:T(8,128)S(1)}, f32[256,128]{1,0:T(8,128)S(1)}, u32[]{:S(2)}, u32[]{:S(2)}) %collective-permute-start.34) | collective-permute-done | bytes 131104 | tf_op jit(solution)/shard_map/ppermute | solution.py:19
  81.6 0.4 collective-permute-done.33.got
  82.1 0.3 shard_map.99
  82.4 0.8 collective-permute-start.36
  83.2 0.5 collective-permute-done.32.got
  84.0 2.5 %collective-permute-done.37.got = f32[256,128]{1,0:T(8,128)S(1)} collective-permute-done((f32[256,128]{1,0:T(8,128)S(1)}, f32[256,128]{1,0:T(8,128)S(1)}, u32[]{:S(2)}, u32[]{:S(2)}) %collective-permute-start.37) | collective-permute-done | bytes 131104 | tf_op jit(solution)/shard_map/ppermute | solution.py:19
  86.8 0.7 collective-permute-start.39
  87.5 1.3 %collective-permute-done.36.got = f32[256,128]{1,0:T(8,128)S(1)} collective-permute-done((f32[256,128]{1,0:T(8,128)S(1)}, f32[256,128]{1,0:T(8,128)S(1)}, u32[]{:S(2)}, u32[]{:S(2)}) %collective-permute-start.36) | collective-permute-done | bytes 131104 | tf_op jit(solution)/shard_map/ppermute | solution.py:19
  89.2 2.6 %collective-permute-done.39.got = f32[256,128]{1,0:T(8,128)S(1)} collective-permute-done((f32[256,128]{1,0:T(8,128)S(1)}, f32[256,128]{1,0:T(8,128)S(1)}, u32[]{:S(2)}, u32[]{:S(2)}) %collective-permute-start.39) | collective-permute-done | bytes 131104 | tf_op jit(solution)/shard_map/ppermute | solution.py:19
  92.3 0.9 collective-permute-done.40.got
  93.5 2.0 %shard_map.108 = f32[1024,256]{1,0:T(8,128)} custom-call(f32[4,128,256]{2,1,0:T(8,128)S(1)} %copy-done.2, f32[7,4,128,256]{3,2,1,0:T(8,128)S(1)} %copy-done, f32[128,256]{1,0:T(8,128)S(1)} %get-tuple-element.94.token.rest_0_, f32[128,256]{1,0:T(8,128)S(1)} %get-tuple-element.95.rest_1_, f32[128,256]{1,0:T(8,128)S(1)} %get-tuple-element.101.token.rest_2_, ...), custom_call_target="tpu_custom_call" | custom-call | flops 805306368 | bytes 12 | tf_op jit(solution)/shard_map/pallas_call | solution.py:335
  (75 shorter events, 6.1 us)
Async XLA Ops:
  0.0 2.0 %copy-start = (f32[7,4,128,256]{3,2,1,0:T(8,128)S(1)}, f32[7,4,128,256]{3,2,1,0:T(8,128)}, u32[]{:S(2)}) copy-start(f32[7,4,128,256]{3,2,1,0:T(8,128)} %factors.69) | copy-start | bytes 11010052
  0.0 2.1 %copy-start.2 = (f32[4,128,256]{2,1,0:T(8,128)S(1)}, f32[4,128,256]{2,1,0:T(8,128)}, u32[]{:S(2)}) copy-start(f32[4,128,256]{2,1,0:T(8,128)} %leaf_in.3) | copy-start | bytes 1572868
  0.0 2.1 %copy-start.4 = (f32[4,256]{1,0:T(4,128)S(1)}, f32[4,256]{1,0:T(4,128)}, u32[]{:S(2)}) copy-start(f32[4,256]{1,0:T(4,128)} %table.1) | copy-start | bytes 12292
  0.0 2.5 %copy-start.3 = (f32[1024,256]{1,0:T(8,128)S(1)}, f32[1024,256]{1,0:T(8,128)}, u32[]{:S(2)}) copy-start(f32[1024,256]{1,0:T(8,128)} %source.1) | copy-start | bytes 3145732
  0.0 14.8 %collective-permute-start.3 = (f32[7,4,128,256]{3,2,1,0:T(8,128)}, f32[7,4,128,256]{3,2,1,0:T(8,128)S(1)}, u32[]{:S(2)}, u32[]{:S(2)}) collective-permute-start(f32[7,4,128,256]{3,2,1,0:T(8,128)} %factors.69), channel_id=1, source_target_pairs={{0,8},{8,0},{16,24},{24,16},{1,9},{9,1},{17,25},{25,17},{2,10},{10... | collective-permute-start | bytes 11010056 | tf_op jit(solution)/shard_map/ppermute | solution.py:19
  2.5 3.1 %copy-start.5 = (s32[4]{0:T(128)S(1)}, s32[4]{0:T(128)}, u32[]{:S(2)}) copy-start(s32[4]{0:T(128)} %index.1) | copy-start | bytes 52
  5.1 2.3 %collective-permute-start.1 = (f32[264,128]{1,0:T(8,128)S(1)}, f32[264,128]{1,0:T(8,128)S(1)}, u32[]{:S(2)}, u32[]{:S(2)}) collective-permute-start(f32[264,128]{1,0:T(8,128)S(1)} %get-tuple-element.61), channel_id=1, source_target_pairs={{0,8},{8,0},{16,24},{24,16},{1,9},{9,1},{17,25},{25,17},{2,10},{10... | collective-permute-start | bytes 405512 | tf_op jit(solution)/shard_map/ppermute | solution.py:19
  5.6 1.2 %collective-permute-start = (s32[4]{0:T(128)S(1)}, s32[4]{0:T(128)S(1)}, u32[]{:S(2)}, u32[]{:S(2)}) collective-permute-start(s32[4]{0:T(128)S(1)} %copy-done.5), channel_id=1, source_target_pairs={{0,8},{8,0},{16,24},{24,16},{1,9},{9,1},{17,25},{25,17},{2,10},{10... | collective-permute-start | bytes 56 | tf_op jit(solution)/shard_map/ppermute | solution.py:19
  6.0 11.3 %collective-permute-start.6 = (f32[256,128]{1,0:T(8,128)S(1)}, f32[256,128]{1,0:T(8,128)S(1)}, u32[]{:S(2)}, u32[]{:S(2)}) collective-permute-start(f32[256,128]{1,0:T(8,128)S(1)} %get-tuple-element.62), channel_id=1, source_target_pairs={{0,8},{8,0},{16,24},{24,16},{1,9},{9,1},{17,25},{25,17},{2,10},{10... | collective-permute-start | bytes 393224 | tf_op jit(solution)/shard_map/ppermute | solution.py:19
  7.4 7.4 %collective-permute-start.2 = (f32[272,128]{1,0:T(8,128)S(1)}, f32[272,128]{1,0:T(8,128)S(1)}, u32[]{:S(2)}, u32[]{:S(2)}) collective-permute-start(f32[272,128]{1,0:T(8,128)S(1)} %shard_map.68.token.own), channel_id=1, source_target_pairs={{0,1},{1,0},{2,3},{3,2},{4,5},{5,4},{6,7},{7,6},{8,9},{9,8},{10,11... | collective-permute-start | bytes 417800 | tf_op jit(solution)/shard_map/ppermute | solution.py:19
  10.4 8.5 %collective-permute-start.5 = (f32[256,128]{1,0:T(8,128)S(1)}, f32[256,128]{1,0:T(8,128)S(1)}, u32[]{:S(2)}, u32[]{:S(2)}) collective-permute-start(f32[256,128]{1,0:T(8,128)S(1)} %shard_map.69.token.own), channel_id=1, source_target_pairs={{0,1},{1,0},{2,3},{3,2},{4,5},{5,4},{6,7},{7,6},{8,9},{9,8},{10,11... | collective-permute-start | bytes 393224 | tf_op jit(solution)/shard_map/ppermute | solution.py:19
  15.1 6.1 %collective-permute-start.4 = (f32[288,128]{1,0:T(8,128)S(1)}, f32[288,128]{1,0:T(8,128)S(1)}, u32[]{:S(2)}, u32[]{:S(2)}) collective-permute-start(f32[288,128]{1,0:T(8,128)S(1)} %shard_map.70.token.own), channel_id=1, source_target_pairs={{0,2},{1,3},{2,0},{3,1},{4,6},{5,7},{6,4},{7,5},{8,10},{9,11},{10,... | collective-permute-start | bytes 442376 | tf_op jit(solution)/shard_map/ppermute | solution.py:19
  17.3 2.4 %copy-start.1 = (f32[4,256,128]{2,1,0:T(8,128)S(1)}, f32[4,256,128]{2,1,0:T(8,128)}, u32[]{:S(2)}) copy-start(f32[4,256,128]{2,1,0:T(8,128)} %leaf_out.7) | copy-start | bytes 1572868
  17.3 9.3 %collective-permute-start.9 = (f32[256,128]{1,0:T(8,128)S(1)}, f32[256,128]{1,0:T(8,128)S(1)}, u32[]{:S(2)}, u32[]{:S(2)}) collective-permute-start(f32[256,128]{1,0:T(8,128)S(1)} %shard_map.71.token.own), channel_id=1, source_target_pairs={{0,1},{1,0},{2,3},{3,2},{4,5},{5,4},{6,7},{7,6},{8,9},{9,8},{10,11... | collective-permute-start | bytes 393224 | tf_op jit(solution)/shard_map/ppermute | solution.py:19
  19.2 9.3 %collective-permute-start.8 = (f32[256,128]{1,0:T(8,128)S(1)}, f32[256,128]{1,0:T(8,128)S(1)}, u32[]{:S(2)}, u32[]{:S(2)}) collective-permute-start(f32[256,128]{1,0:T(8,128)S(1)} %shard_map.72.token.own), channel_id=1, source_target_pairs={{0,2},{1,3},{2,0},{3,1},{4,6},{5,7},{6,4},{7,5},{8,10},{9,11},{10,... | collective-permute-start | bytes 393224 | tf_op jit(solution)/shard_map/ppermute | solution.py:19
  19.7 23.3 %collective-permute-start.11 = (f32[4,256,128]{2,1,0:T(8,128)S(1)}, f32[4,256,128]{2,1,0:T(8,128)S(1)}, u32[]{:S(2)}, u32[]{:S(2)}) collective-permute-start(f32[4,256,128]{2,1,0:T(8,128)S(1)} %copy-done.1), channel_id=1, source_target_pairs={{0,8},{8,0},{16,24},{24,16},{1,9},{9,1},{17,25},{25,17},{2,10},{10... | collective-permute-start | bytes 1572872 | tf_op jit(solution)/shard_map/ppermute | solution.py:19
  21.5 11.9 %collective-permute-start.7 = (f32[320,128]{1,0:T(8,128)S(1)}, f32[320,128]{1,0:T(8,128)S(1)}, u32[]{:S(2)}, u32[]{:S(2)}) collective-permute-start(f32[320,128]{1,0:T(8,128)S(1)} %shard_map.73.token.own), channel_id=1, source_target_pairs={{0,4},{1,5},{2,6},{3,7},{4,0},{5,1},{6,2},{7,3},{8,12},{9,13},{10,... | collective-permute-start | bytes 491528 | tf_op jit(solution)/shard_map/ppermute | solution.py:19
  24.9 10.8 %collective-permute-start.14 = (f32[256,128]{1,0:T(8,128)S(1)}, f32[256,128]{1,0:T(8,128)S(1)}, u32[]{:S(2)}, u32[]{:S(2)}) collective-permute-start(f32[256,128]{1,0:T(8,128)S(1)} %shard_map.74.token.own), channel_id=1, source_target_pairs={{0,1},{1,0},{2,3},{3,2},{4,5},{5,4},{6,7},{7,6},{8,9},{9,8},{10,11... | collective-permute-start | bytes 393224 | tf_op jit(solution)/shard_map/ppermute | solution.py:19
  26.9 11.2 %collective-permute-start.13 = (f32[256,128]{1,0:T(8,128)S(1)}, f32[256,128]{1,0:T(8,128)S(1)}, u32[]{:S(2)}, u32[]{:S(2)}) collective-permute-start(f32[256,128]{1,0:T(8,128)S(1)} %shard_map.75.token.own), channel_id=1, source_target_pairs={{0,2},{1,3},{2,0},{3,1},{4,6},{5,7},{6,4},{7,5},{8,10},{9,11},{10,... | collective-permute-start | bytes 393224 | tf_op jit(solution)/shard_map/ppermute | solution.py:19
  28.8 13.0 %collective-permute-start.12 = (f32[256,128]{1,0:T(8,128)S(1)}, f32[256,128]{1,0:T(8,128)S(1)}, u32[]{:S(2)}, u32[]{:S(2)}) collective-permute-start(f32[256,128]{1,0:T(8,128)S(1)} %shard_map.76.token.own), channel_id=1, source_target_pairs={{0,4},{1,5},{2,6},{3,7},{4,0},{5,1},{6,2},{7,3},{8,12},{9,13},{10,... | collective-permute-start | bytes 393224 | tf_op jit(solution)/shard_map/ppermute | solution.py:19
  33.8 9.1 %collective-permute-start.10 = (f32[384,128]{1,0:T(8,128)S(1)}, f32[384,128]{1,0:T(8,128)S(1)}, u32[]{:S(2)}, u32[]{:S(2)}) collective-permute-start(f32[384,128]{1,0:T(8,128)S(1)} %shard_map.77.token.own.tab_own), channel_id=1, source_target_pairs={{0,16},{8,24},{16,0},{24,8},{1,17},{9,25},{17,1},{25,9},{2,18},{10... | collective-permute-start | bytes 589832 | tf_op jit(solution)/shard_map/ppermute | solution.py:19
  36.0 9.7 %collective-permute-start.18 = (f32[256,128]{1,0:T(8,128)S(1)}, f32[256,128]{1,0:T(8,128)S(1)}, u32[]{:S(2)}, u32[]{:S(2)}) collective-permute-start(f32[256,128]{1,0:T(8,128)S(1)} %shard_map.78.token.own), channel_id=1, source_target_pairs={{0,2},{1,3},{2,0},{3,1},{4,6},{5,7},{6,4},{7,5},{8,10},{9,11},{10,... | collective-permute-start | bytes 393224 | tf_op jit(solution)/shard_map/ppermute | solution.py:19
  38.4 10.0 %collective-permute-start.17 = (f32[256,128]{1,0:T(8,128)S(1)}, f32[256,128]{1,0:T(8,128)S(1)}, u32[]{:S(2)}, u32[]{:S(2)}) collective-permute-start(f32[256,128]{1,0:T(8,128)S(1)} %shard_map.79.token.own), channel_id=1, source_target_pairs={{0,4},{1,5},{2,6},{3,7},{4,0},{5,1},{6,2},{7,3},{8,12},{9,13},{10,... | collective-permute-start | bytes 393224 | tf_op jit(solution)/shard_map/ppermute | solution.py:19
  42.3 7.1 %collective-permute-start.16 = (f32[256,128]{1,0:T(8,128)S(1)}, f32[256,128]{1,0:T(8,128)S(1)}, u32[]{:S(2)}, u32[]{:S(2)}) collective-permute-start(f32[256,128]{1,0:T(8,128)S(1)} %shard_map.80.token.own), channel_id=1, source_target_pairs={{0,16},{8,24},{16,0},{24,8},{1,17},{9,25},{17,1},{25,9},{2,18},{10... | collective-permute-start | bytes 393224 | tf_op jit(solution)/shard_map/ppermute | solution.py:19
  44.1 8.1 %collective-permute-start.15 = (f32[256,128]{1,0:T(8,128)S(1)}, f32[256,128]{1,0:T(8,128)S(1)}, u32[]{:S(2)}, u32[]{:S(2)}) collective-permute-start(f32[256,128]{1,0:T(8,128)S(1)} %get-tuple-element.64), channel_id=1, source_target_pairs={{0,16},{8,24},{16,0},{24,8},{1,17},{9,25},{17,1},{25,9},{2,18},{10... | collective-permute-start | bytes 393224 | tf_op jit(solution)/shard_map/ppermute | solution.py:19
  45.9 8.7 %collective-permute-start.22 = (f32[256,128]{1,0:T(8,128)S(1)}, f32[256,128]{1,0:T(8,128)S(1)}, u32[]{:S(2)}, u32[]{:S(2)}) collective-permute-start(f32[256,128]{1,0:T(8,128)S(1)} %shard_map.82.token.own), channel_id=1, source_target_pairs={{0,4},{1,5},{2,6},{3,7},{4,0},{5,1},{6,2},{7,3},{8,12},{9,13},{10,... | collective-permute-start | bytes 393224 | tf_op jit(solution)/shard_map/ppermute | solution.py:19
  48.9 7.1 %collective-permute-start.21 = (f32[256,128]{1,0:T(8,128)S(1)}, f32[256,128]{1,0:T(8,128)S(1)}, u32[]{:S(2)}, u32[]{:S(2)}) collective-permute-start(f32[256,128]{1,0:T(8,128)S(1)} %shard_map.83.token.own), channel_id=1, source_target_pairs={{0,16},{8,24},{16,0},{24,8},{1,17},{9,25},{17,1},{25,9},{2,18},{10... | collective-permute-start | bytes 393224 | tf_op jit(solution)/shard_map/ppermute | solution.py:19
  50.7 7.9 %collective-permute-start.20 = (f32[256,128]{1,0:T(8,128)S(1)}, f32[256,128]{1,0:T(8,128)S(1)}, u32[]{:S(2)}, u32[]{:S(2)}) collective-permute-start(f32[256,128]{1,0:T(8,128)S(1)} %get-tuple-element.68), channel_id=1, source_target_pairs={{0,16},{8,24},{16,0},{24,8},{1,17},{9,25},{17,1},{25,9},{2,18},{10... | collective-permute-start | bytes 393224 | tf_op jit(solution)/shard_map/ppermute | solution.py:19
  52.9 10.5 %collective-permute-start.19 = (f32[256,128]{1,0:T(8,128)S(1)}, f32[256,128]{1,0:T(8,128)S(1)}, u32[]{:S(2)}, u32[]{:S(2)}) collective-permute-start(f32[256,128]{1,0:T(8,128)S(1)} %get-tuple-element.67), channel_id=1, source_target_pairs={{0,4},{1,5},{2,6},{3,7},{4,0},{5,1},{6,2},{7,3},{8,12},{9,13},{10,... | collective-permute-start | bytes 393224 | tf_op jit(solution)/shard_map/ppermute | solution.py:19
  55.2 8.6 %collective-permute-start.26 = (f32[256,128]{1,0:T(8,128)S(1)}, f32[256,128]{1,0:T(8,128)S(1)}, u32[]{:S(2)}, u32[]{:S(2)}) collective-permute-start(f32[256,128]{1,0:T(8,128)S(1)} %shard_map.86.token.own), channel_id=1, source_target_pairs={{0,16},{8,24},{16,0},{24,8},{1,17},{9,25},{17,1},{25,9},{2,18},{10... | collective-permute-start | bytes 393224 | tf_op jit(solution)/shard_map/ppermute | solution.py:19
  57.1 7.9 %collective-permute-start.25 = (f32[256,128]{1,0:T(8,128)S(1)}, f32[256,128]{1,0:T(8,128)S(1)}, u32[]{:S(2)}, u32[]{:S(2)}) collective-permute-start(f32[256,128]{1,0:T(8,128)S(1)} %get-tuple-element.74), channel_id=1, source_target_pairs={{0,16},{8,24},{16,0},{24,8},{1,17},{9,25},{17,1},{25,9},{2,18},{10... | collective-permute-start | bytes 393224 | tf_op jit(solution)/shard_map/ppermute | solution.py:19
  59.2 8.4 %collective-permute-start.24 = (f32[256,128]{1,0:T(8,128)S(1)}, f32[256,128]{1,0:T(8,128)S(1)}, u32[]{:S(2)}, u32[]{:S(2)}) collective-permute-start(f32[256,128]{1,0:T(8,128)S(1)} %get-tuple-element.73), channel_id=1, source_target_pairs={{0,4},{1,5},{2,6},{3,7},{4,0},{5,1},{6,2},{7,3},{8,12},{9,13},{10,... | collective-permute-start | bytes 393224 | tf_op jit(solution)/shard_map/ppermute | solution.py:19
  63.7 9.0 %collective-permute-start.23 = (f32[256,128]{1,0:T(8,128)S(1)}, f32[256,128]{1,0:T(8,128)S(1)}, u32[]{:S(2)}, u32[]{:S(2)}) collective-permute-start(f32[256,128]{1,0:T(8,128)S(1)} %get-tuple-element.72), channel_id=1, source_target_pairs={{0,2},{1,3},{2,0},{3,1},{4,6},{5,7},{6,4},{7,5},{8,10},{9,11},{10,... | collective-permute-start | bytes 393224 | tf_op jit(solution)/shard_map/ppermute | solution.py:19
  64.9 8.1 %collective-permute-start.30 = (f32[256,128]{1,0:T(8,128)S(1)}, f32[256,128]{1,0:T(8,128)S(1)}, u32[]{:S(2)}, u32[]{:S(2)}) collective-permute-start(f32[256,128]{1,0:T(8,128)S(1)} %get-tuple-element.82), channel_id=1, source_target_pairs={{0,16},{8,24},{16,0},{24,8},{1,17},{9,25},{17,1},{25,9},{2,18},{10... | collective-permute-start | bytes 393224 | tf_op jit(solution)/shard_map/ppermute | solution.py:19
  65.7 8.8 %collective-permute-start.29 = (f32[256,128]{1,0:T(8,128)S(1)}, f32[256,128]{1,0:T(8,128)S(1)}, u32[]{:S(2)}, u32[]{:S(2)}) collective-permute-start(f32[256,128]{1,0:T(8,128)S(1)} %get-tuple-element.81), channel_id=1, source_target_pairs={{0,4},{1,5},{2,6},{3,7},{4,0},{5,1},{6,2},{7,3},{8,12},{9,13},{10,... | collective-permute-start | bytes 393224 | tf_op jit(solution)/shard_map/ppermute | solution.py:19
  67.9 10.4 %collective-permute-start.28 = (f32[256,128]{1,0:T(8,128)S(1)}, f32[256,128]{1,0:T(8,128)S(1)}, u32[]{:S(2)}, u32[]{:S(2)}) collective-permute-start(f32[256,128]{1,0:T(8,128)S(1)} %get-tuple-element.80), channel_id=1, source_target_pairs={{0,2},{1,3},{2,0},{3,1},{4,6},{5,7},{6,4},{7,5},{8,10},{9,11},{10,... | collective-permute-start | bytes 393224 | tf_op jit(solution)/shard_map/ppermute | solution.py:19
  72.9 5.8 %collective-permute-start.27 = (f32[256,128]{1,0:T(8,128)S(1)}, f32[256,128]{1,0:T(8,128)S(1)}, u32[]{:S(2)}, u32[]{:S(2)}) collective-permute-start(f32[256,128]{1,0:T(8,128)S(1)} %get-tuple-element.79), channel_id=1, source_target_pairs={{0,1},{1,0},{2,3},{3,2},{4,5},{5,4},{6,7},{7,6},{8,9},{9,8},{10,11... | collective-permute-start | bytes 393224 | tf_op jit(solution)/shard_map/ppermute | solution.py:19
  73.7 7.4 %collective-permute-start.34 = (f32[256,128]{1,0:T(8,128)S(1)}, f32[256,128]{1,0:T(8,128)S(1)}, u32[]{:S(2)}, u32[]{:S(2)}) collective-permute-start(f32[256,128]{1,0:T(8,128)S(1)} %get-tuple-element.90), channel_id=1, source_target_pairs={{0,4},{1,5},{2,6},{3,7},{4,0},{5,1},{6,2},{7,3},{8,12},{9,13},{10,... | collective-permute-start | bytes 393224 | tf_op jit(solution)/shard_map/ppermute | solution.py:19
  75.0 7.0 %collective-permute-start.33 = (f32[256,128]{1,0:T(8,128)S(1)}, f32[256,128]{1,0:T(8,128)S(1)}, u32[]{:S(2)}, u32[]{:S(2)}) collective-permute-start(f32[256,128]{1,0:T(8,128)S(1)} %get-tuple-element.89), channel_id=1, source_target_pairs={{0,2},{1,3},{2,0},{3,1},{4,6},{5,7},{6,4},{7,5},{8,10},{9,11},{10,... | collective-permute-start | bytes 393224 | tf_op jit(solution)/shard_map/ppermute | solution.py:19
  78.6 5.0 %collective-permute-start.32 = (f32[256,128]{1,0:T(8,128)S(1)}, f32[256,128]{1,0:T(8,128)S(1)}, u32[]{:S(2)}, u32[]{:S(2)}) collective-permute-start(f32[256,128]{1,0:T(8,128)S(1)} %get-tuple-element.88), channel_id=1, source_target_pairs={{0,1},{1,0},{2,3},{3,2},{4,5},{5,4},{6,7},{7,6},{8,9},{9,8},{10,11... | collective-permute-start | bytes 393224 | tf_op jit(solution)/shard_map/ppermute | solution.py:19
  81.5 5.0 %collective-permute-start.37 = (f32[256,128]{1,0:T(8,128)S(1)}, f32[256,128]{1,0:T(8,128)S(1)}, u32[]{:S(2)}, u32[]{:S(2)}) collective-permute-start(f32[256,128]{1,0:T(8,128)S(1)} %get-tuple-element.98), channel_id=1, source_target_pairs={{0,2},{1,3},{2,0},{3,1},{4,6},{5,7},{6,4},{7,5},{8,10},{9,11},{10,... | collective-permute-start | bytes 393224 | tf_op jit(solution)/shard_map/ppermute | solution.py:19
  81.6 2.1 %collective-permute-start.31 = (f32[128,128]{1,0:T(8,128)S(1)}, f32[128,128]{1,0:T(8,128)S(1)}, u32[]{:S(2)}, u32[]{:S(2)}) collective-permute-start(f32[128,128]{1,0:T(8,128)S(1)} %get-tuple-element.87), channel_id=1, source_target_pairs={{0,8},{8,0},{16,24},{24,16},{1,9},{9,1},{17,25},{25,17},{2,10},{10... | collective-permute-start | bytes 196616 | tf_op jit(solution)/shard_map/ppermute | solution.py:19
  82.4 6.4 %collective-permute-start.36 = (f32[256,128]{1,0:T(8,128)S(1)}, f32[256,128]{1,0:T(8,128)S(1)}, u32[]{:S(2)}, u32[]{:S(2)}) collective-permute-start(f32[256,128]{1,0:T(8,128)S(1)} %get-tuple-element.97), channel_id=1, source_target_pairs={{0,1},{1,0},{2,3},{3,2},{4,5},{5,4},{6,7},{7,6},{8,9},{9,8},{10,11... | collective-permute-start | bytes 393224 | tf_op jit(solution)/shard_map/ppermute | solution.py:19
  86.8 5.0 %collective-permute-start.39 = (f32[256,128]{1,0:T(8,128)S(1)}, f32[256,128]{1,0:T(8,128)S(1)}, u32[]{:S(2)}, u32[]{:S(2)}) collective-permute-start(f32[256,128]{1,0:T(8,128)S(1)} %get-tuple-element.104), channel_id=1, source_target_pairs={{0,1},{1,0},{2,3},{3,2},{4,5},{5,4},{6,7},{7,6},{8,9},{9,8},{10,11... | collective-permute-start | bytes 393224 | tf_op jit(solution)/shard_map/ppermute | solution.py:19
  87.5 1.4 %collective-permute-start.35 = (f32[128,128]{1,0:T(8,128)S(1)}, f32[128,128]{1,0:T(8,128)S(1)}, u32[]{:S(2)}, u32[]{:S(2)}) collective-permute-start(f32[128,128]{1,0:T(8,128)S(1)} %get-tuple-element.96), channel_id=1, source_target_pairs={{0,8},{8,0},{16,24},{24,16},{1,9},{9,1},{17,25},{25,17},{2,10},{10... | collective-permute-start | bytes 196616 | tf_op jit(solution)/shard_map/ppermute | solution.py:19
  88.8 3.1 %collective-permute-start.38 = (f32[128,128]{1,0:T(8,128)S(1)}, f32[128,128]{1,0:T(8,128)S(1)}, u32[]{:S(2)}, u32[]{:S(2)}) collective-permute-start(f32[128,128]{1,0:T(8,128)S(1)} %get-tuple-element.103), channel_id=1, source_target_pairs={{0,8},{8,0},{16,24},{24,16},{1,9},{9,1},{17,25},{25,17},{2,10},{10... | collective-permute-start | bytes 196616 | tf_op jit(solution)/shard_map/ppermute | solution.py:19
  91.9 1.3 %collective-permute-start.40 = (f32[128,128]{1,0:T(8,128)S(1)}, f32[128,128]{1,0:T(8,128)S(1)}, u32[]{:S(2)}, u32[]{:S(2)}) collective-permute-start(f32[128,128]{1,0:T(8,128)S(1)} %get-tuple-element.108), channel_id=1, source_target_pairs={{0,8},{8,0},{16,24},{24,16},{1,9},{9,1},{17,25},{25,17},{2,10},{10... | collective-permute-start | bytes 196616 | tf_op jit(solution)/shard_map/ppermute | solution.py:19

commit v7 on v6

--- a/solution.py
+++ b/solution.py
@@ -193,12 +193,13 @@
 
 def leave_kernel(rank, own, got, token, keep, send):
     keep[...] = own[pl.ds(0, rank), :] + got[pl.ds(0, rank), :]
-    send[...] = own[pl.ds(rank, rank), :] + got[pl.ds(rank, rank), :]
+    send[pl.ds(0, rank), :] = own[pl.ds(rank, rank), :] + got[pl.ds(rank, rank), :]
+    send[pl.ds(rank, rank), :] = jnp.zeros((rank, send.shape[1]), jnp.float32)
 
 
 def home_kernel(node, rank, level, own, got, factors, token, keep, send):
     mine = leading()
-    a, b = own[...], got[...]
+    a, b = own[...], got[pl.ds(0, rank), :]
     value = jnp.concatenate([jnp.where(mine, a, b), jnp.where(mine, b, a)], axis=1)
     both = product_turned(split(factors[level, node]), split(value))
     keep[...] = both[:rank]
@@ -223,7 +224,7 @@
 def task_order(chunks, stages):
     order, queue, waits, entered = [], [], 0, 0
     while len(order) < chunks * stages:
-        while entered < chunks and entered * (entered + 1) // 4 <= waits:
+        while entered < chunks and entered <= waits + 1:
             order.append((entered, 0))
             queue.append((entered, 0))
             entered += 1
@@ -282,15 +283,11 @@
         [shape(entry)] * 2, [VMEM] * 3, [VMEM] * 2, unit, size,
     )(mid, factors, keep_a)
     got_b = along(core_level, send_b)
-    hot = call(
-        functools.partial(index_kernel, weight_table.shape[0], ways, col_size, [k - local_bits for k in [core_level] + chain]),
-        shape(2 * nodes * ways, table_rows << (steps + 1)), [SMEM, SMEM, VMEM], VMEM, unit, size,
-    )(block_index, other_index, keep_b)
-    token = hot
+    token = keep_b
     pairs = [None] * nodes
     order = task_order(nodes, 2 * steps + 2)
     for (c, s), after in zip(order, order[1:] + [(1, 0)]):
-        unit = UNIT + (GAIN * max(pairs[0][0].shape[0] - 2 * rank, 0) // 2 if after[0] == 0 and after[1] > 0 else 0)
+        unit = UNIT + (GAIN * max(pairs[0][0].shape[0] - 2 * rank, 0) // 2 if after[0] == 0 and after[1] > 0 and s + c > 0 else 0)
         level = chain[s] if s < steps else chain[2 * steps - 1 - s] if s < 2 * steps else None
         if s == 0:
             extra = table_rows if c == 0 else 0
@@ -300,6 +297,14 @@
                 shape(2 * rank + 2 * extra), [VMEM] * 3, VMEM, unit, size,
             )(keep, got, token)
             pairs[c] = (token, along(level, token))
+            if c == 1:
+                hot = call(
+                    functools.partial(
+                        index_kernel, weight_table.shape[0], ways, col_size, [k - local_bits for k in [core_level] + chain]
+                    ),
+                    shape(2 * nodes * ways, table_rows << (steps + 1)), [SMEM, SMEM, VMEM], VMEM, unit, size,
+                )(block_index, other_index, token)
+                token = hot
         elif s < steps:
             own, got = pairs[c]
             token = call(
@@ -329,7 +334,7 @@
             else:
                 level = core_level
                 token, send = call(
-                    functools.partial(leave_kernel, rank), [shape(rank)] * 2, [VMEM] * 3, [VMEM] * 2, unit, size
+                    functools.partial(leave_kernel, rank), [shape(rank), shape(2 * rank)], [VMEM] * 3, [VMEM] * 2, unit, size
                 )(*pairs[c], token)
             pairs[c] = (token, along(level, send))
     return call(

time: 95.7 us -> 93.7 us (0.979)
  waiting for transfers between devices: 32.7 us -> 23 us
  starting transfers between devices: 39.6 us -> 47.3 us
    ppermute x41, waiting for transfers between devices: 32.7 us -> 23 us  [exchange(): lax.ppermute(value, axis, [(i, i ^ 1 << bit) for i in range(lax.axis_size...]
    ppermute x41, starting transfers between devices: 39.6 us -> 47.3 us  [exchange(): lax.ppermute(value, axis, [(i, i ^ 1 << bit) for i in range(lax.axis_size...]
  transfers between devices with their start and end apart: 41 -> 41, of which waited for: 16 -> 13; matrix products, arithmetic and copies ran while one was open for 0% -> 0% of each run, Pallas kernels for 19% -> 20%
where the time goes in v7:
time: 93.7 us; the launch traced here: 93.5 us
  starting transfers between devices  47.3 us (50%)
  waiting for transfers between devices  23 us (25%)
  Pallas kernels  20.8 us (22%)
  local copies, waits for them, and re-layouts  1.98 us (2%)
    ppermute x41, starting transfers between devices, exchange(): lax.ppermute(value, axis, [(i, i ^ 1 << bit) for i in range(lax.axis_size...  47.3 us
    ppermute x41, waiting for transfers between devices, exchange(): lax.ppermute(value, axis, [(i, i ^ 1 << bit) for i in range(lax.axis_size...  23 us
    pallas_call x12, Pallas kernels, body(): call(functools.partial(backward_kernel, c, rank, level, level + 1 == core...  5.3 us
    pallas_call x4, Pallas kernels, body(): call(functools.partial(middle_kernel, c, nodes, rank, level), [shape(2 *...  4.67 us
    pallas_call x12, Pallas kernels, body(): call(functools.partial(forward_kernel, c, rank, chain[s - 1], chain[s - 1...  4.08 us
    pallas_call x1, Pallas kernels, body(): call(functools.partial(start_kernel, nodes, rank, leaf, local_bits), [jax...  2.57 us
    unnamed x12, local copies, waits for them, and re-layouts  1.98 us
    pallas_call x1, Pallas kernels, body(): call(functools.partial(end_kernel, nodes, rank, leaf, local_bits), shape(...  1.95 us
  transfers between devices with their start and end apart: 41, of which 13 were waited for; matrix products, arithmetic and copies ran while one was open for 0% of the time, Pallas kernels for 20%

profile of v7, /device:TPU:0, one launch (start us, length us, event | category | flops | bytes accessed | tf_op | source)
XLA Modules:
  0.0 93.5 jit_solution(2109082244664200085)
XLA Ops:
  0.0 0.5 collective-permute-start.3
  0.5 1.5 %copy-done = f32[7,4,128,256]{3,2,1,0:T(8,128)S(1)} copy-done((f32[7,4,128,256]{3,2,1,0:T(8,128)S(1)}, f32[7,4,128,256]{3,2,1,0:T(8,128)}, u32[]{:S(2)}) %copy-start) | copy-done | bytes 3670040
  2.1 0.4 copy-done.3
  2.5 2.6 %shard_map.65 = (f32[4,128,256]{2,1,0:T(8,128)S(1)}, f32[264,128]{1,0:T(8,128)S(1)}, f32[264,128]{1,0:T(8,128)S(1)}) custom-call(f32[1024,256]{1,0:T(8,128)S(1)} %copy-done.3, f32[4,128,256]{2,1,0:T(8,128)S(1)} %copy-done.2, f32[7,4,128,256]{3,2,1,0:T(8,128)S(1)} %copy-done, f32[4,256]{1,0:T(4,128)S(1)} %copy-done.4, f32[8,128]{1,0:T(8,128)S(1)} %shard_map.64.lead), custom_call_target="tpu_custom_call" | custom-call | flops 536870912 | bytes 8 | tf_op jit(solution)/shard_map/pallas_call | solution.py:266
  5.1 0.5 collective-permute-start.1
  5.6 0.3 shard_map.66
  6.0 0.7 collective-permute-done.1.got
  6.8 3.0 %collective-permute-start.2 = (f32[272,128]{1,0:T(8,128)S(1)}, f32[272,128]{1,0:T(8,128)S(1)}, u32[]{:S(2)}, u32[]{:S(2)}) collective-permute-start(f32[272,128]{1,0:T(8,128)S(1)} %shard_map.67.token.own), channel_id=1, source_target_pairs={{0,1},{1,0},{2,3},{3,2},{4,5},{5,4},{6,7},{7,6},{8,9},{9,8},{10,11... | collective-permute-start | bytes 417800 | tf_op jit(solution)/shard_map/ppermute | solution.py:19
  9.9 1.1 %collective-permute-done.other_index = s32[4]{0:T(128)S(1)} collective-permute-done((s32[4]{0:T(128)S(1)}, s32[4]{0:T(128)S(1)}, u32[]{:S(2)}, u32[]{:S(2)}) %collective-permute-start) | collective-permute-done | bytes 48 | tf_op jit(solution)/shard_map/ppermute | solution.py:19
  11.0 0.6 shard_map.69.token.hot
  11.7 2.5 %collective-permute-done.2.got = f32[272,128]{1,0:T(8,128)S(1)} collective-permute-done((f32[272,128]{1,0:T(8,128)S(1)}, f32[272,128]{1,0:T(8,128)S(1)}, u32[]{:S(2)}, u32[]{:S(2)}) %collective-permute-start.2) | collective-permute-done | bytes 139296 | tf_op jit(solution)/shard_map/ppermute | solution.py:19
  14.5 2.2 %collective-permute-start.4 = (f32[288,128]{1,0:T(8,128)S(1)}, f32[288,128]{1,0:T(8,128)S(1)}, u32[]{:S(2)}, u32[]{:S(2)}) collective-permute-start(f32[288,128]{1,0:T(8,128)S(1)} %shard_map.70.token.own), channel_id=1, source_target_pairs={{0,2},{1,3},{2,0},{3,1},{4,6},{5,7},{6,4},{7,5},{8,10},{9,11},{10,... | collective-permute-start | bytes 442376 | tf_op jit(solution)/shard_map/ppermute | solution.py:19
  16.7 1.6 %collective-permute-start.10 = (f32[256,128]{1,0:T(8,128)S(1)}, f32[256,128]{1,0:T(8,128)S(1)}, u32[]{:S(2)}, u32[]{:S(2)}) collective-permute-start(f32[256,128]{1,0:T(8,128)S(1)} %shard_map.71.token.own), channel_id=1, source_target_pairs={{0,1},{1,0},{2,3},{3,2},{4,5},{5,4},{6,7},{7,6},{8,9},{9,8},{10,11... | collective-permute-start | bytes 393224 | tf_op jit(solution)/shard_map/ppermute | solution.py:19
  18.5 0.5 collective-permute-start.9
  19.1 1.4 %collective-permute-start.8 = (f32[256,128]{1,0:T(8,128)S(1)}, f32[256,128]{1,0:T(8,128)S(1)}, u32[]{:S(2)}, u32[]{:S(2)}) collective-permute-start(f32[256,128]{1,0:T(8,128)S(1)} %shard_map.73.token.own), channel_id=1, source_target_pairs={{0,1},{1,0},{2,3},{3,2},{4,5},{5,4},{6,7},{7,6},{8,9},{9,8},{10,11... | collective-permute-start | bytes 393224 | tf_op jit(solution)/shard_map/ppermute | solution.py:19
  20.8 3.5 %collective-permute-start.7 = (f32[320,128]{1,0:T(8,128)S(1)}, f32[320,128]{1,0:T(8,128)S(1)}, u32[]{:S(2)}, u32[]{:S(2)}) collective-permute-start(f32[320,128]{1,0:T(8,128)S(1)} %shard_map.74.token.own), channel_id=1, source_target_pairs={{0,4},{1,5},{2,6},{3,7},{4,0},{5,1},{6,2},{7,3},{8,12},{9,13},{10,... | collective-permute-start | bytes 491528 | tf_op jit(solution)/shard_map/ppermute | solution.py:19
  24.5 1.7 %collective-permute-start.15 = (f32[256,128]{1,0:T(8,128)S(1)}, f32[256,128]{1,0:T(8,128)S(1)}, u32[]{:S(2)}, u32[]{:S(2)}) collective-permute-start(f32[256,128]{1,0:T(8,128)S(1)} %shard_map.75.token.own), channel_id=1, source_target_pairs={{0,2},{1,3},{2,0},{3,1},{4,6},{5,7},{6,4},{7,5},{8,10},{9,11},{10,... | collective-permute-start | bytes 393224 | tf_op jit(solution)/shard_map/ppermute | solution.py:19
  26.5 0.6 collective-permute-start.14
  27.4 1.3 %collective-permute-start.13 = (f32[256,128]{1,0:T(8,128)S(1)}, f32[256,128]{1,0:T(8,128)S(1)}, u32[]{:S(2)}, u32[]{:S(2)}) collective-permute-start(f32[256,128]{1,0:T(8,128)S(1)} %shard_map.77.token.own), channel_id=1, source_target_pairs={{0,2},{1,3},{2,0},{3,1},{4,6},{5,7},{6,4},{7,5},{8,10},{9,11},{10,... | collective-permute-start | bytes 393224 | tf_op jit(solution)/shard_map/ppermute | solution.py:19
  28.7 5.3 %collective-permute-done.7.got = f32[320,128]{1,0:T(8,128)S(1)} collective-permute-done((f32[320,128]{1,0:T(8,128)S(1)}, f32[320,128]{1,0:T(8,128)S(1)}, u32[]{:S(2)}, u32[]{:S(2)}) %collective-permute-start.7) | collective-permute-done | bytes 163872 | tf_op jit(solution)/shard_map/ppermute | solution.py:19
  34.0 0.5 shard_map.78.token.own.tab_own
  34.5 2.0 %collective-permute-start.11 = (f32[384,128]{1,0:T(8,128)S(1)}, f32[384,128]{1,0:T(8,128)S(1)}, u32[]{:S(2)}, u32[]{:S(2)}) collective-permute-start(f32[384,128]{1,0:T(8,128)S(1)} %shard_map.78.token.own.tab_own), channel_id=1, source_target_pairs={{0,16},{8,24},{16,0},{24,8},{1,17},{9,25},{17,1},{25,9},{2,18},{10... | collective-permute-start | bytes 589832 | tf_op jit(solution)/shard_map/ppermute | solution.py:19
  36.8 0.9 collective-permute-done.14.got
  37.7 0.5 shard_map.80.token.own
  38.2 3.4 %collective-permute-start.18 = (f32[256,128]{1,0:T(8,128)S(1)}, f32[256,128]{1,0:T(8,128)S(1)}, u32[]{:S(2)}, u32[]{:S(2)}) collective-permute-start(f32[256,128]{1,0:T(8,128)S(1)} %shard_map.80.token.own), channel_id=1, source_target_pairs={{0,16},{8,24},{16,0},{24,8},{1,17},{9,25},{17,1},{25,9},{2,18},{10... | collective-permute-start | bytes 393224 | tf_op jit(solution)/shard_map/ppermute | solution.py:19
  42.0 1.2 %shard_map.82 = (f32[256,128]{1,0:T(8,128)S(1)}, f32[256,128]{1,0:T(8,128)S(1)}) custom-call(f32[16,256]{1,0:T(8,128)S(1)} %shard_map.69.token.hot, f32[384,128]{1,0:T(8,128)S(1)} %shard_map.78.token.own.tab_own, f32[384,128]{1,0:T(8,128)S(1)} %collective-permute-done.11.got.tab_got, f32[384,128]{1,0:T(8,128)S(1)} %shard_map.78.token.own.tab_own, ...), custom_call_target="tpu_custom_call" | custom-call | flops 67108864 | bytes 1 | tf_op jit(solution)/shard_map/pallas_call | solution.py:325
  43.2 0.7 collective-permute-start.16
  43.9 2.4 %collective-permute-done.19.got = f32[256,128]{1,0:T(8,128)S(1)} collective-permute-done((f32[256,128]{1,0:T(8,128)S(1)}, f32[256,128]{1,0:T(8,128)S(1)}, u32[]{:S(2)}, u32[]{:S(2)}) %collective-permute-start.19) | collective-permute-done | bytes 131104 | tf_op jit(solution)/shard_map/ppermute | solution.py:19
  46.2 0.5 shard_map.83.token.own
  46.8 0.5 collective-permute-start.23
  47.3 1.2 %shard_map.84 = (f32[256,128]{1,0:T(8,128)S(1)}, f32[256,128]{1,0:T(8,128)S(1)}) custom-call(f32[16,256]{1,0:T(8,128)S(1)} %shard_map.69.token.hot, f32[256,128]{1,0:T(8,128)S(1)} %shard_map.80.token.own, f32[256,128]{1,0:T(8,128)S(1)} %collective-permute-done.18.got, f32[384,128]{1,0:T(8,128)S(1)} %shard_map.78.token.own.tab_own, ...), custom_call_target="tpu_custom_call" | custom-call | flops 67108864 | bytes 1 | tf_op jit(solution)/shard_map/pallas_call | solution.py:325
  48.4 1.6 %collective-permute-start.22 = (f32[256,128]{1,0:T(8,128)S(1)}, f32[256,128]{1,0:T(8,128)S(1)}, u32[]{:S(2)}, u32[]{:S(2)}) collective-permute-start(f32[256,128]{1,0:T(8,128)S(1)} %get-tuple-element.68), channel_id=1, source_target_pairs={{0,16},{8,24},{16,0},{24,8},{1,17},{9,25},{17,1},{25,9},{2,18},{10... | collective-permute-start | bytes 393224 | tf_op jit(solution)/shard_map/ppermute | solution.py:19
  50.1 0.5 shard_map.85.token.own
  50.6 0.5 collective-permute-start.21
  51.1 0.7 shard_map.86
  51.8 1.5 %collective-permute-start.20 = (f32[256,128]{1,0:T(8,128)S(1)}, f32[256,128]{1,0:T(8,128)S(1)}, u32[]{:S(2)}, u32[]{:S(2)}) collective-permute-start(f32[256,128]{1,0:T(8,128)S(1)} %get-tuple-element.67), channel_id=1, source_target_pairs={{0,4},{1,5},{2,6},{3,7},{4,0},{5,1},{6,2},{7,3},{8,12},{9,13},{10,... | collective-permute-start | bytes 393224 | tf_op jit(solution)/shard_map/ppermute | solution.py:19
  53.4 1.2 %shard_map.87 = (f32[256,128]{1,0:T(8,128)S(1)}, f32[256,128]{1,0:T(8,128)S(1)}) custom-call(f32[16,256]{1,0:T(8,128)S(1)} %shard_map.69.token.hot, f32[256,128]{1,0:T(8,128)S(1)} %shard_map.83.token.own, f32[256,128]{1,0:T(8,128)S(1)} %collective-permute-done.23.got, f32[384,128]{1,0:T(8,128)S(1)} %shard_map.78.token.own.tab_own, ...), custom_call_target="tpu_custom_call" | custom-call | flops 67108864 | bytes 1 | tf_op jit(solution)/shard_map/pallas_call | solution.py:325
  54.7 1.1 %collective-permute-done.22.got = f32[256,128]{1,0:T(8,128)S(1)} collective-permute-done((f32[256,128]{1,0:T(8,128)S(1)}, f32[256,128]{1,0:T(8,128)S(1)}, u32[]{:S(2)}, u32[]{:S(2)}) %collective-permute-start.22) | collective-permute-done | bytes 131104 | tf_op jit(solution)/shard_map/ppermute | solution.py:19
  55.9 0.7 shard_map.88
  56.6 1.8 %collective-permute-start.26 = (f32[256,128]{1,0:T(8,128)S(1)}, f32[256,128]{1,0:T(8,128)S(1)}, u32[]{:S(2)}, u32[]{:S(2)}) collective-permute-start(f32[256,128]{1,0:T(8,128)S(1)} %get-tuple-element.75), channel_id=1, source_target_pairs={{0,4},{1,5},{2,6},{3,7},{4,0},{5,1},{6,2},{7,3},{8,12},{9,13},{10,... | collective-permute-start | bytes 393224 | tf_op jit(solution)/shard_map/ppermute | solution.py:19
  58.4 1.2 %shard_map.89 = (f32[256,128]{1,0:T(8,128)S(1)}, f32[256,128]{1,0:T(8,128)S(1)}) custom-call(f32[16,256]{1,0:T(8,128)S(1)} %shard_map.69.token.hot, f32[256,128]{1,0:T(8,128)S(1)} %shard_map.85.token.own, f32[256,128]{1,0:T(8,128)S(1)} %collective-permute-done.21.got, f32[384,128]{1,0:T(8,128)S(1)} %shard_map.78.token.own.tab_own, ...), custom_call_target="tpu_custom_call" | custom-call | flops 67108864 | bytes 1 | tf_op jit(solution)/shard_map/pallas_call | solution.py:325
  59.5 0.5 collective-permute-start.25
  60.1 0.3 shard_map.90
  60.4 4.9 %collective-permute-start.24 = (f32[256,128]{1,0:T(8,128)S(1)}, f32[256,128]{1,0:T(8,128)S(1)}, u32[]{:S(2)}, u32[]{:S(2)}) collective-permute-start(f32[256,128]{1,0:T(8,128)S(1)} %get-tuple-element.73), channel_id=1, source_target_pairs={{0,2},{1,3},{2,0},{3,1},{4,6},{5,7},{6,4},{7,5},{8,10},{9,11},{10,... | collective-permute-start | bytes 393224 | tf_op jit(solution)/shard_map/ppermute | solution.py:19
  65.3 0.7 shard_map.91
  66.0 0.6 collective-permute-start.31
  66.6 0.3 shard_map.92
  66.9 1.0 %collective-permute-start.30 = (f32[256,128]{1,0:T(8,128)S(1)}, f32[256,128]{1,0:T(8,128)S(1)}, u32[]{:S(2)}, u32[]{:S(2)}) collective-permute-start(f32[256,128]{1,0:T(8,128)S(1)} %get-tuple-element.83), channel_id=1, source_target_pairs={{0,2},{1,3},{2,0},{3,1},{4,6},{5,7},{6,4},{7,5},{8,10},{9,11},{10,... | collective-permute-start | bytes 393224 | tf_op jit(solution)/shard_map/ppermute | solution.py:19
  67.9 0.7 shard_map.93
  68.6 3.5 %collective-permute-start.29 = (f32[256,128]{1,0:T(8,128)S(1)}, f32[256,128]{1,0:T(8,128)S(1)}, u32[]{:S(2)}, u32[]{:S(2)}) collective-permute-start(f32[256,128]{1,0:T(8,128)S(1)} %get-tuple-element.82), channel_id=1, source_target_pairs={{0,4},{1,5},{2,6},{3,7},{4,0},{5,1},{6,2},{7,3},{8,12},{9,13},{10,... | collective-permute-start | bytes 393224 | tf_op jit(solution)/shard_map/ppermute | solution.py:19
  72.1 0.3 shard_map.94
  72.4 1.3 %collective-permute-start.28 = (f32[256,128]{1,0:T(8,128)S(1)}, f32[256,128]{1,0:T(8,128)S(1)}, u32[]{:S(2)}, u32[]{:S(2)}) collective-permute-start(f32[256,128]{1,0:T(8,128)S(1)} %get-tuple-element.81), channel_id=1, source_target_pairs={{0,1},{1,0},{2,3},{3,2},{4,5},{5,4},{6,7},{7,6},{8,9},{9,8},{10,11... | collective-permute-start | bytes 393224 | tf_op jit(solution)/shard_map/ppermute | solution.py:19
  73.8 0.5 shard_map.95
  74.3 1.3 %collective-permute-done.30.got = f32[256,128]{1,0:T(8,128)S(1)} collective-permute-done((f32[256,128]{1,0:T(8,128)S(1)}, f32[256,128]{1,0:T(8,128)S(1)}, u32[]{:S(2)}, u32[]{:S(2)}) %collective-permute-start.30) | collective-permute-done | bytes 131104 | tf_op jit(solution)/shard_map/ppermute | solution.py:19
  75.6 0.3 shard_map.96
  75.9 3.1 %collective-permute-start.34 = (f32[256,128]{1,0:T(8,128)S(1)}, f32[256,128]{1,0:T(8,128)S(1)}, u32[]{:S(2)}, u32[]{:S(2)}) collective-permute-start(f32[256,128]{1,0:T(8,128)S(1)} %get-tuple-element.91), channel_id=1, source_target_pairs={{0,1},{1,0},{2,3},{3,2},{4,5},{5,4},{6,7},{7,6},{8,9},{9,8},{10,11... | collective-permute-start | bytes 393224 | tf_op jit(solution)/shard_map/ppermute | solution.py:19
  79.0 0.3 shard_map.97
  79.6 0.3 shard_map.99
  79.9 2.2 %collective-permute-start.37 = (f32[256,128]{1,0:T(8,128)S(1)}, f32[256,128]{1,0:T(8,128)S(1)}, u32[]{:S(2)}, u32[]{:S(2)}) collective-permute-start(f32[256,128]{1,0:T(8,128)S(1)} %get-tuple-element.99), channel_id=1, source_target_pairs={{0,1},{1,0},{2,3},{3,2},{4,5},{5,4},{6,7},{7,6},{8,9},{9,8},{10,11... | collective-permute-start | bytes 393224 | tf_op jit(solution)/shard_map/ppermute | solution.py:19
  82.1 2.3 %collective-permute-done.33.got = f32[256,128]{1,0:T(8,128)S(1)} collective-permute-done((f32[256,128]{1,0:T(8,128)S(1)}, f32[256,128]{1,0:T(8,128)S(1)}, u32[]{:S(2)}, u32[]{:S(2)}) %collective-permute-start.33) | collective-permute-done | bytes 131104 | tf_op jit(solution)/shard_map/ppermute | solution.py:19
  85.1 0.7 collective-permute-done.37.got
  86.2 3.5 %collective-permute-done.39.got = f32[256,128]{1,0:T(8,128)S(1)} collective-permute-done((f32[256,128]{1,0:T(8,128)S(1)}, f32[256,128]{1,0:T(8,128)S(1)}, u32[]{:S(2)}, u32[]{:S(2)}) %collective-permute-start.39) | collective-permute-done | bytes 131104 | tf_op jit(solution)/shard_map/ppermute | solution.py:19
  90.1 1.0 %collective-permute-done.40.got = f32[256,128]{1,0:T(8,128)S(1)} collective-permute-done((f32[256,128]{1,0:T(8,128)S(1)}, f32[256,128]{1,0:T(8,128)S(1)}, u32[]{:S(2)}, u32[]{:S(2)}) %collective-permute-start.40) | collective-permute-done | bytes 131104 | tf_op jit(solution)/shard_map/ppermute | solution.py:19
  91.4 2.0 %shard_map.108 = f32[1024,256]{1,0:T(8,128)} custom-call(f32[4,128,256]{2,1,0:T(8,128)S(1)} %copy-done.2, f32[7,4,128,256]{3,2,1,0:T(8,128)S(1)} %copy-done, f32[128,256]{1,0:T(8,128)S(1)} %get-tuple-element.96.token.rest_0_, f32[128,256]{1,0:T(8,128)S(1)} %get-tuple-element.97.rest_1_, f32[128,256]{1,0:T(8,128)S(1)} %get-tuple-element.101.token.rest_2_, ...), custom_call_target="tpu_custom_call" | custom-call | flops 805306368 | bytes 12 | tf_op jit(solution)/shard_map/pallas_call | solution.py:340
  (75 shorter events, 5.1 us)
Async XLA Ops:
  0.0 2.0 %copy-start = (f32[7,4,128,256]{3,2,1,0:T(8,128)S(1)}, f32[7,4,128,256]{3,2,1,0:T(8,128)}, u32[]{:S(2)}) copy-start(f32[7,4,128,256]{3,2,1,0:T(8,128)} %factors.69) | copy-start | bytes 11010052
  0.0 2.1 %copy-start.2 = (f32[4,128,256]{2,1,0:T(8,128)S(1)}, f32[4,128,256]{2,1,0:T(8,128)}, u32[]{:S(2)}) copy-start(f32[4,128,256]{2,1,0:T(8,128)} %leaf_in.3) | copy-start | bytes 1572868
  0.0 2.1 %copy-start.4 = (f32[4,256]{1,0:T(4,128)S(1)}, f32[4,256]{1,0:T(4,128)}, u32[]{:S(2)}) copy-start(f32[4,256]{1,0:T(4,128)} %table.1) | copy-start | bytes 12292
  0.0 2.5 %copy-start.3 = (f32[1024,256]{1,0:T(8,128)S(1)}, f32[1024,256]{1,0:T(8,128)}, u32[]{:S(2)}) copy-start(f32[1024,256]{1,0:T(8,128)} %source.1) | copy-start | bytes 3145732
  0.0 14.2 %collective-permute-start.3 = (f32[7,4,128,256]{3,2,1,0:T(8,128)}, f32[7,4,128,256]{3,2,1,0:T(8,128)S(1)}, u32[]{:S(2)}, u32[]{:S(2)}) collective-permute-start(f32[7,4,128,256]{3,2,1,0:T(8,128)} %factors.69), channel_id=1, source_target_pairs={{0,8},{8,0},{16,24},{24,16},{1,9},{9,1},{17,25},{25,17},{2,10},{10... | collective-permute-start | bytes 11010056 | tf_op jit(solution)/shard_map/ppermute | solution.py:19
  5.1 4.8 %copy-start.5 = (s32[4]{0:T(128)S(1)}, s32[4]{0:T(128)}, u32[]{:S(2)}) copy-start(s32[4]{0:T(128)} %index.1) | copy-start | bytes 52
  5.1 1.7 %collective-permute-start.1 = (f32[264,128]{1,0:T(8,128)S(1)}, f32[264,128]{1,0:T(8,128)S(1)}, u32[]{:S(2)}, u32[]{:S(2)}) collective-permute-start(f32[264,128]{1,0:T(8,128)S(1)} %get-tuple-element.59), channel_id=1, source_target_pairs={{0,8},{8,0},{16,24},{24,16},{1,9},{9,1},{17,25},{25,17},{2,10},{10... | collective-permute-start | bytes 405512 | tf_op jit(solution)/shard_map/ppermute | solution.py:19
  5.9 10.7 %collective-permute-start.5 = (f32[256,128]{1,0:T(8,128)S(1)}, f32[256,128]{1,0:T(8,128)S(1)}, u32[]{:S(2)}, u32[]{:S(2)}) collective-permute-start(f32[256,128]{1,0:T(8,128)S(1)} %get-tuple-element.62), channel_id=1, source_target_pairs={{0,8},{8,0},{16,24},{24,16},{1,9},{9,1},{17,25},{25,17},{2,10},{10... | collective-permute-start | bytes 393224 | tf_op jit(solution)/shard_map/ppermute | solution.py:19
  6.8 7.4 %collective-permute-start.2 = (f32[272,128]{1,0:T(8,128)S(1)}, f32[272,128]{1,0:T(8,128)S(1)}, u32[]{:S(2)}, u32[]{:S(2)}) collective-permute-start(f32[272,128]{1,0:T(8,128)S(1)} %shard_map.67.token.own), channel_id=1, source_target_pairs={{0,1},{1,0},{2,3},{3,2},{4,5},{5,4},{6,7},{7,6},{8,9},{9,8},{10,11... | collective-permute-start | bytes 417800 | tf_op jit(solution)/shard_map/ppermute | solution.py:19
  9.7 8.5 %collective-permute-start.6 = (f32[256,128]{1,0:T(8,128)S(1)}, f32[256,128]{1,0:T(8,128)S(1)}, u32[]{:S(2)}, u32[]{:S(2)}) collective-permute-start(f32[256,128]{1,0:T(8,128)S(1)} %shard_map.68.token.own), channel_id=1, source_target_pairs={{0,1},{1,0},{2,3},{3,2},{4,5},{5,4},{6,7},{7,6},{8,9},{9,8},{10,11... | collective-permute-start | bytes 393224 | tf_op jit(solution)/shard_map/ppermute | solution.py:19
  9.8 1.2 %collective-permute-start = (s32[4]{0:T(128)S(1)}, s32[4]{0:T(128)S(1)}, u32[]{:S(2)}, u32[]{:S(2)}) collective-permute-start(s32[4]{0:T(128)S(1)} %copy-done.5), channel_id=1, source_target_pairs={{0,8},{8,0},{16,24},{24,16},{1,9},{9,1},{17,25},{25,17},{2,10},{10... | collective-permute-start | bytes 56 | tf_op jit(solution)/shard_map/ppermute | solution.py:19
  14.5 6.1 %collective-permute-start.4 = (f32[288,128]{1,0:T(8,128)S(1)}, f32[288,128]{1,0:T(8,128)S(1)}, u32[]{:S(2)}, u32[]{:S(2)}) collective-permute-start(f32[288,128]{1,0:T(8,128)S(1)} %shard_map.70.token.own), channel_id=1, source_target_pairs={{0,2},{1,3},{2,0},{3,1},{4,6},{5,7},{6,4},{7,5},{8,10},{9,11},{10,... | collective-permute-start | bytes 442376 | tf_op jit(solution)/shard_map/ppermute | solution.py:19
  16.7 3.8 %copy-start.1 = (f32[4,256,128]{2,1,0:T(8,128)S(1)}, f32[4,256,128]{2,1,0:T(8,128)}, u32[]{:S(2)}) copy-start(f32[4,256,128]{2,1,0:T(8,128)} %leaf_out.7) | copy-start | bytes 1572868
  16.7 7.6 %collective-permute-start.10 = (f32[256,128]{1,0:T(8,128)S(1)}, f32[256,128]{1,0:T(8,128)S(1)}, u32[]{:S(2)}, u32[]{:S(2)}) collective-permute-start(f32[256,128]{1,0:T(8,128)S(1)} %shard_map.71.token.own), channel_id=1, source_target_pairs={{0,1},{1,0},{2,3},{3,2},{4,5},{5,4},{6,7},{7,6},{8,9},{9,8},{10,11... | collective-permute-start | bytes 393224 | tf_op jit(solution)/shard_map/ppermute | solution.py:19
  18.5 7.7 %collective-permute-start.9 = (f32[256,128]{1,0:T(8,128)S(1)}, f32[256,128]{1,0:T(8,128)S(1)}, u32[]{:S(2)}, u32[]{:S(2)}) collective-permute-start(f32[256,128]{1,0:T(8,128)S(1)} %shard_map.72.token.own), channel_id=1, source_target_pairs={{0,2},{1,3},{2,0},{3,1},{4,6},{5,7},{6,4},{7,5},{8,10},{9,11},{10,... | collective-permute-start | bytes 393224 | tf_op jit(solution)/shard_map/ppermute | solution.py:19
  19.1 8.1 %collective-permute-start.8 = (f32[256,128]{1,0:T(8,128)S(1)}, f32[256,128]{1,0:T(8,128)S(1)}, u32[]{:S(2)}, u32[]{:S(2)}) collective-permute-start(f32[256,128]{1,0:T(8,128)S(1)} %shard_map.73.token.own), channel_id=1, source_target_pairs={{0,1},{1,0},{2,3},{3,2},{4,5},{5,4},{6,7},{7,6},{8,9},{9,8},{10,11... | collective-permute-start | bytes 393224 | tf_op jit(solution)/shard_map/ppermute | solution.py:19
  20.5 21.5 %collective-permute-start.12 = (f32[4,256,128]{2,1,0:T(8,128)S(1)}, f32[4,256,128]{2,1,0:T(8,128)S(1)}, u32[]{:S(2)}, u32[]{:S(2)}) collective-permute-start(f32[4,256,128]{2,1,0:T(8,128)S(1)} %copy-done.1), channel_id=1, source_target_pairs={{0,8},{8,0},{16,24},{24,16},{1,9},{9,1},{17,25},{25,17},{2,10},{10... | collective-permute-start | bytes 1572872 | tf_op jit(solution)/shard_map/ppermute | solution.py:19
  20.8 13.2 %collective-permute-start.7 = (f32[320,128]{1,0:T(8,128)S(1)}, f32[320,128]{1,0:T(8,128)S(1)}, u32[]{:S(2)}, u32[]{:S(2)}) collective-permute-start(f32[320,128]{1,0:T(8,128)S(1)} %shard_map.74.token.own), channel_id=1, source_target_pairs={{0,4},{1,5},{2,6},{3,7},{4,0},{5,1},{6,2},{7,3},{8,12},{9,13},{10,... | collective-permute-start | bytes 491528 | tf_op jit(solution)/shard_map/ppermute | solution.py:19
  24.5 11.9 %collective-permute-start.15 = (f32[256,128]{1,0:T(8,128)S(1)}, f32[256,128]{1,0:T(8,128)S(1)}, u32[]{:S(2)}, u32[]{:S(2)}) collective-permute-start(f32[256,128]{1,0:T(8,128)S(1)} %shard_map.75.token.own), channel_id=1, source_target_pairs={{0,2},{1,3},{2,0},{3,1},{4,6},{5,7},{6,4},{7,5},{8,10},{9,11},{10,... | collective-permute-start | bytes 393224 | tf_op jit(solution)/shard_map/ppermute | solution.py:19
  26.5 11.1 %collective-permute-start.14 = (f32[256,128]{1,0:T(8,128)S(1)}, f32[256,128]{1,0:T(8,128)S(1)}, u32[]{:S(2)}, u32[]{:S(2)}) collective-permute-start(f32[256,128]{1,0:T(8,128)S(1)} %shard_map.76.token.own), channel_id=1, source_target_pairs={{0,4},{1,5},{2,6},{3,7},{4,0},{5,1},{6,2},{7,3},{8,12},{9,13},{10,... | collective-permute-start | bytes 393224 | tf_op jit(solution)/shard_map/ppermute | solution.py:19
  27.4 14.2 %collective-permute-start.13 = (f32[256,128]{1,0:T(8,128)S(1)}, f32[256,128]{1,0:T(8,128)S(1)}, u32[]{:S(2)}, u32[]{:S(2)}) collective-permute-start(f32[256,128]{1,0:T(8,128)S(1)} %shard_map.77.token.own), channel_id=1, source_target_pairs={{0,2},{1,3},{2,0},{3,1},{4,6},{5,7},{6,4},{7,5},{8,10},{9,11},{10,... | collective-permute-start | bytes 393224 | tf_op jit(solution)/shard_map/ppermute | solution.py:19
  34.5 7.5 %collective-permute-start.11 = (f32[384,128]{1,0:T(8,128)S(1)}, f32[384,128]{1,0:T(8,128)S(1)}, u32[]{:S(2)}, u32[]{:S(2)}) collective-permute-start(f32[384,128]{1,0:T(8,128)S(1)} %shard_map.78.token.own.tab_own), channel_id=1, source_target_pairs={{0,16},{8,24},{16,0},{24,8},{1,17},{9,25},{17,1},{25,9},{2,18},{10... | collective-permute-start | bytes 589832 | tf_op jit(solution)/shard_map/ppermute | solution.py:19
  36.7 9.5 %collective-permute-start.19 = (f32[256,128]{1,0:T(8,128)S(1)}, f32[256,128]{1,0:T(8,128)S(1)}, u32[]{:S(2)}, u32[]{:S(2)}) collective-permute-start(f32[256,128]{1,0:T(8,128)S(1)} %shard_map.79.token.own), channel_id=1, source_target_pairs={{0,4},{1,5},{2,6},{3,7},{4,0},{5,1},{6,2},{7,3},{8,12},{9,13},{10,... | collective-permute-start | bytes 393224 | tf_op jit(solution)/shard_map/ppermute | solution.py:19
  38.2 9.1 %collective-permute-start.18 = (f32[256,128]{1,0:T(8,128)S(1)}, f32[256,128]{1,0:T(8,128)S(1)}, u32[]{:S(2)}, u32[]{:S(2)}) collective-permute-start(f32[256,128]{1,0:T(8,128)S(1)} %shard_map.80.token.own), channel_id=1, source_target_pairs={{0,16},{8,24},{16,0},{24,8},{1,17},{9,25},{17,1},{25,9},{2,18},{10... | collective-permute-start | bytes 393224 | tf_op jit(solution)/shard_map/ppermute | solution.py:19
  41.9 8.2 %collective-permute-start.17 = (f32[256,128]{1,0:T(8,128)S(1)}, f32[256,128]{1,0:T(8,128)S(1)}, u32[]{:S(2)}, u32[]{:S(2)}) collective-permute-start(f32[256,128]{1,0:T(8,128)S(1)} %shard_map.81.token.own), channel_id=1, source_target_pairs={{0,4},{1,5},{2,6},{3,7},{4,0},{5,1},{6,2},{7,3},{8,12},{9,13},{10,... | collective-permute-start | bytes 393224 | tf_op jit(solution)/shard_map/ppermute | solution.py:19
  43.2 7.9 %collective-permute-start.16 = (f32[256,128]{1,0:T(8,128)S(1)}, f32[256,128]{1,0:T(8,128)S(1)}, u32[]{:S(2)}, u32[]{:S(2)}) collective-permute-start(f32[256,128]{1,0:T(8,128)S(1)} %get-tuple-element.64), channel_id=1, source_target_pairs={{0,16},{8,24},{16,0},{24,8},{1,17},{9,25},{17,1},{25,9},{2,18},{10... | collective-permute-start | bytes 393224 | tf_op jit(solution)/shard_map/ppermute | solution.py:19
  46.8 6.6 %collective-permute-start.23 = (f32[256,128]{1,0:T(8,128)S(1)}, f32[256,128]{1,0:T(8,128)S(1)}, u32[]{:S(2)}, u32[]{:S(2)}) collective-permute-start(f32[256,128]{1,0:T(8,128)S(1)} %shard_map.83.token.own), channel_id=1, source_target_pairs={{0,16},{8,24},{16,0},{24,8},{1,17},{9,25},{17,1},{25,9},{2,18},{10... | collective-permute-start | bytes 393224 | tf_op jit(solution)/shard_map/ppermute | solution.py:19
  48.4 7.4 %collective-permute-start.22 = (f32[256,128]{1,0:T(8,128)S(1)}, f32[256,128]{1,0:T(8,128)S(1)}, u32[]{:S(2)}, u32[]{:S(2)}) collective-permute-start(f32[256,128]{1,0:T(8,128)S(1)} %get-tuple-element.68), channel_id=1, source_target_pairs={{0,16},{8,24},{16,0},{24,8},{1,17},{9,25},{17,1},{25,9},{2,18},{10... | collective-permute-start | bytes 393224 | tf_op jit(solution)/shard_map/ppermute | solution.py:19
  50.6 7.8 %collective-permute-start.21 = (f32[256,128]{1,0:T(8,128)S(1)}, f32[256,128]{1,0:T(8,128)S(1)}, u32[]{:S(2)}, u32[]{:S(2)}) collective-permute-start(f32[256,128]{1,0:T(8,128)S(1)} %shard_map.85.token.own), channel_id=1, source_target_pairs={{0,16},{8,24},{16,0},{24,8},{1,17},{9,25},{17,1},{25,9},{2,18},{10... | collective-permute-start | bytes 393224 | tf_op jit(solution)/shard_map/ppermute | solution.py:19
  51.8 8.2 %collective-permute-start.20 = (f32[256,128]{1,0:T(8,128)S(1)}, f32[256,128]{1,0:T(8,128)S(1)}, u32[]{:S(2)}, u32[]{:S(2)}) collective-permute-start(f32[256,128]{1,0:T(8,128)S(1)} %get-tuple-element.67), channel_id=1, source_target_pairs={{0,4},{1,5},{2,6},{3,7},{4,0},{5,1},{6,2},{7,3},{8,12},{9,13},{10,... | collective-permute-start | bytes 393224 | tf_op jit(solution)/shard_map/ppermute | solution.py:19
  54.5 10.8 %collective-permute-start.27 = (f32[256,128]{1,0:T(8,128)S(1)}, f32[256,128]{1,0:T(8,128)S(1)}, u32[]{:S(2)}, u32[]{:S(2)}) collective-permute-start(f32[256,128]{1,0:T(8,128)S(1)} %get-tuple-element.76), channel_id=1, source_target_pairs={{0,16},{8,24},{16,0},{24,8},{1,17},{9,25},{17,1},{25,9},{2,18},{10... | collective-permute-start | bytes 393224 | tf_op jit(solution)/shard_map/ppermute | solution.py:19
  56.6 10.1 %collective-permute-start.26 = (f32[256,128]{1,0:T(8,128)S(1)}, f32[256,128]{1,0:T(8,128)S(1)}, u32[]{:S(2)}, u32[]{:S(2)}) collective-permute-start(f32[256,128]{1,0:T(8,128)S(1)} %get-tuple-element.75), channel_id=1, source_target_pairs={{0,4},{1,5},{2,6},{3,7},{4,0},{5,1},{6,2},{7,3},{8,12},{9,13},{10,... | collective-permute-start | bytes 393224 | tf_op jit(solution)/shard_map/ppermute | solution.py:19
  59.5 8.4 %collective-permute-start.25 = (f32[256,128]{1,0:T(8,128)S(1)}, f32[256,128]{1,0:T(8,128)S(1)}, u32[]{:S(2)}, u32[]{:S(2)}) collective-permute-start(f32[256,128]{1,0:T(8,128)S(1)} %get-tuple-element.74), channel_id=1, source_target_pairs={{0,16},{8,24},{16,0},{24,8},{1,17},{9,25},{17,1},{25,9},{2,18},{10... | collective-permute-start | bytes 393224 | tf_op jit(solution)/shard_map/ppermute | solution.py:19
  60.4 11.8 %collective-permute-start.24 = (f32[256,128]{1,0:T(8,128)S(1)}, f32[256,128]{1,0:T(8,128)S(1)}, u32[]{:S(2)}, u32[]{:S(2)}) collective-permute-start(f32[256,128]{1,0:T(8,128)S(1)} %get-tuple-element.73), channel_id=1, source_target_pairs={{0,2},{1,3},{2,0},{3,1},{4,6},{5,7},{6,4},{7,5},{8,10},{9,11},{10,... | collective-permute-start | bytes 393224 | tf_op jit(solution)/shard_map/ppermute | solution.py:19
  66.0 7.8 %collective-permute-start.31 = (f32[256,128]{1,0:T(8,128)S(1)}, f32[256,128]{1,0:T(8,128)S(1)}, u32[]{:S(2)}, u32[]{:S(2)}) collective-permute-start(f32[256,128]{1,0:T(8,128)S(1)} %get-tuple-element.84), channel_id=1, source_target_pairs={{0,4},{1,5},{2,6},{3,7},{4,0},{5,1},{6,2},{7,3},{8,12},{9,13},{10,... | collective-permute-start | bytes 393224 | tf_op jit(solution)/shard_map/ppermute | solution.py:19
  66.9 8.7 %collective-permute-start.30 = (f32[256,128]{1,0:T(8,128)S(1)}, f32[256,128]{1,0:T(8,128)S(1)}, u32[]{:S(2)}, u32[]{:S(2)}) collective-permute-start(f32[256,128]{1,0:T(8,128)S(1)} %get-tuple-element.83), channel_id=1, source_target_pairs={{0,2},{1,3},{2,0},{3,1},{4,6},{5,7},{6,4},{7,5},{8,10},{9,11},{10,... | collective-permute-start | bytes 393224 | tf_op jit(solution)/shard_map/ppermute | solution.py:19
  68.6 10.4 %collective-permute-start.29 = (f32[256,128]{1,0:T(8,128)S(1)}, f32[256,128]{1,0:T(8,128)S(1)}, u32[]{:S(2)}, u32[]{:S(2)}) collective-permute-start(f32[256,128]{1,0:T(8,128)S(1)} %get-tuple-element.82), channel_id=1, source_target_pairs={{0,4},{1,5},{2,6},{3,7},{4,0},{5,1},{6,2},{7,3},{8,12},{9,13},{10,... | collective-permute-start | bytes 393224 | tf_op jit(solution)/shard_map/ppermute | solution.py:19
  72.4 7.0 %collective-permute-start.28 = (f32[256,128]{1,0:T(8,128)S(1)}, f32[256,128]{1,0:T(8,128)S(1)}, u32[]{:S(2)}, u32[]{:S(2)}) collective-permute-start(f32[256,128]{1,0:T(8,128)S(1)} %get-tuple-element.81), channel_id=1, source_target_pairs={{0,1},{1,0},{2,3},{3,2},{4,5},{5,4},{6,7},{7,6},{8,9},{9,8},{10,11... | collective-permute-start | bytes 393224 | tf_op jit(solution)/shard_map/ppermute | solution.py:19
  74.2 5.3 %collective-permute-start.35 = (f32[256,128]{1,0:T(8,128)S(1)}, f32[256,128]{1,0:T(8,128)S(1)}, u32[]{:S(2)}, u32[]{:S(2)}) collective-permute-start(f32[256,128]{1,0:T(8,128)S(1)} %get-tuple-element.92), channel_id=1, source_target_pairs={{0,2},{1,3},{2,0},{3,1},{4,6},{5,7},{6,4},{7,5},{8,10},{9,11},{10,... | collective-permute-start | bytes 393224 | tf_op jit(solution)/shard_map/ppermute | solution.py:19
  75.9 6.1 %collective-permute-start.34 = (f32[256,128]{1,0:T(8,128)S(1)}, f32[256,128]{1,0:T(8,128)S(1)}, u32[]{:S(2)}, u32[]{:S(2)}) collective-permute-start(f32[256,128]{1,0:T(8,128)S(1)} %get-tuple-element.91), channel_id=1, source_target_pairs={{0,1},{1,0},{2,3},{3,2},{4,5},{5,4},{6,7},{7,6},{8,9},{9,8},{10,11... | collective-permute-start | bytes 393224 | tf_op jit(solution)/shard_map/ppermute | solution.py:19
  79.3 5.0 %collective-permute-start.33 = (f32[256,128]{1,0:T(8,128)S(1)}, f32[256,128]{1,0:T(8,128)S(1)}, u32[]{:S(2)}, u32[]{:S(2)}) collective-permute-start(f32[256,128]{1,0:T(8,128)S(1)} %get-tuple-element.90), channel_id=1, source_target_pairs={{0,2},{1,3},{2,0},{3,1},{4,6},{5,7},{6,4},{7,5},{8,10},{9,11},{10,... | collective-permute-start | bytes 393224 | tf_op jit(solution)/shard_map/ppermute | solution.py:19
  79.5 5.4 %collective-permute-start.32 = (f32[256,128]{1,0:T(8,128)S(1)}, f32[256,128]{1,0:T(8,128)S(1)}, u32[]{:S(2)}, u32[]{:S(2)}) collective-permute-start(f32[256,128]{1,0:T(8,128)S(1)} %get-tuple-element.89), channel_id=1, source_target_pairs={{0,8},{8,0},{16,24},{24,16},{1,9},{9,1},{17,25},{25,17},{2,10},{10... | collective-permute-start | bytes 393224 | tf_op jit(solution)/shard_map/ppermute | solution.py:19
  79.9 6.0 %collective-permute-start.37 = (f32[256,128]{1,0:T(8,128)S(1)}, f32[256,128]{1,0:T(8,128)S(1)}, u32[]{:S(2)}, u32[]{:S(2)}) collective-permute-start(f32[256,128]{1,0:T(8,128)S(1)} %get-tuple-element.99), channel_id=1, source_target_pairs={{0,1},{1,0},{2,3},{3,2},{4,5},{5,4},{6,7},{7,6},{8,9},{9,8},{10,11... | collective-permute-start | bytes 393224 | tf_op jit(solution)/shard_map/ppermute | solution.py:19
  82.0 3.9 %collective-permute-start.36 = (f32[256,128]{1,0:T(8,128)S(1)}, f32[256,128]{1,0:T(8,128)S(1)}, u32[]{:S(2)}, u32[]{:S(2)}) collective-permute-start(f32[256,128]{1,0:T(8,128)S(1)} %get-tuple-element.98), channel_id=1, source_target_pairs={{0,8},{8,0},{16,24},{24,16},{1,9},{9,1},{17,25},{25,17},{2,10},{10... | collective-permute-start | bytes 393224 | tf_op jit(solution)/shard_map/ppermute | solution.py:19
  84.7 5.0 %collective-permute-start.39 = (f32[256,128]{1,0:T(8,128)S(1)}, f32[256,128]{1,0:T(8,128)S(1)}, u32[]{:S(2)}, u32[]{:S(2)}) collective-permute-start(f32[256,128]{1,0:T(8,128)S(1)} %get-tuple-element.104), channel_id=1, source_target_pairs={{0,1},{1,0},{2,3},{3,2},{4,5},{5,4},{6,7},{7,6},{8,9},{9,8},{10,11... | collective-permute-start | bytes 393224 | tf_op jit(solution)/shard_map/ppermute | solution.py:19
  85.8 4.0 %collective-permute-start.38 = (f32[256,128]{1,0:T(8,128)S(1)}, f32[256,128]{1,0:T(8,128)S(1)}, u32[]{:S(2)}, u32[]{:S(2)}) collective-permute-start(f32[256,128]{1,0:T(8,128)S(1)} %get-tuple-element.103), channel_id=1, source_target_pairs={{0,8},{8,0},{16,24},{24,16},{1,9},{9,1},{17,25},{25,17},{2,10},{10... | collective-permute-start | bytes 393224 | tf_op jit(solution)/shard_map/ppermute | solution.py:19
  89.7 1.4 %collective-permute-start.40 = (f32[256,128]{1,0:T(8,128)S(1)}, f32[256,128]{1,0:T(8,128)S(1)}, u32[]{:S(2)}, u32[]{:S(2)}) collective-permute-start(f32[256,128]{1,0:T(8,128)S(1)} %get-tuple-element.108), channel_id=1, source_target_pairs={{0,8},{8,0},{16,24},{24,16},{1,9},{9,1},{17,25},{25,17},{2,10},{10... | collective-permute-start | bytes 393224 | tf_op jit(solution)/shard_map/ppermute | solution.py:19

commit v8 on v7

--- a/solution.py
+++ b/solution.py
@@ -75,34 +75,20 @@
     return split(jnp.concatenate([a, b], axis=0))
 
 
-def start_kernel(nodes, rank, leaf, local_bits, source, leaf_in, factors, table, lead, mid, keep, send, x, a, f, sems):
-    levels = [pltpu.make_async_copy(factors.at[l], f.at[l], sems.at[2 * nodes + l]) for l in range(local_bits)]
-    xs = [pltpu.make_async_copy(source.at[pl.ds(j * leaf, leaf)], x.at[j], sems.at[j]) for j in range(nodes)]
-    ins = [pltpu.make_async_copy(leaf_in.at[j], a.at[j], sems.at[nodes + j]) for j in range(nodes)]
-    for j in range(nodes):
-        ins[j].start()
-        xs[j].start()
-    for copy in levels:
-        copy.start()
-    values = []
-    for j in range(nodes):
-        ins[j].wait()
-        xs[j].wait()
-        values.append(product(split(a[j]), split(x[j])))
+def start_kernel(nodes, rank, leaf, local_bits, source, leaf_in, factors, table, lead, mid, keep, send):
+    values = [product(split(leaf_in[j]), split(source[pl.ds(j * leaf, leaf), :])) for j in range(nodes)]
     for l in range(local_bits - 1):
-        levels[l].wait()
         parts = [split(v) for v in values]
         values = []
         for j in range(nodes):
             mine, other = parts[j], parts[j ^ 1 << l]
             both = tuple(jnp.concatenate([m, o], axis=0) for m, o in zip(mine, other))
-            values.append(product(split(f[l, j]), both))
+            values.append(product(split(factors[l, j]), both))
     for j in range(nodes):
         mid[j] = values[j]
-    levels[-1].wait()
     mine = leading()
     for j in range(nodes // 2):
-        value = product(split(f[local_bits - 1, j]), stacked(values[j], values[j ^ nodes // 2]))
+        value = product(split(factors[local_bits - 1, j]), stacked(values[j], values[j ^ nodes // 2]))
         rows = pl.ds(j * rank, rank)
         keep[rows, :], send[rows, :] = halves(mine, value)
     rows, half = table.shape[0], keep.shape[1]
@@ -206,15 +192,25 @@
     send[...] = both[rank:]
 
 
-def end_kernel(nodes, rank, leaf, local_bits, leaf_in, factors, *rest):
-    pairs, out, (y, sems) = rest[: 2 * nodes], rest[2 * nodes], rest[2 * nodes + 1 :]
-    values = [pairs[2 * j][...] + pairs[2 * (j ^ nodes // 2) + 1][...] for j in range(nodes)]
-    for l in reversed(range(local_bits - 1)):
-        both = [product_turned(split(factors[l, j]), split(values[j])) for j in range(nodes)]
-        values = [both[j][:rank] + both[j ^ 1 << l][rank:] for j in range(nodes)]
+def early_kernel(nodes, rank, factors, *rest):
+    pairs, token, outs = rest[:nodes], rest[nodes], rest[nodes + 1 :]
+    for k in range(nodes // 2):
+        value = pairs[2 * k][...] + pairs[2 * (k ^ nodes // 4) + 1][...]
+        outs[k][...] = product_turned(split(factors[0, 2 * k]), split(value))
+
+
+def end_kernel(nodes, rank, leaf, leaf_in, factors, *rest):
+    early, pairs, (out, y, sems) = rest[: nodes // 2], rest[nodes // 2 : -3], rest[-3:]
+    odd = []
+    for k in range(nodes // 2):
+        value = pairs[2 * k][...] + pairs[2 * (k ^ nodes // 4) + 1][...]
+        odd.append(product_turned(split(factors[0, 2 * k + 1]), split(value)))
     copies = []
     for j in range(nodes):
-        y[j] = product_turned(split(leaf_in[j]), split(values[j]))
+        mine, other = (early[j // 2], odd[j // 2]) if j % 2 == 0 else (odd[j // 2], early[j // 2])
+        value = mine[pl.ds(0, rank), :] if j % 2 == 0 else mine[:rank]
+        value = value + (other[rank:] if j % 2 == 0 else other[pl.ds(rank, rank), :])
+        y[j] = product_turned(split(leaf_in[j]), split(value))
         copies.append(pltpu.make_async_copy(y.at[j], out.at[pl.ds(j * leaf, leaf)], sems.at[j]))
         copies[-1].start()
     for copy in copies:
@@ -261,27 +257,22 @@
         return jax.ShapeDtypeStruct((rows, columns), f32)
 
     unit, size = UNIT, 1
+    first_levels = factors[:local_bits]
     lead = call(lead_kernel, shape(8), [], VMEM, 1 << 33, 1)()
     entry = nodes // 2 * rank
     mid, keep_a, send_a = call(
         functools.partial(start_kernel, nodes, rank, leaf, local_bits),
         [jax.ShapeDtypeStruct((nodes, rank, width), f32)] + [shape(entry + table_rows)] * 2,
-        [HBM, HBM, HBM, VMEM, VMEM],
+        [VMEM] * 5,
         [VMEM] * 3,
         2 * nodes * unit,
         2 * nodes * size,
-        [
-            pltpu.VMEM((nodes, leaf, width), f32),
-            pltpu.VMEM((nodes, rank, leaf), f32),
-            pltpu.VMEM((local_bits, nodes, rank, 2 * rank), f32),
-            pltpu.SemaphoreType.DMA((2 * nodes + local_bits,)),
-        ],
-    )(source, leaf_in, factors, weight_table, lead)
+    )(source, leaf_in, first_levels, weight_table, lead)
     got_a = along(core_level, send_a)
     keep_b, send_b = call(
         functools.partial(second_kernel, nodes, rank, local_bits - 1),
         [shape(entry)] * 2, [VMEM] * 3, [VMEM] * 2, unit, size,
-    )(mid, factors, keep_a)
+    )(mid, first_levels, keep_a)
     got_b = along(core_level, send_b)
     token = keep_b
     pairs = [None] * nodes
@@ -320,6 +311,12 @@
                 [shape(rank, width)] * 2, [VMEM] * 4, [VMEM] * 2, unit, size,
             )(*pairs[c], factors, token)
             pairs[c] = (token, send)
+            if c == nodes - 2:
+                early = call(
+                    functools.partial(early_kernel, nodes, rank),
+                    [shape(2 * rank, width)] * (nodes // 2), [VMEM] * (2 + nodes), [VMEM] * (nodes // 2), unit, size,
+                )(factors, *[v for pair in pairs[::2] for v in pair], token)
+                token = early[0]
         else:
             if s == steps:
                 token, send = call(
@@ -338,14 +335,14 @@
                 )(*pairs[c], token)
             pairs[c] = (token, along(level, send))
     return call(
-        functools.partial(end_kernel, nodes, rank, leaf, local_bits),
+        functools.partial(end_kernel, nodes, rank, leaf),
         shape(nodes * leaf, width),
-        [VMEM] * (2 + 2 * nodes),
+        [VMEM] * (2 + nodes // 2 + nodes),
         HBM,
         3 * nodes * unit,
         3 * nodes * size,
         [pltpu.VMEM((nodes, leaf, width), f32), pltpu.SemaphoreType.DMA((nodes,))],
-    )(leaf_in, factors, *[v for pair in pairs for v in pair])
+    )(leaf_in, factors, *early, *[v for pair in pairs[1::2] for v in pair])
 
 
 def solution(mesh):

time: 93.7 us -> 93.5 us (level)
  Pallas kernels: 20.8 us -> 19.3 us
    pallas_call x1, Pallas kernels: 2.57 us -> 0.98 us  [body(): call(functools.partial(start_kernel, nodes, rank, leaf, local_bits), [jax...]
    slice x0 -> x1, local copies, waits for them, and re-layouts: none -> 1.29 us  [body(): first_levels = factors[:local_bits]]
    pallas_call x1 -> x2, Pallas kernels: 1.95 us -> 2.14 us  [the longest x1 1.75 us: body(): call(functools.partial(end_kernel, nodes, rank, leaf), shape(nodes * leaf...]
  transfers between devices with their start and end apart: 41 -> 41, of which waited for: 13 -> 13; matrix products, arithmetic and copies ran while one was open for 0% -> 1% of each run, Pallas kernels for 20% -> 19%
where the time goes in v8:
time: 93.5 us; the launch traced here: 93.3 us
  starting transfers between devices  47.2 us (50%)
  waiting for transfers between devices  23.4 us (25%)
  Pallas kernels  19.3 us (21%)
  local copies, waits for them, and re-layouts  2.67 us (3%)
    ppermute x41, starting transfers between devices, exchange(): lax.ppermute(value, axis, [(i, i ^ 1 << bit) for i in range(lax.axis_size...  47.2 us
    ppermute x41, waiting for transfers between devices, exchange(): lax.ppermute(value, axis, [(i, i ^ 1 << bit) for i in range(lax.axis_size...  23.4 us
    pallas_call x12, Pallas kernels, body(): call(functools.partial(backward_kernel, c, rank, level, level + 1 == core...  5.3 us
    pallas_call x4, Pallas kernels, body(): call(functools.partial(middle_kernel, c, nodes, rank, level), [shape(2 *...  4.67 us
    pallas_call x12, Pallas kernels, body(): call(functools.partial(forward_kernel, c, rank, chain[s - 1], chain[s - 1...  4.07 us
  transfers between devices with their start and end apart: 41, of which 13 were waited for; matrix products, arithmetic and copies ran while one was open for 1% of the time, Pallas kernels for 19%

profile of v8, /device:TPU:0, one launch (start us, length us, event | category | flops | bytes accessed | tf_op | source)
XLA Modules:
  0.0 93.3 jit_solution(5269826466795877881)
XLA Ops:
  0.0 0.5 collective-permute-start.3
  0.5 1.3 %slice.3.factors = f32[2,4,128,256]{3,2,1,0:T(8,128)S(1)} slice(f32[7,4,128,256]{3,2,1,0:T(8,128)} %factors.67), slice={[0:2], [0:4], [0:128], [0:256]} | slice | bytes 2097152 | tf_op jit(solution)/shard_map/slice | solution.py:260
  1.8 1.0 %copy-done.2 = f32[4,128,256]{2,1,0:T(8,128)S(1)} copy-done((f32[4,128,256]{2,1,0:T(8,128)S(1)}, f32[4,128,256]{2,1,0:T(8,128)}, u32[]{:S(2)}) %copy-start.2) | copy-done | bytes 524312
  2.8 0.3 copy-done.3
  3.2 1.0 %shard_map.65 = (f32[4,128,256]{2,1,0:T(8,128)S(1)}, f32[264,128]{1,0:T(8,128)S(1)}, f32[264,128]{1,0:T(8,128)S(1)}) custom-call(f32[1024,256]{1,0:T(8,128)S(1)} %copy-done.3, f32[4,128,256]{2,1,0:T(8,128)S(1)} %copy-done.2, f32[2,4,128,256]{3,2,1,0:T(8,128)S(1)} %slice.3.factors, f32[4,256]{1,0:T(4,128)S(1)} %copy-done.4, f32[8,128]{1,0:T(8,128)S(1)} %shard_map.64.lead), custom_call_target="tpu_custom_call" | custom-call | flops 536870912 | bytes 8 | tf_op jit(solution)/shard_map/pallas_call | solution.py:263
  4.3 0.3 shard_map.66
  4.6 0.5 collective-permute-start.5
  5.1 1.6 %collective-permute-done.1.got = f32[264,128]{1,0:T(8,128)S(1)} collective-permute-done((f32[264,128]{1,0:T(8,128)S(1)}, f32[264,128]{1,0:T(8,128)S(1)}, u32[]{:S(2)}, u32[]{:S(2)}) %collective-permute-start.1) | collective-permute-done | bytes 135200 | tf_op jit(solution)/shard_map/ppermute | solution.py:19
  6.7 3.0 %collective-permute-start.2 = (f32[272,128]{1,0:T(8,128)S(1)}, f32[272,128]{1,0:T(8,128)S(1)}, u32[]{:S(2)}, u32[]{:S(2)}) collective-permute-start(f32[272,128]{1,0:T(8,128)S(1)} %shard_map.67.token.own), channel_id=1, source_target_pairs={{0,1},{1,0},{2,3},{3,2},{4,5},{5,4},{6,7},{7,6},{8,9},{9,8},{10,11... | collective-permute-start | bytes 417800 | tf_op jit(solution)/shard_map/ppermute | solution.py:19
  9.8 1.1 %collective-permute-done.other_index = s32[4]{0:T(128)S(1)} collective-permute-done((s32[4]{0:T(128)S(1)}, s32[4]{0:T(128)S(1)}, u32[]{:S(2)}, u32[]{:S(2)}) %collective-permute-start) | collective-permute-done | bytes 48 | tf_op jit(solution)/shard_map/ppermute | solution.py:19
  10.9 0.6 shard_map.69.token.hot
  11.6 2.5 %collective-permute-done.2.got = f32[272,128]{1,0:T(8,128)S(1)} collective-permute-done((f32[272,128]{1,0:T(8,128)S(1)}, f32[272,128]{1,0:T(8,128)S(1)}, u32[]{:S(2)}, u32[]{:S(2)}) %collective-permute-start.2) | collective-permute-done | bytes 139296 | tf_op jit(solution)/shard_map/ppermute | solution.py:19
  14.4 2.2 %collective-permute-start.4 = (f32[288,128]{1,0:T(8,128)S(1)}, f32[288,128]{1,0:T(8,128)S(1)}, u32[]{:S(2)}, u32[]{:S(2)}) collective-permute-start(f32[288,128]{1,0:T(8,128)S(1)} %shard_map.70.token.own), channel_id=1, source_target_pairs={{0,2},{1,3},{2,0},{3,1},{4,6},{5,7},{6,4},{7,5},{8,10},{9,11},{10,... | collective-permute-start | bytes 442376 | tf_op jit(solution)/shard_map/ppermute | solution.py:19
  16.6 1.6 %collective-permute-start.10 = (f32[256,128]{1,0:T(8,128)S(1)}, f32[256,128]{1,0:T(8,128)S(1)}, u32[]{:S(2)}, u32[]{:S(2)}) collective-permute-start(f32[256,128]{1,0:T(8,128)S(1)} %shard_map.71.token.own), channel_id=1, source_target_pairs={{0,1},{1,0},{2,3},{3,2},{4,5},{5,4},{6,7},{7,6},{8,9},{9,8},{10,11... | collective-permute-start | bytes 393224 | tf_op jit(solution)/shard_map/ppermute | solution.py:19
  18.4 0.5 collective-permute-start.9
  19.0 1.4 %collective-permute-start.8 = (f32[256,128]{1,0:T(8,128)S(1)}, f32[256,128]{1,0:T(8,128)S(1)}, u32[]{:S(2)}, u32[]{:S(2)}) collective-permute-start(f32[256,128]{1,0:T(8,128)S(1)} %shard_map.73.token.own), channel_id=1, source_target_pairs={{0,1},{1,0},{2,3},{3,2},{4,5},{5,4},{6,7},{7,6},{8,9},{9,8},{10,11... | collective-permute-start | bytes 393224 | tf_op jit(solution)/shard_map/ppermute | solution.py:19
  20.8 3.4 %collective-permute-start.7 = (f32[320,128]{1,0:T(8,128)S(1)}, f32[320,128]{1,0:T(8,128)S(1)}, u32[]{:S(2)}, u32[]{:S(2)}) collective-permute-start(f32[320,128]{1,0:T(8,128)S(1)} %shard_map.74.token.own), channel_id=1, source_target_pairs={{0,4},{1,5},{2,6},{3,7},{4,0},{5,1},{6,2},{7,3},{8,12},{9,13},{10,... | collective-permute-start | bytes 491528 | tf_op jit(solution)/shard_map/ppermute | solution.py:19
  24.5 1.8 %collective-permute-start.15 = (f32[256,128]{1,0:T(8,128)S(1)}, f32[256,128]{1,0:T(8,128)S(1)}, u32[]{:S(2)}, u32[]{:S(2)}) collective-permute-start(f32[256,128]{1,0:T(8,128)S(1)} %shard_map.75.token.own), channel_id=1, source_target_pairs={{0,2},{1,3},{2,0},{3,1},{4,6},{5,7},{6,4},{7,5},{8,10},{9,11},{10,... | collective-permute-start | bytes 393224 | tf_op jit(solution)/shard_map/ppermute | solution.py:19
  26.6 0.5 collective-permute-start.14
  27.3 1.3 %collective-permute-start.13 = (f32[256,128]{1,0:T(8,128)S(1)}, f32[256,128]{1,0:T(8,128)S(1)}, u32[]{:S(2)}, u32[]{:S(2)}) collective-permute-start(f32[256,128]{1,0:T(8,128)S(1)} %shard_map.77.token.own), channel_id=1, source_target_pairs={{0,2},{1,3},{2,0},{3,1},{4,6},{5,7},{6,4},{7,5},{8,10},{9,11},{10,... | collective-permute-start | bytes 393224 | tf_op jit(solution)/shard_map/ppermute | solution.py:19
  28.6 5.2 %collective-permute-done.7.got = f32[320,128]{1,0:T(8,128)S(1)} collective-permute-done((f32[320,128]{1,0:T(8,128)S(1)}, f32[320,128]{1,0:T(8,128)S(1)}, u32[]{:S(2)}, u32[]{:S(2)}) %collective-permute-start.7) | collective-permute-done | bytes 163872 | tf_op jit(solution)/shard_map/ppermute | solution.py:19
  33.8 0.5 shard_map.78.token.own.tab_own
  34.3 2.0 %collective-permute-start.11 = (f32[384,128]{1,0:T(8,128)S(1)}, f32[384,128]{1,0:T(8,128)S(1)}, u32[]{:S(2)}, u32[]{:S(2)}) collective-permute-start(f32[384,128]{1,0:T(8,128)S(1)} %shard_map.78.token.own.tab_own), channel_id=1, source_target_pairs={{0,16},{8,24},{16,0},{24,8},{1,17},{9,25},{17,1},{25,9},{2,18},{10... | collective-permute-start | bytes 589832 | tf_op jit(solution)/shard_map/ppermute | solution.py:19
  36.7 1.0 %collective-permute-done.14.got = f32[256,128]{1,0:T(8,128)S(1)} collective-permute-done((f32[256,128]{1,0:T(8,128)S(1)}, f32[256,128]{1,0:T(8,128)S(1)}, u32[]{:S(2)}, u32[]{:S(2)}) %collective-permute-start.14) | collective-permute-done | bytes 131104 | tf_op jit(solution)/shard_map/ppermute | solution.py:19
  37.7 0.5 shard_map.80.token.own
  38.2 3.3 %collective-permute-start.18 = (f32[256,128]{1,0:T(8,128)S(1)}, f32[256,128]{1,0:T(8,128)S(1)}, u32[]{:S(2)}, u32[]{:S(2)}) collective-permute-start(f32[256,128]{1,0:T(8,128)S(1)} %shard_map.80.token.own), channel_id=1, source_target_pairs={{0,16},{8,24},{16,0},{24,8},{1,17},{9,25},{17,1},{25,9},{2,18},{10... | collective-permute-start | bytes 393224 | tf_op jit(solution)/shard_map/ppermute | solution.py:19
  41.9 1.2 %shard_map.82 = (f32[256,128]{1,0:T(8,128)S(1)}, f32[256,128]{1,0:T(8,128)S(1)}) custom-call(f32[16,256]{1,0:T(8,128)S(1)} %shard_map.69.token.hot, f32[384,128]{1,0:T(8,128)S(1)} %shard_map.78.token.own.tab_own, f32[384,128]{1,0:T(8,128)S(1)} %collective-permute-done.11.got.tab_got, f32[384,128]{1,0:T(8,128)S(1)} %shard_map.78.token.own.tab_own, ...), custom_call_target="tpu_custom_call" | custom-call | flops 67108864 | bytes 1 | tf_op jit(solution)/shard_map/pallas_call | solution.py:322
  43.0 0.7 collective-permute-start.16
  43.8 2.3 %collective-permute-done.19.got = f32[256,128]{1,0:T(8,128)S(1)} collective-permute-done((f32[256,128]{1,0:T(8,128)S(1)}, f32[256,128]{1,0:T(8,128)S(1)}, u32[]{:S(2)}, u32[]{:S(2)}) %collective-permute-start.19) | collective-permute-done | bytes 131104 | tf_op jit(solution)/shard_map/ppermute | solution.py:19
  46.1 0.5 shard_map.83.token.own
  46.6 0.6 collective-permute-start.23
  47.2 1.2 %shard_map.84 = (f32[256,128]{1,0:T(8,128)S(1)}, f32[256,128]{1,0:T(8,128)S(1)}) custom-call(f32[16,256]{1,0:T(8,128)S(1)} %shard_map.69.token.hot, f32[256,128]{1,0:T(8,128)S(1)} %shard_map.80.token.own, f32[256,128]{1,0:T(8,128)S(1)} %collective-permute-done.18.got, f32[384,128]{1,0:T(8,128)S(1)} %shard_map.78.token.own.tab_own, ...), custom_call_target="tpu_custom_call" | custom-call | flops 67108864 | bytes 1 | tf_op jit(solution)/shard_map/pallas_call | solution.py:322
  48.4 1.6 %collective-permute-start.22 = (f32[256,128]{1,0:T(8,128)S(1)}, f32[256,128]{1,0:T(8,128)S(1)}, u32[]{:S(2)}, u32[]{:S(2)}) collective-permute-start(f32[256,128]{1,0:T(8,128)S(1)} %get-tuple-element.70), channel_id=1, source_target_pairs={{0,16},{8,24},{16,0},{24,8},{1,17},{9,25},{17,1},{25,9},{2,18},{10... | collective-permute-start | bytes 393224 | tf_op jit(solution)/shard_map/ppermute | solution.py:19
  50.0 0.5 shard_map.85.token.own
  50.5 0.6 collective-permute-start.21
  51.0 0.7 shard_map.86
  51.7 1.5 %collective-permute-start.20 = (f32[256,128]{1,0:T(8,128)S(1)}, f32[256,128]{1,0:T(8,128)S(1)}, u32[]{:S(2)}, u32[]{:S(2)}) collective-permute-start(f32[256,128]{1,0:T(8,128)S(1)} %get-tuple-element.69), channel_id=1, source_target_pairs={{0,4},{1,5},{2,6},{3,7},{4,0},{5,1},{6,2},{7,3},{8,12},{9,13},{10,... | collective-permute-start | bytes 393224 | tf_op jit(solution)/shard_map/ppermute | solution.py:19
  53.2 1.2 %shard_map.87 = (f32[256,128]{1,0:T(8,128)S(1)}, f32[256,128]{1,0:T(8,128)S(1)}) custom-call(f32[16,256]{1,0:T(8,128)S(1)} %shard_map.69.token.hot, f32[256,128]{1,0:T(8,128)S(1)} %shard_map.83.token.own, f32[256,128]{1,0:T(8,128)S(1)} %collective-permute-done.23.got, f32[384,128]{1,0:T(8,128)S(1)} %shard_map.78.token.own.tab_own, ...), custom_call_target="tpu_custom_call" | custom-call | flops 67108864 | bytes 1 | tf_op jit(solution)/shard_map/pallas_call | solution.py:322
  54.6 1.1 %collective-permute-done.22.got = f32[256,128]{1,0:T(8,128)S(1)} collective-permute-done((f32[256,128]{1,0:T(8,128)S(1)}, f32[256,128]{1,0:T(8,128)S(1)}, u32[]{:S(2)}, u32[]{:S(2)}) %collective-permute-start.22) | collective-permute-done | bytes 131104 | tf_op jit(solution)/shard_map/ppermute | solution.py:19
  55.7 0.7 shard_map.88
  56.4 1.9 %collective-permute-start.26 = (f32[256,128]{1,0:T(8,128)S(1)}, f32[256,128]{1,0:T(8,128)S(1)}, u32[]{:S(2)}, u32[]{:S(2)}) collective-permute-start(f32[256,128]{1,0:T(8,128)S(1)} %get-tuple-element.77), channel_id=1, source_target_pairs={{0,4},{1,5},{2,6},{3,7},{4,0},{5,1},{6,2},{7,3},{8,12},{9,13},{10,... | collective-permute-start | bytes 393224 | tf_op jit(solution)/shard_map/ppermute | solution.py:19
  58.3 1.2 %shard_map.89 = (f32[256,128]{1,0:T(8,128)S(1)}, f32[256,128]{1,0:T(8,128)S(1)}) custom-call(f32[16,256]{1,0:T(8,128)S(1)} %shard_map.69.token.hot, f32[256,128]{1,0:T(8,128)S(1)} %shard_map.85.token.own, f32[256,128]{1,0:T(8,128)S(1)} %collective-permute-done.21.got, f32[384,128]{1,0:T(8,128)S(1)} %shard_map.78.token.own.tab_own, ...), custom_call_target="tpu_custom_call" | custom-call | flops 67108864 | bytes 1 | tf_op jit(solution)/shard_map/pallas_call | solution.py:322
  59.4 0.6 collective-permute-start.25
  60.0 0.3 shard_map.90
  60.3 4.9 %collective-permute-start.24 = (f32[256,128]{1,0:T(8,128)S(1)}, f32[256,128]{1,0:T(8,128)S(1)}, u32[]{:S(2)}, u32[]{:S(2)}) collective-permute-start(f32[256,128]{1,0:T(8,128)S(1)} %get-tuple-element.75), channel_id=1, source_target_pairs={{0,2},{1,3},{2,0},{3,1},{4,6},{5,7},{6,4},{7,5},{8,10},{9,11},{10,... | collective-permute-start | bytes 393224 | tf_op jit(solution)/shard_map/ppermute | solution.py:19
  65.2 0.7 shard_map.91
  65.9 0.6 collective-permute-start.31
  66.5 0.3 shard_map.92
  66.8 1.0 %collective-permute-start.30 = (f32[256,128]{1,0:T(8,128)S(1)}, f32[256,128]{1,0:T(8,128)S(1)}, u32[]{:S(2)}, u32[]{:S(2)}) collective-permute-start(f32[256,128]{1,0:T(8,128)S(1)} %get-tuple-element.85), channel_id=1, source_target_pairs={{0,2},{1,3},{2,0},{3,1},{4,6},{5,7},{6,4},{7,5},{8,10},{9,11},{10,... | collective-permute-start | bytes 393224 | tf_op jit(solution)/shard_map/ppermute | solution.py:19
  67.8 0.7 shard_map.93
  68.5 3.5 %collective-permute-start.29 = (f32[256,128]{1,0:T(8,128)S(1)}, f32[256,128]{1,0:T(8,128)S(1)}, u32[]{:S(2)}, u32[]{:S(2)}) collective-permute-start(f32[256,128]{1,0:T(8,128)S(1)} %get-tuple-element.84), channel_id=1, source_target_pairs={{0,4},{1,5},{2,6},{3,7},{4,0},{5,1},{6,2},{7,3},{8,12},{9,13},{10,... | collective-permute-start | bytes 393224 | tf_op jit(solution)/shard_map/ppermute | solution.py:19
  72.0 0.3 shard_map.94
  72.3 1.4 %collective-permute-start.28 = (f32[256,128]{1,0:T(8,128)S(1)}, f32[256,128]{1,0:T(8,128)S(1)}, u32[]{:S(2)}, u32[]{:S(2)}) collective-permute-start(f32[256,128]{1,0:T(8,128)S(1)} %get-tuple-element.83), channel_id=1, source_target_pairs={{0,1},{1,0},{2,3},{3,2},{4,5},{5,4},{6,7},{7,6},{8,9},{9,8},{10,11... | collective-permute-start | bytes 393224 | tf_op jit(solution)/shard_map/ppermute | solution.py:19
  73.7 0.5 shard_map.95
  74.3 1.2 %collective-permute-done.30.got = f32[256,128]{1,0:T(8,128)S(1)} collective-permute-done((f32[256,128]{1,0:T(8,128)S(1)}, f32[256,128]{1,0:T(8,128)S(1)}, u32[]{:S(2)}, u32[]{:S(2)}) %collective-permute-start.30) | collective-permute-done | bytes 131104 | tf_op jit(solution)/shard_map/ppermute | solution.py:19
  75.8 3.2 %collective-permute-start.34 = (f32[256,128]{1,0:T(8,128)S(1)}, f32[256,128]{1,0:T(8,128)S(1)}, u32[]{:S(2)}, u32[]{:S(2)}) collective-permute-start(f32[256,128]{1,0:T(8,128)S(1)} %get-tuple-element.93), channel_id=1, source_target_pairs={{0,1},{1,0},{2,3},{3,2},{4,5},{5,4},{6,7},{7,6},{8,9},{9,8},{10,11... | collective-permute-start | bytes 393224 | tf_op jit(solution)/shard_map/ppermute | solution.py:19
  79.5 0.3 shard_map.99
  79.8 2.2 %collective-permute-start.36 = (f32[256,128]{1,0:T(8,128)S(1)}, f32[256,128]{1,0:T(8,128)S(1)}, u32[]{:S(2)}, u32[]{:S(2)}) collective-permute-start(f32[256,128]{1,0:T(8,128)S(1)} %get-tuple-element.100), channel_id=1, source_target_pairs={{0,1},{1,0},{2,3},{3,2},{4,5},{5,4},{6,7},{7,6},{8,9},{9,8},{10,11... | collective-permute-start | bytes 393224 | tf_op jit(solution)/shard_map/ppermute | solution.py:19
  82.0 2.3 %collective-permute-done.33.got = f32[256,128]{1,0:T(8,128)S(1)} collective-permute-done((f32[256,128]{1,0:T(8,128)S(1)}, f32[256,128]{1,0:T(8,128)S(1)}, u32[]{:S(2)}, u32[]{:S(2)}) %collective-permute-start.33) | collective-permute-done | bytes 131104 | tf_op jit(solution)/shard_map/ppermute | solution.py:19
  85.0 0.7 collective-permute-done.36.got
  86.1 3.5 %collective-permute-done.38.got = f32[256,128]{1,0:T(8,128)S(1)} collective-permute-done((f32[256,128]{1,0:T(8,128)S(1)}, f32[256,128]{1,0:T(8,128)S(1)}, u32[]{:S(2)}, u32[]{:S(2)}) %collective-permute-start.38) | collective-permute-done | bytes 131104 | tf_op jit(solution)/shard_map/ppermute | solution.py:19
  90.0 0.4 shard_map.107
  90.4 0.6 collective-permute-done.40.got
  91.4 1.8 %shard_map.109 = f32[1024,256]{1,0:T(8,128)} custom-call(f32[4,128,256]{2,1,0:T(8,128)S(1)} %copy-done.2, f32[7,4,128,256]{3,2,1,0:T(8,128)S(1)} %copy-done, f32[256,256]{1,0:T(8,128)S(1)} %get-tuple-element.109.token.rest_0_, f32[256,256]{1,0:T(8,128)S(1)} %get-tuple-element.110.rest_1_, f32[128,256]{1,0:T(8,128)S(1)} %get-tuple-element.105.token.rest_2_, ...), custom_call_target="tpu_custom_call" | custom-call | flops 805306368 | bytes 12 | tf_op jit(solution)/shard_map/pallas_call | solution.py:337
  (77 shorter events, 5.6 us)
Async XLA Ops:
  0.0 14.1 %collective-permute-start.3 = (f32[7,4,128,256]{3,2,1,0:T(8,128)}, f32[7,4,128,256]{3,2,1,0:T(8,128)S(1)}, u32[]{:S(2)}, u32[]{:S(2)}) collective-permute-start(f32[7,4,128,256]{3,2,1,0:T(8,128)} %factors.67), channel_id=1, source_target_pairs={{0,8},{8,0},{16,24},{24,16},{1,9},{9,1},{17,25},{25,17},{2,10},{10... | collective-permute-start | bytes 11010056 | tf_op jit(solution)/shard_map/ppermute | solution.py:19
  1.8 1.0 %copy-start.2 = (f32[4,128,256]{2,1,0:T(8,128)S(1)}, f32[4,128,256]{2,1,0:T(8,128)}, u32[]{:S(2)}) copy-start(f32[4,128,256]{2,1,0:T(8,128)} %leaf_in.3) | copy-start | bytes 1572868
  1.8 1.4 %copy-start.3 = (f32[1024,256]{1,0:T(8,128)S(1)}, f32[1024,256]{1,0:T(8,128)}, u32[]{:S(2)}) copy-start(f32[1024,256]{1,0:T(8,128)} %source.1) | copy-start | bytes 3145732
  1.8 1.4 %copy-start.4 = (f32[4,256]{1,0:T(4,128)S(1)}, f32[4,256]{1,0:T(4,128)}, u32[]{:S(2)}) copy-start(f32[4,256]{1,0:T(4,128)} %table.1) | copy-start | bytes 12292
  3.2 6.6 %copy-start.5 = (s32[4]{0:T(128)S(1)}, s32[4]{0:T(128)}, u32[]{:S(2)}) copy-start(s32[4]{0:T(128)} %index.1) | copy-start | bytes 52
  3.2 11.0 %copy-start = (f32[7,4,128,256]{3,2,1,0:T(8,128)S(1)}, f32[7,4,128,256]{3,2,1,0:T(8,128)}, u32[]{:S(2)}) copy-start(f32[7,4,128,256]{3,2,1,0:T(8,128)} %factors.67) | copy-start | bytes 11010052
  4.1 2.5 %collective-permute-start.1 = (f32[264,128]{1,0:T(8,128)S(1)}, f32[264,128]{1,0:T(8,128)S(1)}, u32[]{:S(2)}, u32[]{:S(2)}) collective-permute-start(f32[264,128]{1,0:T(8,128)S(1)} %get-tuple-element.61), channel_id=1, source_target_pairs={{0,8},{8,0},{16,24},{24,16},{1,9},{9,1},{17,25},{25,17},{2,10},{10... | collective-permute-start | bytes 405512 | tf_op jit(solution)/shard_map/ppermute | solution.py:19
  4.6 12.0 %collective-permute-start.5 = (f32[256,128]{1,0:T(8,128)S(1)}, f32[256,128]{1,0:T(8,128)S(1)}, u32[]{:S(2)}, u32[]{:S(2)}) collective-permute-start(f32[256,128]{1,0:T(8,128)S(1)} %get-tuple-element.64), channel_id=1, source_target_pairs={{0,8},{8,0},{16,24},{24,16},{1,9},{9,1},{17,25},{25,17},{2,10},{10... | collective-permute-start | bytes 393224 | tf_op jit(solution)/shard_map/ppermute | solution.py:19
  6.7 7.4 %collective-permute-start.2 = (f32[272,128]{1,0:T(8,128)S(1)}, f32[272,128]{1,0:T(8,128)S(1)}, u32[]{:S(2)}, u32[]{:S(2)}) collective-permute-start(f32[272,128]{1,0:T(8,128)S(1)} %shard_map.67.token.own), channel_id=1, source_target_pairs={{0,1},{1,0},{2,3},{3,2},{4,5},{5,4},{6,7},{7,6},{8,9},{9,8},{10,11... | collective-permute-start | bytes 417800 | tf_op jit(solution)/shard_map/ppermute | solution.py:19
  9.7 8.5 %collective-permute-start.6 = (f32[256,128]{1,0:T(8,128)S(1)}, f32[256,128]{1,0:T(8,128)S(1)}, u32[]{:S(2)}, u32[]{:S(2)}) collective-permute-start(f32[256,128]{1,0:T(8,128)S(1)} %shard_map.68.token.own), channel_id=1, source_target_pairs={{0,1},{1,0},{2,3},{3,2},{4,5},{5,4},{6,7},{7,6},{8,9},{9,8},{10,11... | collective-permute-start | bytes 393224 | tf_op jit(solution)/shard_map/ppermute | solution.py:19
  9.8 1.2 %collective-permute-start = (s32[4]{0:T(128)S(1)}, s32[4]{0:T(128)S(1)}, u32[]{:S(2)}, u32[]{:S(2)}) collective-permute-start(s32[4]{0:T(128)S(1)} %copy-done.5), channel_id=1, source_target_pairs={{0,8},{8,0},{16,24},{24,16},{1,9},{9,1},{17,25},{25,17},{2,10},{10... | collective-permute-start | bytes 56 | tf_op jit(solution)/shard_map/ppermute | solution.py:19
  14.4 6.2 %collective-permute-start.4 = (f32[288,128]{1,0:T(8,128)S(1)}, f32[288,128]{1,0:T(8,128)S(1)}, u32[]{:S(2)}, u32[]{:S(2)}) collective-permute-start(f32[288,128]{1,0:T(8,128)S(1)} %shard_map.70.token.own), channel_id=1, source_target_pairs={{0,2},{1,3},{2,0},{3,1},{4,6},{5,7},{6,4},{7,5},{8,10},{9,11},{10,... | collective-permute-start | bytes 442376 | tf_op jit(solution)/shard_map/ppermute | solution.py:19
  16.6 3.8 %copy-start.1 = (f32[4,256,128]{2,1,0:T(8,128)S(1)}, f32[4,256,128]{2,1,0:T(8,128)}, u32[]{:S(2)}) copy-start(f32[4,256,128]{2,1,0:T(8,128)} %leaf_out.7) | copy-start | bytes 1572868
  16.6 7.6 %collective-permute-start.10 = (f32[256,128]{1,0:T(8,128)S(1)}, f32[256,128]{1,0:T(8,128)S(1)}, u32[]{:S(2)}, u32[]{:S(2)}) collective-permute-start(f32[256,128]{1,0:T(8,128)S(1)} %shard_map.71.token.own), channel_id=1, source_target_pairs={{0,1},{1,0},{2,3},{3,2},{4,5},{5,4},{6,7},{7,6},{8,9},{9,8},{10,11... | collective-permute-start | bytes 393224 | tf_op jit(solution)/shard_map/ppermute | solution.py:19
  18.4 7.8 %collective-permute-start.9 = (f32[256,128]{1,0:T(8,128)S(1)}, f32[256,128]{1,0:T(8,128)S(1)}, u32[]{:S(2)}, u32[]{:S(2)}) collective-permute-start(f32[256,128]{1,0:T(8,128)S(1)} %shard_map.72.token.own), channel_id=1, source_target_pairs={{0,2},{1,3},{2,0},{3,1},{4,6},{5,7},{6,4},{7,5},{8,10},{9,11},{10,... | collective-permute-start | bytes 393224 | tf_op jit(solution)/shard_map/ppermute | solution.py:19
  19.0 8.1 %collective-permute-start.8 = (f32[256,128]{1,0:T(8,128)S(1)}, f32[256,128]{1,0:T(8,128)S(1)}, u32[]{:S(2)}, u32[]{:S(2)}) collective-permute-start(f32[256,128]{1,0:T(8,128)S(1)} %shard_map.73.token.own), channel_id=1, source_target_pairs={{0,1},{1,0},{2,3},{3,2},{4,5},{5,4},{6,7},{7,6},{8,9},{9,8},{10,11... | collective-permute-start | bytes 393224 | tf_op jit(solution)/shard_map/ppermute | solution.py:19
  20.4 21.5 %collective-permute-start.12 = (f32[4,256,128]{2,1,0:T(8,128)S(1)}, f32[4,256,128]{2,1,0:T(8,128)S(1)}, u32[]{:S(2)}, u32[]{:S(2)}) collective-permute-start(f32[4,256,128]{2,1,0:T(8,128)S(1)} %copy-done.1), channel_id=1, source_target_pairs={{0,8},{8,0},{16,24},{24,16},{1,9},{9,1},{17,25},{25,17},{2,10},{10... | collective-permute-start | bytes 1572872 | tf_op jit(solution)/shard_map/ppermute | solution.py:19
  20.8 13.0 %collective-permute-start.7 = (f32[320,128]{1,0:T(8,128)S(1)}, f32[320,128]{1,0:T(8,128)S(1)}, u32[]{:S(2)}, u32[]{:S(2)}) collective-permute-start(f32[320,128]{1,0:T(8,128)S(1)} %shard_map.74.token.own), channel_id=1, source_target_pairs={{0,4},{1,5},{2,6},{3,7},{4,0},{5,1},{6,2},{7,3},{8,12},{9,13},{10,... | collective-permute-start | bytes 491528 | tf_op jit(solution)/shard_map/ppermute | solution.py:19
  24.5 11.9 %collective-permute-start.15 = (f32[256,128]{1,0:T(8,128)S(1)}, f32[256,128]{1,0:T(8,128)S(1)}, u32[]{:S(2)}, u32[]{:S(2)}) collective-permute-start(f32[256,128]{1,0:T(8,128)S(1)} %shard_map.75.token.own), channel_id=1, source_target_pairs={{0,2},{1,3},{2,0},{3,1},{4,6},{5,7},{6,4},{7,5},{8,10},{9,11},{10,... | collective-permute-start | bytes 393224 | tf_op jit(solution)/shard_map/ppermute | solution.py:19
  26.6 11.1 %collective-permute-start.14 = (f32[256,128]{1,0:T(8,128)S(1)}, f32[256,128]{1,0:T(8,128)S(1)}, u32[]{:S(2)}, u32[]{:S(2)}) collective-permute-start(f32[256,128]{1,0:T(8,128)S(1)} %shard_map.76.token.own), channel_id=1, source_target_pairs={{0,4},{1,5},{2,6},{3,7},{4,0},{5,1},{6,2},{7,3},{8,12},{9,13},{10,... | collective-permute-start | bytes 393224 | tf_op jit(solution)/shard_map/ppermute | solution.py:19
  27.3 14.2 %collective-permute-start.13 = (f32[256,128]{1,0:T(8,128)S(1)}, f32[256,128]{1,0:T(8,128)S(1)}, u32[]{:S(2)}, u32[]{:S(2)}) collective-permute-start(f32[256,128]{1,0:T(8,128)S(1)} %shard_map.77.token.own), channel_id=1, source_target_pairs={{0,2},{1,3},{2,0},{3,1},{4,6},{5,7},{6,4},{7,5},{8,10},{9,11},{10,... | collective-permute-start | bytes 393224 | tf_op jit(solution)/shard_map/ppermute | solution.py:19
  34.3 7.5 %collective-permute-start.11 = (f32[384,128]{1,0:T(8,128)S(1)}, f32[384,128]{1,0:T(8,128)S(1)}, u32[]{:S(2)}, u32[]{:S(2)}) collective-permute-start(f32[384,128]{1,0:T(8,128)S(1)} %shard_map.78.token.own.tab_own), channel_id=1, source_target_pairs={{0,16},{8,24},{16,0},{24,8},{1,17},{9,25},{17,1},{25,9},{2,18},{10... | collective-permute-start | bytes 589832 | tf_op jit(solution)/shard_map/ppermute | solution.py:19
  36.6 9.5 %collective-permute-start.19 = (f32[256,128]{1,0:T(8,128)S(1)}, f32[256,128]{1,0:T(8,128)S(1)}, u32[]{:S(2)}, u32[]{:S(2)}) collective-permute-start(f32[256,128]{1,0:T(8,128)S(1)} %shard_map.79.token.own), channel_id=1, source_target_pairs={{0,4},{1,5},{2,6},{3,7},{4,0},{5,1},{6,2},{7,3},{8,12},{9,13},{10,... | collective-permute-start | bytes 393224 | tf_op jit(solution)/shard_map/ppermute | solution.py:19
  38.2 9.0 %collective-permute-start.18 = (f32[256,128]{1,0:T(8,128)S(1)}, f32[256,128]{1,0:T(8,128)S(1)}, u32[]{:S(2)}, u32[]{:S(2)}) collective-permute-start(f32[256,128]{1,0:T(8,128)S(1)} %shard_map.80.token.own), channel_id=1, source_target_pairs={{0,16},{8,24},{16,0},{24,8},{1,17},{9,25},{17,1},{25,9},{2,18},{10... | collective-permute-start | bytes 393224 | tf_op jit(solution)/shard_map/ppermute | solution.py:19
  41.8 8.2 %collective-permute-start.17 = (f32[256,128]{1,0:T(8,128)S(1)}, f32[256,128]{1,0:T(8,128)S(1)}, u32[]{:S(2)}, u32[]{:S(2)}) collective-permute-start(f32[256,128]{1,0:T(8,128)S(1)} %shard_map.81.token.own), channel_id=1, source_target_pairs={{0,4},{1,5},{2,6},{3,7},{4,0},{5,1},{6,2},{7,3},{8,12},{9,13},{10,... | collective-permute-start | bytes 393224 | tf_op jit(solution)/shard_map/ppermute | solution.py:19
  43.0 8.0 %collective-permute-start.16 = (f32[256,128]{1,0:T(8,128)S(1)}, f32[256,128]{1,0:T(8,128)S(1)}, u32[]{:S(2)}, u32[]{:S(2)}) collective-permute-start(f32[256,128]{1,0:T(8,128)S(1)} %get-tuple-element.66), channel_id=1, source_target_pairs={{0,16},{8,24},{16,0},{24,8},{1,17},{9,25},{17,1},{25,9},{2,18},{10... | collective-permute-start | bytes 393224 | tf_op jit(solution)/shard_map/ppermute | solution.py:19
  46.6 6.6 %collective-permute-start.23 = (f32[256,128]{1,0:T(8,128)S(1)}, f32[256,128]{1,0:T(8,128)S(1)}, u32[]{:S(2)}, u32[]{:S(2)}) collective-permute-start(f32[256,128]{1,0:T(8,128)S(1)} %shard_map.83.token.own), channel_id=1, source_target_pairs={{0,16},{8,24},{16,0},{24,8},{1,17},{9,25},{17,1},{25,9},{2,18},{10... | collective-permute-start | bytes 393224 | tf_op jit(solution)/shard_map/ppermute | solution.py:19
  48.4 7.3 %collective-permute-start.22 = (f32[256,128]{1,0:T(8,128)S(1)}, f32[256,128]{1,0:T(8,128)S(1)}, u32[]{:S(2)}, u32[]{:S(2)}) collective-permute-start(f32[256,128]{1,0:T(8,128)S(1)} %get-tuple-element.70), channel_id=1, source_target_pairs={{0,16},{8,24},{16,0},{24,8},{1,17},{9,25},{17,1},{25,9},{2,18},{10... | collective-permute-start | bytes 393224 | tf_op jit(solution)/shard_map/ppermute | solution.py:19
  50.5 7.8 %collective-permute-start.21 = (f32[256,128]{1,0:T(8,128)S(1)}, f32[256,128]{1,0:T(8,128)S(1)}, u32[]{:S(2)}, u32[]{:S(2)}) collective-permute-start(f32[256,128]{1,0:T(8,128)S(1)} %shard_map.85.token.own), channel_id=1, source_target_pairs={{0,16},{8,24},{16,0},{24,8},{1,17},{9,25},{17,1},{25,9},{2,18},{10... | collective-permute-start | bytes 393224 | tf_op jit(solution)/shard_map/ppermute | solution.py:19
  51.7 8.2 %collective-permute-start.20 = (f32[256,128]{1,0:T(8,128)S(1)}, f32[256,128]{1,0:T(8,128)S(1)}, u32[]{:S(2)}, u32[]{:S(2)}) collective-permute-start(f32[256,128]{1,0:T(8,128)S(1)} %get-tuple-element.69), channel_id=1, source_target_pairs={{0,4},{1,5},{2,6},{3,7},{4,0},{5,1},{6,2},{7,3},{8,12},{9,13},{10,... | collective-permute-start | bytes 393224 | tf_op jit(solution)/shard_map/ppermute | solution.py:19
  54.4 10.8 %collective-permute-start.27 = (f32[256,128]{1,0:T(8,128)S(1)}, f32[256,128]{1,0:T(8,128)S(1)}, u32[]{:S(2)}, u32[]{:S(2)}) collective-permute-start(f32[256,128]{1,0:T(8,128)S(1)} %get-tuple-element.78), channel_id=1, source_target_pairs={{0,16},{8,24},{16,0},{24,8},{1,17},{9,25},{17,1},{25,9},{2,18},{10... | collective-permute-start | bytes 393224 | tf_op jit(solution)/shard_map/ppermute | solution.py:19
  56.4 10.1 %collective-permute-start.26 = (f32[256,128]{1,0:T(8,128)S(1)}, f32[256,128]{1,0:T(8,128)S(1)}, u32[]{:S(2)}, u32[]{:S(2)}) collective-permute-start(f32[256,128]{1,0:T(8,128)S(1)} %get-tuple-element.77), channel_id=1, source_target_pairs={{0,4},{1,5},{2,6},{3,7},{4,0},{5,1},{6,2},{7,3},{8,12},{9,13},{10,... | collective-permute-start | bytes 393224 | tf_op jit(solution)/shard_map/ppermute | solution.py:19
  59.4 8.4 %collective-permute-start.25 = (f32[256,128]{1,0:T(8,128)S(1)}, f32[256,128]{1,0:T(8,128)S(1)}, u32[]{:S(2)}, u32[]{:S(2)}) collective-permute-start(f32[256,128]{1,0:T(8,128)S(1)} %get-tuple-element.76), channel_id=1, source_target_pairs={{0,16},{8,24},{16,0},{24,8},{1,17},{9,25},{17,1},{25,9},{2,18},{10... | collective-permute-start | bytes 393224 | tf_op jit(solution)/shard_map/ppermute | solution.py:19
  60.3 11.7 %collective-permute-start.24 = (f32[256,128]{1,0:T(8,128)S(1)}, f32[256,128]{1,0:T(8,128)S(1)}, u32[]{:S(2)}, u32[]{:S(2)}) collective-permute-start(f32[256,128]{1,0:T(8,128)S(1)} %get-tuple-element.75), channel_id=1, source_target_pairs={{0,2},{1,3},{2,0},{3,1},{4,6},{5,7},{6,4},{7,5},{8,10},{9,11},{10,... | collective-permute-start | bytes 393224 | tf_op jit(solution)/shard_map/ppermute | solution.py:19
  65.9 7.8 %collective-permute-start.31 = (f32[256,128]{1,0:T(8,128)S(1)}, f32[256,128]{1,0:T(8,128)S(1)}, u32[]{:S(2)}, u32[]{:S(2)}) collective-permute-start(f32[256,128]{1,0:T(8,128)S(1)} %get-tuple-element.86), channel_id=1, source_target_pairs={{0,4},{1,5},{2,6},{3,7},{4,0},{5,1},{6,2},{7,3},{8,12},{9,13},{10,... | collective-permute-start | bytes 393224 | tf_op jit(solution)/shard_map/ppermute | solution.py:19
  66.8 8.7 %collective-permute-start.30 = (f32[256,128]{1,0:T(8,128)S(1)}, f32[256,128]{1,0:T(8,128)S(1)}, u32[]{:S(2)}, u32[]{:S(2)}) collective-permute-start(f32[256,128]{1,0:T(8,128)S(1)} %get-tuple-element.85), channel_id=1, source_target_pairs={{0,2},{1,3},{2,0},{3,1},{4,6},{5,7},{6,4},{7,5},{8,10},{9,11},{10,... | collective-permute-start | bytes 393224 | tf_op jit(solution)/shard_map/ppermute | solution.py:19
  68.5 10.4 %collective-permute-start.29 = (f32[256,128]{1,0:T(8,128)S(1)}, f32[256,128]{1,0:T(8,128)S(1)}, u32[]{:S(2)}, u32[]{:S(2)}) collective-permute-start(f32[256,128]{1,0:T(8,128)S(1)} %get-tuple-element.84), channel_id=1, source_target_pairs={{0,4},{1,5},{2,6},{3,7},{4,0},{5,1},{6,2},{7,3},{8,12},{9,13},{10,... | collective-permute-start | bytes 393224 | tf_op jit(solution)/shard_map/ppermute | solution.py:19
  72.3 7.0 %collective-permute-start.28 = (f32[256,128]{1,0:T(8,128)S(1)}, f32[256,128]{1,0:T(8,128)S(1)}, u32[]{:S(2)}, u32[]{:S(2)}) collective-permute-start(f32[256,128]{1,0:T(8,128)S(1)} %get-tuple-element.83), channel_id=1, source_target_pairs={{0,1},{1,0},{2,3},{3,2},{4,5},{5,4},{6,7},{7,6},{8,9},{9,8},{10,11... | collective-permute-start | bytes 393224 | tf_op jit(solution)/shard_map/ppermute | solution.py:19
  74.2 5.3 %collective-permute-start.35 = (f32[256,128]{1,0:T(8,128)S(1)}, f32[256,128]{1,0:T(8,128)S(1)}, u32[]{:S(2)}, u32[]{:S(2)}) collective-permute-start(f32[256,128]{1,0:T(8,128)S(1)} %get-tuple-element.94), channel_id=1, source_target_pairs={{0,2},{1,3},{2,0},{3,1},{4,6},{5,7},{6,4},{7,5},{8,10},{9,11},{10,... | collective-permute-start | bytes 393224 | tf_op jit(solution)/shard_map/ppermute | solution.py:19
  75.8 6.2 %collective-permute-start.34 = (f32[256,128]{1,0:T(8,128)S(1)}, f32[256,128]{1,0:T(8,128)S(1)}, u32[]{:S(2)}, u32[]{:S(2)}) collective-permute-start(f32[256,128]{1,0:T(8,128)S(1)} %get-tuple-element.93), channel_id=1, source_target_pairs={{0,1},{1,0},{2,3},{3,2},{4,5},{5,4},{6,7},{7,6},{8,9},{9,8},{10,11... | collective-permute-start | bytes 393224 | tf_op jit(solution)/shard_map/ppermute | solution.py:19
  79.3 5.0 %collective-permute-start.33 = (f32[256,128]{1,0:T(8,128)S(1)}, f32[256,128]{1,0:T(8,128)S(1)}, u32[]{:S(2)}, u32[]{:S(2)}) collective-permute-start(f32[256,128]{1,0:T(8,128)S(1)} %get-tuple-element.92), channel_id=1, source_target_pairs={{0,2},{1,3},{2,0},{3,1},{4,6},{5,7},{6,4},{7,5},{8,10},{9,11},{10,... | collective-permute-start | bytes 393224 | tf_op jit(solution)/shard_map/ppermute | solution.py:19
  79.4 5.3 %collective-permute-start.32 = (f32[256,128]{1,0:T(8,128)S(1)}, f32[256,128]{1,0:T(8,128)S(1)}, u32[]{:S(2)}, u32[]{:S(2)}) collective-permute-start(f32[256,128]{1,0:T(8,128)S(1)} %get-tuple-element.91), channel_id=1, source_target_pairs={{0,8},{8,0},{16,24},{24,16},{1,9},{9,1},{17,25},{25,17},{2,10},{10... | collective-permute-start | bytes 393224 | tf_op jit(solution)/shard_map/ppermute | solution.py:19
  79.8 6.0 %collective-permute-start.36 = (f32[256,128]{1,0:T(8,128)S(1)}, f32[256,128]{1,0:T(8,128)S(1)}, u32[]{:S(2)}, u32[]{:S(2)}) collective-permute-start(f32[256,128]{1,0:T(8,128)S(1)} %get-tuple-element.100), channel_id=1, source_target_pairs={{0,1},{1,0},{2,3},{3,2},{4,5},{5,4},{6,7},{7,6},{8,9},{9,8},{10,11... | collective-permute-start | bytes 393224 | tf_op jit(solution)/shard_map/ppermute | solution.py:19
  82.0 3.9 %collective-permute-start.39 = (f32[256,128]{1,0:T(8,128)S(1)}, f32[256,128]{1,0:T(8,128)S(1)}, u32[]{:S(2)}, u32[]{:S(2)}) collective-permute-start(f32[256,128]{1,0:T(8,128)S(1)} %get-tuple-element.104), channel_id=1, source_target_pairs={{0,8},{8,0},{16,24},{24,16},{1,9},{9,1},{17,25},{25,17},{2,10},{10... | collective-permute-start | bytes 393224 | tf_op jit(solution)/shard_map/ppermute | solution.py:19
  84.6 5.0 %collective-permute-start.38 = (f32[256,128]{1,0:T(8,128)S(1)}, f32[256,128]{1,0:T(8,128)S(1)}, u32[]{:S(2)}, u32[]{:S(2)}) collective-permute-start(f32[256,128]{1,0:T(8,128)S(1)} %get-tuple-element.103), channel_id=1, source_target_pairs={{0,1},{1,0},{2,3},{3,2},{4,5},{5,4},{6,7},{7,6},{8,9},{9,8},{10,11... | collective-permute-start | bytes 393224 | tf_op jit(solution)/shard_map/ppermute | solution.py:19
  85.8 4.0 %collective-permute-start.37 = (f32[256,128]{1,0:T(8,128)S(1)}, f32[256,128]{1,0:T(8,128)S(1)}, u32[]{:S(2)}, u32[]{:S(2)}) collective-permute-start(f32[256,128]{1,0:T(8,128)S(1)} %get-tuple-element.102), channel_id=1, source_target_pairs={{0,8},{8,0},{16,24},{24,16},{1,9},{9,1},{17,25},{25,17},{2,10},{10... | collective-permute-start | bytes 393224 | tf_op jit(solution)/shard_map/ppermute | solution.py:19
  89.7 1.4 %collective-permute-start.40 = (f32[256,128]{1,0:T(8,128)S(1)}, f32[256,128]{1,0:T(8,128)S(1)}, u32[]{:S(2)}, u32[]{:S(2)}) collective-permute-start(f32[256,128]{1,0:T(8,128)S(1)} %get-tuple-element.112), channel_id=1, source_target_pairs={{0,8},{8,0},{16,24},{24,16},{1,9},{9,1},{17,25},{25,17},{2,10},{10... | collective-permute-start | bytes 393224 | tf_op jit(solution)/shard_map/ppermute | solution.py:19
